TPU v7x, 32 devices: a whole 2x2x4 slice. The times are simulated.
32 devices in a mesh: row: 8 (over z, core), col: 4 (over y, x).
Axes of the slice: x: 2, y: 2, z: 4, core: 2. Of those that a mesh axis runs over, the one named last changes fastest.
Arguments:
- features: bfloat16 [4096, 768], P(('col', 'row')), may hold values from -6 to 6
- w_neigh: bfloat16 [768, 1024], replicated, may hold values from -0.875 to 0.875
- w_self: bfloat16 [768, 1024], replicated, may hold values from -0.21875 to 0.21875
- bias: float32 [1024], replicated, may hold values from -3 to 3
- cotangent: bfloat16 [4096, 1024], P(('row', 'col')), may hold values from -6 to 6
- block_rows: int32 [8, 4, 24], P('row', 'col'), may hold values from 0 to 3
- block_cols: int32 [8, 4, 24], P('row', 'col'), may hold values from 0 to 7
- block_vals: bfloat16 [8, 4, 24, 128, 128], P('row', 'col'), may hold values from 0 to 1, as said below
- block_count: int32 [8, 4], P('row', 'col'), may hold values from 6 to 24, as said below
Outputs:
- output: bfloat16 [4096, 1024], P(('row', 'col'))
- grad_input: bfloat16 [4096, 768], P(('col', 'row'))
- grad_self: float32 [768, 1024], replicated
- grad_neigh: float32 [768, 1024], replicated
- grad_bias: float32 [1024], replicated
Inputs may be any that keep to these rules, and one draw needn't show every extreme that they name: `block_vals`: block values are non-negative edge weights. `block_count`: some tile in every draw has all 24 slots live.
All inputs are finite; a program needn't handle non-finite values.
Results may differ from a plain program's by a relative error of at most 0.0053.
Values may be sent and summed in bfloat16 or wider, within the bound.
No kernel may reach another device: no remote copies, remote signals or barrier semaphores. Data moves between devices by JAX's collectives and lax.ppermute only.
A program may use at most 128 MiB of HBM per device.

v0:
```python
import math

import jax
import jax.numpy as jnp
from jax import lax
from jax.sharding import PartitionSpec as P


def block_term(
    block_vals, take_ids, put_ids, live_count, source, seg_count, flipped, start_slot, group_size
):
    chosen = lax.dynamic_slice_in_dim(block_vals, start_slot, group_size, 0)
    taken = lax.dynamic_slice_in_dim(take_ids, start_slot, group_size, 0)
    placed = lax.dynamic_slice_in_dim(put_ids, start_slot, group_size, 0)
    slot_ids = start_slot + jnp.arange(group_size, dtype=jnp.int32)
    live_mask = (slot_ids < live_count).astype(chosen.dtype)
    weights = chosen * live_mask[:, None, None]
    gathered = source[taken]
    pattern = "gji,gjw->giw" if flipped else "gij,gjw->giw"
    products = jnp.einsum(pattern, weights, gathered, preferred_element_type=jnp.float32)
    return jax.ops.segment_sum(products, placed, num_segments=seg_count)


def sparse_product(block_vals, take_ids, put_ids, live_count, source, seg_count, flipped):
    slot_total = block_vals.shape[0]
    group_size = min(8, slot_total)
    initial = jnp.zeros((seg_count, source.shape[1], source.shape[2]), jnp.float32)

    def advance(turn, accum):
        start_slot = (turn * group_size).astype(jnp.int32)
        return accum + block_term(
            block_vals,
            take_ids,
            put_ids,
            live_count,
            source,
            seg_count,
            flipped,
            start_slot,
            group_size,
        )

    return lax.fori_loop(0, slot_total // group_size, advance, initial)


def local(
    features, w_neigh, w_self, bias, cotangent, block_rows, block_cols, block_vals, block_count
):
    row_size = lax.axis_size("row")
    col_size = lax.axis_size("col")
    node_dev = features.shape[0]
    hidden_width = w_self.shape[1]
    values = block_vals[0, 0]
    row_ids = block_rows[0, 0]
    col_ids = block_cols[0, 0]
    live_count = block_count[0, 0]
    block_size = values.shape[1]
    slot_total = values.shape[0]
    rows_tile = node_dev * col_size
    cols_tile = node_dev * row_size
    row_index = lax.axis_index("row")
    col_index = lax.axis_index("col")
    owner_col = row_index * col_size // row_size
    is_self = (col_index == owner_col).astype(jnp.float32)
    offset = jnp.clip(row_index * rows_tile - col_index * cols_tile, 0, cols_tile - rows_tile)
    both_w = jnp.concatenate([w_neigh, w_self], axis=1)
    local_proj = jnp.dot(features, both_w, preferred_element_type=jnp.float32).astype(jnp.bfloat16)
    projected = lax.all_gather(local_proj, "row", axis=0, tiled=True)
    neigh_source = projected[:, :hidden_width].reshape(
        cols_tile // block_size, block_size, hidden_width
    )
    agg_part = sparse_product(
        values, col_ids, row_ids, live_count, neigh_source, rows_tile // block_size, False
    )
    agg_part = agg_part.reshape(rows_tile, hidden_width)
    own_rows = lax.dynamic_slice_in_dim(projected, offset, rows_tile, 0)[:, hidden_width:]
    live_mask = (jnp.arange(slot_total, dtype=jnp.int32) < live_count).astype(jnp.float32)
    row_mass = jnp.sum(values, axis=2, dtype=jnp.float32) * live_mask[:, None]
    row_sum = jax.ops.segment_sum(row_mass, row_ids, num_segments=rows_tile // block_size).reshape(
        rows_tile
    )
    self_part = own_rows.astype(jnp.float32) * is_self
    aggregate, own_term, degree = (
        lax.psum_scatter(agg_part, "col", scatter_dimension=0, tiled=True),
        lax.psum_scatter(self_part, "col", scatter_dimension=0, tiled=True),
        lax.psum_scatter(row_sum, "col", scatter_dimension=0, tiled=True),
    )
    inverse = 1.0 / (degree + 1.0)
    preact = own_term + aggregate * inverse[:, None] + bias
    output = jax.nn.elu(preact).astype(jnp.bfloat16)
    slopes = jnp.where(preact > 0, 1.0, jnp.exp(jnp.minimum(preact, 0.0)))
    grad_pre = cotangent.astype(jnp.float32) * slopes
    grad_round = grad_pre.astype(jnp.bfloat16)
    scaled = (grad_pre * inverse[:, None]).astype(jnp.bfloat16)
    group_scaled, group_grad = (
        lax.all_gather(scaled, "col", axis=0, tiled=True),
        lax.all_gather(grad_round, "col", axis=0, tiled=True),
    )
    back_source = group_scaled.reshape(rows_tile // block_size, block_size, hidden_width)
    back_part = sparse_product(
        values, row_ids, col_ids, live_count, back_source, cols_tile // block_size, True
    )
    back_part = back_part.reshape(cols_tile, hidden_width)
    self_back = jnp.zeros((cols_tile, hidden_width), jnp.float32)
    self_back = lax.dynamic_update_slice_in_dim(
        self_back, group_grad.astype(jnp.float32) * is_self, offset, 0
    )
    back_sum, self_sum = (
        lax.psum_scatter(back_part, "row", scatter_dimension=0, tiled=True),
        lax.psum_scatter(self_back, "row", scatter_dimension=0, tiled=True),
    )
    back = back_sum.astype(jnp.bfloat16)
    self_grad = self_sum.astype(jnp.bfloat16)
    part_self = jnp.einsum("nd,nh->dh", features, self_grad, preferred_element_type=jnp.float32)
    part_neigh = jnp.einsum("nd,nh->dh", features, back, preferred_element_type=jnp.float32)
    part_bias = jnp.sum(grad_pre, axis=0)
    total_self, total_neigh, total_bias = lax.psum(
        (part_self, part_neigh, part_bias), ("row", "col")
    )
    factor = 1.0 / math.sqrt(node_dev * row_size * col_size)
    grad_input = jnp.einsum("nh,dh->nd", self_grad, w_self, preferred_element_type=jnp.float32)
    grad_input = grad_input + jnp.einsum(
        "nh,dh->nd", back, w_neigh, preferred_element_type=jnp.float32
    )
    return (
        output,
        grad_input.astype(jnp.bfloat16),
        total_self * factor,
        total_neigh * (32.0 * factor),
        total_bias * factor,
    )


def solution(mesh):
    in_specs = (
        P(("col", "row"), None),
        P(),
        P(),
        P(),
        P(("row", "col"), None),
        P("row", "col", None),
        P("row", "col", None),
        P("row", "col", None, None, None),
        P("row", "col"),
    )
    out_specs = (P(("row", "col"), None), P(("col", "row"), None), P(), P(), P())
    return jax.shard_map(local, mesh=mesh, in_specs=in_specs, out_specs=out_specs, check_vma=False)
```

profile of v0, /device:TPU:0, one launch (start us, length us, event | category | flops | bytes accessed | tf_op | source)
XLA Modules:
  0.0 510.4 jit_solution(18326002514845060259)
XLA Ops:
  8.1 3.7 fusion.17
  11.9 50.6 %all-gather.4.cloned.1.call-done = bf16[1024,2048]{0,1:T(8,128)(2,1)} async-done(((bf16[128,2048]{0,1:T(8,128)(2,1)}), bf16[1024,2048]{0,1:T(8,128)(2,1)}) %all-gather.4.cloned.1.call-update) | async-done | bytes 4194320 | tf_op jit(solution)/shard_map/all_gather | solution.py:68
  71.2 43.6 %while.26 = (s32[]{:T(128)}, f32[4,128,1024]{2,1,0:T(8,128)S(1)}, s32[24]{0:T(128)S(1)}, bf16[24,128,128]{2,1,0:T(8,128)(2,1)S(1)}, s32[]{:T(128)}, /*index=5*/s...) while((s32[]{:T(128)}, f32[4,128,1024]{2,1,0:T(8,128)S(1)}, ...), condition=%wide.region_3.4_spmd, body=%wide.region_1.3_spmd.sunk | while | flops 269616192 | bytes 23335840 | solution.py:43
  75.6 4.3 fusion.52
  80.0 5.8 %scatter_fusion = f32[4,128,1024]{2,1,0:T(8,128)S(1)} fusion(f32[4,128,1024]{2,1,0:T(8,128)S(1)} %get-tuple-element.428, s32[8]{0:T(128)S(1)} %dynamic_slice.64, f32[8,128,1024]{2,1,0:T(8,128)} %fusion.52), kind=kCustom, calls=%fused_computation.2.clone.1 | custom fusion | flops 1048576 | bytes 12582944 | tf_op jit(solution)/shard_map/while/body/eval_jaxpr/scatter-add | solution.py:21
  90.1 4.4 fusion.52
  94.6 5.7 %scatter_fusion = f32[4,128,1024]{2,1,0:T(8,128)S(1)} fusion(f32[4,128,1024]{2,1,0:T(8,128)S(1)} %get-tuple-element.428, s32[8]{0:T(128)S(1)} %dynamic_slice.64, f32[8,128,1024]{2,1,0:T(8,128)} %fusion.52), kind=kCustom, calls=%fused_computation.2.clone.1 | custom fusion | flops 1048576 | bytes 12582944 | tf_op jit(solution)/shard_map/while/body/eval_jaxpr/scatter-add | solution.py:21
  104.7 4.3 fusion.52
  109.1 5.7 %scatter_fusion = f32[4,128,1024]{2,1,0:T(8,128)S(1)} fusion(f32[4,128,1024]{2,1,0:T(8,128)S(1)} %get-tuple-element.428, s32[8]{0:T(128)S(1)} %dynamic_slice.64, f32[8,128,1024]{2,1,0:T(8,128)} %fusion.52), kind=kCustom, calls=%fused_computation.2.clone.1 | custom fusion | flops 1048576 | bytes 12582944 | tf_op jit(solution)/shard_map/while/body/eval_jaxpr/scatter-add | solution.py:21
  120.1 10.3 %all-reduce = f32[512]{0:T(512)S(1)} all-reduce(f32[512]{0:T(512)S(1)} %bitcast.37), channel_id=4, replica_groups=mesh['row'=8,'col'=4] {'col'}, use_global_device_ids=true, to_apply=%region_7.8.clone | all-reduce | flops 512 | bytes 4096
  130.5 20.0 %reduce-scatter.7.cloned.1.call-done = f32[128,1024]{0,1:T(8,128)} async-done(((f32[512,1024]{0,1:T(8,128)}), f32[128,1024]{0,1:T(8,128)}) %reduce-scatter.7.cloned.1.call-update) | async-done | bytes 524304 | tf_op jit(solution)/shard_map/reduce_scatter | solution.py:84
  154.3 26.0 %all-gather.8.cloned.1.call-done = bf16[512,1024]{0,1:T(8,128)(2,1)} async-done(((bf16[128,1024]{0,1:T(8,128)(2,1)}), bf16[512,1024]{0,1:T(8,128)(2,1)}) %all-gather.8.cloned.1.call-update) | async-done | bytes 1048592 | tf_op jit(solution)/shard_map/all_gather | solution.py:96
  184.3 45.4 %while.27 = (s32[]{:T(128)}, f32[8,128,1024]{2,1,0:T(8,128)}, s32[24]{0:T(128)S(1)}, bf16[24,128,128]{1,2,0:T(8,128)(2,1)S(1)}, s32[]{:T(128)}, /*index=5*/s32[2...) while((s32[]{:T(128)}, f32[8,128,1024]{2,1,0:T(8,128)}, ...), condition=%wide.region_11.12_spmd, body=%wide.region_9.11_spmd.sunk | while | flops 269616192 | bytes 29626856 | solution.py:43
  186.5 3.7 fusion.55
  190.3 9.1 %scatter_fusion.1 = f32[8,128,1024]{2,1,0:T(8,128)} fusion(f32[8,128,1024]{2,1,0:T(8,128)} %get-tuple-element.461, s32[8]{0:T(128)S(1)} %dynamic_slice.67, f32[8,128,1024]{2,1,0:T(8,128)} %fusion.55), kind=kCustom, calls=%fused_computation.3.clone.1 | custom fusion | flops 1048576 | bytes 12582944 | tf_op jit(solution)/shard_map/while/body/eval_jaxpr/scatter-add | solution.py:21
  201.6 3.7 fusion.55
  205.4 9.1 %scatter_fusion.1 = f32[8,128,1024]{2,1,0:T(8,128)} fusion(f32[8,128,1024]{2,1,0:T(8,128)} %get-tuple-element.461, s32[8]{0:T(128)S(1)} %dynamic_slice.67, f32[8,128,1024]{2,1,0:T(8,128)} %fusion.55), kind=kCustom, calls=%fused_computation.3.clone.1 | custom fusion | flops 1048576 | bytes 12582944 | tf_op jit(solution)/shard_map/while/body/eval_jaxpr/scatter-add | solution.py:21
  220.4 9.3 %scatter_fusion.1 = f32[8,128,1024]{2,1,0:T(8,128)} fusion(f32[8,128,1024]{2,1,0:T(8,128)} %get-tuple-element.461, s32[8]{0:T(128)S(1)} %dynamic_slice.67, f32[8,128,1024]{2,1,0:T(8,128)} %fusion.55), kind=kCustom, calls=%fused_computation.3.clone.1 | custom fusion | flops 1048576 | bytes 12582944 | tf_op jit(solution)/shard_map/while/body/eval_jaxpr/scatter-add | solution.py:21
  233.9 10.4 %dynamic_update_slice.3 = f32[1024,1024]{0,1:T(8,128)} dynamic-update-slice(f32[1024,1024]{0,1:T(8,128)} %broadcast_in_dim.51, f32[512,1024]{0,1:T(8,128)S(1)} %convert_multiply_fusion, s32[]{:T(128)S(6)} %min.7, s32[]{:T(128)} %constant.109.clone.1) | dynamic-update-slice | bytes 4194308 | tf_op jit(solution)/shard_map/dynamic_update_slice | solution.py:105
  244.4 36.3 %reduce-scatter.11.cloned.1.call-done = f32[128,1024]{1,0:T(8,128)} async-done(((f32[1024,1024]{1,0:T(8,128)}), f32[128,1024]{1,0:T(8,128)}) %reduce-scatter.11.cloned.1.call-update) | async-done | bytes 524304 | tf_op jit(solution)/shard_map/reduce_scatter | solution.py:109
  283.9 47.2 %reduce-scatter.9.cloned.1.call-done = f32[128,1024]{0,1:T(8,128)} async-done(((f32[1024,1024]{0,1:T(8,128)}), f32[128,1024]{0,1:T(8,128)}) %reduce-scatter.9.cloned.1.call-update) | async-done | bytes 524304 | tf_op jit(solution)/shard_map/reduce_scatter | solution.py:110
  336.2 39.6 %psum.23 = f32[1024]{0:T(1024)S(1)} all-reduce(f32[1024]{0:T(1024)S(1)} %get-tuple-element.323), channel_id=1, replica_groups=mesh['row'=8,'col'=4] {'row','col'}, use_global_device_ids=true, to_apply=%region_16.17 | all-reduce | flops 1024 | bytes 8192 | tf_op jit(solution)/shard_map/psum | solution.py:117
  378.5 114.2 %all-reduce.4.cloned.1.call-done = (f32[768,1024]{0,1:T(8,128)}, f32[768,1024]{0,1:T(8,128)}) async-done(((f32[768,1024]{0,1:T(8,128)}, f32[768,1024]{0,1:T(8,128)}), (f32[768,1024]{0,1:T(8,128)}, f32[768,1024]{0,1:T(8,128)})) %all-reduce.4.cloned.1.call-update) | async-done | bytes 6291472 | tf_op jit(solution)/shard_map/psum | solution.py:117
  492.7 4.9 broadcast_multiply_fusion
  (112 shorter events, 66.3 us)
Async XLA Ops:
  7.2 0.9 copy-start
  7.2 55.3 %all-gather.4.cloned.1.call-start = ((), (), s32[]{:S(2)}) async-start(), calls=%async_computation.4 | async-start | bytes 4718592 | tf_op jit(solution)/shard_map/all_gather | solution.py:68
  11.8 118.7 %reduce-scatter.5.cloned.1.call-start = ((), (), s32[]{:S(2)}) async-start(), calls=%async_computation.5 | async-start | bytes 2621440 | tf_op jit(solution)/shard_map/reduce_scatter | solution.py:85
  65.7 84.7 %reduce-scatter.7.cloned.1.call-start = ((), (), s32[]{:S(2)}) async-start(), calls=%async_computation.6 | async-start | bytes 2621440 | tf_op jit(solution)/shard_map/reduce_scatter | solution.py:84
  65.8 1.6 slice-start
  69.9 1.3 copy-start.3
  69.9 1.3 copy-start.11
  69.9 1.3 copy-start.12
  116.7 1.1 copy-start.9
  116.7 2.2 copy-start.13
  116.7 33.8 %copy-start.10 = (f32[1024]{0:T(1024)S(1)}, f32[1024]{0:T(1024)}, u32[]{:S(2)}) copy-start(f32[1024]{0:T(1024)} %param.16) | copy-start | bytes 12292
  116.7 63.6 %all-gather.8.cloned.1.call-start = ((), (), s32[]{:S(2)}) async-start(), calls=%async_computation.9 | async-start | bytes 1310720 | tf_op jit(solution)/shard_map/all_gather | solution.py:96
  153.7 76.1 %all-gather.6.cloned.1.call-start = ((), (), s32[]{:S(2)}) async-start(), calls=%async_computation.7 | async-start | bytes 1310720 | tf_op jit(solution)/shard_map/all_gather | solution.py:97
  154.3 126.3 %reduce-scatter.11.cloned.1.call-start = ((), (), s32[]{:S(2)}) async-start(), calls=%async_computation.10 | async-start | bytes 4718592 | tf_op jit(solution)/shard_map/reduce_scatter | solution.py:109
  190.3 9.1 %copy-start.2 = (bf16[24,128,128]{1,2,0:T(8,128)(2,1)S(1)}, bf16[24,128,128]{1,2,0:T(8,128)(2,1)}, u32[]{:S(2)}) copy-start(bf16[24,128,128]{1,2,0:T(8,128)(2,1)} %copy-done.1) | copy-start | bytes 2359300 | tf_op jit(solution)/shard_map/while
  205.3 9.1 %copy-start.2 = (bf16[24,128,128]{1,2,0:T(8,128)(2,1)S(1)}, bf16[24,128,128]{1,2,0:T(8,128)(2,1)}, u32[]{:S(2)}) copy-start(bf16[24,128,128]{1,2,0:T(8,128)(2,1)} %copy-done.1) | copy-start | bytes 2359300 | tf_op jit(solution)/shard_map/while
  220.4 9.3 %copy-start.2 = (bf16[24,128,128]{1,2,0:T(8,128)(2,1)S(1)}, bf16[24,128,128]{1,2,0:T(8,128)(2,1)}, u32[]{:S(2)}) copy-start(bf16[24,128,128]{1,2,0:T(8,128)(2,1)} %copy-done.1) | copy-start | bytes 2359300 | tf_op jit(solution)/shard_map/while
  229.8 101.4 %reduce-scatter.9.cloned.1.call-start = ((), (), s32[]{:S(2)}) async-start(), calls=%async_computation.8 | async-start | bytes 4718592 | tf_op jit(solution)/shard_map/reduce_scatter | solution.py:110
  244.3 248.4 %all-reduce.4.cloned.1.call-start = ((), (), s32[]{:S(2)}) async-start(), calls=%async_computation.11 | async-start | bytes 12582912 | tf_op jit(solution)/shard_map/psum | solution.py:117
  334.4 0.9 copy-start.8
  334.4 42.0 %copy-start.4 = (f32[128,1024]{0,1:T(8,128)S(1)}, f32[128,1024]{0,1:T(8,128)}, u32[]{:S(2)}) copy-start(f32[128,1024]{0,1:T(8,128)} %reduce-scatter.9.cloned.1.call-done) | copy-start | bytes 1572868
  334.4 42.0 %copy-start.6 = (bf16[768,1024]{1,0:T(8,128)(2,1)S(1)}, bf16[768,1024]{1,0:T(8,128)(2,1)}, u32[]{:S(2)}) copy-start(bf16[768,1024]{1,0:T(8,128)(2,1)} %param.15) | copy-start | bytes 4718596
  334.4 42.6 %copy-start.5 = (f32[128,1024]{1,0:T(8,128)S(1)}, f32[128,1024]{1,0:T(8,128)}, u32[]{:S(2)}) copy-start(f32[128,1024]{1,0:T(8,128)} %reduce-scatter.11.cloned.1.call-done) | copy-start | bytes 1572868
  375.7 1.4 copy-start.7
  (3 other events, 2.6 us)
Sparse Core Ops, SparseCore 0:
  11.9 50.4 all-gather.3
  66.0 33.4 reduce-scatter.4
  116.8 33.5 reduce-scatter.6
  153.8 26.4 all-gather.7
  182.6 26.4 all-gather.5
  229.9 50.7 reduce-scatter.10
  282.9 48.1 reduce-scatter.8
  337.5 155.1 all-reduce.3
where the time goes:
time: 512 us; the launch traced here: 510 us
  waiting for transfers between devices  295 us (58%)
  other arithmetic  63.6 us (12%)
  blocking collectives  49.9 us (10%)
  local copies, waits for them, and re-layouts  49.7 us (10%)
  matrix products  36.3 us (7%)
  between operations  15.6 us (3%)
    psum x1, waiting for transfers between devices, local(): lax.psum((part_self, part_neigh, part_bias), ('row', 'col'))  114 us
    all_gather x1, waiting for transfers between devices, local(): projected = lax.all_gather(local_proj, 'row', axis=0, tiled=True)  50.6 us
    reduce_scatter x1, waiting for transfers between devices, local(): lax.psum_scatter(self_back, 'row', scatter_dimension=0, tiled=True)  47.2 us
    scatter-add x6, other arithmetic, block_term(): return jax.ops.segment_sum(products, placed, num_segments=seg_count)  44.8 us
    psum x1, blocking collectives, local(): lax.psum((part_self, part_neigh, part_bias), ('row', 'col'))  39.6 us
    reduce_scatter x1, waiting for transfers between devices, local(): lax.psum_scatter(back_part, 'row', scatter_dimension=0, tiled=True)  36.3 us
    all_gather x1, waiting for transfers between devices, local(): lax.all_gather(scaled, 'col', axis=0, tiled=True)  26 us
    dot_general x6, matrix products, block_term(): jnp.einsum(pattern, weights, gathered, preferred_element_type=jnp.float32)  24 us
  transfers between devices with their start and end apart: 8, of which 6 were waited for; matrix products, arithmetic and copies ran while one was open for 23% of the time, Pallas kernels for 0%

commit v1 on v0

v1 whole, which is shorter than its diff:
```python
import math

import jax
import jax.numpy as jnp
from jax import lax
from jax.experimental import pallas as pl
from jax.experimental.pallas import tpu as pltpu
from jax.sharding import PartitionSpec as P

F32 = jnp.float32
BF16 = jnp.bfloat16
LANES = 128
EXTRA = 16
VMEM = pl.BlockSpec(memory_space=pltpu.VMEM)
SMEM = pl.BlockSpec(memory_space=pltpu.SMEM)
PARAMS = pltpu.CompilerParams(vmem_limit_bytes=48 * 1024 * 1024)


def call(body, outs, args, scratch=(), smem=0, flops=0):
    moved = sum(math.prod(o.shape) * o.dtype.itemsize for o in outs)
    moved += sum(a.size * a.dtype.itemsize for a in args)
    return pl.pallas_call(
        body,
        out_shape=outs,
        in_specs=[SMEM] * smem + [VMEM] * (len(args) - smem),
        out_specs=[VMEM] * len(outs),
        scratch_shapes=list(scratch),
        compiler_params=PARAMS,
        cost_estimate=pl.CostEstimate(flops=flops, bytes_accessed=moved, transcendentals=0),
    )(*args)


def shape(dims, dtype):
    return jax.ShapeDtypeStruct(tuple(dims), dtype)


def mm(a, b, ca=1, cb=0):
    return lax.dot_general(a, b, (((ca,), (cb,)), ((), ())), preferred_element_type=F32)


def densify(rows, cols, count, values, nd, rs, cs):
    rt, ct, half = nd * cs, nd * rs, rs // 2

    def body(rows_ref, cols_ref, count_ref, values_ref, tile_ref, mass_ref, acc):
        i, j = lax.axis_index("row"), lax.axis_index("col")
        z, c = i // 2, lax.rem(i, 2)
        acc[...] = jnp.zeros_like(acc)

        def add(s, carry):
            row, col = rows_ref[s], cols_ref[s]
            row = lax.rem(row + cs - j, cs)
            turn = lax.rem(z + half - col // 2, half)
            col = jnp.where(lax.rem(col, 2) == c, turn, turn + half)
            r = pl.multiple_of(row * nd, nd)
            c0 = pl.multiple_of(col * nd, nd)
            acc[pl.ds(r, nd), pl.ds(c0, nd)] += values_ref[s].astype(F32)
            return carry

        lax.fori_loop(0, count_ref[0], add, 0)
        tile_ref[...] = acc[...].astype(BF16)
        ones = jnp.ones((8, ct), BF16)
        for k in range(cs):
            place = pl.multiple_of(lax.rem(j + k, cs) * nd, nd)
            mass_ref[:, pl.ds(place, nd)] = mm(ones, tile_ref[k * nd : (k + 1) * nd, :], 1, 1)

    return call(
        body,
        [shape((rt, ct), BF16), shape((8, rt), F32)],
        [rows, cols, count, values],
        [pltpu.VMEM((rt, ct), F32)],
        smem=3,
        flops=2 * 8 * rt * ct,
    )


def forward_parts(tile, blocks, nd, cs):
    width = blocks[0].shape[1]

    def body(*refs):
        tile_ref, feat_refs = refs[0], refs[1 : 1 + len(blocks)]
        outs = refs[1 + len(blocks) :]
        feats = jnp.concatenate([r[...] for r in feat_refs], axis=0)
        for k in range(cs):
            part = mm(tile_ref[k * nd : (k + 1) * nd, :], feats)
            outs[k][...] = part.astype(outs[k].dtype)

    return call(
        body,
        [shape((nd, width), BF16 if k else F32) for k in range(cs)],
        [tile, *blocks],
        flops=2 * tile.size * width,
    )


def activation(own, mean, w_neigh, bias, cotangent):
    nd, hid = own.shape

    def body(own_ref, mean_ref, w_ref, bias_ref, cot_ref, out_ref, grad_ref, sum_ref):
        pre = own_ref[...].astype(F32) + mm(mean_ref[...], w_ref[...]) + bias_ref[...]
        slope = jnp.where(pre > 0, 1.0, jnp.exp(jnp.minimum(pre, 0.0)))
        out_ref[...] = jnp.where(pre > 0, pre, slope - 1.0).astype(BF16)
        grad = cot_ref[...].astype(F32) * slope
        grad_ref[...] = grad.astype(BF16)
        sum_ref[...] = jnp.broadcast_to(jnp.sum(grad, axis=0, keepdims=True), (8, hid))

    return call(
        body,
        [shape((nd, hid), BF16), shape((nd, hid), BF16), shape((8, hid), F32)],
        [own, mean, w_neigh, bias, cotangent],
        flops=2 * mean.size * hid,
    )


def split_pair(total):
    high = total.astype(BF16).astype(F32)
    return jnp.concatenate([high, total - high], axis=0)


def weight_parts(xs, gs, sums, rs, xr, nc):
    cs = len(xs)
    nd, xw = xs[0].shape
    hid = gs[0].shape[1]
    half = rs // 2

    def body(*refs):
        x_refs, g_refs = refs[:cs], refs[cs : 2 * cs]
        sum_ref, keep_ref, send_ref, acc = refs[2 * cs :]
        x_all = jnp.concatenate([r[...] for r in x_refs], axis=0)
        g_all = jnp.concatenate([r[...] for r in g_refs], axis=0)
        acc[...] = mm(x_all, g_all, 0, 0)
        i = lax.axis_index("row")
        z, c = i // 2, lax.rem(i, 2)
        for k in range(half):
            for core, ref in ((c, keep_ref), (1 - c, send_ref)):
                q = 2 * lax.rem(z + k, half) + core
                row = pl.multiple_of((q // nc) * xr, xr)
                col = pl.multiple_of(lax.rem(q, nc) * LANES, LANES)
                ref[k, :xr, :] = acc[pl.ds(row, xr), pl.ds(col, LANES)].astype(ref.dtype)
                ref[k, xr:, :] = split_pair(sum_ref[:, pl.ds(col, LANES)]).astype(ref.dtype)

    dims = (half, xr + EXTRA, LANES)
    return call(
        body,
        [shape(dims, F32), shape(dims, BF16)],
        [*xs, *gs, sums],
        [pltpu.VMEM((xw, hid), F32)],
        flops=2 * cs * nd * xw * hid,
    )


def back_parts(tile, gs, inverse, w_neigh, nd, rs):
    cs = len(gs)
    rt = tile.shape[0]
    depth, hid = w_neigh.shape
    half = rs // 2

    def body(*refs):
        tile_ref, w_ref, inv_ref = refs[:3]
        g_refs = refs[3 : 3 + cs]
        keep_ref, send_ref, scaled = refs[3 + cs :]
        j = lax.axis_index("col")
        for k in range(cs):
            start = pl.multiple_of(lax.rem(j + cs - k, cs) * nd, nd)
            inv = inv_ref[pl.ds(start, nd), :]
            inv = jnp.concatenate([inv] * (depth // LANES), axis=1)
            product = mm(g_refs[k][...], w_ref[...], 1, 1) * inv
            place = (cs - k) % cs * nd
            scaled[place : place + nd, :] = product.astype(BF16)
        for ref, base in ((send_ref, half), (keep_ref, 0)):
            for k in range(half):
                place = (base + (half - k) % half) * nd
                cut = tile_ref[:, place : place + nd]
                ref[k] = mm(cut, scaled[...], 0, 0).astype(ref.dtype)

    dims = (half, nd, depth)
    return call(
        body,
        [shape(dims, F32), shape(dims, BF16)],
        [tile, w_neigh, inverse, *gs],
        [pltpu.VMEM((rt, depth), BF16)],
        flops=2 * rt * depth * (hid + nd * rs),
    )


def pair_sum(keep, came, paired):
    half, rows, width = keep.shape
    main = rows - EXTRA if paired else rows

    def body(keep_ref, came_ref, *outs):
        for k in range(half):
            total = keep_ref[k] + came_ref[k].astype(F32)
            dtype = outs[k].dtype
            outs[k][:main, :] = total[:main].astype(dtype)
            if paired:
                merged = total[main : main + 8] + total[main + 8 :]
                outs[k][main:, :] = split_pair(merged).astype(dtype)

    return call(
        body,
        [shape((rows, width), BF16 if k else F32) for k in range(half)],
        [keep, came],
    )


def last_sum(parts, paired, dtype=BF16):
    rows, width = parts[0].shape
    main = rows - EXTRA if paired else rows

    def body(*refs):
        out_ref = refs[-1]
        total = refs[0][...].astype(F32)
        for ref in refs[1:-1]:
            total = total + ref[...].astype(F32)
        out_ref[:main, :] = total[:main].astype(dtype)
        if paired:
            merged = total[main : main + 8] + total[main + 8 :]
            out_ref[main:, :] = split_pair(merged).astype(dtype)

    return call(body, [shape((rows, width), dtype)], parts)[0]


def assemble(mine, theirs, depth, hid, xr, nc, factors):
    cs, half = len(mine), mine[0].shape[0]
    xw = 2 * depth // cs
    side = cs // 2

    def body(*refs):
        groups = (refs[:cs], refs[cs : 2 * cs])
        self_ref, neigh_ref, bias_ref = refs[2 * cs :]
        i, j = lax.axis_index("row"), lax.axis_index("col")
        z, c = i // 2, lax.rem(i, 2)
        for group, core in zip(groups, (c, 1 - c)):
            for t in range(half):
                q = 2 * lax.rem(z + half - t, half) + core
                col = pl.multiple_of(lax.rem(q, nc) * LANES, LANES)
                turn = q // nc
                for k in range(cs):
                    owner = lax.rem(j + cs - k, cs)
                    row = pl.multiple_of(lax.rem(owner, side) * xw + turn * xr, xr)
                    chunk = group[k][t, :xr, :].astype(F32)

                    @pl.when(owner < side)
                    def _():
                        self_ref[pl.ds(row, xr), pl.ds(col, LANES)] = chunk * factors[0]

                    @pl.when(owner >= side)
                    def _():
                        neigh_ref[pl.ds(row, xr), pl.ds(col, LANES)] = chunk * factors[1]

                @pl.when(turn == 0)
                def _():
                    total = sum(group[k][t, xr:, :].astype(F32) for k in range(cs))
                    bias_ref[:, pl.ds(col, LANES)] = (total[:8] + total[8:]) * factors[0]

    weight = shape((depth, hid), F32)
    return call(body, [weight, weight, shape((8, hid), F32)], [*mine, *theirs])


def local(
    features, w_neigh, w_self, bias, cotangent, block_rows, block_cols, block_vals, block_count
):
    rs = lax.axis_size("row")
    cs = lax.axis_size("col")
    j = lax.axis_index("col")
    nd, depth = features.shape
    hid = w_self.shape[1]
    rt = nd * cs
    half = rs // 2
    xw = 2 * depth // cs
    nc = min(rs, hid // LANES)
    nr = rs // nc
    xr = xw // nr

    def along_col(x, k):
        return lax.ppermute(x, "col", [(s, (s + k) % cs) for s in range(cs)])

    def along_chips(x, k):
        return lax.ppermute(
            x, "row", [(s, 2 * ((s // 2 + k) % half) + s % 2) for s in range(rs)]
        )

    def other_core(x):
        return lax.ppermute(x, "row", [(s, s ^ 1) for s in range(rs)])

    swap = [((b % rs) * cs + b // rs, b) for b in range(rs * cs)]
    blocks = [features] + [along_chips(features, k) for k in range(1, half)]
    blocks = blocks + [other_core(x) for x in blocks]
    own_feat = lax.ppermute(features, ("row", "col"), swap)
    tile, mass = densify(
        block_rows.reshape(-1),
        block_cols.reshape(-1),
        block_count.reshape(-1),
        block_vals[0, 0],
        nd,
        rs,
        cs,
    )
    degree = mass
    for k in range(1, cs):
        degree = degree + along_col(mass, k)
    inverse = 1.0 / (degree[0] + 1.0)
    inverse = jnp.broadcast_to(inverse[:, None], (rt, LANES))
    own = jnp.dot(own_feat, w_self, preferred_element_type=F32).astype(BF16)

    parts = forward_parts(tile, blocks, nd, cs)
    aggregate = parts[0]
    for k in range(1, cs):
        aggregate = aggregate + along_col(parts[k], k).astype(F32)
    own_inverse = lax.dynamic_slice_in_dim(inverse, j * nd, nd, 0)
    mean = (aggregate * own_inverse[:, :1]).astype(BF16)
    output, grad, sums = activation(own, mean, w_neigh, bias[None, :], cotangent)
    both = jnp.concatenate([own_feat, mean], axis=1)

    def cut(k):
        return lax.dynamic_slice_in_dim(both, lax.rem(j + k, cs) * xw, xw, 1)

    xs = [cut(0)] + [along_col(cut(k), k) for k in range(1, cs)]
    gs = [grad] + [along_col(grad, k) for k in range(1, cs)]

    keep, send = weight_parts(xs, gs, sums, rs, xr, nc)
    chunks = pair_sum(keep, other_core(send), True)
    chunk = last_sum([chunks[0]] + [along_chips(chunks[k], k) for k in range(1, half)], True)
    line = jnp.stack([chunk] + [along_chips(chunk, k) for k in range(1, half)])
    mine = [line] + [along_col(line, k) for k in range(1, cs)]
    theirs = [other_core(x) for x in mine]

    keep, send = back_parts(tile, gs, inverse, w_neigh, nd, rs)
    blocks = pair_sum(keep, other_core(send), False)
    self_part = jnp.einsum("nh,dh->nd", grad, w_self, preferred_element_type=F32).astype(BF16)
    self_part = lax.ppermute(self_part, ("row", "col"), [(b, a) for a, b in swap])
    grad_input = last_sum(
        [blocks[0], self_part] + [along_chips(blocks[k], k) for k in range(1, half)], False
    )

    factor = 1.0 / math.sqrt(nd * rs * cs)
    total_self, total_neigh, total_bias = assemble(
        mine, theirs, depth, hid, xr, nc, (factor, 32.0 * factor)
    )
    return output, grad_input, total_self, total_neigh, total_bias[0]


def solution(mesh):
    in_specs = (
        P(("col", "row"), None),
        P(),
        P(),
        P(),
        P(("row", "col"), None),
        P("row", "col", None),
        P("row", "col", None),
        P("row", "col", None, None, None),
        P("row", "col"),
    )
    out_specs = (P(("row", "col"), None), P(("col", "row"), None), P(), P(), P())
    return jax.shard_map(local, mesh=mesh, in_specs=in_specs, out_specs=out_specs, check_vma=False)
```

time: 512 us -> 146 us (0.29)
  waiting for transfers between devices: 295 us -> 65.6 us
  other arithmetic: 63.6 us -> 0.34 us
  starting transfers between devices: 0.33 us -> 59.7 us
  blocking collectives: 49.9 us -> 0 us
  local copies, waits for them, and re-layouts: 49.7 us -> 4.11 us
  matrix products: 36.3 us -> 1.03 us
  between operations: 15.6 us -> 1.51 us
  Pallas kernels: 0 us -> 13.7 us
    psum x1 -> x0, waiting for transfers between devices: 114 us -> none  [local(): lax.psum((part_self, part_neigh, part_bias), ('row', 'col'))]
    reduce_scatter x4 -> x0, waiting for transfers between devices: 103 us -> none  [the longest x1 47.2 us: local(): lax.psum_scatter(self_back, 'row', scatter_dimension=0, tiled=True)]
    all_gather x3 -> x0, waiting for transfers between devices: 76.6 us -> none  [the longest x1 50.6 us: local(): projected = lax.all_gather(local_proj, 'row', axis=0, tiled=True)]
    ppermute x0 -> x39, waiting for transfers between devices: none -> 65.6 us  [the longest x12 38.2 us: along_chips(): lax.ppermute(x, 'row', [(s, 2 * ((s // 2 + k) % half) + s % 2) for s in r...]
    ppermute x0 -> x39, starting transfers between devices: none -> 59.7 us  [the longest x12 21.4 us: along_chips(): lax.ppermute(x, 'row', [(s, 2 * ((s // 2 + k) % half) + s % 2) for s in r...]
    scatter-add x7 -> x0, other arithmetic: 45.5 us -> none  [the longest x6 44.8 us: block_term(): return jax.ops.segment_sum(products, placed, num_segments=seg_count)]
    psum x1 -> x0, blocking collectives: 39.6 us -> none  [local(): lax.psum((part_self, part_neigh, part_bias), ('row', 'col'))]
    dot_general x11 -> x2, matrix products: 36.3 us -> 1.03 us  [the longest x1 0.65 us: local(): jnp.einsum('nh,dh->nd', grad, w_self, preferred_element_type=F32)]
  transfers between devices with their start and end apart: 8 -> 39, of which waited for: 6 -> 17; matrix products, arithmetic and copies ran while one was open for 23% -> 1% of each run, Pallas kernels for 0% -> 5%
where the time goes in v1:
time: 146 us
  waiting for transfers between devices  65.6 us (45%)
  starting transfers between devices  59.7 us (41%)
  Pallas kernels  13.7 us (9%)
  local copies, waits for them, and re-layouts  4.11 us (3%)
  between operations  1.51 us (1%)
    ppermute x12, waiting for transfers between devices, along_chips(): lax.ppermute(x, 'row', [(s, 2 * ((s // 2 + k) % half) + s % 2) for s in r...  38.2 us
    ppermute x15, waiting for transfers between devices, along_col(): return lax.ppermute(x, 'col', [(s, (s + k) % cs) for s in range(cs)])  26.2 us
    ppermute x12, starting transfers between devices, along_chips(): lax.ppermute(x, 'row', [(s, 2 * ((s // 2 + k) % half) + s % 2) for s in r...  21.4 us
    ppermute x15, starting transfers between devices, along_col(): return lax.ppermute(x, 'col', [(s, (s + k) % cs) for s in range(cs)])  18.5 us
    ppermute x10, starting transfers between devices, other_core(): return lax.ppermute(x, 'row', [(s, s ^ 1) for s in range(rs)])  17.5 us
    pallas_call x10, Pallas kernels, call(): pl.pallas_call(body, out_shape=outs, in_specs=[SMEM] * smem + [VMEM] * (l...  13.7 us
    unnamed x16, local copies, waits for them, and re-layouts  3.38 us
  transfers between devices with their start and end apart: 39, of which 17 were waited for; matrix products, arithmetic and copies ran while one was open for 1% of the time, Pallas kernels for 5%

profile of v1, /device:TPU:0, one launch (start us, length us, event | category | flops | bytes accessed | tf_op | source)
XLA Modules:
  0.0 145.9 jit_solution(643385560684631414)
XLA Ops:
  0.6 5.1 %collective-permute-start.3 = (bf16[128,768]{1,0:T(8,128)(2,1)}, bf16[128,768]{1,0:T(8,128)(2,1)S(1)}, u32[]{:S(2)}, u32[]{:S(2)}) collective-permute-start(bf16[128,768]{1,0:T(8,128)(2,1)} %refs_1_.2), channel_id=1, source_target_pairs={{0,24},{4,28},{8,0},{12,4},{16,8},{20,12},{24,16},{28,20},{1,25},{... | collective-permute-start | bytes 589832 | tf_op jit(solution)/shard_map/ppermute | solution.py:278
  11.1 2.8 %collective-permute-start.13 = (f32[8,512]{1,0:T(8,128)S(1)}, f32[8,512]{1,0:T(8,128)S(1)}, u32[]{:S(2)}, u32[]{:S(2)}) collective-permute-start(f32[8,512]{1,0:T(8,128)S(1)} %get-tuple-element.34), channel_id=1, source_target_pairs={{0,3},{1,0},{2,1},{3,2},{4,7},{5,4},{6,5},{7,6},{8,11},{9,8},{10,9... | collective-permute-start | bytes 49160 | tf_op jit(solution)/shard_map/ppermute | solution.py:275
  15.4 2.0 %collective-permute-start.11 = (f32[8,512]{1,0:T(8,128)S(1)}, f32[8,512]{1,0:T(8,128)S(1)}, u32[]{:S(2)}, u32[]{:S(2)}) collective-permute-start(f32[8,512]{1,0:T(8,128)S(1)} %get-tuple-element.34), channel_id=1, source_target_pairs={{0,1},{1,2},{2,3},{3,0},{4,5},{5,6},{6,7},{7,4},{8,9},{9,10},{10,1... | collective-permute-start | bytes 49160 | tf_op jit(solution)/shard_map/ppermute | solution.py:275
  20.8 7.1 %collective-permute-done.2.refs_3_ = bf16[128,768]{1,0:T(8,128)(2,1)S(1)} collective-permute-done((bf16[128,768]{1,0:T(8,128)(2,1)}, bf16[128,768]{1,0:T(8,128)(2,1)S(1)}, u32[]{:S(2)}, u32[]{:S(2)}) %collective-permute-start.2) | collective-permute-done | bytes 196640 | tf_op jit(solution)/shard_map/ppermute | solution.py:278
  35.0 5.3 %collective-permute-done.8 = bf16[128,768]{1,0:T(8,128)(2,1)S(1)} collective-permute-done((bf16[128,768]{1,0:T(8,128)(2,1)S(1)}, bf16[128,768]{1,0:T(8,128)(2,1)S(1)}, u32[]{:S(2)}, u32[]{:S(2)}) %collective-permute-start.8) | collective-permute-done | bytes 196640 | tf_op jit(solution)/shard_map/ppermute | solution.py:275
  40.3 3.5 %collective-permute-done.9 = bf16[128,768]{1,0:T(8,128)(2,1)S(1)} collective-permute-done((bf16[128,768]{1,0:T(8,128)(2,1)S(1)}, bf16[128,768]{1,0:T(8,128)(2,1)S(1)}, u32[]{:S(2)}, u32[]{:S(2)}) %collective-permute-start.9) | collective-permute-done | bytes 196640 | tf_op jit(solution)/shard_map/ppermute | solution.py:275
  45.1 2.0 %collective-permute-start.16 = (bf16[128,1024]{1,0:T(8,128)(2,1)S(1)}, bf16[128,1024]{1,0:T(8,128)(2,1)S(1)}, u32[]{:S(2)}, u32[]{:S(2)}) collective-permute-start(bf16[128,1024]{1,0:T(8,128)(2,1)S(1)} %get-tuple-element.36.refs_3_.refs_4_), channel_id=1, source_target_pairs={{0,3},{1,0},{2,1},{3,2},{4,7},{5,4},{6,5},{7,6},{8,11},{9,8},{10,9... | collective-permute-start | bytes 786440 | tf_op jit(solution)/shard_map/ppermute | solution.py:275
  48.2 2.1 %collective-permute-start.24 = (bf16[128,384]{1,0:T(8,128)(2,1)S(1)}, bf16[128,384]{1,0:T(8,128)(2,1)S(1)}, u32[]{:S(2)}, u32[]{:S(2)}) collective-permute-start(bf16[128,384]{1,0:T(8,128)(2,1)S(1)} %get-tuple-element.53), channel_id=1, source_target_pairs={{0,3},{1,0},{2,1},{3,2},{4,7},{5,4},{6,5},{7,6},{8,11},{9,8},{10,9... | collective-permute-start | bytes 294920 | tf_op jit(solution)/shard_map/ppermute | solution.py:275
  50.9 11.2 %collective-permute-done.24.refs_3_ = bf16[128,384]{1,0:T(8,128)(2,1)S(1)} collective-permute-done((bf16[128,384]{1,0:T(8,128)(2,1)S(1)}, bf16[128,384]{1,0:T(8,128)(2,1)S(1)}, u32[]{:S(2)}, u32[]{:S(2)}) %collective-permute-start.24) | collective-permute-done | bytes 98336 | tf_op jit(solution)/shard_map/ppermute | solution.py:275
  63.6 3.1 %collective-permute-done.23.refs_2_ = bf16[128,384]{1,0:T(8,128)(2,1)S(1)} collective-permute-done((bf16[128,384]{1,0:T(8,128)(2,1)S(1)}, bf16[128,384]{1,0:T(8,128)(2,1)S(1)}, u32[]{:S(2)}, u32[]{:S(2)}) %collective-permute-start.23) | collective-permute-done | bytes 98336 | tf_op jit(solution)/shard_map/ppermute | solution.py:275
  67.7 4.6 %shard_map.131 = (f32[4,128,768]{2,1,0:T(8,128)S(1)}, bf16[4,128,768]{2,1,0:T(8,128)(2,1)S(1)}) custom-call(bf16[512,1024]{1,0:T(8,128)(2,1)S(1)} %get-tuple-element.29.refs_0_, bf16[768,1024]{1,0:T(8,128)(2,1)} %refs_1_.3, f32[512,128]{1,0:T(8,128)S(1)} %broadcast_in_dim.10.refs_2_, bf16[128,1024]{1,0:T(8,128)(2,1)S(1)} %get-tuple-element.36.refs_3_.refs_4_, ...), custom_call_target="tpu_custom_call" | custom-call | flops 1610612736 | bytes 6291456 | tf_op jit(solution)/shard_map/pallas_call | solution.py:22
  73.3 1.9 %collective-permute-start.27 = (bf16[400,128]{1,0:T(8,128)(2,1)S(1)}, bf16[400,128]{1,0:T(8,128)(2,1)S(1)}, u32[]{:S(2)}, u32[]{:S(2)}) collective-permute-start(bf16[400,128]{1,0:T(8,128)(2,1)S(1)} %get-tuple-element.48), channel_id=1, source_target_pairs={{0,16},{4,20},{8,24},{12,28},{16,0},{20,4},{24,8},{28,12},{1,17},{... | collective-permute-start | bytes 307208 | tf_op jit(solution)/shard_map/ppermute | solution.py:278
  75.3 2.8 %collective-permute-start.28 = (bf16[400,128]{1,0:T(8,128)(2,1)S(1)}, bf16[400,128]{1,0:T(8,128)(2,1)S(1)}, u32[]{:S(2)}, u32[]{:S(2)}) collective-permute-start(bf16[400,128]{1,0:T(8,128)(2,1)S(1)} %get-tuple-element.49), channel_id=1, source_target_pairs={{0,24},{4,28},{8,0},{12,4},{16,8},{20,12},{24,16},{28,20},{1,25},{... | collective-permute-start | bytes 307208 | tf_op jit(solution)/shard_map/ppermute | solution.py:278
  78.1 2.5 %collective-permute-done.26.refs_1_ = bf16[400,128]{1,0:T(8,128)(2,1)S(1)} collective-permute-done((bf16[400,128]{1,0:T(8,128)(2,1)S(1)}, bf16[400,128]{1,0:T(8,128)(2,1)S(1)}, u32[]{:S(2)}, u32[]{:S(2)}) %collective-permute-start.26) | collective-permute-done | bytes 102432 | tf_op jit(solution)/shard_map/ppermute | solution.py:278
  80.6 3.5 %collective-permute-done.27.refs_2_ = bf16[400,128]{1,0:T(8,128)(2,1)S(1)} collective-permute-done((bf16[400,128]{1,0:T(8,128)(2,1)S(1)}, bf16[400,128]{1,0:T(8,128)(2,1)S(1)}, u32[]{:S(2)}, u32[]{:S(2)}) %collective-permute-start.27) | collective-permute-done | bytes 102432 | tf_op jit(solution)/shard_map/ppermute | solution.py:278
  84.1 3.4 %collective-permute-start.31 = (bf16[400,128]{1,0:T(8,128)(2,1)S(1)}, bf16[400,128]{1,0:T(8,128)(2,1)S(1)}, u32[]{:S(2)}, u32[]{:S(2)}) collective-permute-start(bf16[400,128]{1,0:T(8,128)(2,1)S(1)} %shard_map.136), channel_id=1, source_target_pairs={{0,24},{4,28},{8,0},{12,4},{16,8},{20,12},{24,16},{28,20},{1,25},{... | collective-permute-start | bytes 307208 | tf_op jit(solution)/shard_map/ppermute | solution.py:278
  88.2 2.7 %collective-permute-done.31 = bf16[400,128]{1,0:T(8,128)(2,1)S(1)} collective-permute-done((bf16[400,128]{1,0:T(8,128)(2,1)S(1)}, bf16[400,128]{1,0:T(8,128)(2,1)S(1)}, u32[]{:S(2)}, u32[]{:S(2)}) %collective-permute-start.31) | collective-permute-done | bytes 102432 | tf_op jit(solution)/shard_map/ppermute | solution.py:278
  90.9 5.5 %collective-permute-done.30 = bf16[400,128]{1,0:T(8,128)(2,1)S(1)} collective-permute-done((bf16[400,128]{1,0:T(8,128)(2,1)S(1)}, bf16[400,128]{1,0:T(8,128)(2,1)S(1)}, u32[]{:S(2)}, u32[]{:S(2)}) %collective-permute-start.30) | collective-permute-done | bytes 102432 | tf_op jit(solution)/shard_map/ppermute | solution.py:278
  96.5 2.6 %collective-permute-start.34 = (bf16[4,400,128]{2,1,0:T(8,128)(2,1)S(1)}, bf16[4,400,128]{2,1,0:T(8,128)(2,1)S(1)}, u32[]{:S(2)}, u32[]{:S(2)}) collective-permute-start(bf16[4,400,128]{2,1,0:T(8,128)(2,1)S(1)} %pad_maximum_fusion.refs_0_), channel_id=1, source_target_pairs={{0,3},{1,0},{2,1},{3,2},{4,7},{5,4},{6,5},{7,6},{8,11},{9,8},{10,9... | collective-permute-start | bytes 1228808 | tf_op jit(solution)/shard_map/ppermute | solution.py:275
  101.9 4.8 %collective-permute-start.19 = (bf16[128,768]{1,0:T(8,128)(2,1)S(1)}, bf16[128,768]{1,0:T(8,128)(2,1)S(1)}, u32[]{:S(2)}, u32[]{:S(2)}) collective-permute-start(bf16[128,768]{1,0:T(8,128)(2,1)S(1)} %get-tuple-element.40), channel_id=1, source_target_pairs={{0,8},{4,12},{8,16},{12,20},{16,24},{20,28},{24,0},{28,4},{1,9},{5... | collective-permute-start | bytes 589832 | tf_op jit(solution)/shard_map/ppermute | solution.py:278
  106.8 15.2 %collective-permute-start.35 = (bf16[4,400,128]{2,1,0:T(8,128)(2,1)S(1)}, bf16[4,400,128]{2,1,0:T(8,128)(2,1)S(1)}, u32[]{:S(2)}, u32[]{:S(2)}) collective-permute-start(bf16[4,400,128]{2,1,0:T(8,128)(2,1)S(1)} %pad_maximum_fusion.refs_0_), channel_id=1, source_target_pairs={{0,4},{4,0},{8,12},{12,8},{16,20},{20,16},{24,28},{28,24},{1,5},{5... | collective-permute-start | bytes 1228808 | tf_op jit(solution)/shard_map/ppermute | solution.py:283
  123.2 10.7 %collective-permute-done.20.refs_3_ = bf16[128,768]{1,0:T(8,128)(2,1)S(1)} collective-permute-done((bf16[128,768]{1,0:T(8,128)(2,1)S(1)}, bf16[128,768]{1,0:T(8,128)(2,1)S(1)}, u32[]{:S(2)}, u32[]{:S(2)}) %collective-permute-start.20) | collective-permute-done | bytes 196640 | tf_op jit(solution)/shard_map/ppermute | solution.py:278
  134.5 6.3 %collective-permute-done.21.refs_4_ = bf16[128,768]{1,0:T(8,128)(2,1)S(1)} collective-permute-done((bf16[128,768]{1,0:T(8,128)(2,1)S(1)}, bf16[128,768]{1,0:T(8,128)(2,1)S(1)}, u32[]{:S(2)}, u32[]{:S(2)}) %collective-permute-start.21) | collective-permute-done | bytes 196640 | tf_op jit(solution)/shard_map/ppermute | solution.py:278
  141.6 3.8 %shard_map.137 = (f32[768,1024]{1,0:T(8,128)}, f32[768,1024]{1,0:T(8,128)}, f32[8,1024]{1,0:T(8,128)S(1)}) custom-call(bf16[4,400,128]{2,1,0:T(8,128)(2,1)S(1)} %pad_maximum_fusion.refs_0_, bf16[4,400,128]{2,1,0:T(8,128)(2,1)S(1)} %collective-permute-done.32.refs_1_, bf16[4,400,128]{2,1,0:T(8,128)(2,1)S(1)} %collective-permute-done.33.refs_2_, ...), custom_call_target="tpu_custom_call" | custom-call | bytes 9601024 | tf_op jit(solution)/shard_map/pallas_call | solution.py:22
  (89 shorter events, 30.0 us)
Async XLA Ops:
  0.6 19.7 %collective-permute-start.3 = (bf16[128,768]{1,0:T(8,128)(2,1)}, bf16[128,768]{1,0:T(8,128)(2,1)S(1)}, u32[]{:S(2)}, u32[]{:S(2)}) collective-permute-start(bf16[128,768]{1,0:T(8,128)(2,1)} %refs_1_.2), channel_id=1, source_target_pairs={{0,24},{4,28},{8,0},{12,4},{16,8},{20,12},{24,16},{28,20},{1,25},{... | collective-permute-start | bytes 589832 | tf_op jit(solution)/shard_map/ppermute | solution.py:278
  5.8 22.2 %collective-permute-start.2 = (bf16[128,768]{1,0:T(8,128)(2,1)}, bf16[128,768]{1,0:T(8,128)(2,1)S(1)}, u32[]{:S(2)}, u32[]{:S(2)}) collective-permute-start(bf16[128,768]{1,0:T(8,128)(2,1)} %refs_1_.2), channel_id=1, source_target_pairs={{0,16},{4,20},{8,24},{12,28},{16,0},{20,4},{24,8},{28,12},{1,17},{... | collective-permute-start | bytes 589832 | tf_op jit(solution)/shard_map/ppermute | solution.py:278
  5.8 22.2 %collective-permute-start.1 = (bf16[128,768]{1,0:T(8,128)(2,1)}, bf16[128,768]{1,0:T(8,128)(2,1)S(1)}, u32[]{:S(2)}, u32[]{:S(2)}) collective-permute-start(bf16[128,768]{1,0:T(8,128)(2,1)} %refs_1_.2), channel_id=1, source_target_pairs={{0,8},{4,12},{8,16},{12,20},{16,24},{20,28},{24,0},{28,4},{1,9},{5... | collective-permute-start | bytes 589832 | tf_op jit(solution)/shard_map/ppermute | solution.py:278
  17.7 16.9 %collective-permute-start = (bf16[128,768]{1,0:T(8,128)(2,1)}, bf16[128,768]{1,0:T(8,128)(2,1)S(1)}, u32[]{:S(2)}, u32[]{:S(2)}) collective-permute-start(bf16[128,768]{1,0:T(8,128)(2,1)} %refs_1_.2), channel_id=1, source_target_pairs={{0,0},{4,1},{8,2},{12,3},{16,4},{20,5},{24,6},{28,7},{1,8},{5,9},{... | collective-permute-start | bytes 589832 | tf_op jit(solution)/shard_map/ppermute | solution.py:288
  33.0 10.8 %collective-permute-start.9 = (bf16[128,768]{1,0:T(8,128)(2,1)S(1)}, bf16[128,768]{1,0:T(8,128)(2,1)S(1)}, u32[]{:S(2)}, u32[]{:S(2)}) collective-permute-start(bf16[128,768]{1,0:T(8,128)(2,1)S(1)} %get-tuple-element.32), channel_id=1, source_target_pairs={{0,2},{1,3},{2,0},{3,1},{4,6},{5,7},{6,4},{7,5},{8,10},{9,11},{10,... | collective-permute-start | bytes 589832 | tf_op jit(solution)/shard_map/ppermute | solution.py:275
  33.0 10.7 %collective-permute-start.10 = (bf16[128,768]{1,0:T(8,128)(2,1)S(1)}, bf16[128,768]{1,0:T(8,128)(2,1)S(1)}, u32[]{:S(2)}, u32[]{:S(2)}) collective-permute-start(bf16[128,768]{1,0:T(8,128)(2,1)S(1)} %get-tuple-element.33), channel_id=1, source_target_pairs={{0,3},{1,0},{2,1},{3,2},{4,7},{5,4},{6,5},{7,6},{8,11},{9,8},{10,9... | collective-permute-start | bytes 589832 | tf_op jit(solution)/shard_map/ppermute | solution.py:275
  45.1 21.6 %collective-permute-start.16 = (bf16[128,1024]{1,0:T(8,128)(2,1)S(1)}, bf16[128,1024]{1,0:T(8,128)(2,1)S(1)}, u32[]{:S(2)}, u32[]{:S(2)}) collective-permute-start(bf16[128,1024]{1,0:T(8,128)(2,1)S(1)} %get-tuple-element.36.refs_3_.refs_4_), channel_id=1, source_target_pairs={{0,3},{1,0},{2,1},{3,2},{4,7},{5,4},{6,5},{7,6},{8,11},{9,8},{10,9... | collective-permute-start | bytes 786440 | tf_op jit(solution)/shard_map/ppermute | solution.py:275
  47.1 19.6 %collective-permute-start.15 = (bf16[128,1024]{1,0:T(8,128)(2,1)S(1)}, bf16[128,1024]{1,0:T(8,128)(2,1)S(1)}, u32[]{:S(2)}, u32[]{:S(2)}) collective-permute-start(bf16[128,1024]{1,0:T(8,128)(2,1)S(1)} %get-tuple-element.36.refs_3_.refs_4_), channel_id=1, source_target_pairs={{0,2},{1,3},{2,0},{3,1},{4,6},{5,7},{6,4},{7,5},{8,10},{9,11},{10,... | collective-permute-start | bytes 786440 | tf_op jit(solution)/shard_map/ppermute | solution.py:275
  47.1 19.5 %collective-permute-start.14 = (bf16[128,1024]{1,0:T(8,128)(2,1)S(1)}, bf16[128,1024]{1,0:T(8,128)(2,1)S(1)}, u32[]{:S(2)}, u32[]{:S(2)}) collective-permute-start(bf16[128,1024]{1,0:T(8,128)(2,1)S(1)} %get-tuple-element.36.refs_3_.refs_4_), channel_id=1, source_target_pairs={{0,1},{1,2},{2,3},{3,0},{4,5},{5,6},{6,7},{7,4},{8,9},{9,10},{10,1... | collective-permute-start | bytes 786440 | tf_op jit(solution)/shard_map/ppermute | solution.py:275
  48.2 13.9 %collective-permute-start.24 = (bf16[128,384]{1,0:T(8,128)(2,1)S(1)}, bf16[128,384]{1,0:T(8,128)(2,1)S(1)}, u32[]{:S(2)}, u32[]{:S(2)}) collective-permute-start(bf16[128,384]{1,0:T(8,128)(2,1)S(1)} %get-tuple-element.53), channel_id=1, source_target_pairs={{0,3},{1,0},{2,1},{3,2},{4,7},{5,4},{6,5},{7,6},{8,11},{9,8},{10,9... | collective-permute-start | bytes 294920 | tf_op jit(solution)/shard_map/ppermute | solution.py:275
  50.3 13.3 %collective-permute-start.22 = (bf16[128,384]{1,0:T(8,128)(2,1)S(1)}, bf16[128,384]{1,0:T(8,128)(2,1)S(1)}, u32[]{:S(2)}, u32[]{:S(2)}) collective-permute-start(bf16[128,384]{1,0:T(8,128)(2,1)S(1)} %get-tuple-element.55), channel_id=1, source_target_pairs={{0,1},{1,2},{2,3},{3,0},{4,5},{5,6},{6,7},{7,4},{8,9},{9,10},{10,1... | collective-permute-start | bytes 294920 | tf_op jit(solution)/shard_map/ppermute | solution.py:275
  72.3 29.5 %collective-permute-start.17 = (bf16[4,128,768]{2,1,0:T(8,128)(2,1)S(1)}, bf16[4,128,768]{2,1,0:T(8,128)(2,1)S(1)}, u32[]{:S(2)}, u32[]{:S(2)}) collective-permute-start(bf16[4,128,768]{2,1,0:T(8,128)(2,1)S(1)} %get-tuple-element.38), channel_id=1, source_target_pairs={{0,4},{4,0},{8,12},{12,8},{16,20},{20,16},{24,28},{28,24},{1,5},{5... | collective-permute-start | bytes 2359304 | tf_op jit(solution)/shard_map/ppermute | solution.py:283
  73.3 10.7 %collective-permute-start.27 = (bf16[400,128]{1,0:T(8,128)(2,1)S(1)}, bf16[400,128]{1,0:T(8,128)(2,1)S(1)}, u32[]{:S(2)}, u32[]{:S(2)}) collective-permute-start(bf16[400,128]{1,0:T(8,128)(2,1)S(1)} %get-tuple-element.48), channel_id=1, source_target_pairs={{0,16},{4,20},{8,24},{12,28},{16,0},{20,4},{24,8},{28,12},{1,17},{... | collective-permute-start | bytes 307208 | tf_op jit(solution)/shard_map/ppermute | solution.py:278
  75.3 8.8 %collective-permute-start.28 = (bf16[400,128]{1,0:T(8,128)(2,1)S(1)}, bf16[400,128]{1,0:T(8,128)(2,1)S(1)}, u32[]{:S(2)}, u32[]{:S(2)}) collective-permute-start(bf16[400,128]{1,0:T(8,128)(2,1)S(1)} %get-tuple-element.49), channel_id=1, source_target_pairs={{0,24},{4,28},{8,0},{12,4},{16,8},{20,12},{24,16},{28,20},{1,25},{... | collective-permute-start | bytes 307208 | tf_op jit(solution)/shard_map/ppermute | solution.py:278
  87.6 8.8 %collective-permute-start.30 = (bf16[400,128]{1,0:T(8,128)(2,1)S(1)}, bf16[400,128]{1,0:T(8,128)(2,1)S(1)}, u32[]{:S(2)}, u32[]{:S(2)}) collective-permute-start(bf16[400,128]{1,0:T(8,128)(2,1)S(1)} %shard_map.136), channel_id=1, source_target_pairs={{0,16},{4,20},{8,24},{12,28},{16,0},{20,4},{24,8},{28,12},{1,17},{... | collective-permute-start | bytes 307208 | tf_op jit(solution)/shard_map/ppermute | solution.py:278
  96.5 25.5 %collective-permute-start.34 = (bf16[4,400,128]{2,1,0:T(8,128)(2,1)S(1)}, bf16[4,400,128]{2,1,0:T(8,128)(2,1)S(1)}, u32[]{:S(2)}, u32[]{:S(2)}) collective-permute-start(bf16[4,400,128]{2,1,0:T(8,128)(2,1)S(1)} %pad_maximum_fusion.refs_0_), channel_id=1, source_target_pairs={{0,3},{1,0},{2,1},{3,2},{4,7},{5,4},{6,5},{7,6},{8,11},{9,8},{10,9... | collective-permute-start | bytes 1228808 | tf_op jit(solution)/shard_map/ppermute | solution.py:275
  99.0 23.0 %collective-permute-start.33 = (bf16[4,400,128]{2,1,0:T(8,128)(2,1)S(1)}, bf16[4,400,128]{2,1,0:T(8,128)(2,1)S(1)}, u32[]{:S(2)}, u32[]{:S(2)}) collective-permute-start(bf16[4,400,128]{2,1,0:T(8,128)(2,1)S(1)} %pad_maximum_fusion.refs_0_), channel_id=1, source_target_pairs={{0,2},{1,3},{2,0},{3,1},{4,6},{5,7},{6,4},{7,5},{8,10},{9,11},{10,... | collective-permute-start | bytes 1228808 | tf_op jit(solution)/shard_map/ppermute | solution.py:275
  100.4 22.1 %collective-permute-start.32 = (bf16[4,400,128]{2,1,0:T(8,128)(2,1)S(1)}, bf16[4,400,128]{2,1,0:T(8,128)(2,1)S(1)}, u32[]{:S(2)}, u32[]{:S(2)}) collective-permute-start(bf16[4,400,128]{2,1,0:T(8,128)(2,1)S(1)} %pad_maximum_fusion.refs_0_), channel_id=1, source_target_pairs={{0,1},{1,2},{2,3},{3,0},{4,5},{5,6},{6,7},{7,4},{8,9},{9,10},{10,1... | collective-permute-start | bytes 1228808 | tf_op jit(solution)/shard_map/ppermute | solution.py:275
  101.9 20.7 %collective-permute-start.19 = (bf16[128,768]{1,0:T(8,128)(2,1)S(1)}, bf16[128,768]{1,0:T(8,128)(2,1)S(1)}, u32[]{:S(2)}, u32[]{:S(2)}) collective-permute-start(bf16[128,768]{1,0:T(8,128)(2,1)S(1)} %get-tuple-element.40), channel_id=1, source_target_pairs={{0,8},{4,12},{8,16},{12,20},{16,24},{20,28},{24,0},{28,4},{1,9},{5... | collective-permute-start | bytes 589832 | tf_op jit(solution)/shard_map/ppermute | solution.py:278
  106.8 34.8 %collective-permute-start.35 = (bf16[4,400,128]{2,1,0:T(8,128)(2,1)S(1)}, bf16[4,400,128]{2,1,0:T(8,128)(2,1)S(1)}, u32[]{:S(2)}, u32[]{:S(2)}) collective-permute-start(bf16[4,400,128]{2,1,0:T(8,128)(2,1)S(1)} %pad_maximum_fusion.refs_0_), channel_id=1, source_target_pairs={{0,4},{4,0},{8,12},{12,8},{16,20},{20,16},{24,28},{28,24},{1,5},{5... | collective-permute-start | bytes 1228808 | tf_op jit(solution)/shard_map/ppermute | solution.py:283
  122.0 19.5 %collective-permute-start.38 = (bf16[4,400,128]{2,1,0:T(8,128)(2,1)S(1)}, bf16[4,400,128]{2,1,0:T(8,128)(2,1)S(1)}, u32[]{:S(2)}, u32[]{:S(2)}) collective-permute-start(bf16[4,400,128]{2,1,0:T(8,128)(2,1)S(1)} %collective-permute-done.34.refs_3_), channel_id=1, source_target_pairs={{0,4},{4,0},{8,12},{12,8},{16,20},{20,16},{24,28},{28,24},{1,5},{5... | collective-permute-start | bytes 1228808 | tf_op jit(solution)/shard_map/ppermute | solution.py:283
  122.0 19.5 %collective-permute-start.37 = (bf16[4,400,128]{2,1,0:T(8,128)(2,1)S(1)}, bf16[4,400,128]{2,1,0:T(8,128)(2,1)S(1)}, u32[]{:S(2)}, u32[]{:S(2)}) collective-permute-start(bf16[4,400,128]{2,1,0:T(8,128)(2,1)S(1)} %collective-permute-done.33.refs_2_), channel_id=1, source_target_pairs={{0,4},{4,0},{8,12},{12,8},{16,20},{20,16},{24,28},{28,24},{1,5},{5... | collective-permute-start | bytes 1228808 | tf_op jit(solution)/shard_map/ppermute | solution.py:283
  122.5 19.0 %collective-permute-start.36 = (bf16[4,400,128]{2,1,0:T(8,128)(2,1)S(1)}, bf16[4,400,128]{2,1,0:T(8,128)(2,1)S(1)}, u32[]{:S(2)}, u32[]{:S(2)}) collective-permute-start(bf16[4,400,128]{2,1,0:T(8,128)(2,1)S(1)} %collective-permute-done.32.refs_1_), channel_id=1, source_target_pairs={{0,4},{4,0},{8,12},{12,8},{16,20},{20,16},{24,28},{28,24},{1,5},{5... | collective-permute-start | bytes 1228808 | tf_op jit(solution)/shard_map/ppermute | solution.py:283
  122.6 11.3 %collective-permute-start.20 = (bf16[128,768]{1,0:T(8,128)(2,1)S(1)}, bf16[128,768]{1,0:T(8,128)(2,1)S(1)}, u32[]{:S(2)}, u32[]{:S(2)}) collective-permute-start(bf16[128,768]{1,0:T(8,128)(2,1)S(1)} %get-tuple-element.41), channel_id=1, source_target_pairs={{0,16},{4,20},{8,24},{12,28},{16,0},{20,4},{24,8},{28,12},{1,17},{... | collective-permute-start | bytes 589832 | tf_op jit(solution)/shard_map/ppermute | solution.py:278
  (23 other events, 156.9 us)

commit v2 on v1

v2 whole, which is shorter than its diff:
```python
import math

import jax
import jax.numpy as jnp
from jax import lax
from jax.experimental import pallas as pl
from jax.experimental.pallas import tpu as pltpu
from jax.sharding import PartitionSpec as P

F32 = jnp.float32
BF16 = jnp.bfloat16
LANES = 128
EXTRA = 16
VMEM = pl.BlockSpec(memory_space=pltpu.VMEM)
SMEM = pl.BlockSpec(memory_space=pltpu.SMEM)
PARAMS = pltpu.CompilerParams(vmem_limit_bytes=48 * 1024 * 1024)


def call(body, outs, args, scratch=(), smem=0, flops=0, after=()):
    count = len(args)
    moved = sum(math.prod(o.shape) * o.dtype.itemsize for o in outs)
    moved += sum(a.size * a.dtype.itemsize for a in args)

    def run(*refs):
        body(*refs[:count], *refs[count + len(after) :])

    return pl.pallas_call(
        run,
        out_shape=outs,
        in_specs=[SMEM] * smem
        + [VMEM] * (count - smem)
        + [pl.BlockSpec(memory_space=pl.ANY)] * len(after),
        out_specs=[VMEM] * len(outs),
        scratch_shapes=list(scratch),
        compiler_params=PARAMS,
        cost_estimate=pl.CostEstimate(flops=flops, bytes_accessed=moved, transcendentals=0),
    )(*args, *after)


def follow(x, after):
    def body(x_ref, out_ref):
        out_ref[...] = x_ref[...]

    return call(body, [shape(x.shape, x.dtype)], [x], after=after)[0]


def shape(dims, dtype):
    return jax.ShapeDtypeStruct(tuple(dims), dtype)


def mm(a, b, ca=1, cb=0):
    return lax.dot_general(a, b, (((ca,), (cb,)), ((), ())), preferred_element_type=F32)


def stack(parts, after):
    def body(*refs):
        for k, ref in enumerate(refs[:-1]):
            refs[-1][k] = ref[...]

    out = shape((len(parts), *parts[0].shape), parts[0].dtype)
    return call(body, [out], parts, after=after)[0]


def densify(rows, cols, count, values, nd, rs, cs):
    rt, ct, half = nd * cs, nd * rs, rs // 2

    def body(rows_ref, cols_ref, count_ref, values_ref, tile_ref, turned_ref, mass_ref, acc):
        i, j = lax.axis_index("row"), lax.axis_index("col")
        z, c = i // 2, lax.rem(i, 2)
        acc[...] = jnp.zeros_like(acc)

        def add(s, carry):
            row, col = rows_ref[s], cols_ref[s]
            row = lax.rem(row + cs - j, cs)
            turn = lax.rem(z + half - col // 2, half)
            col = jnp.where(lax.rem(col, 2) == c, turn, turn + half)
            r = pl.multiple_of(row * nd, nd)
            c0 = pl.multiple_of(col * nd, nd)
            acc[pl.ds(r, nd), pl.ds(c0, nd)] += values_ref[s].astype(F32)
            return carry

        lax.fori_loop(0, count_ref[0], add, 0)
        tile_ref[...] = acc[...].astype(BF16)
        for k in range(rs):
            cut = acc[:, k * nd : (k + 1) * nd]
            turned_ref[k * nd : (k + 1) * nd, :] = cut.T.astype(BF16)
        ones = jnp.ones((8, ct), BF16)
        for k in range(cs):
            place = pl.multiple_of(lax.rem(j + k, cs) * nd, nd)
            mass_ref[:, pl.ds(place, nd)] = mm(ones, tile_ref[k * nd : (k + 1) * nd, :], 1, 1)

    return call(
        body,
        [shape((rt, ct), BF16), shape((ct, rt), BF16), shape((8, rt), F32)],
        [rows, cols, count, values],
        [pltpu.VMEM((rt, ct), F32)],
        smem=3,
        flops=2 * 8 * rt * ct,
    )


def forward_parts(tile, blocks, nd, cs):
    width = blocks[0].shape[1]

    def body(*refs):
        tile_ref, feat_refs = refs[0], refs[1 : 1 + len(blocks)]
        outs = refs[1 + len(blocks) :]
        feats = jnp.concatenate([r[...] for r in feat_refs], axis=0)
        parts = mm(tile_ref[...], feats)
        for k in range(cs):
            outs[k][...] = parts[k * nd : (k + 1) * nd].astype(outs[k].dtype)

    return call(
        body,
        [shape((nd, width), BF16 if k else F32) for k in range(cs)],
        [tile, *blocks],
        flops=2 * tile.size * width,
    )


def activation(parts, inverse, own, own_feat, w_neigh, bias, cotangent):
    cs = len(parts)
    nd, hid = own.shape
    depth = own_feat.shape[1]
    xw = 2 * depth // cs

    def body(*refs):
        part_refs = refs[:cs]
        inv_ref, own_ref, feat_ref, w_ref, bias_ref, cot_ref = refs[cs : cs + 6]
        out_ref, sum_ref, *packs = refs[cs + 6 : -1]
        both = refs[-1]
        j = lax.axis_index("col")
        inv = inv_ref[pl.ds(pl.multiple_of(j * nd, nd), nd), :]
        total = sum(r[...].astype(F32) for r in part_refs)
        mean = (total * jnp.concatenate([inv] * (depth // LANES), axis=1)).astype(BF16)
        both[:, :depth] = feat_ref[...]
        both[:, depth:] = mean
        pre = own_ref[...].astype(F32) + mm(mean, w_ref[...]) + bias_ref[...]
        slope = jnp.where(pre > 0, 1.0, jnp.exp(jnp.minimum(pre, 0.0)))
        out_ref[...] = jnp.where(pre > 0, pre, slope - 1.0).astype(BF16)
        grad = cot_ref[...].astype(F32) * slope
        sum_ref[...] = jnp.broadcast_to(jnp.sum(grad, axis=0, keepdims=True), (8, hid))
        grad = grad.astype(BF16)
        for k in range(cs):
            packs[k][:, :hid] = grad
            target = lax.rem(j + k, cs)
            if xw % LANES == 0:
                start = pl.multiple_of(target * xw, LANES)
                packs[k][:, hid:] = both[:, pl.ds(start, xw)]
            else:
                for d in range(cs):

                    @pl.when(target == d)
                    def _():
                        packs[k][:, hid:] = both[:, d * xw : (d + 1) * xw]

    return call(
        body,
        [shape((nd, hid), BF16), shape((8, hid), F32)] + [shape((nd, hid + xw), BF16)] * cs,
        [*parts, inverse, own, own_feat, w_neigh, bias, cotangent],
        [pltpu.VMEM((nd, 2 * depth), BF16)],
        flops=2 * own_feat.size * hid,
    )


def split_pair(total):
    high = total.astype(BF16).astype(F32)
    return jnp.concatenate([high, total - high], axis=0)


def weight_parts(packs, sums, rs, xr, nc):
    cs = len(packs)
    hid = sums.shape[1]
    nd, xw = packs[0].shape[0], packs[0].shape[1] - hid
    half = rs // 2

    def body(*refs):
        pack_refs = refs[:cs]
        sum_ref, keep_ref, send_ref, acc = refs[cs:]
        x_all = jnp.concatenate([r[:, hid:] for r in pack_refs], axis=0)
        g_all = jnp.concatenate([r[:, :hid] for r in pack_refs], axis=0)
        acc[...] = mm(x_all, g_all, 0, 0)
        i = lax.axis_index("row")
        z, c = i // 2, lax.rem(i, 2)
        for k in range(half):
            for core, ref in ((c, keep_ref), (1 - c, send_ref)):
                q = 2 * lax.rem(z + k, half) + core
                row = pl.multiple_of((q // nc) * xr, xr)
                col = pl.multiple_of(lax.rem(q, nc) * LANES, LANES)
                ref[k, :xr, :] = acc[pl.ds(row, xr), pl.ds(col, LANES)].astype(ref.dtype)
                ref[k, xr:, :] = split_pair(sum_ref[:, pl.ds(col, LANES)]).astype(ref.dtype)

    dims = (half, xr + EXTRA, LANES)
    return call(
        body,
        [shape(dims, F32), shape(dims, BF16)],
        [*packs, sums],
        [pltpu.VMEM((xw, hid), F32)],
        flops=2 * cs * nd * xw * hid,
    )


def scaled_parts(packs, inverse, w_neigh, w_self, after):
    cs = len(packs)
    nd = packs[0].shape[0]
    depth, hid = w_neigh.shape

    def body(*refs):
        w_ref, ws_ref, inv_ref = refs[:3]
        pack_refs = refs[3 : 3 + cs]
        scaled_ref, self_ref = refs[3 + cs :]
        i, j = lax.axis_index("row"), lax.axis_index("col")
        grads = jnp.concatenate([pack_refs[(cs - r) % cs][:, :hid] for r in range(cs)], axis=0)
        product = mm(grads, w_ref[...], 1, 1)
        for r in range(cs):
            start = pl.multiple_of(lax.rem(j + r, cs) * nd, nd)
            inv = inv_ref[pl.ds(start, nd), :]
            inv = jnp.concatenate([inv] * (depth // LANES), axis=1)
            rows = slice(r * nd, (r + 1) * nd)
            scaled_ref[rows, :] = (product[rows] * inv).astype(BF16)

        @pl.when(i * cs // lax.axis_size("row") == j)
        def _():
            self_ref[...] = mm(grads, ws_ref[...], 1, 1)

        @pl.when(i * cs // lax.axis_size("row") != j)
        def _():
            self_ref[...] = jnp.zeros_like(self_ref)

    dims = (cs * nd, depth)
    return call(
        body,
        [shape(dims, BF16), shape(dims, F32)],
        [w_neigh, w_self, inverse, *packs],
        flops=2 * cs * nd * hid * depth,
        after=after,
    )


def back_parts(turned, scaled, self_part, nd, cs, rs, after):
    depth = scaled.shape[1]
    half = rs // 2

    def body(tile_ref, scaled_ref, self_ref, keep_ref, send_ref, acc):
        i, j = lax.axis_index("row"), lax.axis_index("col")
        z, c = i // 2, lax.rem(i, 2)
        acc[...] = mm(tile_ref[...], scaled_ref[...])

        @pl.when(i * cs // rs == j)
        def _():
            for r in range(cs):
                q = i * cs - j * rs + lax.rem(j + r, cs)
                turn = lax.rem(z + half - q // 2, half)
                place = jnp.where(lax.rem(q, 2) == c, turn, turn + half) * nd
                acc[pl.ds(pl.multiple_of(place, nd), nd), :] += self_ref[r * nd : (r + 1) * nd]

        for ref, base in ((send_ref, half), (keep_ref, 0)):
            for k in range(half):
                place = (base + (half - k) % half) * nd
                ref[k] = acc[place : place + nd, :].astype(ref.dtype)

    dims = (half, nd, depth)
    return call(
        body,
        [shape(dims, F32), shape(dims, BF16)],
        [turned, scaled, self_part],
        [pltpu.VMEM((rs * nd, depth), F32)],
        flops=2 * turned.size * depth,
        after=after,
    )


def pair_sum(keep, came, paired, after=()):
    half, rows, width = keep.shape
    main = rows - EXTRA if paired else rows

    def body(keep_ref, came_ref, *outs):
        for k in range(half):
            total = keep_ref[k] + came_ref[k].astype(F32)
            dtype = outs[k].dtype
            outs[k][:main, :] = total[:main].astype(dtype)
            if paired:
                merged = total[main : main + 8] + total[main + 8 :]
                outs[k][main:, :] = split_pair(merged).astype(dtype)

    return call(
        body,
        [shape((rows, width), BF16 if k else F32) for k in range(half)],
        [keep, came],
        after=after,
    )


def last_sum(parts, paired, dtype=BF16):
    rows, width = parts[0].shape
    main = rows - EXTRA if paired else rows

    def body(*refs):
        out_ref = refs[-1]
        total = refs[0][...].astype(F32)
        for ref in refs[1:-1]:
            total = total + ref[...].astype(F32)
        out_ref[:main, :] = total[:main].astype(dtype)
        if paired:
            merged = total[main : main + 8] + total[main + 8 :]
            out_ref[main:, :] = split_pair(merged).astype(dtype)

    return call(body, [shape((rows, width), dtype)], parts)[0]


def assemble(pieces, depth, hid, xr, nc, half, cs, factors, after):
    xw = 2 * depth // cs
    side = cs // 2

    def body(*refs):
        piece_refs = refs[: len(pieces)]
        self_ref, neigh_ref, bias_ref = refs[len(pieces) :]
        i, j = lax.axis_index("row"), lax.axis_index("col")
        z, c = i // 2, lax.rem(i, 2)
        bias_ref[...] = jnp.zeros_like(bias_ref)
        for ref, (array, first, owner_of, mine) in zip(piece_refs, pieces):
            owner = owner_of(j)
            for t in range(array.shape[0]):
                q = 2 * lax.rem(z + half - first - t, half) + (c if mine else 1 - c)
                col = pl.multiple_of(lax.rem(q, nc) * LANES, LANES)
                turn = q // nc
                row = pl.multiple_of(lax.rem(owner, side) * xw + turn * xr, xr)
                chunk = ref[t, :xr, :].astype(F32)

                @pl.when(owner < side)
                def _():
                    self_ref[pl.ds(row, xr), pl.ds(col, LANES)] = chunk * factors[0]

                @pl.when(owner >= side)
                def _():
                    neigh_ref[pl.ds(row, xr), pl.ds(col, LANES)] = chunk * factors[1]

                @pl.when(turn == 0)
                def _():
                    total = ref[t, xr:, :].astype(F32)
                    total = (total[:1] + total[8:9]) * factors[0]
                    bias_ref[:, pl.ds(col, LANES)] += total

    weight = shape((depth, hid), F32)
    outs = [weight, weight, shape((1, hid), F32)]
    return call(body, outs, [p[0] for p in pieces], after=after)


def local(
    features, w_neigh, w_self, bias, cotangent, block_rows, block_cols, block_vals, block_count
):
    rs = lax.axis_size("row")
    cs = lax.axis_size("col")
    nd, depth = features.shape
    hid = w_self.shape[1]
    rt = nd * cs
    half = rs // 2
    xw = 2 * depth // cs
    nc = min(rs, hid // LANES)
    nr = rs // nc
    xr = xw // nr

    def along_col(x, k):
        return lax.ppermute(x, "col", [(s, (s + k) % cs) for s in range(cs)])

    def along_chips(x, k):
        return lax.ppermute(
            x, "row", [(s, 2 * ((s // 2 + k) % half) + s % 2) for s in range(rs)]
        )

    def other_core(x):
        return lax.ppermute(x, "row", [(s, s ^ 1) for s in range(rs)])

    def from_shift(k):
        return lambda own: lax.rem(own + cs - k, cs)

    def from_flip(bits):
        return lambda own: own ^ bits

    def flip_col(x, bits):
        return lax.ppermute(x, "col", [(s, s ^ bits) for s in range(cs)])

    blocks = [features] + [along_chips(features, k) for k in range(1, half)]
    blocks = blocks + [other_core(x) for x in blocks]
    own_feat = lax.ppermute(
        follow(features, blocks[1:half]),
        ("row", "col"),
        [((b % rs) * cs + b // rs, b) for b in range(rs * cs)],
    )
    tile, turned, mass = densify(
        block_rows.reshape(-1),
        block_cols.reshape(-1),
        block_count.reshape(-1),
        block_vals[0, 0],
        nd,
        rs,
        cs,
    )
    degree = mass
    for k in range(1, cs):
        degree = degree + along_col(mass, k)
    inverse = 1.0 / (degree[0] + 1.0)
    inverse = jnp.broadcast_to(inverse[:, None], (rt, LANES))
    own = jnp.dot(own_feat, w_self, preferred_element_type=F32).astype(BF16)

    parts = forward_parts(tile, blocks, nd, cs)
    parts = [parts[0]] + [along_col(parts[k], k) for k in range(1, cs)]
    output, sums, *packs = activation(
        parts, inverse, own, own_feat, w_neigh, bias[None, :], cotangent
    )
    packs = [packs[0]] + [along_col(packs[k], k) for k in range(1, cs)]

    keep, send = weight_parts(packs, sums, rs, xr, nc)
    came = other_core(send)
    scaled, self_part = scaled_parts(packs, inverse, w_neigh, w_self, [keep])
    chunks = pair_sum(keep, came, True)
    chunk = last_sum([chunks[0]] + [along_chips(chunks[k], k) for k in range(1, half)], True)
    line = [chunk] + [along_chips(chunk, k) for k in range(1, half)]

    keep, send = back_parts(turned, scaled, self_part, nd, cs, rs, [chunks[1]])
    blocks = pair_sum(keep, other_core(send), False, line[1:])
    grad_input = last_sum(
        [blocks[0]] + [along_chips(blocks[k], k) for k in range(1, half)], False
    )

    line = stack(line, [blocks[1]])
    if cs == 4 and half % 2 == 0:
        first, second = flip_col(line, 1), flip_col(line, 2)
        mine = [
            (line, 0, from_flip(0)),
            (first, 0, from_flip(1)),
            (second, 0, from_flip(2)),
            (flip_col(first[: half // 2], 2), 0, from_flip(3)),
            (flip_col(second[half // 2 :], 1), half // 2, from_flip(3)),
        ]
    else:
        mine = [(line, 0, from_shift(0))]
        mine += [(along_col(line, k), 0, from_shift(k)) for k in range(1, cs)]
    pieces = [(*piece, True) for piece in mine]
    pieces += [(other_core(array), first, owner, False) for array, first, owner in mine]
    factor = 1.0 / math.sqrt(nd * rs * cs)
    total_self, total_neigh, total_bias = assemble(
        pieces, depth, hid, xr, nc, half, cs, (factor, 32.0 * factor), [grad_input]
    )
    return output, grad_input, total_self, total_neigh, total_bias.reshape(-1)


def solution(mesh):
    in_specs = (
        P(("col", "row"), None),
        P(),
        P(),
        P(),
        P(("row", "col"), None),
        P("row", "col", None),
        P("row", "col", None),
        P("row", "col", None, None, None),
        P("row", "col"),
    )
    out_specs = (P(("row", "col"), None), P(("col", "row"), None), P(), P(), P())
    return jax.shard_map(local, mesh=mesh, in_specs=in_specs, out_specs=out_specs, check_vma=False)
```

time: 146 us -> 124 us (0.85)
  starting transfers between devices: 59.7 us -> 42.2 us
  waiting for transfers between devices: 65.6 us -> 60.1 us
  Pallas kernels: 13.7 us -> 15.2 us
    ppermute x10 -> x11, starting transfers between devices: 17.5 us -> 4.65 us  [other_core(): return lax.ppermute(x, 'row', [(s, s ^ 1) for s in range(rs)])]
    ppermute x12, waiting for transfers between devices: 38.2 us -> 28.7 us  [along_chips(): lax.ppermute(x, 'row', [(s, 2 * ((s // 2 + k) % half) + s % 2) for s in r...]
    ppermute x2 -> x5, waiting for transfers between devices: 0.01 us -> 6.74 us  [the longest x4 6.73 us: flip_col(): return lax.ppermute(x, 'col', [(s, s ^ bits) for s in range(cs)])]
    ppermute x15 -> x9, waiting for transfers between devices: 26.2 us -> 22.7 us  [along_col(): return lax.ppermute(x, 'col', [(s, (s + k) % cs) for s in range(cs)])]
    ppermute x12, starting transfers between devices: 21.4 us -> 18 us  [along_chips(): lax.ppermute(x, 'row', [(s, 2 * ((s // 2 + k) % half) + s % 2) for s in r...]
    ppermute x15 -> x9, starting transfers between devices: 18.5 us -> 15.2 us  [along_col(): return lax.ppermute(x, 'col', [(s, (s + k) % cs) for s in range(cs)])]
    ppermute x2 -> x5, starting transfers between devices: 2.25 us -> 4.29 us  [the longest x4 3.48 us: flip_col(): return lax.ppermute(x, 'col', [(s, s ^ bits) for s in range(cs)])]
    pallas_call x10 -> x13, Pallas kernels: 13.7 us -> 15.2 us  [call(): pl.pallas_call(run, out_shape=outs, in_specs=[SMEM] * smem + [VMEM] * (co...]
  transfers between devices with their start and end apart: 39 -> 37, of which waited for: 17 -> 19; matrix products, arithmetic and copies ran while one was open for 1% -> 0% of each run, Pallas kernels for 5% -> 6%
where the time goes in v2:
time: 124 us
  waiting for transfers between devices  60.1 us (48%)
  starting transfers between devices  42.2 us (34%)
  Pallas kernels  15.2 us (12%)
  local copies, waits for them, and re-layouts  4.47 us (4%)
  between operations  1.5 us (1%)
    ppermute x12, waiting for transfers between devices, along_chips(): lax.ppermute(x, 'row', [(s, 2 * ((s // 2 + k) % half) + s % 2) for s in r...  28.7 us
    ppermute x9, waiting for transfers between devices, along_col(): return lax.ppermute(x, 'col', [(s, (s + k) % cs) for s in range(cs)])  22.7 us
    ppermute x12, starting transfers between devices, along_chips(): lax.ppermute(x, 'row', [(s, 2 * ((s // 2 + k) % half) + s % 2) for s in r...  18 us
    ppermute x9, starting transfers between devices, along_col(): return lax.ppermute(x, 'col', [(s, (s + k) % cs) for s in range(cs)])  15.2 us
    pallas_call x13, Pallas kernels, call(): pl.pallas_call(run, out_shape=outs, in_specs=[SMEM] * smem + [VMEM] * (co...  15.2 us
    ppermute x4, waiting for transfers between devices, flip_col(): return lax.ppermute(x, 'col', [(s, s ^ bits) for s in range(cs)])  6.73 us
    ppermute x11, starting transfers between devices, other_core(): return lax.ppermute(x, 'row', [(s, s ^ 1) for s in range(rs)])  4.65 us
    unnamed x20, local copies, waits for them, and re-layouts  4.32 us
  transfers between devices with their start and end apart: 37, of which 19 were waited for; matrix products, arithmetic and copies ran while one was open for 0% of the time, Pallas kernels for 6%

profile of v2, /device:TPU:0, one launch (start us, length us, event | category | flops | bytes accessed | tf_op | source)
XLA Modules:
  0.0 123.8 jit_solution(14969194192016159438)
XLA Ops:
  0.6 5.1 %collective-permute-start.2 = (bf16[128,768]{1,0:T(8,128)(2,1)}, bf16[128,768]{1,0:T(8,128)(2,1)S(1)}, u32[]{:S(2)}, u32[]{:S(2)}) collective-permute-start(bf16[128,768]{1,0:T(8,128)(2,1)} %refs_0_.2), channel_id=1, source_target_pairs={{0,24},{4,28},{8,0},{12,4},{16,8},{20,12},{24,16},{28,20},{1,25},{... | collective-permute-start | bytes 589832 | tf_op jit(solution)/shard_map/ppermute | solution.py:367
  9.8 1.8 %shard_map.128 = (bf16[512,1024]{1,0:T(8,128)(2,1)S(1)}, bf16[1024,512]{1,0:T(8,128)(2,1)S(1)}, f32[8,512]{1,0:T(8,128)S(1)}) custom-call(s32[24]{0:T(128)S(1)} %bitcast.12, s32[24]{0:T(128)S(1)} %bitcast.13, s32[1]{0:T(128)} %bitcast.9.refs_2_, bf16[24,128,128]{2,1,0:T(8,128)(2,1)S(1)} %bitcast.10), custom_call_target="tpu_custom_call" | custom-call | flops 8388608 | bytes 2900164 | tf_op jit(solution)/shard_map/pallas_call | solution.py:27
  11.7 2.3 %collective-permute-start.12 = (f32[8,512]{1,0:T(8,128)S(1)}, f32[8,512]{1,0:T(8,128)S(1)}, u32[]{:S(2)}, u32[]{:S(2)}) collective-permute-start(f32[8,512]{1,0:T(8,128)S(1)} %get-tuple-element.40), channel_id=1, source_target_pairs={{0,3},{1,0},{2,1},{3,2},{4,7},{5,4},{6,5},{7,6},{8,11},{9,8},{10,9... | collective-permute-start | bytes 49160 | tf_op jit(solution)/shard_map/ppermute | solution.py:364
  15.2 7.5 %collective-permute-done.1.refs_3_.refs_2_ = bf16[128,768]{1,0:T(8,128)(2,1)S(1)} collective-permute-done((bf16[128,768]{1,0:T(8,128)(2,1)}, bf16[128,768]{1,0:T(8,128)(2,1)S(1)}, u32[]{:S(2)}, u32[]{:S(2)}) %collective-permute-start.1) | collective-permute-done | bytes 196640 | tf_op jit(solution)/shard_map/ppermute | solution.py:367
  24.4 2.9 %collective-permute-start.6 = (bf16[128,768]{1,0:T(8,128)(2,1)S(1)}, bf16[128,768]{1,0:T(8,128)(2,1)S(1)}, u32[]{:S(2)}, u32[]{:S(2)}) collective-permute-start(bf16[128,768]{1,0:T(8,128)(2,1)S(1)} %collective-permute-done.2.refs_4_.refs_3_), channel_id=1, source_target_pairs={{0,4},{4,0},{8,12},{12,8},{16,20},{20,16},{24,28},{28,24},{1,5},{5... | collective-permute-start | bytes 589832 | tf_op jit(solution)/shard_map/ppermute | solution.py:372
  31.3 2.7 %collective-permute-start.8 = (bf16[128,768]{1,0:T(8,128)(2,1)S(1)}, bf16[128,768]{1,0:T(8,128)(2,1)S(1)}, u32[]{:S(2)}, u32[]{:S(2)}) collective-permute-start(bf16[128,768]{1,0:T(8,128)(2,1)S(1)} %get-tuple-element.38), channel_id=1, source_target_pairs={{0,2},{1,3},{2,0},{3,1},{4,6},{5,7},{6,4},{7,5},{8,10},{9,11},{10,... | collective-permute-start | bytes 589832 | tf_op jit(solution)/shard_map/ppermute | solution.py:364
  33.9 2.8 %collective-permute-start.9 = (bf16[128,768]{1,0:T(8,128)(2,1)S(1)}, bf16[128,768]{1,0:T(8,128)(2,1)S(1)}, u32[]{:S(2)}, u32[]{:S(2)}) collective-permute-start(bf16[128,768]{1,0:T(8,128)(2,1)S(1)} %get-tuple-element.39), channel_id=1, source_target_pairs={{0,3},{1,0},{2,1},{3,2},{4,7},{5,4},{6,5},{7,6},{8,11},{9,8},{10,9... | collective-permute-start | bytes 589832 | tf_op jit(solution)/shard_map/ppermute | solution.py:364
  37.2 3.6 %collective-permute-done.7.refs_1_ = bf16[128,768]{1,0:T(8,128)(2,1)S(1)} collective-permute-done((bf16[128,768]{1,0:T(8,128)(2,1)S(1)}, bf16[128,768]{1,0:T(8,128)(2,1)S(1)}, u32[]{:S(2)}, u32[]{:S(2)}) %collective-permute-start.7) | collective-permute-done | bytes 196640 | tf_op jit(solution)/shard_map/ppermute | solution.py:364
  40.8 4.3 %collective-permute-done.8.refs_2_ = bf16[128,768]{1,0:T(8,128)(2,1)S(1)} collective-permute-done((bf16[128,768]{1,0:T(8,128)(2,1)S(1)}, bf16[128,768]{1,0:T(8,128)(2,1)S(1)}, u32[]{:S(2)}, u32[]{:S(2)}) %collective-permute-start.8) | collective-permute-done | bytes 196640 | tf_op jit(solution)/shard_map/ppermute | solution.py:364
  47.8 3.1 %collective-permute-start.15 = (bf16[128,1408]{1,0:T(8,128)(2,1)S(1)}, bf16[128,1408]{1,0:T(8,128)(2,1)S(1)}, u32[]{:S(2)}, u32[]{:S(2)}) collective-permute-start(bf16[128,1408]{1,0:T(8,128)(2,1)S(1)} %get-tuple-element.45), channel_id=1, source_target_pairs={{0,2},{1,3},{2,0},{3,1},{4,6},{5,7},{6,4},{7,5},{8,10},{9,11},{10,... | collective-permute-start | bytes 1081352 | tf_op jit(solution)/shard_map/ppermute | solution.py:364
  52.0 7.6 %collective-permute-done.14.refs_1_.refs_4_ = bf16[128,1408]{1,0:T(8,128)(2,1)S(1)} collective-permute-done((bf16[128,1408]{1,0:T(8,128)(2,1)S(1)}, bf16[128,1408]{1,0:T(8,128)(2,1)S(1)}, u32[]{:S(2)}, u32[]{:S(2)}) %collective-permute-start.14) | collective-permute-done | bytes 360480 | tf_op jit(solution)/shard_map/ppermute | solution.py:364
  59.6 6.8 %collective-permute-done.15.refs_2_.refs_5_ = bf16[128,1408]{1,0:T(8,128)(2,1)S(1)} collective-permute-done((bf16[128,1408]{1,0:T(8,128)(2,1)S(1)}, bf16[128,1408]{1,0:T(8,128)(2,1)S(1)}, u32[]{:S(2)}, u32[]{:S(2)}) %collective-permute-start.15) | collective-permute-done | bytes 360480 | tf_op jit(solution)/shard_map/ppermute | solution.py:364
  67.3 3.9 %shard_map.133 = (bf16[512,768]{1,0:T(8,128)(2,1)S(1)}, f32[512,768]{1,0:T(8,128)S(1)}) custom-call(bf16[768,1024]{1,0:T(8,128)(2,1)} %refs_0_.3, bf16[768,1024]{1,0:T(8,128)(2,1)} %refs_1_.3, f32[512,128]{1,0:T(8,128)S(1)} %broadcast_in_dim.4.refs_4_.refs_2_, bf16[128,1408]{1,0:T(8,128)(2,1)S(1)} %get-tuple-element.43.refs_0_.refs_3_, ...), custom_call_target="tpu_custom_call" | custom-call | flops 805306368 | bytes 7208960 | tf_op jit(solution)/shard_map/pallas_call | solution.py:27
  73.2 1.9 %collective-permute-start.21 = (bf16[400,128]{1,0:T(8,128)(2,1)S(1)}, bf16[400,128]{1,0:T(8,128)(2,1)S(1)}, u32[]{:S(2)}, u32[]{:S(2)}) collective-permute-start(bf16[400,128]{1,0:T(8,128)(2,1)S(1)} %get-tuple-element.57), channel_id=1, source_target_pairs={{0,24},{4,28},{8,0},{12,4},{16,8},{20,12},{24,16},{28,20},{1,25},{... | collective-permute-start | bytes 307208 | tf_op jit(solution)/shard_map/ppermute | solution.py:367
  75.8 7.1 %collective-permute-done.20.refs_2_ = bf16[400,128]{1,0:T(8,128)(2,1)S(1)} collective-permute-done((bf16[400,128]{1,0:T(8,128)(2,1)S(1)}, bf16[400,128]{1,0:T(8,128)(2,1)S(1)}, u32[]{:S(2)}, u32[]{:S(2)}) %collective-permute-start.20) | collective-permute-done | bytes 102432 | tf_op jit(solution)/shard_map/ppermute | solution.py:367
  83.0 3.3 %collective-permute-start.24 = (bf16[400,128]{1,0:T(8,128)(2,1)S(1)}, bf16[400,128]{1,0:T(8,128)(2,1)S(1)}, u32[]{:S(2)}, u32[]{:S(2)}) collective-permute-start(bf16[400,128]{1,0:T(8,128)(2,1)S(1)} %shard_map.136.refs_0_), channel_id=1, source_target_pairs={{0,24},{4,28},{8,0},{12,4},{16,8},{20,12},{24,16},{28,20},{1,25},{... | collective-permute-start | bytes 307208 | tf_op jit(solution)/shard_map/ppermute | solution.py:367
  88.1 1.7 %collective-permute-done.24.refs_4_.refs_3_ = bf16[400,128]{1,0:T(8,128)(2,1)S(1)} collective-permute-done((bf16[400,128]{1,0:T(8,128)(2,1)S(1)}, bf16[400,128]{1,0:T(8,128)(2,1)S(1)}, u32[]{:S(2)}, u32[]{:S(2)}) %collective-permute-start.24) | collective-permute-done | bytes 102432 | tf_op jit(solution)/shard_map/ppermute | solution.py:367
  89.7 6.7 %collective-permute-done.23.refs_3_.refs_2_ = bf16[400,128]{1,0:T(8,128)(2,1)S(1)} collective-permute-done((bf16[400,128]{1,0:T(8,128)(2,1)S(1)}, bf16[400,128]{1,0:T(8,128)(2,1)S(1)}, u32[]{:S(2)}, u32[]{:S(2)}) %collective-permute-start.23) | collective-permute-done | bytes 102432 | tf_op jit(solution)/shard_map/ppermute | solution.py:367
  98.5 2.3 %collective-permute-start.26 = (bf16[128,768]{1,0:T(8,128)(2,1)S(1)}, bf16[128,768]{1,0:T(8,128)(2,1)S(1)}, u32[]{:S(2)}, u32[]{:S(2)}) collective-permute-start(bf16[128,768]{1,0:T(8,128)(2,1)S(1)} %get-tuple-element.60), channel_id=1, source_target_pairs={{0,16},{4,20},{8,24},{12,28},{16,0},{20,4},{24,8},{28,12},{1,17},{... | collective-permute-start | bytes 589832 | tf_op jit(solution)/shard_map/ppermute | solution.py:367
  102.8 4.5 %collective-permute-done.29.refs_2_ = bf16[4,400,128]{2,1,0:T(8,128)(2,1)S(1)} collective-permute-done((bf16[4,400,128]{2,1,0:T(8,128)(2,1)S(1)}, bf16[4,400,128]{2,1,0:T(8,128)(2,1)S(1)}, u32[]{:S(2)}, u32[]{:S(2)}) %collective-permute-start.29) | collective-permute-done | bytes 409632 | tf_op jit(solution)/shard_map/ppermute | solution.py:381
  108.6 2.8 %collective-permute-done.26.refs_2_ = bf16[128,768]{1,0:T(8,128)(2,1)S(1)} collective-permute-done((bf16[128,768]{1,0:T(8,128)(2,1)S(1)}, bf16[128,768]{1,0:T(8,128)(2,1)S(1)}, u32[]{:S(2)}, u32[]{:S(2)}) %collective-permute-start.26) | collective-permute-done | bytes 196640 | tf_op jit(solution)/shard_map/ppermute | solution.py:367
  112.1 2.8 %collective-permute-done.27.refs_3_ = bf16[128,768]{1,0:T(8,128)(2,1)S(1)} collective-permute-done((bf16[128,768]{1,0:T(8,128)(2,1)S(1)}, bf16[128,768]{1,0:T(8,128)(2,1)S(1)}, u32[]{:S(2)}, u32[]{:S(2)}) %collective-permute-start.27) | collective-permute-done | bytes 196640 | tf_op jit(solution)/shard_map/ppermute | solution.py:367
  115.5 2.0 %collective-permute-done.30.refs_3_ = bf16[2,400,128]{2,1,0:T(8,128)(2,1)S(1)} collective-permute-done((bf16[2,400,128]{2,1,0:T(8,128)(2,1)S(1)}, bf16[2,400,128]{2,1,0:T(8,128)(2,1)S(1)}, u32[]{:S(2)}, u32[]{:S(2)}) %collective-permute-start.30) | collective-permute-done | bytes 204832 | tf_op jit(solution)/shard_map/ppermute | solution.py:381
  119.9 3.9 %shard_map.140 = (f32[768,1024]{1,0:T(8,128)}, f32[768,1024]{1,0:T(8,128)}, f32[1,1024]{1,0:T(1,128)}) custom-call(bf16[4,400,128]{2,1,0:T(8,128)(2,1)S(1)} %shard_map.139.refs_0_, bf16[4,400,128]{2,1,0:T(8,128)(2,1)S(1)} %collective-permute-done.28.refs_1_, bf16[4,400,128]{2,1,0:T(8,128)(2,1)S(1)} %collective-permute-done.29.refs_2_, ...), custom_call_target="tpu_custom_call" | custom-call | bytes 9572352 | tf_op jit(solution)/shard_map/pallas_call | solution.py:27
  (88 shorter events, 28.8 us)
Async XLA Ops:
  0.6 13.7 %collective-permute-start.2 = (bf16[128,768]{1,0:T(8,128)(2,1)}, bf16[128,768]{1,0:T(8,128)(2,1)S(1)}, u32[]{:S(2)}, u32[]{:S(2)}) collective-permute-start(bf16[128,768]{1,0:T(8,128)(2,1)} %refs_0_.2), channel_id=1, source_target_pairs={{0,24},{4,28},{8,0},{12,4},{16,8},{20,12},{24,16},{28,20},{1,25},{... | collective-permute-start | bytes 589832 | tf_op jit(solution)/shard_map/ppermute | solution.py:367
  5.7 16.9 %collective-permute-start.1 = (bf16[128,768]{1,0:T(8,128)(2,1)}, bf16[128,768]{1,0:T(8,128)(2,1)S(1)}, u32[]{:S(2)}, u32[]{:S(2)}) collective-permute-start(bf16[128,768]{1,0:T(8,128)(2,1)} %refs_0_.2), channel_id=1, source_target_pairs={{0,16},{4,20},{8,24},{12,28},{16,0},{20,4},{24,8},{28,12},{1,17},{... | collective-permute-start | bytes 589832 | tf_op jit(solution)/shard_map/ppermute | solution.py:367
  5.7 16.9 %collective-permute-start = (bf16[128,768]{1,0:T(8,128)(2,1)}, bf16[128,768]{1,0:T(8,128)(2,1)S(1)}, u32[]{:S(2)}, u32[]{:S(2)}) collective-permute-start(bf16[128,768]{1,0:T(8,128)(2,1)} %refs_0_.2), channel_id=1, source_target_pairs={{0,8},{4,12},{8,16},{12,20},{16,24},{20,28},{24,0},{28,4},{1,9},{5... | collective-permute-start | bytes 589832 | tf_op jit(solution)/shard_map/ppermute | solution.py:367
  11.7 12.8 %collective-permute-start.12 = (f32[8,512]{1,0:T(8,128)S(1)}, f32[8,512]{1,0:T(8,128)S(1)}, u32[]{:S(2)}, u32[]{:S(2)}) collective-permute-start(f32[8,512]{1,0:T(8,128)S(1)} %get-tuple-element.40), channel_id=1, source_target_pairs={{0,3},{1,0},{2,1},{3,2},{4,7},{5,4},{6,5},{7,6},{8,11},{9,8},{10,9... | collective-permute-start | bytes 49160 | tf_op jit(solution)/shard_map/ppermute | solution.py:364
  13.9 13.4 %collective-permute-start.11 = (f32[8,512]{1,0:T(8,128)S(1)}, f32[8,512]{1,0:T(8,128)S(1)}, u32[]{:S(2)}, u32[]{:S(2)}) collective-permute-start(f32[8,512]{1,0:T(8,128)S(1)} %get-tuple-element.40), channel_id=1, source_target_pairs={{0,2},{1,3},{2,0},{3,1},{4,6},{5,7},{6,4},{7,5},{8,10},{9,11},{10,... | collective-permute-start | bytes 49160 | tf_op jit(solution)/shard_map/ppermute | solution.py:364
  14.3 13.1 %collective-permute-start.10 = (f32[8,512]{1,0:T(8,128)S(1)}, f32[8,512]{1,0:T(8,128)S(1)}, u32[]{:S(2)}, u32[]{:S(2)}) collective-permute-start(f32[8,512]{1,0:T(8,128)S(1)} %get-tuple-element.40), channel_id=1, source_target_pairs={{0,1},{1,2},{2,3},{3,0},{4,5},{5,6},{6,7},{7,4},{8,9},{9,10},{10,1... | collective-permute-start | bytes 49160 | tf_op jit(solution)/shard_map/ppermute | solution.py:364
  23.6 13.2 %collective-permute-start.13 = (bf16[128,768]{1,0:T(8,128)(2,1)S(1)}, bf16[128,768]{1,0:T(8,128)(2,1)S(1)}, u32[]{:S(2)}, u32[]{:S(2)}) collective-permute-start(bf16[128,768]{1,0:T(8,128)(2,1)S(1)} %shard_map.130), channel_id=1, source_target_pairs={{0,0},{4,1},{8,2},{12,3},{16,4},{20,5},{24,6},{28,7},{1,8},{5,9},{... | collective-permute-start | bytes 589832 | tf_op jit(solution)/shard_map/ppermute | solution.py:385
  30.1 10.7 %collective-permute-start.7 = (bf16[128,768]{1,0:T(8,128)(2,1)S(1)}, bf16[128,768]{1,0:T(8,128)(2,1)S(1)}, u32[]{:S(2)}, u32[]{:S(2)}) collective-permute-start(bf16[128,768]{1,0:T(8,128)(2,1)S(1)} %get-tuple-element.37), channel_id=1, source_target_pairs={{0,1},{1,2},{2,3},{3,0},{4,5},{5,6},{6,7},{7,4},{8,9},{9,10},{10,1... | collective-permute-start | bytes 589832 | tf_op jit(solution)/shard_map/ppermute | solution.py:364
  31.3 13.8 %collective-permute-start.8 = (bf16[128,768]{1,0:T(8,128)(2,1)S(1)}, bf16[128,768]{1,0:T(8,128)(2,1)S(1)}, u32[]{:S(2)}, u32[]{:S(2)}) collective-permute-start(bf16[128,768]{1,0:T(8,128)(2,1)S(1)} %get-tuple-element.38), channel_id=1, source_target_pairs={{0,2},{1,3},{2,0},{3,1},{4,6},{5,7},{6,4},{7,5},{8,10},{9,11},{10,... | collective-permute-start | bytes 589832 | tf_op jit(solution)/shard_map/ppermute | solution.py:364
  33.9 11.6 %collective-permute-start.9 = (bf16[128,768]{1,0:T(8,128)(2,1)S(1)}, bf16[128,768]{1,0:T(8,128)(2,1)S(1)}, u32[]{:S(2)}, u32[]{:S(2)}) collective-permute-start(bf16[128,768]{1,0:T(8,128)(2,1)S(1)} %get-tuple-element.39), channel_id=1, source_target_pairs={{0,3},{1,0},{2,1},{3,2},{4,7},{5,4},{6,5},{7,6},{8,11},{9,8},{10,9... | collective-permute-start | bytes 589832 | tf_op jit(solution)/shard_map/ppermute | solution.py:364
  46.9 12.7 %collective-permute-start.14 = (bf16[128,1408]{1,0:T(8,128)(2,1)S(1)}, bf16[128,1408]{1,0:T(8,128)(2,1)S(1)}, u32[]{:S(2)}, u32[]{:S(2)}) collective-permute-start(bf16[128,1408]{1,0:T(8,128)(2,1)S(1)} %get-tuple-element.44), channel_id=1, source_target_pairs={{0,1},{1,2},{2,3},{3,0},{4,5},{5,6},{6,7},{7,4},{8,9},{9,10},{10,1... | collective-permute-start | bytes 1081352 | tf_op jit(solution)/shard_map/ppermute | solution.py:364
  47.8 18.6 %collective-permute-start.15 = (bf16[128,1408]{1,0:T(8,128)(2,1)S(1)}, bf16[128,1408]{1,0:T(8,128)(2,1)S(1)}, u32[]{:S(2)}, u32[]{:S(2)}) collective-permute-start(bf16[128,1408]{1,0:T(8,128)(2,1)S(1)} %get-tuple-element.45), channel_id=1, source_target_pairs={{0,2},{1,3},{2,0},{3,1},{4,6},{5,7},{6,4},{7,5},{8,10},{9,11},{10,... | collective-permute-start | bytes 1081352 | tf_op jit(solution)/shard_map/ppermute | solution.py:364
  50.9 15.5 %collective-permute-start.16 = (bf16[128,1408]{1,0:T(8,128)(2,1)S(1)}, bf16[128,1408]{1,0:T(8,128)(2,1)S(1)}, u32[]{:S(2)}, u32[]{:S(2)}) collective-permute-start(bf16[128,1408]{1,0:T(8,128)(2,1)S(1)} %get-tuple-element.46), channel_id=1, source_target_pairs={{0,3},{1,0},{2,1},{3,2},{4,7},{5,4},{6,5},{7,6},{8,11},{9,8},{10,9... | collective-permute-start | bytes 1081352 | tf_op jit(solution)/shard_map/ppermute | solution.py:364
  72.7 23.8 %collective-permute-start.18 = (bf16[4,128,768]{2,1,0:T(8,128)(2,1)S(1)}, bf16[4,128,768]{2,1,0:T(8,128)(2,1)S(1)}, u32[]{:S(2)}, u32[]{:S(2)}) collective-permute-start(bf16[4,128,768]{2,1,0:T(8,128)(2,1)S(1)} %get-tuple-element.54), channel_id=1, source_target_pairs={{0,4},{4,0},{8,12},{12,8},{16,20},{20,16},{24,28},{28,24},{1,5},{5... | collective-permute-start | bytes 2359304 | tf_op jit(solution)/shard_map/ppermute | solution.py:372
  73.2 9.6 %collective-permute-start.20 = (bf16[400,128]{1,0:T(8,128)(2,1)S(1)}, bf16[400,128]{1,0:T(8,128)(2,1)S(1)}, u32[]{:S(2)}, u32[]{:S(2)}) collective-permute-start(bf16[400,128]{1,0:T(8,128)(2,1)S(1)} %get-tuple-element.56), channel_id=1, source_target_pairs={{0,16},{4,20},{8,24},{12,28},{16,0},{20,4},{24,8},{28,12},{1,17},{... | collective-permute-start | bytes 307208 | tf_op jit(solution)/shard_map/ppermute | solution.py:367
  73.2 9.7 %collective-permute-start.21 = (bf16[400,128]{1,0:T(8,128)(2,1)S(1)}, bf16[400,128]{1,0:T(8,128)(2,1)S(1)}, u32[]{:S(2)}, u32[]{:S(2)}) collective-permute-start(bf16[400,128]{1,0:T(8,128)(2,1)S(1)} %get-tuple-element.57), channel_id=1, source_target_pairs={{0,24},{4,28},{8,0},{12,4},{16,8},{20,12},{24,16},{28,20},{1,25},{... | collective-permute-start | bytes 307208 | tf_op jit(solution)/shard_map/ppermute | solution.py:367
  86.3 10.1 %collective-permute-start.23 = (bf16[400,128]{1,0:T(8,128)(2,1)S(1)}, bf16[400,128]{1,0:T(8,128)(2,1)S(1)}, u32[]{:S(2)}, u32[]{:S(2)}) collective-permute-start(bf16[400,128]{1,0:T(8,128)(2,1)S(1)} %shard_map.136.refs_0_), channel_id=1, source_target_pairs={{0,16},{4,20},{8,24},{12,28},{16,0},{20,4},{24,8},{28,12},{1,17},{... | collective-permute-start | bytes 307208 | tf_op jit(solution)/shard_map/ppermute | solution.py:367
  87.1 9.4 %collective-permute-start.22 = (bf16[400,128]{1,0:T(8,128)(2,1)S(1)}, bf16[400,128]{1,0:T(8,128)(2,1)S(1)}, u32[]{:S(2)}, u32[]{:S(2)}) collective-permute-start(bf16[400,128]{1,0:T(8,128)(2,1)S(1)} %shard_map.136.refs_0_), channel_id=1, source_target_pairs={{0,8},{4,12},{8,16},{12,20},{16,24},{20,28},{24,0},{28,4},{1,9},{5... | collective-permute-start | bytes 307208 | tf_op jit(solution)/shard_map/ppermute | solution.py:367
  96.7 10.6 %collective-permute-start.29 = (bf16[4,400,128]{2,1,0:T(8,128)(2,1)S(1)}, bf16[4,400,128]{2,1,0:T(8,128)(2,1)S(1)}, u32[]{:S(2)}, u32[]{:S(2)}) collective-permute-start(bf16[4,400,128]{2,1,0:T(8,128)(2,1)S(1)} %shard_map.139.refs_0_), channel_id=1, source_target_pairs={{0,2},{1,3},{2,0},{3,1},{4,6},{5,7},{6,4},{7,5},{8,10},{9,11},{10,... | collective-permute-start | bytes 1228808 | tf_op jit(solution)/shard_map/ppermute | solution.py:381
  97.3 10.3 %collective-permute-start.28 = (bf16[4,400,128]{2,1,0:T(8,128)(2,1)S(1)}, bf16[4,400,128]{2,1,0:T(8,128)(2,1)S(1)}, u32[]{:S(2)}, u32[]{:S(2)}) collective-permute-start(bf16[4,400,128]{2,1,0:T(8,128)(2,1)S(1)} %shard_map.139.refs_0_), channel_id=1, source_target_pairs={{0,1},{1,0},{2,3},{3,2},{4,5},{5,4},{6,7},{7,6},{8,9},{9,8},{10,11... | collective-permute-start | bytes 1228808 | tf_op jit(solution)/shard_map/ppermute | solution.py:381
  98.5 12.9 %collective-permute-start.26 = (bf16[128,768]{1,0:T(8,128)(2,1)S(1)}, bf16[128,768]{1,0:T(8,128)(2,1)S(1)}, u32[]{:S(2)}, u32[]{:S(2)}) collective-permute-start(bf16[128,768]{1,0:T(8,128)(2,1)S(1)} %get-tuple-element.60), channel_id=1, source_target_pairs={{0,16},{4,20},{8,24},{12,28},{16,0},{20,4},{24,8},{28,12},{1,17},{... | collective-permute-start | bytes 589832 | tf_op jit(solution)/shard_map/ppermute | solution.py:367
  100.8 14.1 %collective-permute-start.27 = (bf16[128,768]{1,0:T(8,128)(2,1)S(1)}, bf16[128,768]{1,0:T(8,128)(2,1)S(1)}, u32[]{:S(2)}, u32[]{:S(2)}) collective-permute-start(bf16[128,768]{1,0:T(8,128)(2,1)S(1)} %get-tuple-element.61), channel_id=1, source_target_pairs={{0,24},{4,28},{8,0},{12,4},{16,8},{20,12},{24,16},{28,20},{1,25},{... | collective-permute-start | bytes 589832 | tf_op jit(solution)/shard_map/ppermute | solution.py:367
  101.3 13.7 %collective-permute-start.25 = (bf16[128,768]{1,0:T(8,128)(2,1)S(1)}, bf16[128,768]{1,0:T(8,128)(2,1)S(1)}, u32[]{:S(2)}, u32[]{:S(2)}) collective-permute-start(bf16[128,768]{1,0:T(8,128)(2,1)S(1)} %get-tuple-element.59.refs_4_), channel_id=1, source_target_pairs={{0,8},{4,12},{8,16},{12,20},{16,24},{20,28},{24,0},{28,4},{1,9},{5... | collective-permute-start | bytes 589832 | tf_op jit(solution)/shard_map/ppermute | solution.py:367
  107.3 11.0 %collective-permute-start.32 = (bf16[4,400,128]{2,1,0:T(8,128)(2,1)S(1)}, bf16[4,400,128]{2,1,0:T(8,128)(2,1)S(1)}, u32[]{:S(2)}, u32[]{:S(2)}) collective-permute-start(bf16[4,400,128]{2,1,0:T(8,128)(2,1)S(1)} %shard_map.139.refs_0_), channel_id=1, source_target_pairs={{0,4},{4,0},{8,12},{12,8},{16,20},{20,16},{24,28},{28,24},{1,5},{5... | collective-permute-start | bytes 1228808 | tf_op jit(solution)/shard_map/ppermute | solution.py:372
  (23 other events, 139.7 us)

commit v3 on v2

v3 whole, which is shorter than its diff:
```python
import math

import jax
import jax.numpy as jnp
from jax import lax
from jax.experimental import pallas as pl
from jax.experimental.pallas import tpu as pltpu
from jax.sharding import PartitionSpec as P

F32 = jnp.float32
BF16 = jnp.bfloat16
LANES = 128
EXTRA = 16
VMEM = pl.BlockSpec(memory_space=pltpu.VMEM)
SMEM = pl.BlockSpec(memory_space=pltpu.SMEM)
PARAMS = pltpu.CompilerParams(vmem_limit_bytes=48 * 1024 * 1024)


def call(body, outs, args, scratch=(), smem=0, flops=0, after=()):
    count = len(args)
    moved = sum(math.prod(o.shape) * o.dtype.itemsize for o in outs)
    moved += sum(a.size * a.dtype.itemsize for a in args)

    def run(*refs):
        body(*refs[:count], *refs[count + len(after) :])

    return pl.pallas_call(
        run,
        out_shape=outs,
        in_specs=[SMEM] * smem
        + [VMEM] * (count - smem)
        + [pl.BlockSpec(memory_space=pl.ANY)] * len(after),
        out_specs=[VMEM] * len(outs),
        scratch_shapes=list(scratch),
        compiler_params=PARAMS,
        cost_estimate=pl.CostEstimate(flops=flops, bytes_accessed=moved, transcendentals=0),
    )(*args, *after)


def shape(dims, dtype):
    return jax.ShapeDtypeStruct(tuple(dims), dtype)


def mm(a, b, ca=1, cb=0):
    return lax.dot_general(a, b, (((ca,), (cb,)), ((), ())), preferred_element_type=F32)


def follow(x, after):
    def body(x_ref, out_ref):
        out_ref[...] = x_ref[...]

    return call(body, [shape(x.shape, x.dtype)], [x], after=after)[0]


def turn(weights, after):
    def body(*refs):
        for ref, out_ref in zip(refs, refs[len(weights) :]):
            out_ref[...] = ref[...].T

    return call(body, [shape(w.shape[::-1], w.dtype) for w in weights], weights, after=after)


def stack(parts, after):
    def body(*refs):
        for k, ref in enumerate(refs[:-1]):
            refs[-1][k] = ref[...]

    out = shape((len(parts), *parts[0].shape), parts[0].dtype)
    return call(body, [out], parts, after=after)[0]


def densify(rows, cols, count, values, nd, rs, cs, after):
    rt, ct, half = nd * cs, nd * rs, rs // 2

    def body(rows_ref, cols_ref, count_ref, values_ref, tile_ref, turned_ref, mass_ref, acc):
        i, j = lax.axis_index("row"), lax.axis_index("col")
        z, c = i // 2, lax.rem(i, 2)
        acc[...] = jnp.zeros_like(acc)

        def add(s, carry):
            col = cols_ref[s]
            row = rows_ref[s] ^ j
            col = (z ^ (col // 2)) + half * (lax.rem(col, 2) ^ c)
            r = pl.multiple_of(row * nd, nd)
            c0 = pl.multiple_of(col * nd, nd)
            acc[pl.ds(r, nd), pl.ds(c0, nd)] += values_ref[s].astype(F32)
            return carry

        lax.fori_loop(0, count_ref[0], add, 0)
        tile_ref[...] = acc[...].astype(BF16)
        ones = jnp.ones((8, ct), BF16)
        for k in range(cs):
            place = pl.multiple_of((j ^ k) * nd, nd)
            mass_ref[:, pl.ds(place, nd)] = mm(ones, tile_ref[k * nd : (k + 1) * nd, :], 1, 1)
        for k in range(rs):
            cut = acc[:, k * nd : (k + 1) * nd]
            turned_ref[k * nd : (k + 1) * nd, :] = cut.T.astype(BF16)

    return call(
        body,
        [shape((rt, ct), BF16), shape((ct, rt), BF16), shape((8, rt), F32)],
        [rows, cols, count, values],
        [pltpu.VMEM((rt, ct), F32)],
        smem=3,
        flops=2 * 8 * rt * ct,
        after=after,
    )


def forward_parts(tile, blocks, nd, cs, after):
    width = blocks[0].shape[1]

    def body(*refs):
        tile_ref, feat_refs = refs[0], refs[1 : 1 + len(blocks)]
        outs = refs[1 + len(blocks) :]
        feats = jnp.concatenate([r[...] for r in feat_refs], axis=0)
        parts = mm(tile_ref[...], feats)
        for k in range(cs):
            outs[k][...] = parts[k * nd : (k + 1) * nd].astype(outs[k].dtype)

    return call(
        body,
        [shape((nd, width), BF16 if k else F32) for k in range(cs)],
        [tile, *blocks],
        flops=2 * tile.size * width,
        after=after,
    )


def activation(parts, inverse, own, own_feat, w_neigh, bias, cotangent, after):
    cs = len(parts)
    nd, hid = own.shape
    depth = own_feat.shape[1]
    xw = 2 * depth // cs

    def body(*refs):
        part_refs = refs[:cs]
        inv_ref, own_ref, feat_ref, w_ref, bias_ref, cot_ref = refs[cs : cs + 6]
        out_ref, sum_ref, *packs = refs[cs + 6 : -1]
        both = refs[-1]
        j = lax.axis_index("col")
        inv = inv_ref[pl.ds(pl.multiple_of(j * nd, nd), nd), :]
        total = sum(r[...].astype(F32) for r in part_refs)
        mean = (total * jnp.concatenate([inv] * (depth // LANES), axis=1)).astype(BF16)
        both[:, :depth] = feat_ref[...]
        both[:, depth:] = mean
        pre = own_ref[...].astype(F32) + mm(mean, w_ref[...]) + bias_ref[...]
        slope = jnp.where(pre > 0, 1.0, jnp.exp(jnp.minimum(pre, 0.0)))
        out_ref[...] = jnp.where(pre > 0, pre, slope - 1.0).astype(BF16)
        grad = cot_ref[...].astype(F32) * slope
        sum_ref[...] = jnp.broadcast_to(jnp.sum(grad, axis=0, keepdims=True), (8, hid))
        grad = grad.astype(BF16)
        for k in range(cs):
            packs[k][:, :hid] = grad
            target = j ^ k
            if xw % LANES == 0:
                start = pl.multiple_of(target * xw, LANES)
                packs[k][:, hid:] = both[:, pl.ds(start, xw)]
            else:
                for d in range(cs):

                    @pl.when(target == d)
                    def _():
                        packs[k][:, hid:] = both[:, d * xw : (d + 1) * xw]

    return call(
        body,
        [shape((nd, hid), BF16), shape((8, hid), F32)] + [shape((nd, hid + xw), BF16)] * cs,
        [*parts, inverse, own, own_feat, w_neigh, bias, cotangent],
        [pltpu.VMEM((nd, 2 * depth), BF16)],
        flops=2 * own_feat.size * hid,
        after=after,
    )


def split_pair(total):
    high = total.astype(BF16).astype(F32)
    return jnp.concatenate([high, total - high], axis=0)


def weight_parts(packs, sums, rs, xr, nc):
    cs = len(packs)
    hid = sums.shape[1]
    nd, xw = packs[0].shape[0], packs[0].shape[1] - hid
    half = rs // 2

    def body(*refs):
        pack_refs = refs[:cs]
        sum_ref, keep_ref, send_ref, acc = refs[cs:]
        x_all = jnp.concatenate([r[:, hid:] for r in pack_refs], axis=0)
        g_all = jnp.concatenate([r[:, :hid] for r in pack_refs], axis=0)
        acc[...] = mm(x_all, g_all, 0, 0)
        i = lax.axis_index("row")
        z, c = i // 2, lax.rem(i, 2)
        for k in range(half):
            for core, ref in ((c, keep_ref), (1 - c, send_ref)):
                q = 2 * (z ^ k) + core
                row = pl.multiple_of((q // nc) * xr, xr)
                col = pl.multiple_of(lax.rem(q, nc) * LANES, LANES)
                ref[k, :xr, :] = acc[pl.ds(row, xr), pl.ds(col, LANES)].astype(ref.dtype)
                ref[k, xr:, :] = split_pair(sum_ref[:, pl.ds(col, LANES)]).astype(ref.dtype)

    dims = (half, xr + EXTRA, LANES)
    return call(
        body,
        [shape(dims, F32), shape(dims, BF16)],
        [*packs, sums],
        [pltpu.VMEM((xw, hid), F32)],
        flops=2 * cs * nd * xw * hid,
    )


def scaled_parts(packs, inverse, turned_neigh, turned_self, rs, after):
    cs = len(packs)
    nd = packs[0].shape[0]
    hid, depth = turned_neigh.shape

    def body(neigh_ref, own_ref, inv_ref, *refs):
        pack_refs, scaled_ref, self_ref = refs[:cs], refs[cs], refs[cs + 1]
        i, j = lax.axis_index("row"), lax.axis_index("col")
        grads = jnp.concatenate([r[:, :hid] for r in pack_refs], axis=0)
        product = mm(grads, neigh_ref[...])
        for r in range(cs):
            inv = inv_ref[pl.ds(pl.multiple_of((j ^ r) * nd, nd), nd), :]
            inv = jnp.concatenate([inv] * (depth // LANES), axis=1)
            rows = slice(r * nd, (r + 1) * nd)
            scaled_ref[rows, :] = (product[rows] * inv).astype(BF16)

        @pl.when(i * cs // rs == j)
        def _():
            self_ref[...] = mm(grads, own_ref[...])

    return call(
        body,
        [shape((cs * nd, depth), BF16), shape((cs * nd, depth), F32)],
        [turned_neigh, turned_self, inverse, *packs],
        flops=4 * cs * nd * hid * depth,
        after=after,
    )


def halving_order(count):
    order = [0]
    step = count // 2
    while step:
        order = order + [d + step for d in order]
        step //= 2
    return order


def back_parts(turned, scaled, self_part, nd, cs, rs, after):
    depth = scaled.shape[1]
    half = rs // 2

    def body(tile_ref, scaled_ref, self_ref, keep_ref, send_ref, acc):
        i, j = lax.axis_index("row"), lax.axis_index("col")
        z, c = i // 2, lax.rem(i, 2)
        acc[...] = mm(tile_ref[...], scaled_ref[...])

        @pl.when(i * cs // rs == j)
        def _():
            for r in range(cs):
                q = i * cs - j * rs + (j ^ r)
                place = ((z ^ (q // 2)) + half * (lax.rem(q, 2) ^ c)) * nd
                acc[pl.ds(pl.multiple_of(place, nd), nd), :] += self_ref[r * nd : (r + 1) * nd]

        for ref, base in ((send_ref, half), (keep_ref, 0)):
            for k, distance in enumerate(halving_order(half)):
                place = (base + distance) * nd
                ref[k] = acc[place : place + nd, :].astype(ref.dtype)

    dims = (half, nd, depth)
    return call(
        body,
        [shape(dims, F32), shape(dims, BF16)],
        [turned, scaled, self_part],
        [pltpu.VMEM((rs * nd, depth), F32)],
        flops=2 * turned.size * depth,
        after=after,
    )


def fold(keep, came, after=()):
    count, rows, width = keep.shape
    half = count // 2

    def body(keep_ref, came_ref, *outs):
        total = keep_ref[...] + came_ref[...].astype(F32)
        if count == 1:
            outs[0][...] = total[0].astype(BF16)
        else:
            outs[0][...] = total[:half]
            outs[1][...] = total[half:].astype(BF16)

    if count == 1:
        return call(body, [shape((rows, width), BF16)], [keep, came], after=after)[0]
    dims = (half, rows, width)
    return call(body, [shape(dims, F32), shape(dims, BF16)], [keep, came], after=after)


def pair_sum(keep, came):
    half, rows, width = keep.shape
    main = rows - EXTRA

    def body(keep_ref, came_ref, *outs):
        for k in range(half):
            total = keep_ref[k] + came_ref[k].astype(F32)
            dtype = outs[k].dtype
            outs[k][:main, :] = total[:main].astype(dtype)
            merged = total[main : main + 8] + total[main + 8 :]
            outs[k][main:, :] = split_pair(merged).astype(dtype)

    return call(
        body,
        [shape((rows, width), BF16 if k else F32) for k in range(half)],
        [keep, came],
    )


def last_sum(parts):
    rows, width = parts[0].shape
    main = rows - EXTRA

    def body(*refs):
        out_ref = refs[-1]
        total = refs[0][...]
        for ref in refs[1:-1]:
            total = total + ref[...].astype(F32)
        out_ref[:main, :] = total[:main].astype(BF16)
        merged = total[main : main + 8] + total[main + 8 :]
        out_ref[main:, :] = split_pair(merged).astype(BF16)

    return call(body, [shape((rows, width), BF16)], parts)[0]


def assemble(pieces, mine, begun, depth, hid, xr, nc, cs, factors, after):
    xw = 2 * depth // cs
    side = cs // 2
    copies = sum(len(distances) for _, distances, _ in pieces)
    arrays = [array for array, _, _ in pieces]
    inputs = arrays + list(begun)
    weight = shape((depth, hid), F32)

    def body(*refs):
        piece_refs = refs[: len(pieces)]
        self_ref, neigh_ref, bias_ref, staged, sems = refs[-5:]
        i, j = lax.axis_index("row"), lax.axis_index("col")
        z, c = i // 2, lax.rem(i, 2)
        if begun:
            bias_ref[...] = refs[len(inputs) - 1][...]
        else:
            bias_ref[...] = jnp.zeros_like(bias_ref)
        waits = []
        at = 0
        for ref, (_, distances, column) in zip(piece_refs, pieces):
            owner = j ^ column
            first = owner < side
            for t, distance in enumerate(distances):
                q = 2 * (z ^ distance) + (c if mine else 1 - c)
                col = pl.multiple_of(lax.rem(q, nc) * LANES, LANES)
                turn = q // nc
                row = pl.multiple_of(lax.rem(owner, side) * xw + turn * xr, xr)
                scale = jnp.where(first, factors[0], factors[1])
                staged[at] = ref[t, :xr, :].astype(F32) * scale
                for target, here in ((self_ref, first), (neigh_ref, jnp.logical_not(first))):
                    copy = pltpu.make_async_copy(
                        staged.at[at],
                        target.at[pl.ds(row, xr), pl.ds(col, LANES)],
                        sems.at[at],
                    )
                    pl.when(here)(copy.start)
                    waits.append((here, copy))

                @pl.when(turn == 0)
                def _():
                    total = ref[t, xr:, :].astype(F32)
                    total = (total[:1] + total[8:9]) * factors[0]
                    bias_ref[:, pl.ds(col, LANES)] += total

                at += 1
        for here, copy in waits:
            pl.when(here)(copy.wait)

    def run(*refs):
        body(*refs[: len(inputs)], *refs[len(inputs) + len(after) :])

    somewhere = pl.BlockSpec(memory_space=pl.ANY)
    moved = 2 * copies * xr * LANES * 6
    return pl.pallas_call(
        run,
        out_shape=[weight, weight, shape((1, hid), F32)],
        in_specs=[VMEM] * len(arrays)
        + ([somewhere, somewhere, VMEM] if begun else [])
        + [somewhere] * len(after),
        out_specs=[somewhere, somewhere, VMEM],
        scratch_shapes=[
            pltpu.VMEM((copies, xr, LANES), F32),
            pltpu.SemaphoreType.DMA((copies,)),
        ],
        input_output_aliases={len(arrays): 0, len(arrays) + 1: 1} if begun else {},
        compiler_params=PARAMS,
        cost_estimate=pl.CostEstimate(flops=0, bytes_accessed=moved, transcendentals=0),
    )(*inputs, *after)


def local(
    features, w_neigh, w_self, bias, cotangent, block_rows, block_cols, block_vals, block_count
):
    rs = lax.axis_size("row")
    cs = lax.axis_size("col")
    nd, depth = features.shape
    hid = w_self.shape[1]
    rt = nd * cs
    half = rs // 2
    xw = 2 * depth // cs
    nc = min(rs, hid // LANES)
    nr = rs // nc
    xr = xw // nr

    def along_col(x, k):
        return lax.ppermute(x, "col", [(s, s ^ k) for s in range(cs)])

    def along_chips(x, k):
        return lax.ppermute(x, "row", [(s, s ^ (2 * k)) for s in range(rs)])

    def other_core(x):
        return lax.ppermute(x, "row", [(s, s ^ 1) for s in range(rs)])

    def gather_chips(x, after=()):
        found = {0: x}
        step = half // 2
        while step:
            if step == 1 and after:
                last = {d: follow(y, after) if d else y for d, y in found.items()}
            else:
                last = found
            found.update({d + step: along_chips(last[d], step) for d in list(found)})
            step //= 2
        return [found[d] for d in range(half)]

    swap = [((b % rs) * cs + b // rs, b) for b in range(rs * cs)]
    across = other_core(features)
    own_feat = lax.ppermute(features, ("row", "col"), swap)
    tile, turned, mass = densify(
        block_rows.reshape(-1),
        block_cols.reshape(-1),
        block_count.reshape(-1),
        block_vals[0, 0],
        nd,
        rs,
        cs,
        [across],
    )
    blocks = gather_chips(features, [mass])
    blocks = blocks + [across] + [other_core(x) for x in blocks[1:]]
    degree = mass
    for k in range(1, cs):
        degree = degree + along_col(mass, k)
    inverse = 1.0 / (degree[0] + 1.0)
    inverse = jnp.broadcast_to(inverse[:, None], (rt, LANES))
    own = jnp.dot(own_feat, w_self, preferred_element_type=F32).astype(BF16)

    parts = forward_parts(tile, blocks, nd, cs, [own_feat])
    turned_neigh, turned_self = turn([w_neigh, w_self], [parts[0]])
    parts = [parts[0]] + [along_col(parts[k], k) for k in range(1, cs)]
    output, sums, *packs = activation(
        parts, inverse, own, own_feat, w_neigh, bias[None, :], cotangent, [turned_neigh]
    )
    packs = [packs[0]] + [along_col(packs[k], k) for k in range(1, cs)]

    keep, send = weight_parts(packs, sums, rs, xr, nc)
    came = other_core(send)
    scaled, self_part = scaled_parts(packs, inverse, turned_neigh, turned_self, rs, [keep])
    chunks = pair_sum(keep, came)
    back_after = [chunks[1]]
    chunks = [chunks[0]] + [along_chips(chunks[k], k) for k in range(1, half)]
    line = gather_chips(last_sum(chunks))

    keep, send = back_parts(turned, scaled, self_part, nd, cs, rs, back_after)
    keep, send = fold(keep, other_core(send), line[1:])
    line = stack(line, [send])
    step = 1
    while step < half:
        folded = fold(keep, along_chips(send, step))
        keep, send = folded if 2 * step < half else (folded, None)
        step *= 2
    grad_input = keep

    distances = list(range(half))
    mine = [(line, distances, 0)]
    if cs == 4 and half % 2 == 0:
        mid = half // 2
        first, second = along_col(line, 1), along_col(line, 2)
        mine += [
            (first, distances, 1),
            (second, distances, 2),
            (along_col(first[:mid], 2), distances[:mid], 3),
            (along_col(second[mid:], 1), distances[mid:], 3),
        ]
    else:
        mine += [(along_col(line, k), distances, k) for k in range(1, cs)]
    theirs = [(other_core(array), where, column) for array, where, column in mine]
    factor = 1.0 / math.sqrt(nd * rs * cs)
    sizes = (depth, hid, xr, nc, cs, (factor, 32.0 * factor))
    begun = assemble(mine, True, (), *sizes, ())
    total_self, total_neigh, total_bias = assemble(theirs, False, begun, *sizes, [grad_input])
    return output, grad_input, total_self, total_neigh, total_bias.reshape(-1)


def solution(mesh):
    in_specs = (
        P(("col", "row"), None),
        P(),
        P(),
        P(),
        P(("row", "col"), None),
        P("row", "col", None),
        P("row", "col", None),
        P("row", "col", None, None, None),
        P("row", "col"),
    )
    out_specs = (P(("row", "col"), None), P(("col", "row"), None), P(), P(), P())
    return jax.shard_map(local, mesh=mesh, in_specs=in_specs, out_specs=out_specs, check_vma=False)
```

time: 124 us -> 122 us (0.984)
  starting transfers between devices: 42.2 us -> 28.4 us
  waiting for transfers between devices: 60.1 us -> 67.5 us
  Pallas kernels: 15.2 us -> 17.6 us
  matrix products: 0.38 us -> 1.78 us
    ppermute x26 -> x25, starting transfers between devices: 37.5 us -> 26 us  [the longest x11 12.4 us: along_chips(): return lax.ppermute(x, 'row', [(s, s ^ 2 * k) for s in range(rs)])]
    ppermute x26 -> x25, waiting for transfers between devices: 58.2 us -> 67.5 us  [the longest x11 48 us: along_chips(): return lax.ppermute(x, 'row', [(s, s ^ 2 * k) for s in range(rs)])]
    pallas_call x0 -> x2, Pallas kernels: none -> 4.22 us  [assemble(): pl.pallas_call(run, out_shape=[weight, weight, shape((1, hid), F32)], in_...]
    ppermute x11, starting transfers between devices: 4.65 us -> 2.31 us  [other_core(): return lax.ppermute(x, 'row', [(s, s ^ 1) for s in range(rs)])]
    pallas_call x13 -> x14, Pallas kernels: 15.2 us -> 13.4 us  [call(): pl.pallas_call(run, out_shape=outs, in_specs=[SMEM] * smem + [VMEM] * (co...]
    ppermute x11, waiting for transfers between devices: 1.88 us -> 0.03 us  [other_core(): return lax.ppermute(x, 'row', [(s, s ^ 1) for s in range(rs)])]
    dot_general x1, matrix products: 0.38 us -> 1.78 us  [local(): own = jnp.dot(own_feat, w_self, preferred_element_type=F32).astype(BF16)]
  transfers between devices with their start and end apart: 37 -> 36, of which waited for: 19 -> 13; matrix products, arithmetic and copies ran while one was open for 0% -> 1% of each run, Pallas kernels for 6% -> 9%
where the time goes in v3:
time: 122 us
  waiting for transfers between devices  67.5 us (55%)
  starting transfers between devices  28.4 us (23%)
  Pallas kernels  17.6 us (14%)
  local copies, waits for them, and re-layouts  4.89 us (4%)
  matrix products  1.78 us (1%)
  between operations  1.62 us (1%)
    ppermute x11, waiting for transfers between devices, along_chips(): return lax.ppermute(x, 'row', [(s, s ^ 2 * k) for s in range(rs)])  48 us
    ppermute x13, waiting for transfers between devices, along_col(): return lax.ppermute(x, 'col', [(s, s ^ k) for s in range(cs)])  19.5 us
    pallas_call x14, Pallas kernels, call(): pl.pallas_call(run, out_shape=outs, in_specs=[SMEM] * smem + [VMEM] * (co...  13.4 us
    ppermute x11, starting transfers between devices, along_chips(): return lax.ppermute(x, 'row', [(s, s ^ 2 * k) for s in range(rs)])  12.4 us
    ppermute x13, starting transfers between devices, along_col(): return lax.ppermute(x, 'col', [(s, s ^ k) for s in range(cs)])  12.1 us
    unnamed x20, local copies, waits for them, and re-layouts  4.74 us
    pallas_call x2, Pallas kernels, assemble(): pl.pallas_call(run, out_shape=[weight, weight, shape((1, hid), F32)], in_...  4.22 us
  transfers between devices with their start and end apart: 36, of which 13 were waited for; matrix products, arithmetic and copies ran while one was open for 1% of the time, Pallas kernels for 9%

profile of v3, /device:TPU:0, one launch (start us, length us, event | category | flops | bytes accessed | tf_op | source)
XLA Modules:
  0.0 121.7 jit_solution(10711344816413494670)
XLA Ops:
  1.2 3.7 %collective-permute-start.2 = (bf16[128,768]{1,0:T(8,128)(2,1)}, bf16[128,768]{1,0:T(8,128)(2,1)S(1)}, u32[]{:S(2)}, u32[]{:S(2)}) collective-permute-start(bf16[128,768]{1,0:T(8,128)(2,1)} %refs_1_.2), channel_id=1, source_target_pairs={{0,16},{4,20},{8,24},{12,28},{16,0},{20,4},{24,8},{28,12},{1,17},{... | collective-permute-start | bytes 589832 | tf_op jit(solution)/shard_map/ppermute | solution.py:424
  4.8 1.6 %collective-permute-start.1 = (bf16[128,768]{1,0:T(8,128)(2,1)}, bf16[128,768]{1,0:T(8,128)(2,1)S(1)}, u32[]{:S(2)}, u32[]{:S(2)}) collective-permute-start(bf16[128,768]{1,0:T(8,128)(2,1)} %refs_1_.2), channel_id=1, source_target_pairs={{0,8},{4,12},{8,0},{12,4},{16,24},{20,28},{24,16},{28,20},{1,9},{5... | collective-permute-start | bytes 589832 | tf_op jit(solution)/shard_map/ppermute | solution.py:424
  11.1 1.6 %shard_map.128 = (bf16[512,1024]{1,0:T(8,128)(2,1)S(1)}, bf16[1024,512]{1,0:T(8,128)(2,1)S(1)}, f32[8,512]{1,0:T(8,128)S(1)}) custom-call(s32[24]{0:T(128)S(1)} %bitcast.12, s32[24]{0:T(128)S(1)} %bitcast.13, s32[1]{0:T(128)} %bitcast.9.refs_2_, bf16[24,128,128]{2,1,0:T(8,128)(2,1)S(1)} %bitcast.10, bf16[128,768]{1,0:T(8,128)(2,1)S(1)} %collective-permute-done.refs_4_.refs_5_), custom_call_target="tpu_custom_call" | custom-call | flops 8388608 | bytes 2900164 | tf_op jit(solution)/shard_map/pallas_call | solution.py:27
  12.7 2.4 %collective-permute-done.2.refs_0_.refs_3_ = bf16[128,768]{1,0:T(8,128)(2,1)S(1)} collective-permute-done((bf16[128,768]{1,0:T(8,128)(2,1)}, bf16[128,768]{1,0:T(8,128)(2,1)S(1)}, u32[]{:S(2)}, u32[]{:S(2)}) %collective-permute-start.2) | collective-permute-done | bytes 196640 | tf_op jit(solution)/shard_map/ppermute | solution.py:424
  16.2 2.3 %collective-permute-start.13 = (f32[8,512]{1,0:T(8,128)S(1)}, f32[8,512]{1,0:T(8,128)S(1)}, u32[]{:S(2)}, u32[]{:S(2)}) collective-permute-start(f32[8,512]{1,0:T(8,128)S(1)} %get-tuple-element.41.refs_1_), channel_id=1, source_target_pairs={{0,3},{1,2},{2,1},{3,0},{4,7},{5,6},{6,5},{7,4},{8,11},{9,10},{10,... | collective-permute-start | bytes 49160 | tf_op jit(solution)/shard_map/ppermute | solution.py:421
  18.6 5.0 %collective-permute-done.1.refs_2_ = bf16[128,768]{1,0:T(8,128)(2,1)S(1)} collective-permute-done((bf16[128,768]{1,0:T(8,128)(2,1)}, bf16[128,768]{1,0:T(8,128)(2,1)S(1)}, u32[]{:S(2)}, u32[]{:S(2)}) %collective-permute-start.1) | collective-permute-done | bytes 196640 | tf_op jit(solution)/shard_map/ppermute | solution.py:424
  24.1 7.8 %collective-permute-done.3.refs_4_ = bf16[128,768]{1,0:T(8,128)(2,1)S(1)} collective-permute-done((bf16[128,768]{1,0:T(8,128)(2,1)S(1)}, bf16[128,768]{1,0:T(8,128)(2,1)S(1)}, u32[]{:S(2)}, u32[]{:S(2)}) %collective-permute-start.3) | collective-permute-done | bytes 196640 | tf_op jit(solution)/shard_map/ppermute | solution.py:424
  31.9 1.8 %convolution_convert_fusion.refs_5_ = bf16[128,1024]{1,0:T(8,128)(2,1)S(1)} fusion(bf16[128,768]{1,0:T(8,128)(2,1)S(1)} %collective-permute-done.7.refs_9_.refs_6_, bf16[768,1024]{1,0:T(8,128)(2,1)} %refs_1_.3), kind=kOutput, calls=%fused_computation | convolution fusion | flops 201457664 | bytes 2031616 | tf_op jit(solution)/shard_map/dot_general | solution.py:461
  34.8 2.1 %collective-permute-start.8 = (bf16[128,768]{1,0:T(8,128)(2,1)S(1)}, bf16[128,768]{1,0:T(8,128)(2,1)S(1)}, u32[]{:S(2)}, u32[]{:S(2)}) collective-permute-start(bf16[128,768]{1,0:T(8,128)(2,1)S(1)} %get-tuple-element.43), channel_id=1, source_target_pairs={{0,1},{1,0},{2,3},{3,2},{4,5},{5,4},{6,7},{7,6},{8,9},{9,8},{10,11... | collective-permute-start | bytes 589832 | tf_op jit(solution)/shard_map/ppermute | solution.py:421
  38.5 2.3 %shard_map.131 = (bf16[1024,768]{1,0:T(8,128)(2,1)S(1)}, bf16[1024,768]{1,0:T(8,128)(2,1)S(1)}) custom-call(bf16[768,1024]{1,0:T(8,128)(2,1)S(1)} %copy-done, bf16[768,1024]{1,0:T(8,128)(2,1)} %refs_1_.3, f32[128,768]{1,0:T(8,128)S(1)} %get-tuple-element.42.refs_2_.refs_0_), custom_call_target="tpu_custom_call" | custom-call | bytes 6291456 | tf_op jit(solution)/shard_map/pallas_call | solution.py:27
  43.1 4.8 %collective-permute-done.9.refs_2_ = bf16[128,768]{1,0:T(8,128)(2,1)S(1)} collective-permute-done((bf16[128,768]{1,0:T(8,128)(2,1)S(1)}, bf16[128,768]{1,0:T(8,128)(2,1)S(1)}, u32[]{:S(2)}, u32[]{:S(2)}) %collective-permute-start.9) | collective-permute-done | bytes 196640 | tf_op jit(solution)/shard_map/ppermute | solution.py:421
  51.0 1.7 %collective-permute-start.16 = (bf16[128,1408]{1,0:T(8,128)(2,1)S(1)}, bf16[128,1408]{1,0:T(8,128)(2,1)S(1)}, u32[]{:S(2)}, u32[]{:S(2)}) collective-permute-start(bf16[128,1408]{1,0:T(8,128)(2,1)S(1)} %get-tuple-element.53), channel_id=1, source_target_pairs={{0,3},{1,2},{2,1},{3,0},{4,7},{5,6},{6,5},{7,4},{8,11},{9,10},{10,... | collective-permute-start | bytes 1081352 | tf_op jit(solution)/shard_map/ppermute | solution.py:421
  52.8 7.9 %collective-permute-done.14.refs_1_.refs_4_ = bf16[128,1408]{1,0:T(8,128)(2,1)S(1)} collective-permute-done((bf16[128,1408]{1,0:T(8,128)(2,1)S(1)}, bf16[128,1408]{1,0:T(8,128)(2,1)S(1)}, u32[]{:S(2)}, u32[]{:S(2)}) %collective-permute-start.14) | collective-permute-done | bytes 360480 | tf_op jit(solution)/shard_map/ppermute | solution.py:421
  60.6 6.2 %collective-permute-done.15.refs_2_.refs_5_ = bf16[128,1408]{1,0:T(8,128)(2,1)S(1)} collective-permute-done((bf16[128,1408]{1,0:T(8,128)(2,1)S(1)}, bf16[128,1408]{1,0:T(8,128)(2,1)S(1)}, u32[]{:S(2)}, u32[]{:S(2)}) %collective-permute-start.15) | collective-permute-done | bytes 360480 | tf_op jit(solution)/shard_map/ppermute | solution.py:421
  67.7 3.8 %shard_map.134 = (bf16[512,768]{1,0:T(8,128)(2,1)S(1)}, f32[512,768]{1,0:T(8,128)S(1)}) custom-call(bf16[1024,768]{1,0:T(8,128)(2,1)} %copy-done.1, bf16[1024,768]{1,0:T(8,128)(2,1)} %copy-done.8, f32[512,128]{1,0:T(8,128)S(1)} %broadcast_in_dim.4.refs_4_.refs_2_, bf16[128,1408]{1,0:T(8,128)(2,1)S(1)} %get-tuple-element.50.refs_0_.refs_3_, ...), custom_call_target="tpu_custom_call" | custom-call | flops 1610612736 | bytes 7208960 | tf_op jit(solution)/shard_map/pallas_call | solution.py:27
  74.0 1.9 %collective-permute-start.21 = (bf16[400,128]{1,0:T(8,128)(2,1)S(1)}, bf16[400,128]{1,0:T(8,128)(2,1)S(1)}, u32[]{:S(2)}, u32[]{:S(2)}) collective-permute-start(bf16[400,128]{1,0:T(8,128)(2,1)S(1)} %get-tuple-element.64), channel_id=1, source_target_pairs={{0,24},{4,28},{8,16},{12,20},{16,8},{20,12},{24,0},{28,4},{1,25},{... | collective-permute-start | bytes 307208 | tf_op jit(solution)/shard_map/ppermute | solution.py:424
  77.0 6.5 %collective-permute-done.20.refs_2_ = bf16[400,128]{1,0:T(8,128)(2,1)S(1)} collective-permute-done((bf16[400,128]{1,0:T(8,128)(2,1)S(1)}, bf16[400,128]{1,0:T(8,128)(2,1)S(1)}, u32[]{:S(2)}, u32[]{:S(2)}) %collective-permute-start.20) | collective-permute-done | bytes 102432 | tf_op jit(solution)/shard_map/ppermute | solution.py:424
  84.9 1.6 %collective-permute-start.23 = (bf16[400,128]{1,0:T(8,128)(2,1)S(1)}, bf16[400,128]{1,0:T(8,128)(2,1)S(1)}, u32[]{:S(2)}, u32[]{:S(2)}) collective-permute-start(bf16[400,128]{1,0:T(8,128)(2,1)S(1)} %shard_map.137.refs_0_), channel_id=1, source_target_pairs={{0,16},{4,20},{8,24},{12,28},{16,0},{20,4},{24,8},{28,12},{1,17},{... | collective-permute-start | bytes 307208 | tf_op jit(solution)/shard_map/ppermute | solution.py:424
  87.2 5.6 %collective-permute-done.23.refs_3_.refs_2_ = bf16[400,128]{1,0:T(8,128)(2,1)S(1)} collective-permute-done((bf16[400,128]{1,0:T(8,128)(2,1)S(1)}, bf16[400,128]{1,0:T(8,128)(2,1)S(1)}, u32[]{:S(2)}, u32[]{:S(2)}) %collective-permute-start.23) | collective-permute-done | bytes 102432 | tf_op jit(solution)/shard_map/ppermute | solution.py:424
  93.0 5.5 %collective-permute-done.24.refs_4_.refs_3_ = bf16[400,128]{1,0:T(8,128)(2,1)S(1)} collective-permute-done((bf16[400,128]{1,0:T(8,128)(2,1)S(1)}, bf16[400,128]{1,0:T(8,128)(2,1)S(1)}, u32[]{:S(2)}, u32[]{:S(2)}) %collective-permute-start.24) | collective-permute-done | bytes 102432 | tf_op jit(solution)/shard_map/ppermute | solution.py:424
  99.7 7.9 %collective-permute-done.25.refs_1_ = bf16[2,128,768]{2,1,0:T(8,128)(2,1)S(1)} collective-permute-done((bf16[2,128,768]{2,1,0:T(8,128)(2,1)S(1)}, bf16[2,128,768]{2,1,0:T(8,128)(2,1)S(1)}, u32[]{:S(2)}, u32[]{:S(2)}) %collective-permute-start.25) | collective-permute-done | bytes 393248 | tf_op jit(solution)/shard_map/ppermute | solution.py:424
  110.0 6.1 %collective-permute-done.26.refs_1_ = bf16[1,128,768]{2,1,0:T(8,128)(2,1)S(1)} collective-permute-done((bf16[1,128,768]{2,1,0:T(8,128)(2,1)S(1)}, bf16[1,128,768]{2,1,0:T(8,128)(2,1)S(1)}, u32[]{:S(2)}, u32[]{:S(2)}) %collective-permute-start.26) | collective-permute-done | bytes 196640 | tf_op jit(solution)/shard_map/ppermute | solution.py:424
  117.4 1.8 %shard_map.142 = (f32[768,1024]{1,0:T(8,128)}, f32[768,1024]{1,0:T(8,128)}, f32[1,1024]{1,0:T(1,128)S(1)}) custom-call(bf16[4,400,128]{2,1,0:T(8,128)(2,1)S(1)} %shard_map.141.refs_0_, bf16[4,400,128]{2,1,0:T(8,128)(2,1)S(1)} %collective-permute-done.28.refs_1_, bf16[4,400,128]{2,1,0:T(8,128)(2,1)S(1)} %collective-permute-done.30.refs_2_, ...), custom_call_target="tpu_custom_call" | custom-call | bytes 9437184 | tf_op jit(solution)/shard_map/pallas_call | solution.py:389
  119.3 2.4 %shard_map.143 = (f32[768,1024]{1,0:T(8,128)}, f32[768,1024]{1,0:T(8,128)}, f32[1,1024]{1,0:T(1,128)}) custom-call(bf16[4,400,128]{2,1,0:T(8,128)(2,1)S(1)} %collective-permute-done.27.refs_0_, bf16[4,400,128]{2,1,0:T(8,128)(2,1)S(1)} %collective-permute-done.29.refs_1_, ...), custom_call_target="tpu_custom_call", output_to_operand_aliasing={{0}: (5, {}), {1}: (6, {})} | custom-call | bytes 9437184 | tf_op jit(solution)/shard_map/pallas_call | solution.py:389
  (89 shorter events, 26.0 us)
Async XLA Ops:
  1.2 13.9 %collective-permute-start.2 = (bf16[128,768]{1,0:T(8,128)(2,1)}, bf16[128,768]{1,0:T(8,128)(2,1)S(1)}, u32[]{:S(2)}, u32[]{:S(2)}) collective-permute-start(bf16[128,768]{1,0:T(8,128)(2,1)} %refs_1_.2), channel_id=1, source_target_pairs={{0,16},{4,20},{8,24},{12,28},{16,0},{20,4},{24,8},{28,12},{1,17},{... | collective-permute-start | bytes 589832 | tf_op jit(solution)/shard_map/ppermute | solution.py:424
  4.8 18.8 %collective-permute-start.1 = (bf16[128,768]{1,0:T(8,128)(2,1)}, bf16[128,768]{1,0:T(8,128)(2,1)S(1)}, u32[]{:S(2)}, u32[]{:S(2)}) collective-permute-start(bf16[128,768]{1,0:T(8,128)(2,1)} %refs_1_.2), channel_id=1, source_target_pairs={{0,8},{4,12},{8,0},{12,4},{16,24},{20,28},{24,16},{28,20},{1,9},{5... | collective-permute-start | bytes 589832 | tf_op jit(solution)/shard_map/ppermute | solution.py:424
  6.4 17.2 %collective-permute-start.7 = (bf16[128,768]{1,0:T(8,128)(2,1)}, bf16[128,768]{1,0:T(8,128)(2,1)S(1)}, u32[]{:S(2)}, u32[]{:S(2)}) collective-permute-start(bf16[128,768]{1,0:T(8,128)(2,1)} %refs_1_.2), channel_id=1, source_target_pairs={{0,0},{4,1},{8,2},{12,3},{16,4},{20,5},{24,6},{28,7},{1,8},{5,9},{... | collective-permute-start | bytes 589832 | tf_op jit(solution)/shard_map/ppermute | solution.py:443
  15.1 16.8 %collective-permute-start.3 = (bf16[128,768]{1,0:T(8,128)(2,1)S(1)}, bf16[128,768]{1,0:T(8,128)(2,1)S(1)}, u32[]{:S(2)}, u32[]{:S(2)}) collective-permute-start(bf16[128,768]{1,0:T(8,128)(2,1)S(1)} %shard_map.129), channel_id=1, source_target_pairs={{0,8},{4,12},{8,0},{12,4},{16,24},{20,28},{24,16},{28,20},{1,9},{5... | collective-permute-start | bytes 589832 | tf_op jit(solution)/shard_map/ppermute | solution.py:424
  16.2 20.7 %collective-permute-start.13 = (f32[8,512]{1,0:T(8,128)S(1)}, f32[8,512]{1,0:T(8,128)S(1)}, u32[]{:S(2)}, u32[]{:S(2)}) collective-permute-start(f32[8,512]{1,0:T(8,128)S(1)} %get-tuple-element.41.refs_1_), channel_id=1, source_target_pairs={{0,3},{1,2},{2,1},{3,0},{4,7},{5,6},{6,5},{7,4},{8,11},{9,10},{10,... | collective-permute-start | bytes 49160 | tf_op jit(solution)/shard_map/ppermute | solution.py:421
  18.5 20.0 %collective-permute-start.12 = (f32[8,512]{1,0:T(8,128)S(1)}, f32[8,512]{1,0:T(8,128)S(1)}, u32[]{:S(2)}, u32[]{:S(2)}) collective-permute-start(f32[8,512]{1,0:T(8,128)S(1)} %get-tuple-element.41.refs_1_), channel_id=1, source_target_pairs={{0,2},{1,3},{2,0},{3,1},{4,6},{5,7},{6,4},{7,5},{8,10},{9,11},{10,... | collective-permute-start | bytes 49160 | tf_op jit(solution)/shard_map/ppermute | solution.py:421
  23.6 10.1 %collective-permute-start.5 = (bf16[128,768]{1,0:T(8,128)(2,1)S(1)}, bf16[128,768]{1,0:T(8,128)(2,1)S(1)}, u32[]{:S(2)}, u32[]{:S(2)}) collective-permute-start(bf16[128,768]{1,0:T(8,128)(2,1)S(1)} %collective-permute-done.2.refs_0_.refs_3_), channel_id=1, source_target_pairs={{0,4},{4,0},{8,12},{12,8},{16,20},{20,16},{24,28},{28,24},{1,5},{5... | collective-permute-start | bytes 589832 | tf_op jit(solution)/shard_map/ppermute | solution.py:427
  23.6 10.2 %collective-permute-start.4 = (bf16[128,768]{1,0:T(8,128)(2,1)S(1)}, bf16[128,768]{1,0:T(8,128)(2,1)S(1)}, u32[]{:S(2)}, u32[]{:S(2)}) collective-permute-start(bf16[128,768]{1,0:T(8,128)(2,1)S(1)} %collective-permute-done.1.refs_2_), channel_id=1, source_target_pairs={{0,4},{4,0},{8,12},{12,8},{16,20},{20,16},{24,28},{28,24},{1,5},{5... | collective-permute-start | bytes 589832 | tf_op jit(solution)/shard_map/ppermute | solution.py:427
  34.8 8.3 %collective-permute-start.8 = (bf16[128,768]{1,0:T(8,128)(2,1)S(1)}, bf16[128,768]{1,0:T(8,128)(2,1)S(1)}, u32[]{:S(2)}, u32[]{:S(2)}) collective-permute-start(bf16[128,768]{1,0:T(8,128)(2,1)S(1)} %get-tuple-element.43), channel_id=1, source_target_pairs={{0,1},{1,0},{2,3},{3,2},{4,5},{5,4},{6,7},{7,6},{8,9},{9,8},{10,11... | collective-permute-start | bytes 589832 | tf_op jit(solution)/shard_map/ppermute | solution.py:421
  36.9 11.0 %collective-permute-start.9 = (bf16[128,768]{1,0:T(8,128)(2,1)S(1)}, bf16[128,768]{1,0:T(8,128)(2,1)S(1)}, u32[]{:S(2)}, u32[]{:S(2)}) collective-permute-start(bf16[128,768]{1,0:T(8,128)(2,1)S(1)} %get-tuple-element.44), channel_id=1, source_target_pairs={{0,2},{1,3},{2,0},{3,1},{4,6},{5,7},{6,4},{7,5},{8,10},{9,11},{10,... | collective-permute-start | bytes 589832 | tf_op jit(solution)/shard_map/ppermute | solution.py:421
  36.9 11.0 %collective-permute-start.10 = (bf16[128,768]{1,0:T(8,128)(2,1)S(1)}, bf16[128,768]{1,0:T(8,128)(2,1)S(1)}, u32[]{:S(2)}, u32[]{:S(2)}) collective-permute-start(bf16[128,768]{1,0:T(8,128)(2,1)S(1)} %get-tuple-element.45), channel_id=1, source_target_pairs={{0,3},{1,2},{2,1},{3,0},{4,7},{5,6},{6,5},{7,4},{8,11},{9,10},{10,... | collective-permute-start | bytes 589832 | tf_op jit(solution)/shard_map/ppermute | solution.py:421
  49.3 11.3 %collective-permute-start.14 = (bf16[128,1408]{1,0:T(8,128)(2,1)S(1)}, bf16[128,1408]{1,0:T(8,128)(2,1)S(1)}, u32[]{:S(2)}, u32[]{:S(2)}) collective-permute-start(bf16[128,1408]{1,0:T(8,128)(2,1)S(1)} %get-tuple-element.51), channel_id=1, source_target_pairs={{0,1},{1,0},{2,3},{3,2},{4,5},{5,4},{6,7},{7,6},{8,9},{9,8},{10,11... | collective-permute-start | bytes 1081352 | tf_op jit(solution)/shard_map/ppermute | solution.py:421
  49.6 17.2 %collective-permute-start.15 = (bf16[128,1408]{1,0:T(8,128)(2,1)S(1)}, bf16[128,1408]{1,0:T(8,128)(2,1)S(1)}, u32[]{:S(2)}, u32[]{:S(2)}) collective-permute-start(bf16[128,1408]{1,0:T(8,128)(2,1)S(1)} %get-tuple-element.52), channel_id=1, source_target_pairs={{0,2},{1,3},{2,0},{3,1},{4,6},{5,7},{6,4},{7,5},{8,10},{9,11},{10,... | collective-permute-start | bytes 1081352 | tf_op jit(solution)/shard_map/ppermute | solution.py:421
  51.0 15.8 %collective-permute-start.16 = (bf16[128,1408]{1,0:T(8,128)(2,1)S(1)}, bf16[128,1408]{1,0:T(8,128)(2,1)S(1)}, u32[]{:S(2)}, u32[]{:S(2)}) collective-permute-start(bf16[128,1408]{1,0:T(8,128)(2,1)S(1)} %get-tuple-element.53), channel_id=1, source_target_pairs={{0,3},{1,2},{2,1},{3,0},{4,7},{5,6},{6,5},{7,4},{8,11},{9,10},{10,... | collective-permute-start | bytes 1081352 | tf_op jit(solution)/shard_map/ppermute | solution.py:421
  73.0 25.5 %collective-permute-start.18 = (bf16[4,128,768]{2,1,0:T(8,128)(2,1)S(1)}, bf16[4,128,768]{2,1,0:T(8,128)(2,1)S(1)}, u32[]{:S(2)}, u32[]{:S(2)}) collective-permute-start(bf16[4,128,768]{2,1,0:T(8,128)(2,1)S(1)} %get-tuple-element.61), channel_id=1, source_target_pairs={{0,4},{4,0},{8,12},{12,8},{16,20},{20,16},{24,28},{28,24},{1,5},{5... | collective-permute-start | bytes 2359304 | tf_op jit(solution)/shard_map/ppermute | solution.py:427
  73.6 10.0 %collective-permute-start.20 = (bf16[400,128]{1,0:T(8,128)(2,1)S(1)}, bf16[400,128]{1,0:T(8,128)(2,1)S(1)}, u32[]{:S(2)}, u32[]{:S(2)}) collective-permute-start(bf16[400,128]{1,0:T(8,128)(2,1)S(1)} %get-tuple-element.63), channel_id=1, source_target_pairs={{0,16},{4,20},{8,24},{12,28},{16,0},{20,4},{24,8},{28,12},{1,17},{... | collective-permute-start | bytes 307208 | tf_op jit(solution)/shard_map/ppermute | solution.py:424
  74.0 9.6 %collective-permute-start.21 = (bf16[400,128]{1,0:T(8,128)(2,1)S(1)}, bf16[400,128]{1,0:T(8,128)(2,1)S(1)}, u32[]{:S(2)}, u32[]{:S(2)}) collective-permute-start(bf16[400,128]{1,0:T(8,128)(2,1)S(1)} %get-tuple-element.64), channel_id=1, source_target_pairs={{0,24},{4,28},{8,16},{12,20},{16,8},{20,12},{24,0},{28,4},{1,25},{... | collective-permute-start | bytes 307208 | tf_op jit(solution)/shard_map/ppermute | solution.py:424
  75.9 9.0 %collective-permute-start.19 = (bf16[400,128]{1,0:T(8,128)(2,1)S(1)}, bf16[400,128]{1,0:T(8,128)(2,1)S(1)}, u32[]{:S(2)}, u32[]{:S(2)}) collective-permute-start(bf16[400,128]{1,0:T(8,128)(2,1)S(1)} %get-tuple-element.59.refs_3_), channel_id=1, source_target_pairs={{0,8},{4,12},{8,0},{12,4},{16,24},{20,28},{24,16},{28,20},{1,9},{5... | collective-permute-start | bytes 307208 | tf_op jit(solution)/shard_map/ppermute | solution.py:424
  98.7 8.9 %collective-permute-start.25 = (bf16[2,128,768]{2,1,0:T(8,128)(2,1)S(1)}, bf16[2,128,768]{2,1,0:T(8,128)(2,1)S(1)}, u32[]{:S(2)}, u32[]{:S(2)}) collective-permute-start(bf16[2,128,768]{2,1,0:T(8,128)(2,1)S(1)} %get-tuple-element.66.refs_4_), channel_id=1, source_target_pairs={{0,8},{4,12},{8,0},{12,4},{16,24},{20,28},{24,16},{28,20},{1,9},{5... | collective-permute-start | bytes 1179656 | tf_op jit(solution)/shard_map/ppermute | solution.py:424
  98.8 9.1 %collective-permute-start.30 = (bf16[4,400,128]{2,1,0:T(8,128)(2,1)S(1)}, bf16[4,400,128]{2,1,0:T(8,128)(2,1)S(1)}, u32[]{:S(2)}, u32[]{:S(2)}) collective-permute-start(bf16[4,400,128]{2,1,0:T(8,128)(2,1)S(1)} %shard_map.141.refs_0_), channel_id=1, source_target_pairs={{0,2},{1,3},{2,0},{3,1},{4,6},{5,7},{6,4},{7,5},{8,10},{9,11},{10,... | collective-permute-start | bytes 1228808 | tf_op jit(solution)/shard_map/ppermute | solution.py:421
  99.3 10.0 %collective-permute-start.28 = (bf16[4,400,128]{2,1,0:T(8,128)(2,1)S(1)}, bf16[4,400,128]{2,1,0:T(8,128)(2,1)S(1)}, u32[]{:S(2)}, u32[]{:S(2)}) collective-permute-start(bf16[4,400,128]{2,1,0:T(8,128)(2,1)S(1)} %shard_map.141.refs_0_), channel_id=1, source_target_pairs={{0,1},{1,0},{2,3},{3,2},{4,5},{5,4},{6,7},{7,6},{8,9},{9,8},{10,11... | collective-permute-start | bytes 1228808 | tf_op jit(solution)/shard_map/ppermute | solution.py:421
  107.7 8.4 %collective-permute-start.26 = (bf16[1,128,768]{2,1,0:T(8,128)(2,1)S(1)}, bf16[1,128,768]{2,1,0:T(8,128)(2,1)S(1)}, u32[]{:S(2)}, u32[]{:S(2)}) collective-permute-start(bf16[1,128,768]{2,1,0:T(8,128)(2,1)S(1)} %get-tuple-element.68), channel_id=1, source_target_pairs={{0,16},{4,20},{8,24},{12,28},{16,0},{20,4},{24,8},{28,12},{1,17},{... | collective-permute-start | bytes 589832 | tf_op jit(solution)/shard_map/ppermute | solution.py:424
  107.8 11.5 %collective-permute-start.27 = (bf16[4,400,128]{2,1,0:T(8,128)(2,1)S(1)}, bf16[4,400,128]{2,1,0:T(8,128)(2,1)S(1)}, u32[]{:S(2)}, u32[]{:S(2)}) collective-permute-start(bf16[4,400,128]{2,1,0:T(8,128)(2,1)S(1)} %shard_map.141.refs_0_), channel_id=1, source_target_pairs={{0,4},{4,0},{8,12},{12,8},{16,20},{20,16},{24,28},{28,24},{1,5},{5... | collective-permute-start | bytes 1228808 | tf_op jit(solution)/shard_map/ppermute | solution.py:427
  110.0 9.2 %collective-permute-start.31 = (bf16[4,400,128]{2,1,0:T(8,128)(2,1)S(1)}, bf16[4,400,128]{2,1,0:T(8,128)(2,1)S(1)}, u32[]{:S(2)}, u32[]{:S(2)}) collective-permute-start(bf16[4,400,128]{2,1,0:T(8,128)(2,1)S(1)} %collective-permute-done.30.refs_2_), channel_id=1, source_target_pairs={{0,4},{4,0},{8,12},{12,8},{16,20},{20,16},{24,28},{28,24},{1,5},{5... | collective-permute-start | bytes 1228808 | tf_op jit(solution)/shard_map/ppermute | solution.py:427
  (22 other events, 116.3 us)

commit v4 on v3

--- a/solution.py
+++ b/solution.py
@@ -72,7 +72,7 @@
 def densify(rows, cols, count, values, nd, rs, cs, after):
     rt, ct, half = nd * cs, nd * rs, rs // 2
 
-    def body(rows_ref, cols_ref, count_ref, values_ref, tile_ref, turned_ref, mass_ref, acc):
+    def body(rows_ref, cols_ref, count_ref, values_ref, tile_ref, turned_ref, acc):
         i, j = lax.axis_index("row"), lax.axis_index("col")
         z, c = i // 2, lax.rem(i, 2)
         acc[...] = jnp.zeros_like(acc)
@@ -88,41 +88,65 @@
 
         lax.fori_loop(0, count_ref[0], add, 0)
         tile_ref[...] = acc[...].astype(BF16)
+        for k in range(rs):
+            cut = acc[:, k * nd : (k + 1) * nd]
+            turned_ref[k * nd : (k + 1) * nd, :] = cut.T.astype(BF16)
+
+    return call(
+        body,
+        [shape((rt, ct), BF16), shape((ct, rt), BF16)],
+        [rows, cols, count, values],
+        [pltpu.VMEM((rt, ct), F32)],
+        smem=3,
+        flops=rt * ct,
+        after=after,
+    )
+
+
+def tile_columns(tile_ref, places, nd):
+    return jnp.concatenate([tile_ref[:, p * nd : (p + 1) * nd] for p in places], axis=1)
+
+
+def forward_first(tile, places, blocks, nd, cs, after):
+    rt, ct = tile.shape
+    width = blocks[0].shape[1]
+
+    def body(*refs):
+        tile_ref, feat_refs = refs[0], refs[1 : 1 + len(blocks)]
+        sum_ref, mass_ref = refs[1 + len(blocks) :]
+        j = lax.axis_index("col")
+        feats = jnp.concatenate([r[...] for r in feat_refs], axis=0)
+        sum_ref[...] = mm(tile_columns(tile_ref, places, nd), feats)
         ones = jnp.ones((8, ct), BF16)
         for k in range(cs):
             place = pl.multiple_of((j ^ k) * nd, nd)
             mass_ref[:, pl.ds(place, nd)] = mm(ones, tile_ref[k * nd : (k + 1) * nd, :], 1, 1)
-        for k in range(rs):
-            cut = acc[:, k * nd : (k + 1) * nd]
-            turned_ref[k * nd : (k + 1) * nd, :] = cut.T.astype(BF16)
-
-    return call(
-        body,
-        [shape((rt, ct), BF16), shape((ct, rt), BF16), shape((8, rt), F32)],
-        [rows, cols, count, values],
-        [pltpu.VMEM((rt, ct), F32)],
-        smem=3,
-        flops=2 * 8 * rt * ct,
-        after=after,
-    )
-
-
-def forward_parts(tile, blocks, nd, cs, after):
+
+    return call(
+        body,
+        [shape((rt, width), F32), shape((8, rt), F32)],
+        [tile, *blocks],
+        flops=2 * rt * len(places) * nd * width,
+        after=after,
+    )
+
+
+def forward_parts(begun, tile, places, blocks, nd, cs, after):
     width = blocks[0].shape[1]
 
     def body(*refs):
-        tile_ref, feat_refs = refs[0], refs[1 : 1 + len(blocks)]
-        outs = refs[1 + len(blocks) :]
+        sum_ref, tile_ref, feat_refs = refs[0], refs[1], refs[2 : 2 + len(blocks)]
+        outs = refs[2 + len(blocks) :]
         feats = jnp.concatenate([r[...] for r in feat_refs], axis=0)
-        parts = mm(tile_ref[...], feats)
+        parts = sum_ref[...] + mm(tile_columns(tile_ref, places, nd), feats)
         for k in range(cs):
             outs[k][...] = parts[k * nd : (k + 1) * nd].astype(outs[k].dtype)
 
     return call(
         body,
         [shape((nd, width), BF16 if k else F32) for k in range(cs)],
-        [tile, *blocks],
-        flops=2 * tile.size * width,
+        [begun, tile, *blocks],
+        flops=2 * tile.shape[0] * len(places) * nd * width,
         after=after,
     )
 
@@ -178,7 +202,7 @@
     return jnp.concatenate([high, total - high], axis=0)
 
 
-def weight_parts(packs, sums, rs, xr, nc):
+def weight_parts(packs, sums, rs, xr, nc, after):
     cs = len(packs)
     hid = sums.shape[1]
     nd, xw = packs[0].shape[0], packs[0].shape[1] - hid
@@ -207,21 +231,23 @@
         [*packs, sums],
         [pltpu.VMEM((xw, hid), F32)],
         flops=2 * cs * nd * xw * hid,
-    )
-
-
-def scaled_parts(packs, inverse, turned_neigh, turned_self, rs, after):
-    cs = len(packs)
+        after=after,
+    )
+
+
+def scaled_parts(packs, first, inverse, turned_neigh, turned_self, cs, rs, after=()):
+    count = len(packs)
     nd = packs[0].shape[0]
     hid, depth = turned_neigh.shape
 
     def body(neigh_ref, own_ref, inv_ref, *refs):
-        pack_refs, scaled_ref, self_ref = refs[:cs], refs[cs], refs[cs + 1]
+        pack_refs, scaled_ref, self_ref = refs[:count], refs[count], refs[count + 1]
         i, j = lax.axis_index("row"), lax.axis_index("col")
         grads = jnp.concatenate([r[:, :hid] for r in pack_refs], axis=0)
         product = mm(grads, neigh_ref[...])
-        for r in range(cs):
-            inv = inv_ref[pl.ds(pl.multiple_of((j ^ r) * nd, nd), nd), :]
+        for r in range(count):
+            start = pl.multiple_of((j ^ (first + r)) * nd, nd)
+            inv = inv_ref[pl.ds(start, nd), :]
             inv = jnp.concatenate([inv] * (depth // LANES), axis=1)
             rows = slice(r * nd, (r + 1) * nd)
             scaled_ref[rows, :] = (product[rows] * inv).astype(BF16)
@@ -232,9 +258,9 @@
 
     return call(
         body,
-        [shape((cs * nd, depth), BF16), shape((cs * nd, depth), F32)],
+        [shape((count * nd, depth), BF16), shape((count * nd, depth), F32)],
         [turned_neigh, turned_self, inverse, *packs],
-        flops=4 * cs * nd * hid * depth,
+        flops=4 * count * nd * hid * depth,
         after=after,
     )
 
@@ -248,21 +274,26 @@
     return order
 
 
-def back_parts(turned, scaled, self_part, nd, cs, rs, after):
-    depth = scaled.shape[1]
+def back_parts(turned, scaled, self_parts, nd, cs, rs, after):
+    depth = scaled[0].shape[1]
     half = rs // 2
-
-    def body(tile_ref, scaled_ref, self_ref, keep_ref, send_ref, acc):
+    count = len(scaled)
+    each = cs // count
+
+    def body(tile_ref, *refs):
+        scaled_refs, self_refs = refs[:count], refs[count : 2 * count]
+        keep_ref, send_ref, acc = refs[2 * count :]
         i, j = lax.axis_index("row"), lax.axis_index("col")
         z, c = i // 2, lax.rem(i, 2)
-        acc[...] = mm(tile_ref[...], scaled_ref[...])
+        acc[...] = mm(tile_ref[...], jnp.concatenate([r[...] for r in scaled_refs], axis=0))
 
         @pl.when(i * cs // rs == j)
         def _():
             for r in range(cs):
                 q = i * cs - j * rs + (j ^ r)
                 place = ((z ^ (q // 2)) + half * (lax.rem(q, 2) ^ c)) * nd
-                acc[pl.ds(pl.multiple_of(place, nd), nd), :] += self_ref[r * nd : (r + 1) * nd]
+                rows = slice(r % each * nd, (r % each + 1) * nd)
+                acc[pl.ds(pl.multiple_of(place, nd), nd), :] += self_refs[r // each][rows]
 
         for ref, base in ((send_ref, half), (keep_ref, 0)):
             for k, distance in enumerate(halving_order(half)):
@@ -273,7 +304,7 @@
     return call(
         body,
         [shape(dims, F32), shape(dims, BF16)],
-        [turned, scaled, self_part],
+        [turned, *scaled, *self_parts],
         [pltpu.VMEM((rs * nd, depth), F32)],
         flops=2 * turned.size * depth,
         after=after,
@@ -426,22 +457,41 @@
     def other_core(x):
         return lax.ppermute(x, "row", [(s, s ^ 1) for s in range(rs)])
 
-    def gather_chips(x, after=()):
+    def gather_chips(x):
         found = {0: x}
         step = half // 2
         while step:
-            if step == 1 and after:
-                last = {d: follow(y, after) if d else y for d, y in found.items()}
-            else:
-                last = found
-            found.update({d + step: along_chips(last[d], step) for d in list(found)})
+            found.update({d + step: along_chips(found[d], step) for d in list(found)})
             step //= 2
         return [found[d] for d in range(half)]
 
-    swap = [((b % rs) * cs + b // rs, b) for b in range(rs * cs)]
-    across = other_core(features)
-    own_feat = lax.ppermute(features, ("row", "col"), swap)
-    tile, turned, mass = densify(
+    if rs == 2 * cs:
+
+        def send_own(block, t):
+            pairs = []
+            for z in range(half):
+                for core in range(2):
+                    q = 2 * (z ^ t) + core
+                    source = (2 * z + core) * cs + z
+                    pairs.append((source, (2 * z + q // cs) * cs + q % cs))
+            return lax.ppermute(block, ("row", "col"), pairs)
+
+    else:
+        swap = [((b % rs) * cs + b // rs, b) for b in range(rs * cs)]
+
+        def send_own(block, t):
+            return lax.ppermute(block, ("row", "col"), swap if t == 0 else [])
+
+    near = along_chips(features, 1)
+    mine_first = {0: features, 1: near}
+    step = half // 2
+    while step > 1:
+        evens = [d for d in mine_first if d % 2 == 0]
+        mine_first.update({d + step: along_chips(mine_first[d], step) for d in evens})
+        step //= 2
+    theirs_first = {0: other_core(features), 1: other_core(near)}
+    own_feats = {0: send_own(features, 0)}
+    tile, turned = densify(
         block_rows.reshape(-1),
         block_cols.reshape(-1),
         block_count.reshape(-1),
@@ -449,18 +499,36 @@
         nd,
         rs,
         cs,
-        [across],
-    )
-    blocks = gather_chips(features, [mass])
-    blocks = blocks + [across] + [other_core(x) for x in blocks[1:]]
+        [near, theirs_first[0], own_feats[0]],
+    )
+    mine_first.update(
+        {d: follow(x, [tile, theirs_first[1]]) for d, x in mine_first.items() if d > 1}
+    )
+    mine_last = {d + 1: along_chips(x, 1) for d, x in mine_first.items() if d > 1}
+    theirs_first.update({d: other_core(x) for d, x in mine_first.items() if d > 1})
+    theirs_last = {d: other_core(x) for d, x in mine_last.items()}
+    own_feats.update({d: send_own(x, d) for d, x in mine_first.items() if d})
+    own_feats.update({d: send_own(x, d) for d, x in mine_last.items()})
+
+    def placed(mine, theirs):
+        places = list(mine) + [half + d for d in theirs]
+        return places, [*mine.values(), *theirs.values()]
+
+    begun, mass = forward_first(
+        tile, *placed(mine_first, theirs_first), nd, cs, [own_feats[1]]
+    )
+    evens = [x for d, x in own_feats.items() if d and d % 2 == 0]
+    parts = forward_parts(begun, tile, *placed(mine_last, theirs_last), nd, cs, evens)
+    own_feat = sum(list(own_feats.values())[1:], own_feats[0])
     degree = mass
-    for k in range(1, cs):
-        degree = degree + along_col(mass, k)
+    step = 1
+    while step < cs:
+        degree = degree + along_col(degree, step)
+        step *= 2
     inverse = 1.0 / (degree[0] + 1.0)
     inverse = jnp.broadcast_to(inverse[:, None], (rt, LANES))
     own = jnp.dot(own_feat, w_self, preferred_element_type=F32).astype(BF16)
 
-    parts = forward_parts(tile, blocks, nd, cs, [own_feat])
     turned_neigh, turned_self = turn([w_neigh, w_self], [parts[0]])
     parts = [parts[0]] + [along_col(parts[k], k) for k in range(1, cs)]
     output, sums, *packs = activation(
@@ -468,15 +536,19 @@
     )
     packs = [packs[0]] + [along_col(packs[k], k) for k in range(1, cs)]
 
-    keep, send = weight_parts(packs, sums, rs, xr, nc)
+    mid = cs // 2
+    scaled_args = (inverse, turned_neigh, turned_self, cs, rs)
+    early = scaled_parts(packs[:mid], 0, *scaled_args)
+    keep, send = weight_parts(packs, sums, rs, xr, nc, early[:1])
     came = other_core(send)
-    scaled, self_part = scaled_parts(packs, inverse, turned_neigh, turned_self, rs, [keep])
+    late = scaled_parts(packs[mid:], mid, *scaled_args, [keep])
+    scaled, self_parts = zip(early, late)
     chunks = pair_sum(keep, came)
     back_after = [chunks[1]]
     chunks = [chunks[0]] + [along_chips(chunks[k], k) for k in range(1, half)]
     line = gather_chips(last_sum(chunks))
 
-    keep, send = back_parts(turned, scaled, self_part, nd, cs, rs, back_after)
+    keep, send = back_parts(turned, scaled, self_parts, nd, cs, rs, back_after)
     keep, send = fold(keep, other_core(send), line[1:])
     line = stack(line, [send])
     step = 1

time: 122 us -> 117 us (0.959)
  waiting for transfers between devices: 67.5 us -> 60.7 us
  starting transfers between devices: 28.4 us -> 34.4 us
  local copies, waits for them, and re-layouts: 4.89 us -> 2.63 us
  matrix products: 1.78 us -> 0.38 us
    ppermute x11, waiting for transfers between devices: 48 us -> 34.8 us  [along_chips(): return lax.ppermute(x, 'row', [(s, s ^ 2 * k) for s in range(rs)])]
    ppermute x1 -> x4, starting transfers between devices: 1.57 us -> 7.81 us  [send_own(): return lax.ppermute(block, ('row', 'col'), pairs)]
    ppermute x13 -> x12, waiting for transfers between devices: 19.5 us -> 23.1 us  [along_col(): return lax.ppermute(x, 'col', [(s, s ^ k) for s in range(cs)])]
    ppermute x11, waiting for transfers between devices: 0.03 us -> 2.86 us  [other_core(): return lax.ppermute(x, 'row', [(s, s ^ 1) for s in range(rs)])]
    unnamed x20 -> x22, local copies, waits for them, and re-layouts: 4.74 us -> 2.48 us
    dot_general x1, matrix products: 1.78 us -> 0.38 us  [local(): own = jnp.dot(own_feat, w_self, preferred_element_type=F32).astype(BF16)]
    ppermute x11, starting transfers between devices: 2.31 us -> 3.54 us  [other_core(): return lax.ppermute(x, 'row', [(s, s ^ 1) for s in range(rs)])]
    pallas_call x14 -> x16, Pallas kernels: 13.4 us -> 12.1 us  [call(): pl.pallas_call(run, out_shape=outs, in_specs=[SMEM] * smem + [VMEM] * (co...]
  transfers between devices with their start and end apart: 36 -> 38, of which waited for: 13 -> 19; matrix products, arithmetic and copies ran while one was open for 1% -> 0% of each run, Pallas kernels for 9% -> 9%
where the time goes in v4:
time: 117 us; the launch traced here: 116 us
  waiting for transfers between devices  60.7 us (52%)
  starting transfers between devices  34.4 us (29%)
  Pallas kernels  16.4 us (14%)
  local copies, waits for them, and re-layouts  2.63 us (2%)
  between operations  1.65 us (1%)
    ppermute x11, waiting for transfers between devices, along_chips(): return lax.ppermute(x, 'row', [(s, s ^ 2 * k) for s in range(rs)])  34.8 us
    ppermute x12, waiting for transfers between devices, along_col(): return lax.ppermute(x, 'col', [(s, s ^ k) for s in range(cs)])  23.1 us
    pallas_call x16, Pallas kernels, call(): pl.pallas_call(run, out_shape=outs, in_specs=[SMEM] * smem + [VMEM] * (co...  12.1 us
    ppermute x12, starting transfers between devices, along_col(): return lax.ppermute(x, 'col', [(s, s ^ k) for s in range(cs)])  11.7 us
    ppermute x11, starting transfers between devices, along_chips(): return lax.ppermute(x, 'row', [(s, s ^ 2 * k) for s in range(rs)])  11.4 us
    ppermute x4, starting transfers between devices, send_own(): return lax.ppermute(block, ('row', 'col'), pairs)  7.81 us
    pallas_call x2, Pallas kernels, assemble(): pl.pallas_call(run, out_shape=[weight, weight, shape((1, hid), F32)], in_...  4.22 us
    ppermute x11, starting transfers between devices, other_core(): return lax.ppermute(x, 'row', [(s, s ^ 1) for s in range(rs)])  3.54 us
  transfers between devices with their start and end apart: 38, of which 19 were waited for; matrix products, arithmetic and copies ran while one was open for 0% of the time, Pallas kernels for 9%

profile of v4, /device:TPU:0, one launch (start us, length us, event | category | flops | bytes accessed | tf_op | source)
XLA Modules:
  0.0 116.2 jit_solution(16077882093504260591)
XLA Ops:
  0.6 3.1 %collective-permute-start = (bf16[128,768]{1,0:T(8,128)(2,1)}, bf16[128,768]{1,0:T(8,128)(2,1)S(1)}, u32[]{:S(2)}, u32[]{:S(2)}) collective-permute-start(bf16[128,768]{1,0:T(8,128)(2,1)} %refs_1_.2), channel_id=1, source_target_pairs={{0,8},{4,12},{8,0},{12,4},{16,24},{20,28},{24,16},{28,20},{1,9},{5... | collective-permute-start | bytes 589832 | tf_op jit(solution)/shard_map/ppermute | solution.py:455
  3.7 1.6 %collective-permute-start.2 = (bf16[128,768]{1,0:T(8,128)(2,1)}, bf16[128,768]{1,0:T(8,128)(2,1)S(1)}, u32[]{:S(2)}, u32[]{:S(2)}) collective-permute-start(bf16[128,768]{1,0:T(8,128)(2,1)} %refs_1_.2), channel_id=1, source_target_pairs={{0,0},{4,1},{9,10},{13,11},{18,20},{22,21},{27,30},{31,31}} | collective-permute-start | bytes 589832 | tf_op jit(solution)/shard_map/ppermute | solution.py:477
  5.3 2.0 %collective-permute-start.1 = (bf16[128,768]{1,0:T(8,128)(2,1)}, bf16[128,768]{1,0:T(8,128)(2,1)S(1)}, u32[]{:S(2)}, u32[]{:S(2)}) collective-permute-start(bf16[128,768]{1,0:T(8,128)(2,1)} %refs_1_.2), channel_id=1, source_target_pairs={{0,4},{4,0},{8,12},{12,8},{16,20},{20,16},{24,28},{28,24},{1,5},{5... | collective-permute-start | bytes 589832 | tf_op jit(solution)/shard_map/ppermute | solution.py:458
  7.3 1.5 %collective-permute-done.refs_4_.refs_2_ = bf16[128,768]{1,0:T(8,128)(2,1)S(1)} collective-permute-done((bf16[128,768]{1,0:T(8,128)(2,1)}, bf16[128,768]{1,0:T(8,128)(2,1)S(1)}, u32[]{:S(2)}, u32[]{:S(2)}) %collective-permute-start) | collective-permute-done | bytes 196640 | tf_op jit(solution)/shard_map/ppermute | solution.py:455
  9.5 3.6 %collective-permute-start.6 = (bf16[128,768]{1,0:T(8,128)(2,1)S(1)}, bf16[128,768]{1,0:T(8,128)(2,1)S(1)}, u32[]{:S(2)}, u32[]{:S(2)}) collective-permute-start(bf16[128,768]{1,0:T(8,128)(2,1)S(1)} %collective-permute-done.refs_4_.refs_2_), channel_id=1, source_target_pairs={{0,2},{4,3},{9,8},{13,9},{18,22},{22,23},{27,28},{31,29}} | collective-permute-start | bytes 589832 | tf_op jit(solution)/shard_map/ppermute | solution.py:477
  15.6 1.5 %shard_map.128 = (bf16[512,1024]{1,0:T(8,128)(2,1)S(1)}, bf16[1024,512]{1,0:T(8,128)(2,1)S(1)}) custom-call(s32[24]{0:T(128)S(1)} %bitcast.12, s32[24]{0:T(128)S(1)} %bitcast.13, s32[1]{0:T(128)} %bitcast.9.refs_2_, bf16[24,128,128]{2,1,0:T(8,128)(2,1)S(1)} %bitcast.10, bf16[128,768]{1,0:T(8,128)(2,1)S(1)} %collective-permute-done.refs_4_.refs_2_, ...), custom_call_target="tpu_custom_call" | custom-call | flops 524288 | bytes 2883780 | tf_op jit(solution)/shard_map/pallas_call | solution.py:27
  17.1 1.8 %collective-permute-done.3.refs_0_ = bf16[128,768]{1,0:T(8,128)(2,1)S(1)} collective-permute-done((bf16[128,768]{1,0:T(8,128)(2,1)}, bf16[128,768]{1,0:T(8,128)(2,1)S(1)}, u32[]{:S(2)}, u32[]{:S(2)}) %collective-permute-start.3) | collective-permute-done | bytes 196640 | tf_op jit(solution)/shard_map/ppermute | solution.py:455
  21.8 3.7 %collective-permute-done.13 = f32[8,512]{1,0:T(8,128)S(1)} collective-permute-done((f32[8,512]{1,0:T(8,128)S(1)}, f32[8,512]{1,0:T(8,128)S(1)}, u32[]{:S(2)}, u32[]{:S(2)}) %collective-permute-start.13) | collective-permute-done | bytes 16416 | tf_op jit(solution)/shard_map/ppermute | solution.py:452
  31.0 3.4 %collective-permute-start.12 = (bf16[128,768]{1,0:T(8,128)(2,1)S(1)}, bf16[128,768]{1,0:T(8,128)(2,1)S(1)}, u32[]{:S(2)}, u32[]{:S(2)}) collective-permute-start(bf16[128,768]{1,0:T(8,128)(2,1)S(1)} %get-tuple-element.48), channel_id=1, source_target_pairs={{0,3},{1,2},{2,1},{3,0},{4,7},{5,6},{6,5},{7,4},{8,11},{9,10},{10,... | collective-permute-start | bytes 589832 | tf_op jit(solution)/shard_map/ppermute | solution.py:452
  34.4 2.4 %shard_map.132 = (bf16[1024,768]{1,0:T(8,128)(2,1)S(1)}, bf16[1024,768]{1,0:T(8,128)(2,1)S(1)}) custom-call(bf16[768,1024]{1,0:T(8,128)(2,1)S(1)} %copy-done.2, bf16[768,1024]{1,0:T(8,128)(2,1)} %refs_1_.3, f32[128,768]{1,0:T(8,128)S(1)} %get-tuple-element.45.refs_2_.refs_0_), custom_call_target="tpu_custom_call" | custom-call | bytes 6291456 | tf_op jit(solution)/shard_map/pallas_call | solution.py:27
  38.6 4.1 %collective-permute-done.11.refs_2_ = bf16[128,768]{1,0:T(8,128)(2,1)S(1)} collective-permute-done((bf16[128,768]{1,0:T(8,128)(2,1)S(1)}, bf16[128,768]{1,0:T(8,128)(2,1)S(1)}, u32[]{:S(2)}, u32[]{:S(2)}) %collective-permute-start.11) | collective-permute-done | bytes 196640 | tf_op jit(solution)/shard_map/ppermute | solution.py:452
  45.3 2.4 %collective-permute-start.18 = (bf16[128,1408]{1,0:T(8,128)(2,1)S(1)}, bf16[128,1408]{1,0:T(8,128)(2,1)S(1)}, u32[]{:S(2)}, u32[]{:S(2)}) collective-permute-start(bf16[128,1408]{1,0:T(8,128)(2,1)S(1)} %get-tuple-element.58), channel_id=1, source_target_pairs={{0,3},{1,2},{2,1},{3,0},{4,7},{5,6},{6,5},{7,4},{8,11},{9,10},{10,... | collective-permute-start | bytes 1081352 | tf_op jit(solution)/shard_map/ppermute | solution.py:452
  47.7 7.8 %collective-permute-done.16.refs_4_.refs_1_ = bf16[128,1408]{1,0:T(8,128)(2,1)S(1)} collective-permute-done((bf16[128,1408]{1,0:T(8,128)(2,1)S(1)}, bf16[128,1408]{1,0:T(8,128)(2,1)S(1)}, u32[]{:S(2)}, u32[]{:S(2)}) %collective-permute-start.16) | collective-permute-done | bytes 360480 | tf_op jit(solution)/shard_map/ppermute | solution.py:452
  56.6 5.7 %collective-permute-done.17.refs_2_.refs_3_ = bf16[128,1408]{1,0:T(8,128)(2,1)S(1)} collective-permute-done((bf16[128,1408]{1,0:T(8,128)(2,1)S(1)}, bf16[128,1408]{1,0:T(8,128)(2,1)S(1)}, u32[]{:S(2)}, u32[]{:S(2)}) %collective-permute-start.17) | collective-permute-done | bytes 360480 | tf_op jit(solution)/shard_map/ppermute | solution.py:452
  66.6 4.7 %collective-permute-start.22 = (bf16[400,128]{1,0:T(8,128)(2,1)S(1)}, bf16[400,128]{1,0:T(8,128)(2,1)S(1)}, u32[]{:S(2)}, u32[]{:S(2)}) collective-permute-start(bf16[400,128]{1,0:T(8,128)(2,1)S(1)} %get-tuple-element.69), channel_id=1, source_target_pairs={{0,16},{4,20},{8,24},{12,28},{16,0},{20,4},{24,8},{28,12},{1,17},{... | collective-permute-start | bytes 307208 | tf_op jit(solution)/shard_map/ppermute | solution.py:455
  71.9 7.0 %collective-permute-done.22.refs_2_ = bf16[400,128]{1,0:T(8,128)(2,1)S(1)} collective-permute-done((bf16[400,128]{1,0:T(8,128)(2,1)S(1)}, bf16[400,128]{1,0:T(8,128)(2,1)S(1)}, u32[]{:S(2)}, u32[]{:S(2)}) %collective-permute-start.22) | collective-permute-done | bytes 102432 | tf_op jit(solution)/shard_map/ppermute | solution.py:455
  78.9 1.6 %collective-permute-done.21.refs_1_ = bf16[400,128]{1,0:T(8,128)(2,1)S(1)} collective-permute-done((bf16[400,128]{1,0:T(8,128)(2,1)S(1)}, bf16[400,128]{1,0:T(8,128)(2,1)S(1)}, u32[]{:S(2)}, u32[]{:S(2)}) %collective-permute-start.21) | collective-permute-done | bytes 102432 | tf_op jit(solution)/shard_map/ppermute | solution.py:455
  80.5 1.7 %collective-permute-start.25 = (bf16[400,128]{1,0:T(8,128)(2,1)S(1)}, bf16[400,128]{1,0:T(8,128)(2,1)S(1)}, u32[]{:S(2)}, u32[]{:S(2)}) collective-permute-start(bf16[400,128]{1,0:T(8,128)(2,1)S(1)} %shard_map.139.refs_0_), channel_id=1, source_target_pairs={{0,16},{4,20},{8,24},{12,28},{16,0},{20,4},{24,8},{28,12},{1,17},{... | collective-permute-start | bytes 307208 | tf_op jit(solution)/shard_map/ppermute | solution.py:455
  82.9 5.1 %collective-permute-done.25.refs_3_.refs_2_ = bf16[400,128]{1,0:T(8,128)(2,1)S(1)} collective-permute-done((bf16[400,128]{1,0:T(8,128)(2,1)S(1)}, bf16[400,128]{1,0:T(8,128)(2,1)S(1)}, u32[]{:S(2)}, u32[]{:S(2)}) %collective-permute-start.25) | collective-permute-done | bytes 102432 | tf_op jit(solution)/shard_map/ppermute | solution.py:455
  88.3 5.3 %collective-permute-done.26.refs_4_.refs_3_ = bf16[400,128]{1,0:T(8,128)(2,1)S(1)} collective-permute-done((bf16[400,128]{1,0:T(8,128)(2,1)S(1)}, bf16[400,128]{1,0:T(8,128)(2,1)S(1)}, u32[]{:S(2)}, u32[]{:S(2)}) %collective-permute-start.26) | collective-permute-done | bytes 102432 | tf_op jit(solution)/shard_map/ppermute | solution.py:455
  95.6 7.2 %collective-permute-done.27.refs_1_ = bf16[2,128,768]{2,1,0:T(8,128)(2,1)S(1)} collective-permute-done((bf16[2,128,768]{2,1,0:T(8,128)(2,1)S(1)}, bf16[2,128,768]{2,1,0:T(8,128)(2,1)S(1)}, u32[]{:S(2)}, u32[]{:S(2)}) %collective-permute-start.27) | collective-permute-done | bytes 393248 | tf_op jit(solution)/shard_map/ppermute | solution.py:455
  105.3 5.3 %collective-permute-done.28.refs_1_ = bf16[1,128,768]{2,1,0:T(8,128)(2,1)S(1)} collective-permute-done((bf16[1,128,768]{2,1,0:T(8,128)(2,1)S(1)}, bf16[1,128,768]{2,1,0:T(8,128)(2,1)S(1)}, u32[]{:S(2)}, u32[]{:S(2)}) %collective-permute-start.28) | collective-permute-done | bytes 196640 | tf_op jit(solution)/shard_map/ppermute | solution.py:455
  111.9 1.8 %shard_map.144 = (f32[768,1024]{1,0:T(8,128)}, f32[768,1024]{1,0:T(8,128)}, f32[1,1024]{1,0:T(1,128)S(1)}) custom-call(bf16[4,400,128]{2,1,0:T(8,128)(2,1)S(1)} %shard_map.143.refs_0_, bf16[4,400,128]{2,1,0:T(8,128)(2,1)S(1)} %collective-permute-done.30.refs_1_, bf16[4,400,128]{2,1,0:T(8,128)(2,1)S(1)} %collective-permute-done.32.refs_2_, ...), custom_call_target="tpu_custom_call" | custom-call | bytes 9437184 | tf_op jit(solution)/shard_map/pallas_call | solution.py:420
  113.8 2.4 %shard_map.145 = (f32[768,1024]{1,0:T(8,128)}, f32[768,1024]{1,0:T(8,128)}, f32[1,1024]{1,0:T(1,128)}) custom-call(bf16[4,400,128]{2,1,0:T(8,128)(2,1)S(1)} %collective-permute-done.29.refs_0_, bf16[4,400,128]{2,1,0:T(8,128)(2,1)S(1)} %collective-permute-done.31.refs_1_, ...), custom_call_target="tpu_custom_call", output_to_operand_aliasing={{0}: (5, {}), {1}: (6, {})} | custom-call | bytes 9437184 | tf_op jit(solution)/shard_map/pallas_call | solution.py:420
  (99 shorter events, 27.9 us)
Async XLA Ops:
  0.6 8.2 %collective-permute-start = (bf16[128,768]{1,0:T(8,128)(2,1)}, bf16[128,768]{1,0:T(8,128)(2,1)S(1)}, u32[]{:S(2)}, u32[]{:S(2)}) collective-permute-start(bf16[128,768]{1,0:T(8,128)(2,1)} %refs_1_.2), channel_id=1, source_target_pairs={{0,8},{4,12},{8,0},{12,4},{16,24},{20,28},{24,16},{28,20},{1,9},{5... | collective-permute-start | bytes 589832 | tf_op jit(solution)/shard_map/ppermute | solution.py:455
  3.7 9.4 %collective-permute-start.2 = (bf16[128,768]{1,0:T(8,128)(2,1)}, bf16[128,768]{1,0:T(8,128)(2,1)S(1)}, u32[]{:S(2)}, u32[]{:S(2)}) collective-permute-start(bf16[128,768]{1,0:T(8,128)(2,1)} %refs_1_.2), channel_id=1, source_target_pairs={{0,0},{4,1},{9,10},{13,11},{18,20},{22,21},{27,30},{31,31}} | collective-permute-start | bytes 589832 | tf_op jit(solution)/shard_map/ppermute | solution.py:477
  5.3 7.8 %collective-permute-start.1 = (bf16[128,768]{1,0:T(8,128)(2,1)}, bf16[128,768]{1,0:T(8,128)(2,1)S(1)}, u32[]{:S(2)}, u32[]{:S(2)}) collective-permute-start(bf16[128,768]{1,0:T(8,128)(2,1)} %refs_1_.2), channel_id=1, source_target_pairs={{0,4},{4,0},{8,12},{12,8},{16,20},{20,16},{24,28},{28,24},{1,5},{5... | collective-permute-start | bytes 589832 | tf_op jit(solution)/shard_map/ppermute | solution.py:458
  7.3 11.6 %collective-permute-start.3 = (bf16[128,768]{1,0:T(8,128)(2,1)}, bf16[128,768]{1,0:T(8,128)(2,1)S(1)}, u32[]{:S(2)}, u32[]{:S(2)}) collective-permute-start(bf16[128,768]{1,0:T(8,128)(2,1)} %refs_1_.2), channel_id=1, source_target_pairs={{0,16},{4,20},{8,24},{12,28},{16,0},{20,4},{24,8},{28,12},{1,17},{... | collective-permute-start | bytes 589832 | tf_op jit(solution)/shard_map/ppermute | solution.py:455
  8.8 10.1 %collective-permute-start.4 = (bf16[128,768]{1,0:T(8,128)(2,1)S(1)}, bf16[128,768]{1,0:T(8,128)(2,1)S(1)}, u32[]{:S(2)}, u32[]{:S(2)}) collective-permute-start(bf16[128,768]{1,0:T(8,128)(2,1)S(1)} %collective-permute-done.refs_4_.refs_2_), channel_id=1, source_target_pairs={{0,4},{4,0},{8,12},{12,8},{16,20},{20,16},{24,28},{28,24},{1,5},{5... | collective-permute-start | bytes 589832 | tf_op jit(solution)/shard_map/ppermute | solution.py:458
  9.5 10.1 %collective-permute-start.6 = (bf16[128,768]{1,0:T(8,128)(2,1)S(1)}, bf16[128,768]{1,0:T(8,128)(2,1)S(1)}, u32[]{:S(2)}, u32[]{:S(2)}) collective-permute-start(bf16[128,768]{1,0:T(8,128)(2,1)S(1)} %collective-permute-done.refs_4_.refs_2_), channel_id=1, source_target_pairs={{0,2},{4,3},{9,8},{13,9},{18,22},{22,23},{27,28},{31,29}} | collective-permute-start | bytes 589832 | tf_op jit(solution)/shard_map/ppermute | solution.py:477
  19.6 8.0 %collective-permute-start.7 = (bf16[128,768]{1,0:T(8,128)(2,1)S(1)}, bf16[128,768]{1,0:T(8,128)(2,1)S(1)}, u32[]{:S(2)}, u32[]{:S(2)}) collective-permute-start(bf16[128,768]{1,0:T(8,128)(2,1)S(1)} %shard_map.129.refs_3_), channel_id=1, source_target_pairs={{0,8},{4,12},{8,0},{12,4},{16,24},{20,28},{24,16},{28,20},{1,9},{5... | collective-permute-start | bytes 589832 | tf_op jit(solution)/shard_map/ppermute | solution.py:455
  27.6 9.2 %collective-permute-start.15 = (bf16[128,768]{1,0:T(8,128)(2,1)S(1)}, bf16[128,768]{1,0:T(8,128)(2,1)S(1)}, u32[]{:S(2)}, u32[]{:S(2)}) collective-permute-start(bf16[128,768]{1,0:T(8,128)(2,1)S(1)} %collective-permute-done.7.refs_2_), channel_id=1, source_target_pairs={{0,6},{4,7},{9,12},{13,13},{18,18},{22,19},{27,24},{31,25}} | collective-permute-start | bytes 589832 | tf_op jit(solution)/shard_map/ppermute | solution.py:477
  30.8 7.8 %collective-permute-start.10 = (bf16[128,768]{1,0:T(8,128)(2,1)S(1)}, bf16[128,768]{1,0:T(8,128)(2,1)S(1)}, u32[]{:S(2)}, u32[]{:S(2)}) collective-permute-start(bf16[128,768]{1,0:T(8,128)(2,1)S(1)} %get-tuple-element.46), channel_id=1, source_target_pairs={{0,1},{1,0},{2,3},{3,2},{4,5},{5,4},{6,7},{7,6},{8,9},{9,8},{10,11... | collective-permute-start | bytes 589832 | tf_op jit(solution)/shard_map/ppermute | solution.py:452
  30.9 11.9 %collective-permute-start.11 = (bf16[128,768]{1,0:T(8,128)(2,1)S(1)}, bf16[128,768]{1,0:T(8,128)(2,1)S(1)}, u32[]{:S(2)}, u32[]{:S(2)}) collective-permute-start(bf16[128,768]{1,0:T(8,128)(2,1)S(1)} %get-tuple-element.47), channel_id=1, source_target_pairs={{0,2},{1,3},{2,0},{3,1},{4,6},{5,7},{6,4},{7,5},{8,10},{9,11},{10,... | collective-permute-start | bytes 589832 | tf_op jit(solution)/shard_map/ppermute | solution.py:452
  31.0 11.8 %collective-permute-start.12 = (bf16[128,768]{1,0:T(8,128)(2,1)S(1)}, bf16[128,768]{1,0:T(8,128)(2,1)S(1)}, u32[]{:S(2)}, u32[]{:S(2)}) collective-permute-start(bf16[128,768]{1,0:T(8,128)(2,1)S(1)} %get-tuple-element.48), channel_id=1, source_target_pairs={{0,3},{1,2},{2,1},{3,0},{4,7},{5,6},{6,5},{7,4},{8,11},{9,10},{10,... | collective-permute-start | bytes 589832 | tf_op jit(solution)/shard_map/ppermute | solution.py:452
  44.2 11.3 %collective-permute-start.16 = (bf16[128,1408]{1,0:T(8,128)(2,1)S(1)}, bf16[128,1408]{1,0:T(8,128)(2,1)S(1)}, u32[]{:S(2)}, u32[]{:S(2)}) collective-permute-start(bf16[128,1408]{1,0:T(8,128)(2,1)S(1)} %get-tuple-element.55), channel_id=1, source_target_pairs={{0,1},{1,0},{2,3},{3,2},{4,5},{5,4},{6,7},{7,6},{8,9},{9,8},{10,11... | collective-permute-start | bytes 1081352 | tf_op jit(solution)/shard_map/ppermute | solution.py:452
  45.2 17.1 %collective-permute-start.17 = (bf16[128,1408]{1,0:T(8,128)(2,1)S(1)}, bf16[128,1408]{1,0:T(8,128)(2,1)S(1)}, u32[]{:S(2)}, u32[]{:S(2)}) collective-permute-start(bf16[128,1408]{1,0:T(8,128)(2,1)S(1)} %get-tuple-element.57), channel_id=1, source_target_pairs={{0,2},{1,3},{2,0},{3,1},{4,6},{5,7},{6,4},{7,5},{8,10},{9,11},{10,... | collective-permute-start | bytes 1081352 | tf_op jit(solution)/shard_map/ppermute | solution.py:452
  45.3 17.0 %collective-permute-start.18 = (bf16[128,1408]{1,0:T(8,128)(2,1)S(1)}, bf16[128,1408]{1,0:T(8,128)(2,1)S(1)}, u32[]{:S(2)}, u32[]{:S(2)}) collective-permute-start(bf16[128,1408]{1,0:T(8,128)(2,1)S(1)} %get-tuple-element.58), channel_id=1, source_target_pairs={{0,3},{1,2},{2,1},{3,0},{4,7},{5,6},{6,5},{7,4},{8,11},{9,10},{10,... | collective-permute-start | bytes 1081352 | tf_op jit(solution)/shard_map/ppermute | solution.py:452
  66.4 27.2 %collective-permute-start.20 = (bf16[4,128,768]{2,1,0:T(8,128)(2,1)S(1)}, bf16[4,128,768]{2,1,0:T(8,128)(2,1)S(1)}, u32[]{:S(2)}, u32[]{:S(2)}) collective-permute-start(bf16[4,128,768]{2,1,0:T(8,128)(2,1)S(1)} %get-tuple-element.67), channel_id=1, source_target_pairs={{0,4},{4,0},{8,12},{12,8},{16,20},{20,16},{24,28},{28,24},{1,5},{5... | collective-permute-start | bytes 2359304 | tf_op jit(solution)/shard_map/ppermute | solution.py:458
  66.6 12.2 %collective-permute-start.22 = (bf16[400,128]{1,0:T(8,128)(2,1)S(1)}, bf16[400,128]{1,0:T(8,128)(2,1)S(1)}, u32[]{:S(2)}, u32[]{:S(2)}) collective-permute-start(bf16[400,128]{1,0:T(8,128)(2,1)S(1)} %get-tuple-element.69), channel_id=1, source_target_pairs={{0,16},{4,20},{8,24},{12,28},{16,0},{20,4},{24,8},{28,12},{1,17},{... | collective-permute-start | bytes 307208 | tf_op jit(solution)/shard_map/ppermute | solution.py:455
  71.3 7.6 %collective-permute-start.23 = (bf16[400,128]{1,0:T(8,128)(2,1)S(1)}, bf16[400,128]{1,0:T(8,128)(2,1)S(1)}, u32[]{:S(2)}, u32[]{:S(2)}) collective-permute-start(bf16[400,128]{1,0:T(8,128)(2,1)S(1)} %get-tuple-element.70), channel_id=1, source_target_pairs={{0,24},{4,28},{8,16},{12,20},{16,8},{20,12},{24,0},{28,4},{1,25},{... | collective-permute-start | bytes 307208 | tf_op jit(solution)/shard_map/ppermute | solution.py:455
  71.3 9.2 %collective-permute-start.21 = (bf16[400,128]{1,0:T(8,128)(2,1)S(1)}, bf16[400,128]{1,0:T(8,128)(2,1)S(1)}, u32[]{:S(2)}, u32[]{:S(2)}) collective-permute-start(bf16[400,128]{1,0:T(8,128)(2,1)S(1)} %get-tuple-element.65.refs_5_), channel_id=1, source_target_pairs={{0,8},{4,12},{8,0},{12,4},{16,24},{20,28},{24,16},{28,20},{1,9},{5... | collective-permute-start | bytes 307208 | tf_op jit(solution)/shard_map/ppermute | solution.py:455
  93.8 8.9 %collective-permute-start.27 = (bf16[2,128,768]{2,1,0:T(8,128)(2,1)S(1)}, bf16[2,128,768]{2,1,0:T(8,128)(2,1)S(1)}, u32[]{:S(2)}, u32[]{:S(2)}) collective-permute-start(bf16[2,128,768]{2,1,0:T(8,128)(2,1)S(1)} %get-tuple-element.72.refs_4_), channel_id=1, source_target_pairs={{0,8},{4,12},{8,0},{12,4},{16,24},{20,28},{24,16},{28,20},{1,9},{5... | collective-permute-start | bytes 1179656 | tf_op jit(solution)/shard_map/ppermute | solution.py:455
  93.9 9.1 %collective-permute-start.32 = (bf16[4,400,128]{2,1,0:T(8,128)(2,1)S(1)}, bf16[4,400,128]{2,1,0:T(8,128)(2,1)S(1)}, u32[]{:S(2)}, u32[]{:S(2)}) collective-permute-start(bf16[4,400,128]{2,1,0:T(8,128)(2,1)S(1)} %shard_map.143.refs_0_), channel_id=1, source_target_pairs={{0,2},{1,3},{2,0},{3,1},{4,6},{5,7},{6,4},{7,5},{8,10},{9,11},{10,... | collective-permute-start | bytes 1228808 | tf_op jit(solution)/shard_map/ppermute | solution.py:452
  94.8 9.1 %collective-permute-start.30 = (bf16[4,400,128]{2,1,0:T(8,128)(2,1)S(1)}, bf16[4,400,128]{2,1,0:T(8,128)(2,1)S(1)}, u32[]{:S(2)}, u32[]{:S(2)}) collective-permute-start(bf16[4,400,128]{2,1,0:T(8,128)(2,1)S(1)} %shard_map.143.refs_0_), channel_id=1, source_target_pairs={{0,1},{1,0},{2,3},{3,2},{4,5},{5,4},{6,7},{7,6},{8,9},{9,8},{10,11... | collective-permute-start | bytes 1228808 | tf_op jit(solution)/shard_map/ppermute | solution.py:452
  102.8 7.8 %collective-permute-start.28 = (bf16[1,128,768]{2,1,0:T(8,128)(2,1)S(1)}, bf16[1,128,768]{2,1,0:T(8,128)(2,1)S(1)}, u32[]{:S(2)}, u32[]{:S(2)}) collective-permute-start(bf16[1,128,768]{2,1,0:T(8,128)(2,1)S(1)} %get-tuple-element.74), channel_id=1, source_target_pairs={{0,16},{4,20},{8,24},{12,28},{16,0},{20,4},{24,8},{28,12},{1,17},{... | collective-permute-start | bytes 589832 | tf_op jit(solution)/shard_map/ppermute | solution.py:455
  103.0 10.7 %collective-permute-start.29 = (bf16[4,400,128]{2,1,0:T(8,128)(2,1)S(1)}, bf16[4,400,128]{2,1,0:T(8,128)(2,1)S(1)}, u32[]{:S(2)}, u32[]{:S(2)}) collective-permute-start(bf16[4,400,128]{2,1,0:T(8,128)(2,1)S(1)} %shard_map.143.refs_0_), channel_id=1, source_target_pairs={{0,4},{4,0},{8,12},{12,8},{16,20},{20,16},{24,28},{28,24},{1,5},{5... | collective-permute-start | bytes 1228808 | tf_op jit(solution)/shard_map/ppermute | solution.py:458
  105.3 8.5 %collective-permute-start.33 = (bf16[4,400,128]{2,1,0:T(8,128)(2,1)S(1)}, bf16[4,400,128]{2,1,0:T(8,128)(2,1)S(1)}, u32[]{:S(2)}, u32[]{:S(2)}) collective-permute-start(bf16[4,400,128]{2,1,0:T(8,128)(2,1)S(1)} %collective-permute-done.32.refs_2_), channel_id=1, source_target_pairs={{0,4},{4,0},{8,12},{12,8},{16,20},{20,16},{24,28},{28,24},{1,5},{5... | collective-permute-start | bytes 1228808 | tf_op jit(solution)/shard_map/ppermute | solution.py:458
  (25 other events, 105.3 us)

commit v5 on v4

--- a/solution.py
+++ b/solution.py
@@ -60,12 +60,18 @@
     return call(body, [shape(w.shape[::-1], w.dtype) for w in weights], weights, after=after)
 
 
-def stack(parts, after):
+def stack(parts, joined=False, after=()):
+    count = parts[0].shape[0] if joined else 1
+
     def body(*refs):
         for k, ref in enumerate(refs[:-1]):
-            refs[-1][k] = ref[...]
-
-    out = shape((len(parts), *parts[0].shape), parts[0].dtype)
+            if joined:
+                refs[-1][k * count : (k + 1) * count] = ref[...]
+            else:
+                refs[-1][k] = ref[...]
+
+    dims = parts[0].shape[1:] if joined else parts[0].shape
+    out = shape((len(parts) * count, *dims), parts[0].dtype)
     return call(body, [out], parts, after=after)[0]
 
 
@@ -107,31 +113,39 @@
     return jnp.concatenate([tile_ref[:, p * nd : (p + 1) * nd] for p in places], axis=1)
 
 
-def forward_first(tile, places, blocks, nd, cs, after):
+def row_sums(tile, nd, cs, after):
     rt, ct = tile.shape
-    width = blocks[0].shape[1]
-
-    def body(*refs):
-        tile_ref, feat_refs = refs[0], refs[1 : 1 + len(blocks)]
-        sum_ref, mass_ref = refs[1 + len(blocks) :]
+
+    def body(tile_ref, mass_ref):
         j = lax.axis_index("col")
-        feats = jnp.concatenate([r[...] for r in feat_refs], axis=0)
-        sum_ref[...] = mm(tile_columns(tile_ref, places, nd), feats)
         ones = jnp.ones((8, ct), BF16)
         for k in range(cs):
             place = pl.multiple_of((j ^ k) * nd, nd)
             mass_ref[:, pl.ds(place, nd)] = mm(ones, tile_ref[k * nd : (k + 1) * nd, :], 1, 1)
 
-    return call(
-        body,
-        [shape((rt, width), F32), shape((8, rt), F32)],
+    return call(body, [shape((8, rt), F32)], [tile], flops=16 * tile.size, after=after)[0]
+
+
+def forward_first(tile, places, blocks, nd, after):
+    rt = tile.shape[0]
+    width = blocks[0].shape[1]
+
+    def body(*refs):
+        tile_ref, feat_refs = refs[0], refs[1 : 1 + len(blocks)]
+        sum_ref = refs[1 + len(blocks)]
+        feats = jnp.concatenate([r[...] for r in feat_refs], axis=0)
+        sum_ref[...] = mm(tile_columns(tile_ref, places, nd), feats)
+
+    return call(
+        body,
+        [shape((rt, width), F32)],
         [tile, *blocks],
         flops=2 * rt * len(places) * nd * width,
         after=after,
-    )
-
-
-def forward_parts(begun, tile, places, blocks, nd, cs, after):
+    )[0]
+
+
+def forward_parts(begun, tile, places, blocks, nd, cs, after=()):
     width = blocks[0].shape[1]
 
     def body(*refs):
@@ -151,7 +165,7 @@
     )
 
 
-def activation(parts, inverse, own, own_feat, w_neigh, bias, cotangent, after):
+def activation(parts, inverse, own, own_feat, w_neigh, bias, cotangent):
     cs = len(parts)
     nd, hid = own.shape
     depth = own_feat.shape[1]
@@ -193,7 +207,6 @@
         [*parts, inverse, own, own_feat, w_neigh, bias, cotangent],
         [pltpu.VMEM((nd, 2 * depth), BF16)],
         flops=2 * own_feat.size * hid,
-        after=after,
     )
 
 
@@ -364,10 +377,10 @@
     return call(body, [shape((rows, width), BF16)], parts)[0]
 
 
-def assemble(pieces, mine, begun, depth, hid, xr, nc, cs, factors, after):
+def assemble(pieces, begun, depth, hid, xr, nc, cs, factors, after):
     xw = 2 * depth // cs
     side = cs // 2
-    copies = sum(len(distances) for _, distances, _ in pieces)
+    copies = sum(len(where) for _, where, _ in pieces)
     arrays = [array for array, _, _ in pieces]
     inputs = arrays + list(begun)
     weight = shape((depth, hid), F32)
@@ -383,10 +396,10 @@
             bias_ref[...] = jnp.zeros_like(bias_ref)
         waits = []
         at = 0
-        for ref, (_, distances, column) in zip(piece_refs, pieces):
-            owner = j ^ column
-            first = owner < side
-            for t, distance in enumerate(distances):
+        for ref, (_, where, mine) in zip(piece_refs, pieces):
+            for t, (distance, column) in enumerate(where):
+                owner = j ^ column
+                first = owner < side
                 q = 2 * (z ^ distance) + (c if mine else 1 - c)
                 col = pl.multiple_of(lax.rem(q, nc) * LANES, LANES)
                 turn = q // nc
@@ -491,6 +504,7 @@
         step //= 2
     theirs_first = {0: other_core(features), 1: other_core(near)}
     own_feats = {0: send_own(features, 0)}
+    turned_neigh, turned_self = turn([w_neigh, w_self], [theirs_first[0]])
     tile, turned = densify(
         block_rows.reshape(-1),
         block_cols.reshape(-1),
@@ -499,7 +513,7 @@
         nd,
         rs,
         cs,
-        [near, theirs_first[0], own_feats[0]],
+        [near, turned_neigh, own_feats[0]],
     )
     mine_first.update(
         {d: follow(x, [tile, theirs_first[1]]) for d, x in mine_first.items() if d > 1}
@@ -508,31 +522,29 @@
     theirs_first.update({d: other_core(x) for d, x in mine_first.items() if d > 1})
     theirs_last = {d: other_core(x) for d, x in mine_last.items()}
     own_feats.update({d: send_own(x, d) for d, x in mine_first.items() if d})
-    own_feats.update({d: send_own(x, d) for d, x in mine_last.items()})
 
     def placed(mine, theirs):
         places = list(mine) + [half + d for d in theirs]
         return places, [*mine.values(), *theirs.values()]
 
-    begun, mass = forward_first(
-        tile, *placed(mine_first, theirs_first), nd, cs, [own_feats[1]]
+    begun = forward_first(
+        tile, *placed(mine_first, theirs_first), nd, [own_feats[0], own_feats[1]]
     )
     evens = [x for d, x in own_feats.items() if d and d % 2 == 0]
     parts = forward_parts(begun, tile, *placed(mine_last, theirs_last), nd, cs, evens)
+    own_feats.update({d: send_own(follow(x, parts[:1]), d) for d, x in mine_last.items()})
     own_feat = sum(list(own_feats.values())[1:], own_feats[0])
+    mass = row_sums(tile, nd, cs, parts[1:2])
     degree = mass
-    step = 1
-    while step < cs:
-        degree = degree + along_col(degree, step)
-        step *= 2
-    inverse = 1.0 / (degree[0] + 1.0)
-    inverse = jnp.broadcast_to(inverse[:, None], (rt, LANES))
+    for k in range(1, cs):
+        degree = degree + along_col(mass, k)
+    inverse = 1.0 / (degree[:1] + 1.0)
+    inverse = jnp.broadcast_to(inverse[0][:, None], (rt, LANES))
     own = jnp.dot(own_feat, w_self, preferred_element_type=F32).astype(BF16)
 
-    turned_neigh, turned_self = turn([w_neigh, w_self], [parts[0]])
     parts = [parts[0]] + [along_col(parts[k], k) for k in range(1, cs)]
     output, sums, *packs = activation(
-        parts, inverse, own, own_feat, w_neigh, bias[None, :], cotangent, [turned_neigh]
+        parts, inverse, own, own_feat, w_neigh, bias[None, :], cotangent
     )
     packs = [packs[0]] + [along_col(packs[k], k) for k in range(1, cs)]
 
@@ -546,36 +558,46 @@
     chunks = pair_sum(keep, came)
     back_after = [chunks[1]]
     chunks = [chunks[0]] + [along_chips(chunks[k], k) for k in range(1, half)]
-    line = gather_chips(last_sum(chunks))
+    chunk = last_sum(chunks)
+    line = gather_chips(chunk)
 
     keep, send = back_parts(turned, scaled, self_parts, nd, cs, rs, back_after)
-    keep, send = fold(keep, other_core(send), line[1:])
-    line = stack(line, [send])
-    step = 1
+    keep, send = fold(keep, other_core(send), [chunk])
+    keep, send = fold(keep, along_chips(send, 1))
+    line = stack(line, after=[send])
+    step = 2
     while step < half:
         folded = fold(keep, along_chips(send, step))
         keep, send = folded if 2 * step < half else (folded, None)
         step *= 2
     grad_input = keep
 
+    def at(where, k):
+        return [(d, k) for d in where]
+
     distances = list(range(half))
-    mine = [(line, distances, 0)]
-    if cs == 4 and half % 2 == 0:
-        mid = half // 2
-        first, second = along_col(line, 1), along_col(line, 2)
-        mine += [
-            (first, distances, 1),
-            (second, distances, 2),
-            (along_col(first[:mid], 2), distances[:mid], 3),
-            (along_col(second[mid:], 1), distances[mid:], 3),
-        ]
-    else:
-        mine += [(along_col(line, k), distances, k) for k in range(1, cs)]
-    theirs = [(other_core(array), where, column) for array, where, column in mine]
     factor = 1.0 / math.sqrt(nd * rs * cs)
     sizes = (depth, hid, xr, nc, cs, (factor, 32.0 * factor))
-    begun = assemble(mine, True, (), *sizes, ())
-    total_self, total_neigh, total_bias = assemble(theirs, False, begun, *sizes, [grad_input])
+
+    def both_cores(array, where):
+        return [(array, where, True), (other_core(array), where, False)]
+
+    if cs == 4:
+        first, second = along_col(line, 1), along_col(line, 2)
+        near = [line, first, second]
+    else:
+        near = [line] + [along_col(line, k) for k in range(1, cs - 1)]
+    near = stack(near, joined=True, after=[grad_input])
+    near_where = sum((at(distances, k) for k in range(cs - 1)), [])
+    begun = assemble(both_cores(near, near_where), (), *sizes, ())
+    if cs == 4:
+        mid = half // 2
+        rest = [along_col(first[:mid], 2), along_col(second[mid:], 1)]
+    else:
+        rest = [along_col(line, cs - 1)]
+    rest = stack(rest, joined=True, after=begun[2:])
+    pieces = both_cores(rest, at(distances, cs - 1))
+    total_self, total_neigh, total_bias = assemble(pieces, begun, *sizes, ())
     return output, grad_input, total_self, total_neigh, total_bias.reshape(-1)
 
 

time: 117 us -> 124 us (1.060)
  starting transfers between devices: 34.4 us -> 46.3 us
  waiting for transfers between devices: 60.7 us -> 56.6 us
    ppermute x12 -> x13, waiting for transfers between devices: 23.1 us -> 15.2 us  [along_col(): return lax.ppermute(x, 'col', [(s, s ^ k) for s in range(cs)])]
    ppermute x11, starting transfers between devices: 11.4 us -> 18.9 us  [along_chips(): return lax.ppermute(x, 'row', [(s, s ^ 2 * k) for s in range(rs)])]
    ppermute x4, waiting for transfers between devices: 0.01 us -> 7.18 us  [send_own(): return lax.ppermute(block, ('row', 'col'), pairs)]
    ppermute x11, waiting for transfers between devices: 34.8 us -> 30.9 us  [along_chips(): return lax.ppermute(x, 'row', [(s, s ^ 2 * k) for s in range(rs)])]
    ppermute x12 -> x13, starting transfers between devices: 11.7 us -> 14.8 us  [along_col(): return lax.ppermute(x, 'col', [(s, s ^ k) for s in range(cs)])]
    ppermute x4, starting transfers between devices: 7.81 us -> 9.87 us  [send_own(): return lax.ppermute(block, ('row', 'col'), pairs)]
    ppermute x11 -> x8, starting transfers between devices: 3.54 us -> 2.79 us  [other_core(): return lax.ppermute(x, 'row', [(s, s ^ 1) for s in range(rs)])]
    ppermute x11 -> x8, waiting for transfers between devices: 2.86 us -> 3.31 us  [other_core(): return lax.ppermute(x, 'row', [(s, s ^ 1) for s in range(rs)])]
  transfers between devices with their start and end apart: 38 -> 36, of which waited for: 19 -> 18; matrix products, arithmetic and copies ran while one was open for 0% -> 0% of each run, Pallas kernels for 9% -> 8%
where the time goes in v5:
time: 124 us
  waiting for transfers between devices  56.6 us (46%)
  starting transfers between devices  46.3 us (37%)
  Pallas kernels  16.2 us (13%)
  local copies, waits for them, and re-layouts  2.52 us (2%)
  between operations  1.69 us (1%)
    ppermute x11, waiting for transfers between devices, along_chips(): return lax.ppermute(x, 'row', [(s, s ^ 2 * k) for s in range(rs)])  30.9 us
    ppermute x11, starting transfers between devices, along_chips(): return lax.ppermute(x, 'row', [(s, s ^ 2 * k) for s in range(rs)])  18.9 us
    ppermute x13, waiting for transfers between devices, along_col(): return lax.ppermute(x, 'col', [(s, s ^ k) for s in range(cs)])  15.2 us
    ppermute x13, starting transfers between devices, along_col(): return lax.ppermute(x, 'col', [(s, s ^ k) for s in range(cs)])  14.8 us
    pallas_call x20, Pallas kernels, call(): pl.pallas_call(run, out_shape=outs, in_specs=[SMEM] * smem + [VMEM] * (co...  12 us
    ppermute x4, starting transfers between devices, send_own(): return lax.ppermute(block, ('row', 'col'), pairs)  9.87 us
    ppermute x4, waiting for transfers between devices, send_own(): return lax.ppermute(block, ('row', 'col'), pairs)  7.18 us
    pallas_call x2, Pallas kernels, assemble(): pl.pallas_call(run, out_shape=[weight, weight, shape((1, hid), F32)], in_...  4.19 us
  transfers between devices with their start and end apart: 36, of which 18 were waited for; matrix products, arithmetic and copies ran while one was open for 0% of the time, Pallas kernels for 8%

profile of v5, /device:TPU:0, one launch (start us, length us, event | category | flops | bytes accessed | tf_op | source)
XLA Modules:
  0.0 123.8 jit_solution(3327027082364018556)
XLA Ops:
  0.6 3.1 %collective-permute-start = (bf16[128,768]{1,0:T(8,128)(2,1)}, bf16[128,768]{1,0:T(8,128)(2,1)S(1)}, u32[]{:S(2)}, u32[]{:S(2)}) collective-permute-start(bf16[128,768]{1,0:T(8,128)(2,1)} %refs_1_.3), channel_id=1, source_target_pairs={{0,8},{4,12},{8,0},{12,4},{16,24},{20,28},{24,16},{28,20},{1,9},{5... | collective-permute-start | bytes 589832 | tf_op jit(solution)/shard_map/ppermute | solution.py:468
  5.3 1.7 %collective-permute-start.3 = (bf16[128,768]{1,0:T(8,128)(2,1)}, bf16[128,768]{1,0:T(8,128)(2,1)S(1)}, u32[]{:S(2)}, u32[]{:S(2)}) collective-permute-start(bf16[128,768]{1,0:T(8,128)(2,1)} %refs_1_.3), channel_id=1, source_target_pairs={{0,16},{4,20},{8,24},{12,28},{16,0},{20,4},{24,8},{28,12},{1,17},{... | collective-permute-start | bytes 589832 | tf_op jit(solution)/shard_map/ppermute | solution.py:468
  7.0 1.8 %collective-permute-done.refs_4_.refs_2_ = bf16[128,768]{1,0:T(8,128)(2,1)S(1)} collective-permute-done((bf16[128,768]{1,0:T(8,128)(2,1)}, bf16[128,768]{1,0:T(8,128)(2,1)S(1)}, u32[]{:S(2)}, u32[]{:S(2)}) %collective-permute-start) | collective-permute-done | bytes 196640 | tf_op jit(solution)/shard_map/ppermute | solution.py:468
  10.9 2.3 %shard_map.128 = (bf16[1024,768]{1,0:T(8,128)(2,1)S(1)}, bf16[1024,768]{1,0:T(8,128)(2,1)S(1)}) custom-call(bf16[768,1024]{1,0:T(8,128)(2,1)S(1)} %copy-done, bf16[768,1024]{1,0:T(8,128)(2,1)} %refs_1_.2, bf16[128,768]{1,0:T(8,128)(2,1)S(1)} %collective-permute-done.1.refs_2_.refs_4_), custom_call_target="tpu_custom_call" | custom-call | bytes 6291456 | tf_op jit(solution)/shard_map/pallas_call | solution.py:27
  14.6 3.3 %collective-permute-done.3.refs_0_ = bf16[128,768]{1,0:T(8,128)(2,1)S(1)} collective-permute-done((bf16[128,768]{1,0:T(8,128)(2,1)}, bf16[128,768]{1,0:T(8,128)(2,1)S(1)}, u32[]{:S(2)}, u32[]{:S(2)}) %collective-permute-start.3) | collective-permute-done | bytes 196640 | tf_op jit(solution)/shard_map/ppermute | solution.py:468
  17.9 4.1 %collective-permute-start.6 = (bf16[128,768]{1,0:T(8,128)(2,1)S(1)}, bf16[128,768]{1,0:T(8,128)(2,1)S(1)}, u32[]{:S(2)}, u32[]{:S(2)}) collective-permute-start(bf16[128,768]{1,0:T(8,128)(2,1)S(1)} %collective-permute-done.refs_4_.refs_2_), channel_id=1, source_target_pairs={{0,2},{4,3},{9,8},{13,9},{18,22},{22,23},{27,28},{31,29}} | collective-permute-start | bytes 589832 | tf_op jit(solution)/shard_map/ppermute | solution.py:490
  22.3 2.2 %collective-permute-start.9 = (bf16[128,768]{1,0:T(8,128)(2,1)S(1)}, bf16[128,768]{1,0:T(8,128)(2,1)S(1)}, u32[]{:S(2)}, u32[]{:S(2)}) collective-permute-start(bf16[128,768]{1,0:T(8,128)(2,1)S(1)} %shard_map.130.refs_3_), channel_id=1, source_target_pairs={{0,4},{4,5},{9,14},{13,15},{18,16},{22,17},{27,26},{31,27}} | collective-permute-start | bytes 589832 | tf_op jit(solution)/shard_map/ppermute | solution.py:490
  27.3 2.5 %collective-permute-start.15 = (f32[8,512]{1,0:T(8,128)S(1)}, f32[8,512]{1,0:T(8,128)S(1)}, u32[]{:S(2)}, u32[]{:S(2)}) collective-permute-start(f32[8,512]{1,0:T(8,128)S(1)} %shard_map.133), channel_id=1, source_target_pairs={{0,3},{1,2},{2,1},{3,0},{4,7},{5,6},{6,5},{7,4},{8,11},{9,10},{10,... | collective-permute-start | bytes 49160 | tf_op jit(solution)/shard_map/ppermute | solution.py:465
  31.8 2.0 %collective-permute-start.11 = (bf16[128,768]{1,0:T(8,128)(2,1)S(1)}, bf16[128,768]{1,0:T(8,128)(2,1)S(1)}, u32[]{:S(2)}, u32[]{:S(2)}) collective-permute-start(bf16[128,768]{1,0:T(8,128)(2,1)S(1)} %get-tuple-element.45), channel_id=1, source_target_pairs={{0,2},{1,3},{2,0},{3,1},{4,6},{5,7},{6,4},{7,5},{8,10},{9,11},{10,... | collective-permute-start | bytes 589832 | tf_op jit(solution)/shard_map/ppermute | solution.py:465
  34.4 1.9 %collective-permute-start.16 = (bf16[128,768]{1,0:T(8,128)(2,1)S(1)}, bf16[128,768]{1,0:T(8,128)(2,1)S(1)}, u32[]{:S(2)}, u32[]{:S(2)}) collective-permute-start(bf16[128,768]{1,0:T(8,128)(2,1)S(1)} %shard_map.134), channel_id=1, source_target_pairs={{0,6},{4,7},{9,12},{13,13},{18,18},{22,19},{27,24},{31,25}} | collective-permute-start | bytes 589832 | tf_op jit(solution)/shard_map/ppermute | solution.py:490
  36.4 7.0 %collective-permute-done.16 = bf16[128,768]{1,0:T(8,128)(2,1)S(1)} collective-permute-done((bf16[128,768]{1,0:T(8,128)(2,1)S(1)}, bf16[128,768]{1,0:T(8,128)(2,1)S(1)}, u32[]{:S(2)}, u32[]{:S(2)}) %collective-permute-start.16) | collective-permute-done | bytes 196640 | tf_op jit(solution)/shard_map/ppermute | solution.py:490
  46.6 2.2 %collective-permute-start.19 = (bf16[128,1408]{1,0:T(8,128)(2,1)S(1)}, bf16[128,1408]{1,0:T(8,128)(2,1)S(1)}, u32[]{:S(2)}, u32[]{:S(2)}) collective-permute-start(bf16[128,1408]{1,0:T(8,128)(2,1)S(1)} %get-tuple-element.54), channel_id=1, source_target_pairs={{0,3},{1,2},{2,1},{3,0},{4,7},{5,6},{6,5},{7,4},{8,11},{9,10},{10,... | collective-permute-start | bytes 1081352 | tf_op jit(solution)/shard_map/ppermute | solution.py:465
  48.8 7.8 %collective-permute-done.17.refs_4_.refs_1_ = bf16[128,1408]{1,0:T(8,128)(2,1)S(1)} collective-permute-done((bf16[128,1408]{1,0:T(8,128)(2,1)S(1)}, bf16[128,1408]{1,0:T(8,128)(2,1)S(1)}, u32[]{:S(2)}, u32[]{:S(2)}) %collective-permute-start.17) | collective-permute-done | bytes 360480 | tf_op jit(solution)/shard_map/ppermute | solution.py:465
  57.7 4.5 %collective-permute-done.19.refs_3_.refs_4_ = bf16[128,1408]{1,0:T(8,128)(2,1)S(1)} collective-permute-done((bf16[128,1408]{1,0:T(8,128)(2,1)S(1)}, bf16[128,1408]{1,0:T(8,128)(2,1)S(1)}, u32[]{:S(2)}, u32[]{:S(2)}) %collective-permute-start.19) | collective-permute-done | bytes 360480 | tf_op jit(solution)/shard_map/ppermute | solution.py:465
  63.1 1.9 %collective-permute-start.20 = (bf16[4,400,128]{2,1,0:T(8,128)(2,1)S(1)}, bf16[4,400,128]{2,1,0:T(8,128)(2,1)S(1)}, u32[]{:S(2)}, u32[]{:S(2)}) collective-permute-start(bf16[4,400,128]{2,1,0:T(8,128)(2,1)S(1)} %get-tuple-element.60), channel_id=1, source_target_pairs={{0,4},{4,0},{8,12},{12,8},{16,20},{20,16},{24,28},{28,24},{1,5},{5... | collective-permute-start | bytes 1228808 | tf_op jit(solution)/shard_map/ppermute | solution.py:471
  69.6 2.8 %collective-permute-start.24 = (bf16[400,128]{1,0:T(8,128)(2,1)S(1)}, bf16[400,128]{1,0:T(8,128)(2,1)S(1)}, u32[]{:S(2)}, u32[]{:S(2)}) collective-permute-start(bf16[400,128]{1,0:T(8,128)(2,1)S(1)} %get-tuple-element.66), channel_id=1, source_target_pairs={{0,24},{4,28},{8,16},{12,20},{16,8},{20,12},{24,0},{28,4},{1,25},{... | collective-permute-start | bytes 307208 | tf_op jit(solution)/shard_map/ppermute | solution.py:468
  72.3 6.9 %collective-permute-done.23.refs_2_ = bf16[400,128]{1,0:T(8,128)(2,1)S(1)} collective-permute-done((bf16[400,128]{1,0:T(8,128)(2,1)S(1)}, bf16[400,128]{1,0:T(8,128)(2,1)S(1)}, u32[]{:S(2)}, u32[]{:S(2)}) %collective-permute-start.23) | collective-permute-done | bytes 102432 | tf_op jit(solution)/shard_map/ppermute | solution.py:468
  84.4 8.3 %collective-permute-done.28.refs_2_ = bf16[400,128]{1,0:T(8,128)(2,1)S(1)} collective-permute-done((bf16[400,128]{1,0:T(8,128)(2,1)S(1)}, bf16[400,128]{1,0:T(8,128)(2,1)S(1)}, u32[]{:S(2)}, u32[]{:S(2)}) %collective-permute-start.28) | collective-permute-done | bytes 102432 | tf_op jit(solution)/shard_map/ppermute | solution.py:468
  92.7 3.9 %collective-permute-start.29 = (bf16[400,128]{1,0:T(8,128)(2,1)S(1)}, bf16[400,128]{1,0:T(8,128)(2,1)S(1)}, u32[]{:S(2)}, u32[]{:S(2)}) collective-permute-start(bf16[400,128]{1,0:T(8,128)(2,1)S(1)} %collective-permute-done.28.refs_2_), channel_id=1, source_target_pairs={{0,8},{4,12},{8,0},{12,4},{16,24},{20,28},{24,16},{28,20},{1,9},{5... | collective-permute-start | bytes 307208 | tf_op jit(solution)/shard_map/ppermute | solution.py:468
  96.7 2.6 %collective-permute-done.29.refs_3_ = bf16[400,128]{1,0:T(8,128)(2,1)S(1)} collective-permute-done((bf16[400,128]{1,0:T(8,128)(2,1)S(1)}, bf16[400,128]{1,0:T(8,128)(2,1)S(1)}, u32[]{:S(2)}, u32[]{:S(2)}) %collective-permute-start.29) | collective-permute-done | bytes 102432 | tf_op jit(solution)/shard_map/ppermute | solution.py:468
  103.1 7.0 %collective-permute-done.26.refs_1_ = bf16[1,128,768]{2,1,0:T(8,128)(2,1)S(1)} collective-permute-done((bf16[1,128,768]{2,1,0:T(8,128)(2,1)S(1)}, bf16[1,128,768]{2,1,0:T(8,128)(2,1)S(1)}, u32[]{:S(2)}, u32[]{:S(2)}) %collective-permute-start.26) | collective-permute-done | bytes 196640 | tf_op jit(solution)/shard_map/ppermute | solution.py:468
  114.9 2.4 %shard_map.147 = (f32[768,1024]{1,0:T(8,128)}, f32[768,1024]{1,0:T(8,128)}, f32[1,1024]{1,0:T(1,128)S(1)}) custom-call(bf16[12,400,128]{2,1,0:T(8,128)(2,1)S(1)} %shard_map.146.refs_0_, bf16[12,400,128]{2,1,0:T(8,128)(2,1)S(1)} %collective-permute-done.34.refs_1_), custom_call_target="tpu_custom_call" | custom-call | bytes 14155776 | tf_op jit(solution)/shard_map/pallas_call | solution.py:433
  117.3 2.3 %collective-permute-done.33.refs_1_ = bf16[2,400,128]{2,1,0:T(8,128)(2,1)S(1)} collective-permute-done((bf16[2,400,128]{2,1,0:T(8,128)(2,1)S(1)}, bf16[2,400,128]{2,1,0:T(8,128)(2,1)S(1)}, u32[]{:S(2)}, u32[]{:S(2)}) %collective-permute-start.33) | collective-permute-done | bytes 204832 | tf_op jit(solution)/shard_map/ppermute | solution.py:465
  122.0 1.8 %shard_map.149 = (f32[768,1024]{1,0:T(8,128)}, f32[768,1024]{1,0:T(8,128)}, f32[1,1024]{1,0:T(1,128)}) custom-call(bf16[4,400,128]{2,1,0:T(8,128)(2,1)S(1)} %shard_map.148.refs_0_, bf16[4,400,128]{2,1,0:T(8,128)(2,1)S(1)} %collective-permute-done.35.refs_1_, f32[768,1024]{1,0:T(8,128)} %get-tuple-element.72.refs_2_, ...), custom_call_target="tpu_custom_call", output_to_operand_aliasing={{0}: (2, {}), {1}: (3, {})} | custom-call | bytes 4718592 | tf_op jit(solution)/shard_map/pallas_call | solution.py:433
  (96 shorter events, 35.7 us)
Async XLA Ops:
  0.6 8.2 %collective-permute-start = (bf16[128,768]{1,0:T(8,128)(2,1)}, bf16[128,768]{1,0:T(8,128)(2,1)S(1)}, u32[]{:S(2)}, u32[]{:S(2)}) collective-permute-start(bf16[128,768]{1,0:T(8,128)(2,1)} %refs_1_.3), channel_id=1, source_target_pairs={{0,8},{4,12},{8,0},{12,4},{16,24},{20,28},{24,16},{28,20},{1,9},{5... | collective-permute-start | bytes 589832 | tf_op jit(solution)/shard_map/ppermute | solution.py:468
  3.7 9.5 %collective-permute-start.2 = (bf16[128,768]{1,0:T(8,128)(2,1)}, bf16[128,768]{1,0:T(8,128)(2,1)S(1)}, u32[]{:S(2)}, u32[]{:S(2)}) collective-permute-start(bf16[128,768]{1,0:T(8,128)(2,1)} %refs_1_.3), channel_id=1, source_target_pairs={{0,0},{4,1},{9,10},{13,11},{18,20},{22,21},{27,30},{31,31}} | collective-permute-start | bytes 589832 | tf_op jit(solution)/shard_map/ppermute | solution.py:490
  5.3 12.5 %collective-permute-start.3 = (bf16[128,768]{1,0:T(8,128)(2,1)}, bf16[128,768]{1,0:T(8,128)(2,1)S(1)}, u32[]{:S(2)}, u32[]{:S(2)}) collective-permute-start(bf16[128,768]{1,0:T(8,128)(2,1)} %refs_1_.3), channel_id=1, source_target_pairs={{0,16},{4,20},{8,24},{12,28},{16,0},{20,4},{24,8},{28,12},{1,17},{... | collective-permute-start | bytes 589832 | tf_op jit(solution)/shard_map/ppermute | solution.py:468
  8.8 9.0 %collective-permute-start.4 = (bf16[128,768]{1,0:T(8,128)(2,1)S(1)}, bf16[128,768]{1,0:T(8,128)(2,1)S(1)}, u32[]{:S(2)}, u32[]{:S(2)}) collective-permute-start(bf16[128,768]{1,0:T(8,128)(2,1)S(1)} %collective-permute-done.refs_4_.refs_2_), channel_id=1, source_target_pairs={{0,4},{4,0},{8,12},{12,8},{16,20},{20,16},{24,28},{28,24},{1,5},{5... | collective-permute-start | bytes 589832 | tf_op jit(solution)/shard_map/ppermute | solution.py:471
  17.9 7.3 %collective-permute-start.6 = (bf16[128,768]{1,0:T(8,128)(2,1)S(1)}, bf16[128,768]{1,0:T(8,128)(2,1)S(1)}, u32[]{:S(2)}, u32[]{:S(2)}) collective-permute-start(bf16[128,768]{1,0:T(8,128)(2,1)S(1)} %collective-permute-done.refs_4_.refs_2_), channel_id=1, source_target_pairs={{0,2},{4,3},{9,8},{13,9},{18,22},{22,23},{27,28},{31,29}} | collective-permute-start | bytes 589832 | tf_op jit(solution)/shard_map/ppermute | solution.py:490
  30.8 13.1 %collective-permute-start.10 = (bf16[128,768]{1,0:T(8,128)(2,1)S(1)}, bf16[128,768]{1,0:T(8,128)(2,1)S(1)}, u32[]{:S(2)}, u32[]{:S(2)}) collective-permute-start(bf16[128,768]{1,0:T(8,128)(2,1)S(1)} %get-tuple-element.44.refs_1_), channel_id=1, source_target_pairs={{0,1},{1,0},{2,3},{3,2},{4,5},{5,4},{6,7},{7,6},{8,9},{9,8},{10,11... | collective-permute-start | bytes 589832 | tf_op jit(solution)/shard_map/ppermute | solution.py:465
  31.8 12.1 %collective-permute-start.11 = (bf16[128,768]{1,0:T(8,128)(2,1)S(1)}, bf16[128,768]{1,0:T(8,128)(2,1)S(1)}, u32[]{:S(2)}, u32[]{:S(2)}) collective-permute-start(bf16[128,768]{1,0:T(8,128)(2,1)S(1)} %get-tuple-element.45), channel_id=1, source_target_pairs={{0,2},{1,3},{2,0},{3,1},{4,6},{5,7},{6,4},{7,5},{8,10},{9,11},{10,... | collective-permute-start | bytes 589832 | tf_op jit(solution)/shard_map/ppermute | solution.py:465
  33.8 10.1 %collective-permute-start.12 = (bf16[128,768]{1,0:T(8,128)(2,1)S(1)}, bf16[128,768]{1,0:T(8,128)(2,1)S(1)}, u32[]{:S(2)}, u32[]{:S(2)}) collective-permute-start(bf16[128,768]{1,0:T(8,128)(2,1)S(1)} %get-tuple-element.46), channel_id=1, source_target_pairs={{0,3},{1,2},{2,1},{3,0},{4,7},{5,6},{6,5},{7,4},{8,11},{9,10},{10,... | collective-permute-start | bytes 589832 | tf_op jit(solution)/shard_map/ppermute | solution.py:465
  34.4 9.0 %collective-permute-start.16 = (bf16[128,768]{1,0:T(8,128)(2,1)S(1)}, bf16[128,768]{1,0:T(8,128)(2,1)S(1)}, u32[]{:S(2)}, u32[]{:S(2)}) collective-permute-start(bf16[128,768]{1,0:T(8,128)(2,1)S(1)} %shard_map.134), channel_id=1, source_target_pairs={{0,6},{4,7},{9,12},{13,13},{18,18},{22,19},{27,24},{31,25}} | collective-permute-start | bytes 589832 | tf_op jit(solution)/shard_map/ppermute | solution.py:490
  45.3 11.3 %collective-permute-start.17 = (bf16[128,1408]{1,0:T(8,128)(2,1)S(1)}, bf16[128,1408]{1,0:T(8,128)(2,1)S(1)}, u32[]{:S(2)}, u32[]{:S(2)}) collective-permute-start(bf16[128,1408]{1,0:T(8,128)(2,1)S(1)} %get-tuple-element.51), channel_id=1, source_target_pairs={{0,1},{1,0},{2,3},{3,2},{4,5},{5,4},{6,7},{7,6},{8,9},{9,8},{10,11... | collective-permute-start | bytes 1081352 | tf_op jit(solution)/shard_map/ppermute | solution.py:465
  45.3 12.4 %collective-permute-start.18 = (bf16[128,1408]{1,0:T(8,128)(2,1)S(1)}, bf16[128,1408]{1,0:T(8,128)(2,1)S(1)}, u32[]{:S(2)}, u32[]{:S(2)}) collective-permute-start(bf16[128,1408]{1,0:T(8,128)(2,1)S(1)} %get-tuple-element.53), channel_id=1, source_target_pairs={{0,2},{1,3},{2,0},{3,1},{4,6},{5,7},{6,4},{7,5},{8,10},{9,11},{10,... | collective-permute-start | bytes 1081352 | tf_op jit(solution)/shard_map/ppermute | solution.py:465
  46.6 15.7 %collective-permute-start.19 = (bf16[128,1408]{1,0:T(8,128)(2,1)S(1)}, bf16[128,1408]{1,0:T(8,128)(2,1)S(1)}, u32[]{:S(2)}, u32[]{:S(2)}) collective-permute-start(bf16[128,1408]{1,0:T(8,128)(2,1)S(1)} %get-tuple-element.54), channel_id=1, source_target_pairs={{0,3},{1,2},{2,1},{3,0},{4,7},{5,6},{6,5},{7,4},{8,11},{9,10},{10,... | collective-permute-start | bytes 1081352 | tf_op jit(solution)/shard_map/ppermute | solution.py:465
  67.8 12.1 %collective-permute-start.21 = (bf16[4,128,768]{2,1,0:T(8,128)(2,1)S(1)}, bf16[4,128,768]{2,1,0:T(8,128)(2,1)S(1)}, u32[]{:S(2)}, u32[]{:S(2)}) collective-permute-start(bf16[4,128,768]{2,1,0:T(8,128)(2,1)S(1)} %get-tuple-element.63), channel_id=1, source_target_pairs={{0,4},{4,0},{8,12},{12,8},{16,20},{20,16},{24,28},{28,24},{1,5},{5... | collective-permute-start | bytes 2359304 | tf_op jit(solution)/shard_map/ppermute | solution.py:471
  68.2 11.1 %collective-permute-start.23 = (bf16[400,128]{1,0:T(8,128)(2,1)S(1)}, bf16[400,128]{1,0:T(8,128)(2,1)S(1)}, u32[]{:S(2)}, u32[]{:S(2)}) collective-permute-start(bf16[400,128]{1,0:T(8,128)(2,1)S(1)} %get-tuple-element.65), channel_id=1, source_target_pairs={{0,16},{4,20},{8,24},{12,28},{16,0},{20,4},{24,8},{28,12},{1,17},{... | collective-permute-start | bytes 307208 | tf_op jit(solution)/shard_map/ppermute | solution.py:468
  69.6 9.7 %collective-permute-start.24 = (bf16[400,128]{1,0:T(8,128)(2,1)S(1)}, bf16[400,128]{1,0:T(8,128)(2,1)S(1)}, u32[]{:S(2)}, u32[]{:S(2)}) collective-permute-start(bf16[400,128]{1,0:T(8,128)(2,1)S(1)} %get-tuple-element.66), channel_id=1, source_target_pairs={{0,24},{4,28},{8,16},{12,20},{16,8},{20,12},{24,0},{28,4},{1,25},{... | collective-permute-start | bytes 307208 | tf_op jit(solution)/shard_map/ppermute | solution.py:468
  72.3 7.5 %collective-permute-start.22 = (bf16[400,128]{1,0:T(8,128)(2,1)S(1)}, bf16[400,128]{1,0:T(8,128)(2,1)S(1)}, u32[]{:S(2)}, u32[]{:S(2)}) collective-permute-start(bf16[400,128]{1,0:T(8,128)(2,1)S(1)} %get-tuple-element.61.refs_5_), channel_id=1, source_target_pairs={{0,8},{4,12},{8,0},{12,4},{16,24},{20,28},{24,16},{28,20},{1,9},{5... | collective-permute-start | bytes 307208 | tf_op jit(solution)/shard_map/ppermute | solution.py:468
  80.1 16.5 %collective-permute-start.25 = (bf16[2,128,768]{2,1,0:T(8,128)(2,1)S(1)}, bf16[2,128,768]{2,1,0:T(8,128)(2,1)S(1)}, u32[]{:S(2)}, u32[]{:S(2)}) collective-permute-start(bf16[2,128,768]{2,1,0:T(8,128)(2,1)S(1)} %get-tuple-element.68), channel_id=1, source_target_pairs={{0,8},{4,12},{8,0},{12,4},{16,24},{20,28},{24,16},{28,20},{1,9},{5... | collective-permute-start | bytes 1179656 | tf_op jit(solution)/shard_map/ppermute | solution.py:468
  81.5 11.1 %collective-permute-start.28 = (bf16[400,128]{1,0:T(8,128)(2,1)S(1)}, bf16[400,128]{1,0:T(8,128)(2,1)S(1)}, u32[]{:S(2)}, u32[]{:S(2)}) collective-permute-start(bf16[400,128]{1,0:T(8,128)(2,1)S(1)} %shard_map.141.refs_2_.refs_0_), channel_id=1, source_target_pairs={{0,16},{4,20},{8,24},{12,28},{16,0},{20,4},{24,8},{28,12},{1,17},{... | collective-permute-start | bytes 307208 | tf_op jit(solution)/shard_map/ppermute | solution.py:468
  83.0 13.7 %collective-permute-start.27 = (bf16[400,128]{1,0:T(8,128)(2,1)S(1)}, bf16[400,128]{1,0:T(8,128)(2,1)S(1)}, u32[]{:S(2)}, u32[]{:S(2)}) collective-permute-start(bf16[400,128]{1,0:T(8,128)(2,1)S(1)} %shard_map.141.refs_2_.refs_0_), channel_id=1, source_target_pairs={{0,8},{4,12},{8,0},{12,4},{16,24},{20,28},{24,16},{28,20},{1,9},{5... | collective-permute-start | bytes 307208 | tf_op jit(solution)/shard_map/ppermute | solution.py:468
  99.2 11.7 %collective-permute-start.32 = (bf16[4,400,128]{2,1,0:T(8,128)(2,1)S(1)}, bf16[4,400,128]{2,1,0:T(8,128)(2,1)S(1)}, u32[]{:S(2)}, u32[]{:S(2)}) collective-permute-start(bf16[4,400,128]{2,1,0:T(8,128)(2,1)S(1)} %shard_map.145.refs_0_), channel_id=1, source_target_pairs={{0,2},{1,3},{2,0},{3,1},{4,6},{5,7},{6,4},{7,5},{8,10},{9,11},{10,... | collective-permute-start | bytes 1228808 | tf_op jit(solution)/shard_map/ppermute | solution.py:465
  100.1 10.8 %collective-permute-start.30 = (bf16[4,400,128]{2,1,0:T(8,128)(2,1)S(1)}, bf16[4,400,128]{2,1,0:T(8,128)(2,1)S(1)}, u32[]{:S(2)}, u32[]{:S(2)}) collective-permute-start(bf16[4,400,128]{2,1,0:T(8,128)(2,1)S(1)} %shard_map.145.refs_0_), channel_id=1, source_target_pairs={{0,1},{1,0},{2,3},{3,2},{4,5},{5,4},{6,7},{7,6},{8,9},{9,8},{10,11... | collective-permute-start | bytes 1228808 | tf_op jit(solution)/shard_map/ppermute | solution.py:465
  101.5 8.7 %collective-permute-start.26 = (bf16[1,128,768]{2,1,0:T(8,128)(2,1)S(1)}, bf16[1,128,768]{2,1,0:T(8,128)(2,1)S(1)}, u32[]{:S(2)}, u32[]{:S(2)}) collective-permute-start(bf16[1,128,768]{2,1,0:T(8,128)(2,1)S(1)} %get-tuple-element.70.refs_4_), channel_id=1, source_target_pairs={{0,16},{4,20},{8,24},{12,28},{16,0},{20,4},{24,8},{28,12},{1,17},{... | collective-permute-start | bytes 589832 | tf_op jit(solution)/shard_map/ppermute | solution.py:468
  112.0 7.5 %collective-permute-start.33 = (bf16[2,400,128]{2,1,0:T(8,128)(2,1)S(1)}, bf16[2,400,128]{2,1,0:T(8,128)(2,1)S(1)}, u32[]{:S(2)}, u32[]{:S(2)}) collective-permute-start(bf16[2,400,128]{2,1,0:T(8,128)(2,1)S(1)} %slice.17), channel_id=1, source_target_pairs={{0,1},{1,0},{2,3},{3,2},{4,5},{5,4},{6,7},{7,6},{8,9},{9,8},{10,11... | collective-permute-start | bytes 614408 | tf_op jit(solution)/shard_map/ppermute | solution.py:465
  112.9 7.3 %collective-permute-start.31 = (bf16[2,400,128]{2,1,0:T(8,128)(2,1)S(1)}, bf16[2,400,128]{2,1,0:T(8,128)(2,1)S(1)}, u32[]{:S(2)}, u32[]{:S(2)}) collective-permute-start(bf16[2,400,128]{2,1,0:T(8,128)(2,1)S(1)} %slice.16), channel_id=1, source_target_pairs={{0,2},{1,3},{2,0},{3,1},{4,6},{5,7},{6,4},{7,5},{8,10},{9,11},{10,... | collective-permute-start | bytes 614408 | tf_op jit(solution)/shard_map/ppermute | solution.py:465
  (22 other events, 114.7 us)

commit v6 on v5

--- a/solution.py
+++ b/solution.py
@@ -165,24 +165,26 @@
     )
 
 
-def activation(parts, inverse, own, own_feat, w_neigh, bias, cotangent):
-    cs = len(parts)
-    nd, hid = own.shape
-    depth = own_feat.shape[1]
+def activation(parts, own_feats, inverse, w_neigh, w_self, bias, cotangent):
+    cs, count = len(parts), len(own_feats)
+    nd, hid = cotangent.shape
+    depth = own_feats[0].shape[1]
     xw = 2 * depth // cs
 
     def body(*refs):
-        part_refs = refs[:cs]
-        inv_ref, own_ref, feat_ref, w_ref, bias_ref, cot_ref = refs[cs : cs + 6]
-        out_ref, sum_ref, *packs = refs[cs + 6 : -1]
+        part_refs, feat_refs = refs[:cs], refs[cs : cs + count]
+        inv_ref, wn_ref, ws_ref, bias_ref, cot_ref = refs[cs + count : cs + count + 5]
+        out_ref, sum_ref, *packs = refs[cs + count + 5 : -1]
         both = refs[-1]
         j = lax.axis_index("col")
         inv = inv_ref[pl.ds(pl.multiple_of(j * nd, nd), nd), :]
+        feats = sum(r[...].astype(F32) for r in feat_refs).astype(BF16)
+        own = mm(feats, ws_ref[...]).astype(BF16).astype(F32)
         total = sum(r[...].astype(F32) for r in part_refs)
         mean = (total * jnp.concatenate([inv] * (depth // LANES), axis=1)).astype(BF16)
-        both[:, :depth] = feat_ref[...]
+        both[:, :depth] = feats
         both[:, depth:] = mean
-        pre = own_ref[...].astype(F32) + mm(mean, w_ref[...]) + bias_ref[...]
+        pre = own + mm(mean, wn_ref[...]) + bias_ref[...]
         slope = jnp.where(pre > 0, 1.0, jnp.exp(jnp.minimum(pre, 0.0)))
         out_ref[...] = jnp.where(pre > 0, pre, slope - 1.0).astype(BF16)
         grad = cot_ref[...].astype(F32) * slope
@@ -204,9 +206,9 @@
     return call(
         body,
         [shape((nd, hid), BF16), shape((8, hid), F32)] + [shape((nd, hid + xw), BF16)] * cs,
-        [*parts, inverse, own, own_feat, w_neigh, bias, cotangent],
+        [*parts, *own_feats, inverse, w_neigh, w_self, bias, cotangent],
         [pltpu.VMEM((nd, 2 * depth), BF16)],
-        flops=2 * own_feat.size * hid,
+        flops=4 * nd * depth * hid,
     )
 
 
@@ -471,12 +473,7 @@
         return lax.ppermute(x, "row", [(s, s ^ 1) for s in range(rs)])
 
     def gather_chips(x):
-        found = {0: x}
-        step = half // 2
-        while step:
-            found.update({d + step: along_chips(found[d], step) for d in list(found)})
-            step //= 2
-        return [found[d] for d in range(half)]
+        return [x] + [along_chips(x, k) for k in range(1, half)]
 
     if rs == 2 * cs:
 
@@ -495,16 +492,10 @@
         def send_own(block, t):
             return lax.ppermute(block, ("row", "col"), swap if t == 0 else [])
 
-    near = along_chips(features, 1)
-    mine_first = {0: features, 1: near}
-    step = half // 2
-    while step > 1:
-        evens = [d for d in mine_first if d % 2 == 0]
-        mine_first.update({d + step: along_chips(mine_first[d], step) for d in evens})
-        step //= 2
-    theirs_first = {0: other_core(features), 1: other_core(near)}
-    own_feats = {0: send_own(features, 0)}
-    turned_neigh, turned_self = turn([w_neigh, w_self], [theirs_first[0]])
+    blocks = gather_chips(features)
+    theirs = [other_core(x) for x in blocks]
+    own_feats = [send_own(blocks[0], 0)]
+    turned_neigh, turned_self = turn([w_neigh, w_self], [theirs[0], own_feats[0]])
     tile, turned = densify(
         block_rows.reshape(-1),
         block_cols.reshape(-1),
@@ -513,38 +504,25 @@
         nd,
         rs,
         cs,
-        [near, turned_neigh, own_feats[0]],
-    )
-    mine_first.update(
-        {d: follow(x, [tile, theirs_first[1]]) for d, x in mine_first.items() if d > 1}
-    )
-    mine_last = {d + 1: along_chips(x, 1) for d, x in mine_first.items() if d > 1}
-    theirs_first.update({d: other_core(x) for d, x in mine_first.items() if d > 1})
-    theirs_last = {d: other_core(x) for d, x in mine_last.items()}
-    own_feats.update({d: send_own(x, d) for d, x in mine_first.items() if d})
-
-    def placed(mine, theirs):
-        places = list(mine) + [half + d for d in theirs]
-        return places, [*mine.values(), *theirs.values()]
-
-    begun = forward_first(
-        tile, *placed(mine_first, theirs_first), nd, [own_feats[0], own_feats[1]]
-    )
-    evens = [x for d, x in own_feats.items() if d and d % 2 == 0]
-    parts = forward_parts(begun, tile, *placed(mine_last, theirs_last), nd, cs, evens)
-    own_feats.update({d: send_own(follow(x, parts[:1]), d) for d, x in mine_last.items()})
-    own_feat = sum(list(own_feats.values())[1:], own_feats[0])
-    mass = row_sums(tile, nd, cs, parts[1:2])
+        [turned_neigh],
+    )
+    mass = row_sums(tile, nd, cs, ())
     degree = mass
     for k in range(1, cs):
         degree = degree + along_col(mass, k)
     inverse = 1.0 / (degree[:1] + 1.0)
+
+    def placed(distances):
+        places = distances + [half + d for d in distances]
+        return places, [blocks[d] for d in distances] + [theirs[d] for d in distances]
+
+    begun = forward_first(tile, *placed([0, 1]), nd, [inverse])
+    parts = forward_parts(begun, tile, *placed(list(range(2, half))), nd, cs)
+    own_feats += [send_own(blocks[d], d) for d in range(1, half)]
     inverse = jnp.broadcast_to(inverse[0][:, None], (rt, LANES))
-    own = jnp.dot(own_feat, w_self, preferred_element_type=F32).astype(BF16)
-
     parts = [parts[0]] + [along_col(parts[k], k) for k in range(1, cs)]
     output, sums, *packs = activation(
-        parts, inverse, own, own_feat, w_neigh, bias[None, :], cotangent
+        parts, own_feats, inverse, w_neigh, w_self, bias[None, :], cotangent
     )
     packs = [packs[0]] + [along_col(packs[k], k) for k in range(1, cs)]
 
@@ -556,19 +534,18 @@
     late = scaled_parts(packs[mid:], mid, *scaled_args, [keep])
     scaled, self_parts = zip(early, late)
     chunks = pair_sum(keep, came)
-    back_after = [chunks[1]]
     chunks = [chunks[0]] + [along_chips(chunks[k], k) for k in range(1, half)]
-    chunk = last_sum(chunks)
-    line = gather_chips(chunk)
-
-    keep, send = back_parts(turned, scaled, self_parts, nd, cs, rs, back_after)
-    keep, send = fold(keep, other_core(send), [chunk])
+    line = gather_chips(last_sum(chunks))
+
+    keep, send = back_parts(turned, scaled, self_parts, nd, cs, rs, chunks[1:])
+    keep, send = fold(keep, other_core(send), line[1:])
+    line = stack(line, after=[send])
     keep, send = fold(keep, along_chips(send, 1))
-    line = stack(line, after=[send])
+    folded = [keep]
     step = 2
     while step < half:
-        folded = fold(keep, along_chips(send, step))
-        keep, send = folded if 2 * step < half else (folded, None)
+        last = fold(keep, along_chips(send, step))
+        keep, send = last if 2 * step < half else (last, None)
         step *= 2
     grad_input = keep
 
@@ -587,7 +564,7 @@
         near = [line, first, second]
     else:
         near = [line] + [along_col(line, k) for k in range(1, cs - 1)]
-    near = stack(near, joined=True, after=[grad_input])
+    near = stack(near, joined=True, after=folded)
     near_where = sum((at(distances, k) for k in range(cs - 1)), [])
     begun = assemble(both_cores(near, near_where), (), *sizes, ())
     if cs == 4:
@@ -595,7 +572,7 @@
         rest = [along_col(first[:mid], 2), along_col(second[mid:], 1)]
     else:
         rest = [along_col(line, cs - 1)]
-    rest = stack(rest, joined=True, after=begun[2:])
+    rest = stack(rest, joined=True, after=[begun[2], grad_input])
     pieces = both_cores(rest, at(distances, cs - 1))
     total_self, total_neigh, total_bias = assemble(pieces, begun, *sizes, ())
     return output, grad_input, total_self, total_neigh, total_bias.reshape(-1)

time: 124 us -> 130 us (1.048)
  waiting for transfers between devices: 56.6 us -> 64.7 us
  starting transfers between devices: 46.3 us -> 43.5 us
  Pallas kernels: 16.2 us -> 18.2 us
    ppermute x11, waiting for transfers between devices: 30.9 us -> 39.5 us  [along_chips(): return lax.ppermute(x, 'row', [(s, s ^ 2 * k) for s in range(rs)])]
    ppermute x4, waiting for transfers between devices: 7.18 us -> 0.01 us  [send_own(): return lax.ppermute(block, ('row', 'col'), pairs)]
    ppermute x13, waiting for transfers between devices: 15.2 us -> 21.7 us  [along_col(): return lax.ppermute(x, 'col', [(s, s ^ k) for s in range(cs)])]
    ppermute x11, starting transfers between devices: 18.9 us -> 12.7 us  [along_chips(): return lax.ppermute(x, 'row', [(s, s ^ 2 * k) for s in range(rs)])]
    ppermute x8, starting transfers between devices: 2.79 us -> 5.62 us  [other_core(): return lax.ppermute(x, 'row', [(s, s ^ 1) for s in range(rs)])]
    pallas_call x20 -> x18, Pallas kernels: 12 us -> 14 us  [call(): pl.pallas_call(run, out_shape=outs, in_specs=[SMEM] * smem + [VMEM] * (co...]
  transfers between devices with their start and end apart: 36 -> 36, of which waited for: 18 -> 14; matrix products, arithmetic and copies ran while one was open for 0% -> 0% of each run, Pallas kernels for 8% -> 8%
where the time goes in v6:
time: 130 us
  waiting for transfers between devices  64.7 us (50%)
  starting transfers between devices  43.5 us (33%)
  Pallas kernels  18.2 us (14%)
  between operations  1.71 us (1%)
  local copies, waits for them, and re-layouts  1.59 us (1%)
    ppermute x11, waiting for transfers between devices, along_chips(): return lax.ppermute(x, 'row', [(s, s ^ 2 * k) for s in range(rs)])  39.5 us
    ppermute x13, waiting for transfers between devices, along_col(): return lax.ppermute(x, 'col', [(s, s ^ k) for s in range(cs)])  21.7 us
    ppermute x13, starting transfers between devices, along_col(): return lax.ppermute(x, 'col', [(s, s ^ k) for s in range(cs)])  14.8 us
    pallas_call x18, Pallas kernels, call(): pl.pallas_call(run, out_shape=outs, in_specs=[SMEM] * smem + [VMEM] * (co...  14 us
    ppermute x11, starting transfers between devices, along_chips(): return lax.ppermute(x, 'row', [(s, s ^ 2 * k) for s in range(rs)])  12.7 us
    ppermute x4, starting transfers between devices, send_own(): return lax.ppermute(block, ('row', 'col'), pairs)  10.5 us
    ppermute x8, starting transfers between devices, other_core(): return lax.ppermute(x, 'row', [(s, s ^ 1) for s in range(rs)])  5.62 us
    pallas_call x2, Pallas kernels, assemble(): pl.pallas_call(run, out_shape=[weight, weight, shape((1, hid), F32)], in_...  4.19 us
  transfers between devices with their start and end apart: 36, of which 14 were waited for; matrix products, arithmetic and copies ran while one was open for 0% of the time, Pallas kernels for 8%

profile of v6, /device:TPU:0, one launch (start us, length us, event | category | flops | bytes accessed | tf_op | source)
XLA Modules:
  0.0 129.8 jit_solution(13340630740337028534)
XLA Ops:
  2.2 3.5 %collective-permute-start = (bf16[128,768]{1,0:T(8,128)(2,1)}, bf16[128,768]{1,0:T(8,128)(2,1)S(1)}, u32[]{:S(2)}, u32[]{:S(2)}) collective-permute-start(bf16[128,768]{1,0:T(8,128)(2,1)} %refs_1_.3), channel_id=1, source_target_pairs={{0,4},{4,0},{8,12},{12,8},{16,20},{20,16},{24,28},{28,24},{1,5},{5... | collective-permute-start | bytes 589832 | tf_op jit(solution)/shard_map/ppermute | solution.py:473
  7.3 1.8 %collective-permute-start.7 = (bf16[128,768]{1,0:T(8,128)(2,1)}, bf16[128,768]{1,0:T(8,128)(2,1)S(1)}, u32[]{:S(2)}, u32[]{:S(2)}) collective-permute-start(bf16[128,768]{1,0:T(8,128)(2,1)} %refs_1_.3), channel_id=1, source_target_pairs={{0,16},{4,20},{8,24},{12,28},{16,0},{20,4},{24,8},{28,12},{1,17},{... | collective-permute-start | bytes 589832 | tf_op jit(solution)/shard_map/ppermute | solution.py:470
  11.3 2.3 %shard_map.128 = (bf16[1024,768]{1,0:T(8,128)(2,1)S(1)}, bf16[1024,768]{1,0:T(8,128)(2,1)S(1)}) custom-call(bf16[768,1024]{1,0:T(8,128)(2,1)S(1)} %copy-done, bf16[768,1024]{1,0:T(8,128)(2,1)} %refs_10_.1, bf16[128,768]{1,0:T(8,128)(2,1)S(1)} %collective-permute-done.refs_2_.refs_3_, bf16[128,768]{1,0:T(8,128)(2,1)S(1)} %collective-permute-done.1.refs_3_.refs_4_), custom_call_target="tpu_custom_call" | custom-call | bytes 6291456 | tf_op jit(solution)/shard_map/pallas_call | solution.py:27
  15.4 1.8 %collective-permute-start.6 = (f32[8,512]{1,0:T(8,128)S(1)}, f32[8,512]{1,0:T(8,128)S(1)}, u32[]{:S(2)}, u32[]{:S(2)}) collective-permute-start(f32[8,512]{1,0:T(8,128)S(1)} %shard_map.130), channel_id=1, source_target_pairs={{0,3},{1,2},{2,1},{3,0},{4,7},{5,6},{6,5},{7,4},{8,11},{9,10},{10,... | collective-permute-start | bytes 49160 | tf_op jit(solution)/shard_map/ppermute | solution.py:467
  18.9 3.9 %collective-permute-start.14 = (bf16[128,768]{1,0:T(8,128)(2,1)S(1)}, bf16[128,768]{1,0:T(8,128)(2,1)S(1)}, u32[]{:S(2)}, u32[]{:S(2)}) collective-permute-start(bf16[128,768]{1,0:T(8,128)(2,1)S(1)} %collective-permute-done.2.refs_2_), channel_id=1, source_target_pairs={{0,2},{4,3},{9,8},{13,9},{18,22},{22,23},{27,28},{31,29}} | collective-permute-start | bytes 589832 | tf_op jit(solution)/shard_map/ppermute | solution.py:487
  22.8 3.8 %collective-permute-done.7.refs_2_ = bf16[128,768]{1,0:T(8,128)(2,1)S(1)} collective-permute-done((bf16[128,768]{1,0:T(8,128)(2,1)}, bf16[128,768]{1,0:T(8,128)(2,1)S(1)}, u32[]{:S(2)}, u32[]{:S(2)}) %collective-permute-start.7) | collective-permute-done | bytes 196640 | tf_op jit(solution)/shard_map/ppermute | solution.py:470
  26.6 2.7 %collective-permute-start.16 = (bf16[128,768]{1,0:T(8,128)(2,1)S(1)}, bf16[128,768]{1,0:T(8,128)(2,1)S(1)}, u32[]{:S(2)}, u32[]{:S(2)}) collective-permute-start(bf16[128,768]{1,0:T(8,128)(2,1)S(1)} %collective-permute-done.8.refs_3_), channel_id=1, source_target_pairs={{0,6},{4,7},{9,12},{13,13},{18,18},{22,19},{27,24},{31,25}} | collective-permute-start | bytes 589832 | tf_op jit(solution)/shard_map/ppermute | solution.py:487
  31.2 2.3 %collective-permute-start.15 = (bf16[128,768]{1,0:T(8,128)(2,1)S(1)}, bf16[128,768]{1,0:T(8,128)(2,1)S(1)}, u32[]{:S(2)}, u32[]{:S(2)}) collective-permute-start(bf16[128,768]{1,0:T(8,128)(2,1)S(1)} %collective-permute-done.7.refs_2_), channel_id=1, source_target_pairs={{0,4},{4,5},{9,14},{13,15},{18,16},{22,17},{27,26},{31,27}} | collective-permute-start | bytes 589832 | tf_op jit(solution)/shard_map/ppermute | solution.py:487
  35.0 3.4 %collective-permute-start.13 = (bf16[128,768]{1,0:T(8,128)(2,1)S(1)}, bf16[128,768]{1,0:T(8,128)(2,1)S(1)}, u32[]{:S(2)}, u32[]{:S(2)}) collective-permute-start(bf16[128,768]{1,0:T(8,128)(2,1)S(1)} %get-tuple-element.46), channel_id=1, source_target_pairs={{0,3},{1,2},{2,1},{3,0},{4,7},{5,6},{6,5},{7,4},{8,11},{9,10},{10,... | collective-permute-start | bytes 589832 | tf_op jit(solution)/shard_map/ppermute | solution.py:467
  38.3 4.3 %collective-permute-done.11.refs_1_ = bf16[128,768]{1,0:T(8,128)(2,1)S(1)} collective-permute-done((bf16[128,768]{1,0:T(8,128)(2,1)S(1)}, bf16[128,768]{1,0:T(8,128)(2,1)S(1)}, u32[]{:S(2)}, u32[]{:S(2)}) %collective-permute-start.11) | collective-permute-done | bytes 196640 | tf_op jit(solution)/shard_map/ppermute | solution.py:467
  42.6 3.3 %collective-permute-done.12.refs_2_ = bf16[128,768]{1,0:T(8,128)(2,1)S(1)} collective-permute-done((bf16[128,768]{1,0:T(8,128)(2,1)S(1)}, bf16[128,768]{1,0:T(8,128)(2,1)S(1)}, u32[]{:S(2)}, u32[]{:S(2)}) %collective-permute-start.12) | collective-permute-done | bytes 196640 | tf_op jit(solution)/shard_map/ppermute | solution.py:467
  46.1 3.2 %shard_map.133 = (bf16[128,1024]{1,0:T(8,128)(2,1)}, f32[8,1024]{1,0:T(8,128)S(1)}, bf16[128,1408]{1,0:T(8,128)(2,1)S(1)}, bf16[128,1408]{1,0:T(8,128)(2,1)S(1)}...) custom-call(f32[128,768]{1,0:T(8,128)S(1)} %get-tuple-element.43.refs_0_, ...), custom_call_target="tpu_custom_call" | custom-call | flops 402653184 | bytes 7180288 | tf_op jit(solution)/shard_map/pallas_call | solution.py:27
  52.8 7.9 %collective-permute-done.17.refs_4_.refs_1_ = bf16[128,1408]{1,0:T(8,128)(2,1)S(1)} collective-permute-done((bf16[128,1408]{1,0:T(8,128)(2,1)S(1)}, bf16[128,1408]{1,0:T(8,128)(2,1)S(1)}, u32[]{:S(2)}, u32[]{:S(2)}) %collective-permute-start.17) | collective-permute-done | bytes 360480 | tf_op jit(solution)/shard_map/ppermute | solution.py:467
  61.8 6.1 %collective-permute-done.18.refs_2_.refs_3_ = bf16[128,1408]{1,0:T(8,128)(2,1)S(1)} collective-permute-done((bf16[128,1408]{1,0:T(8,128)(2,1)S(1)}, bf16[128,1408]{1,0:T(8,128)(2,1)S(1)}, u32[]{:S(2)}, u32[]{:S(2)}) %collective-permute-start.18) | collective-permute-done | bytes 360480 | tf_op jit(solution)/shard_map/ppermute | solution.py:467
  72.4 2.6 %collective-permute-start.23 = (bf16[400,128]{1,0:T(8,128)(2,1)S(1)}, bf16[400,128]{1,0:T(8,128)(2,1)S(1)}, u32[]{:S(2)}, u32[]{:S(2)}) collective-permute-start(bf16[400,128]{1,0:T(8,128)(2,1)S(1)} %get-tuple-element.63), channel_id=1, source_target_pairs={{0,24},{4,28},{8,16},{12,20},{16,8},{20,12},{24,0},{28,4},{1,25},{... | collective-permute-start | bytes 307208 | tf_op jit(solution)/shard_map/ppermute | solution.py:470
  76.7 5.0 %collective-permute-done.22.refs_6_.refs_2_ = bf16[400,128]{1,0:T(8,128)(2,1)S(1)} collective-permute-done((bf16[400,128]{1,0:T(8,128)(2,1)S(1)}, bf16[400,128]{1,0:T(8,128)(2,1)S(1)}, u32[]{:S(2)}, u32[]{:S(2)}) %collective-permute-start.22) | collective-permute-done | bytes 102432 | tf_op jit(solution)/shard_map/ppermute | solution.py:470
  84.5 2.0 %collective-permute-start.26 = (bf16[400,128]{1,0:T(8,128)(2,1)S(1)}, bf16[400,128]{1,0:T(8,128)(2,1)S(1)}, u32[]{:S(2)}, u32[]{:S(2)}) collective-permute-start(bf16[400,128]{1,0:T(8,128)(2,1)S(1)} %shard_map.139.refs_0_), channel_id=1, source_target_pairs={{0,16},{4,20},{8,24},{12,28},{16,0},{20,4},{24,8},{28,12},{1,17},{... | collective-permute-start | bytes 307208 | tf_op jit(solution)/shard_map/ppermute | solution.py:470
  87.7 3.2 %collective-permute-done.27.refs_4_.refs_3_ = bf16[400,128]{1,0:T(8,128)(2,1)S(1)} collective-permute-done((bf16[400,128]{1,0:T(8,128)(2,1)S(1)}, bf16[400,128]{1,0:T(8,128)(2,1)S(1)}, u32[]{:S(2)}, u32[]{:S(2)}) %collective-permute-start.27) | collective-permute-done | bytes 102432 | tf_op jit(solution)/shard_map/ppermute | solution.py:470
  90.8 5.5 %collective-permute-done.26.refs_3_.refs_2_ = bf16[400,128]{1,0:T(8,128)(2,1)S(1)} collective-permute-done((bf16[400,128]{1,0:T(8,128)(2,1)S(1)}, bf16[400,128]{1,0:T(8,128)(2,1)S(1)}, u32[]{:S(2)}, u32[]{:S(2)}) %collective-permute-start.26) | collective-permute-done | bytes 102432 | tf_op jit(solution)/shard_map/ppermute | solution.py:470
  96.6 1.8 %collective-permute-start.32 = (bf16[4,400,128]{2,1,0:T(8,128)(2,1)S(1)}, bf16[4,400,128]{2,1,0:T(8,128)(2,1)S(1)}, u32[]{:S(2)}, u32[]{:S(2)}) collective-permute-start(bf16[4,400,128]{2,1,0:T(8,128)(2,1)S(1)} %shard_map.143.refs_0_), channel_id=1, source_target_pairs={{0,2},{1,3},{2,0},{3,1},{4,6},{5,7},{6,4},{7,5},{8,10},{9,11},{10,... | collective-permute-start | bytes 1228808 | tf_op jit(solution)/shard_map/ppermute | solution.py:467
  98.7 10.2 %collective-permute-done.28.refs_1_ = bf16[2,128,768]{2,1,0:T(8,128)(2,1)S(1)} collective-permute-done((bf16[2,128,768]{2,1,0:T(8,128)(2,1)S(1)}, bf16[2,128,768]{2,1,0:T(8,128)(2,1)S(1)}, u32[]{:S(2)}, u32[]{:S(2)}) %collective-permute-start.28) | collective-permute-done | bytes 393248 | tf_op jit(solution)/shard_map/ppermute | solution.py:470
  111.8 11.1 %collective-permute-done.29.refs_1_ = bf16[1,128,768]{2,1,0:T(8,128)(2,1)S(1)} collective-permute-done((bf16[1,128,768]{2,1,0:T(8,128)(2,1)S(1)}, bf16[1,128,768]{2,1,0:T(8,128)(2,1)S(1)}, u32[]{:S(2)}, u32[]{:S(2)}) %collective-permute-start.29) | collective-permute-done | bytes 196640 | tf_op jit(solution)/shard_map/ppermute | solution.py:470
  123.7 2.4 %shard_map.145 = (f32[768,1024]{1,0:T(8,128)}, f32[768,1024]{1,0:T(8,128)}, f32[1,1024]{1,0:T(1,128)S(1)}) custom-call(bf16[12,400,128]{2,1,0:T(8,128)(2,1)S(1)} %shard_map.144.refs_0_, bf16[12,400,128]{2,1,0:T(8,128)(2,1)S(1)} %collective-permute-done.34.refs_1_), custom_call_target="tpu_custom_call" | custom-call | bytes 14155776 | tf_op jit(solution)/shard_map/pallas_call | solution.py:435
  128.0 1.8 %shard_map.147 = (f32[768,1024]{1,0:T(8,128)}, f32[768,1024]{1,0:T(8,128)}, f32[1,1024]{1,0:T(1,128)}) custom-call(bf16[4,400,128]{2,1,0:T(8,128)(2,1)S(1)} %shard_map.146.refs_0_, bf16[4,400,128]{2,1,0:T(8,128)(2,1)S(1)} %collective-permute-done.35.refs_1_, f32[768,1024]{1,0:T(8,128)} %get-tuple-element.72.refs_2_, ...), custom_call_target="tpu_custom_call", output_to_operand_aliasing={{0}: (2, {}), {1}: (3, {})} | custom-call | bytes 4718592 | tf_op jit(solution)/shard_map/pallas_call | solution.py:435
  (90 shorter events, 32.2 us)
Async XLA Ops:
  5.7 12.2 %collective-permute-start.2 = (bf16[128,768]{1,0:T(8,128)(2,1)}, bf16[128,768]{1,0:T(8,128)(2,1)S(1)}, u32[]{:S(2)}, u32[]{:S(2)}) collective-permute-start(bf16[128,768]{1,0:T(8,128)(2,1)} %refs_1_.3), channel_id=1, source_target_pairs={{0,8},{4,12},{8,0},{12,4},{16,24},{20,28},{24,16},{28,20},{1,9},{5... | collective-permute-start | bytes 589832 | tf_op jit(solution)/shard_map/ppermute | solution.py:470
  5.7 13.2 %collective-permute-start.8 = (bf16[128,768]{1,0:T(8,128)(2,1)}, bf16[128,768]{1,0:T(8,128)(2,1)S(1)}, u32[]{:S(2)}, u32[]{:S(2)}) collective-permute-start(bf16[128,768]{1,0:T(8,128)(2,1)} %refs_1_.3), channel_id=1, source_target_pairs={{0,24},{4,28},{8,16},{12,20},{16,8},{20,12},{24,0},{28,4},{1,25},{... | collective-permute-start | bytes 589832 | tf_op jit(solution)/shard_map/ppermute | solution.py:470
  7.3 19.3 %collective-permute-start.7 = (bf16[128,768]{1,0:T(8,128)(2,1)}, bf16[128,768]{1,0:T(8,128)(2,1)S(1)}, u32[]{:S(2)}, u32[]{:S(2)}) collective-permute-start(bf16[128,768]{1,0:T(8,128)(2,1)} %refs_1_.3), channel_id=1, source_target_pairs={{0,16},{4,20},{8,24},{12,28},{16,0},{20,4},{24,8},{28,12},{1,17},{... | collective-permute-start | bytes 589832 | tf_op jit(solution)/shard_map/ppermute | solution.py:470
  15.4 11.2 %collective-permute-start.6 = (f32[8,512]{1,0:T(8,128)S(1)}, f32[8,512]{1,0:T(8,128)S(1)}, u32[]{:S(2)}, u32[]{:S(2)}) collective-permute-start(f32[8,512]{1,0:T(8,128)S(1)} %shard_map.130), channel_id=1, source_target_pairs={{0,3},{1,2},{2,1},{3,0},{4,7},{5,6},{6,5},{7,4},{8,11},{9,10},{10,... | collective-permute-start | bytes 49160 | tf_op jit(solution)/shard_map/ppermute | solution.py:467
  17.2 12.1 %collective-permute-start.5 = (f32[8,512]{1,0:T(8,128)S(1)}, f32[8,512]{1,0:T(8,128)S(1)}, u32[]{:S(2)}, u32[]{:S(2)}) collective-permute-start(f32[8,512]{1,0:T(8,128)S(1)} %shard_map.130), channel_id=1, source_target_pairs={{0,2},{1,3},{2,0},{3,1},{4,6},{5,7},{6,4},{7,5},{8,10},{9,11},{10,... | collective-permute-start | bytes 49160 | tf_op jit(solution)/shard_map/ppermute | solution.py:467
  17.9 13.2 %collective-permute-start.4 = (f32[8,512]{1,0:T(8,128)S(1)}, f32[8,512]{1,0:T(8,128)S(1)}, u32[]{:S(2)}, u32[]{:S(2)}) collective-permute-start(f32[8,512]{1,0:T(8,128)S(1)} %shard_map.130), channel_id=1, source_target_pairs={{0,1},{1,0},{2,3},{3,2},{4,5},{5,4},{6,7},{7,6},{8,9},{9,8},{10,11... | collective-permute-start | bytes 49160 | tf_op jit(solution)/shard_map/ppermute | solution.py:467
  18.9 16.0 %collective-permute-start.14 = (bf16[128,768]{1,0:T(8,128)(2,1)S(1)}, bf16[128,768]{1,0:T(8,128)(2,1)S(1)}, u32[]{:S(2)}, u32[]{:S(2)}) collective-permute-start(bf16[128,768]{1,0:T(8,128)(2,1)S(1)} %collective-permute-done.2.refs_2_), channel_id=1, source_target_pairs={{0,2},{4,3},{9,8},{13,9},{18,22},{22,23},{27,28},{31,29}} | collective-permute-start | bytes 589832 | tf_op jit(solution)/shard_map/ppermute | solution.py:487
  26.6 11.7 %collective-permute-start.16 = (bf16[128,768]{1,0:T(8,128)(2,1)S(1)}, bf16[128,768]{1,0:T(8,128)(2,1)S(1)}, u32[]{:S(2)}, u32[]{:S(2)}) collective-permute-start(bf16[128,768]{1,0:T(8,128)(2,1)S(1)} %collective-permute-done.8.refs_3_), channel_id=1, source_target_pairs={{0,6},{4,7},{9,12},{13,13},{18,18},{22,19},{27,24},{31,25}} | collective-permute-start | bytes 589832 | tf_op jit(solution)/shard_map/ppermute | solution.py:487
  34.9 11.1 %collective-permute-start.12 = (bf16[128,768]{1,0:T(8,128)(2,1)S(1)}, bf16[128,768]{1,0:T(8,128)(2,1)S(1)}, u32[]{:S(2)}, u32[]{:S(2)}) collective-permute-start(bf16[128,768]{1,0:T(8,128)(2,1)S(1)} %get-tuple-element.45), channel_id=1, source_target_pairs={{0,2},{1,3},{2,0},{3,1},{4,6},{5,7},{6,4},{7,5},{8,10},{9,11},{10,... | collective-permute-start | bytes 589832 | tf_op jit(solution)/shard_map/ppermute | solution.py:467
  35.0 11.0 %collective-permute-start.13 = (bf16[128,768]{1,0:T(8,128)(2,1)S(1)}, bf16[128,768]{1,0:T(8,128)(2,1)S(1)}, u32[]{:S(2)}, u32[]{:S(2)}) collective-permute-start(bf16[128,768]{1,0:T(8,128)(2,1)S(1)} %get-tuple-element.46), channel_id=1, source_target_pairs={{0,3},{1,2},{2,1},{3,0},{4,7},{5,6},{6,5},{7,4},{8,11},{9,10},{10,... | collective-permute-start | bytes 589832 | tf_op jit(solution)/shard_map/ppermute | solution.py:467
  49.3 11.3 %collective-permute-start.17 = (bf16[128,1408]{1,0:T(8,128)(2,1)S(1)}, bf16[128,1408]{1,0:T(8,128)(2,1)S(1)}, u32[]{:S(2)}, u32[]{:S(2)}) collective-permute-start(bf16[128,1408]{1,0:T(8,128)(2,1)S(1)} %get-tuple-element.51), channel_id=1, source_target_pairs={{0,1},{1,0},{2,3},{3,2},{4,5},{5,4},{6,7},{7,6},{8,9},{9,8},{10,11... | collective-permute-start | bytes 1081352 | tf_op jit(solution)/shard_map/ppermute | solution.py:467
  50.9 16.9 %collective-permute-start.18 = (bf16[128,1408]{1,0:T(8,128)(2,1)S(1)}, bf16[128,1408]{1,0:T(8,128)(2,1)S(1)}, u32[]{:S(2)}, u32[]{:S(2)}) collective-permute-start(bf16[128,1408]{1,0:T(8,128)(2,1)S(1)} %get-tuple-element.53), channel_id=1, source_target_pairs={{0,2},{1,3},{2,0},{3,1},{4,6},{5,7},{6,4},{7,5},{8,10},{9,11},{10,... | collective-permute-start | bytes 1081352 | tf_op jit(solution)/shard_map/ppermute | solution.py:467
  51.7 16.1 %collective-permute-start.19 = (bf16[128,1408]{1,0:T(8,128)(2,1)S(1)}, bf16[128,1408]{1,0:T(8,128)(2,1)S(1)}, u32[]{:S(2)}, u32[]{:S(2)}) collective-permute-start(bf16[128,1408]{1,0:T(8,128)(2,1)S(1)} %get-tuple-element.54), channel_id=1, source_target_pairs={{0,3},{1,2},{2,1},{3,0},{4,7},{5,6},{6,5},{7,4},{8,11},{9,10},{10,... | collective-permute-start | bytes 1081352 | tf_op jit(solution)/shard_map/ppermute | solution.py:467
  70.6 11.1 %collective-permute-start.22 = (bf16[400,128]{1,0:T(8,128)(2,1)S(1)}, bf16[400,128]{1,0:T(8,128)(2,1)S(1)}, u32[]{:S(2)}, u32[]{:S(2)}) collective-permute-start(bf16[400,128]{1,0:T(8,128)(2,1)S(1)} %get-tuple-element.62), channel_id=1, source_target_pairs={{0,16},{4,20},{8,24},{12,28},{16,0},{20,4},{24,8},{28,12},{1,17},{... | collective-permute-start | bytes 307208 | tf_op jit(solution)/shard_map/ppermute | solution.py:470
  83.1 13.3 %collective-permute-start.24 = (bf16[4,128,768]{2,1,0:T(8,128)(2,1)S(1)}, bf16[4,128,768]{2,1,0:T(8,128)(2,1)S(1)}, u32[]{:S(2)}, u32[]{:S(2)}) collective-permute-start(bf16[4,128,768]{2,1,0:T(8,128)(2,1)S(1)} %get-tuple-element.65), channel_id=1, source_target_pairs={{0,4},{4,0},{8,12},{12,8},{16,20},{20,16},{24,28},{28,24},{1,5},{5... | collective-permute-start | bytes 2359304 | tf_op jit(solution)/shard_map/ppermute | solution.py:473
  84.5 11.9 %collective-permute-start.26 = (bf16[400,128]{1,0:T(8,128)(2,1)S(1)}, bf16[400,128]{1,0:T(8,128)(2,1)S(1)}, u32[]{:S(2)}, u32[]{:S(2)}) collective-permute-start(bf16[400,128]{1,0:T(8,128)(2,1)S(1)} %shard_map.139.refs_0_), channel_id=1, source_target_pairs={{0,16},{4,20},{8,24},{12,28},{16,0},{20,4},{24,8},{28,12},{1,17},{... | collective-permute-start | bytes 307208 | tf_op jit(solution)/shard_map/ppermute | solution.py:470
  86.5 9.8 %collective-permute-start.25 = (bf16[400,128]{1,0:T(8,128)(2,1)S(1)}, bf16[400,128]{1,0:T(8,128)(2,1)S(1)}, u32[]{:S(2)}, u32[]{:S(2)}) collective-permute-start(bf16[400,128]{1,0:T(8,128)(2,1)S(1)} %shard_map.139.refs_0_), channel_id=1, source_target_pairs={{0,8},{4,12},{8,0},{12,4},{16,24},{20,28},{24,16},{28,20},{1,9},{5... | collective-permute-start | bytes 307208 | tf_op jit(solution)/shard_map/ppermute | solution.py:470
  96.6 12.4 %collective-permute-start.32 = (bf16[4,400,128]{2,1,0:T(8,128)(2,1)S(1)}, bf16[4,400,128]{2,1,0:T(8,128)(2,1)S(1)}, u32[]{:S(2)}, u32[]{:S(2)}) collective-permute-start(bf16[4,400,128]{2,1,0:T(8,128)(2,1)S(1)} %shard_map.143.refs_0_), channel_id=1, source_target_pairs={{0,2},{1,3},{2,0},{3,1},{4,6},{5,7},{6,4},{7,5},{8,10},{9,11},{10,... | collective-permute-start | bytes 1228808 | tf_op jit(solution)/shard_map/ppermute | solution.py:467
  98.4 10.8 %collective-permute-start.30 = (bf16[4,400,128]{2,1,0:T(8,128)(2,1)S(1)}, bf16[4,400,128]{2,1,0:T(8,128)(2,1)S(1)}, u32[]{:S(2)}, u32[]{:S(2)}) collective-permute-start(bf16[4,400,128]{2,1,0:T(8,128)(2,1)S(1)} %shard_map.143.refs_0_), channel_id=1, source_target_pairs={{0,1},{1,0},{2,3},{3,2},{4,5},{5,4},{6,7},{7,6},{8,9},{9,8},{10,11... | collective-permute-start | bytes 1228808 | tf_op jit(solution)/shard_map/ppermute | solution.py:467
  98.7 10.2 %collective-permute-start.28 = (bf16[2,128,768]{2,1,0:T(8,128)(2,1)S(1)}, bf16[2,128,768]{2,1,0:T(8,128)(2,1)S(1)}, u32[]{:S(2)}, u32[]{:S(2)}) collective-permute-start(bf16[2,128,768]{2,1,0:T(8,128)(2,1)S(1)} %get-tuple-element.68.refs_4_), channel_id=1, source_target_pairs={{0,8},{4,12},{8,0},{12,4},{16,24},{20,28},{24,16},{28,20},{1,9},{5... | collective-permute-start | bytes 1179656 | tf_op jit(solution)/shard_map/ppermute | solution.py:470
  109.3 14.4 %collective-permute-start.34 = (bf16[12,400,128]{2,1,0:T(8,128)(2,1)S(1)}, bf16[12,400,128]{2,1,0:T(8,128)(2,1)S(1)}, u32[]{:S(2)}, u32[]{:S(2)}) collective-permute-start(bf16[12,400,128]{2,1,0:T(8,128)(2,1)S(1)} %shard_map.144.refs_0_), channel_id=1, source_target_pairs={{0,4},{4,0},{8,12},{12,8},{16,20},{20,16},{24,28},{28,24},{1,5},{5... | collective-permute-start | bytes 3686408 | tf_op jit(solution)/shard_map/ppermute | solution.py:473
  109.4 16.7 %collective-permute-start.33 = (bf16[2,400,128]{2,1,0:T(8,128)(2,1)S(1)}, bf16[2,400,128]{2,1,0:T(8,128)(2,1)S(1)}, u32[]{:S(2)}, u32[]{:S(2)}) collective-permute-start(bf16[2,400,128]{2,1,0:T(8,128)(2,1)S(1)} %slice.17), channel_id=1, source_target_pairs={{0,1},{1,0},{2,3},{3,2},{4,5},{5,4},{6,7},{7,6},{8,9},{9,8},{10,11... | collective-permute-start | bytes 614408 | tf_op jit(solution)/shard_map/ppermute | solution.py:467
  111.0 15.1 %collective-permute-start.31 = (bf16[2,400,128]{2,1,0:T(8,128)(2,1)S(1)}, bf16[2,400,128]{2,1,0:T(8,128)(2,1)S(1)}, u32[]{:S(2)}, u32[]{:S(2)}) collective-permute-start(bf16[2,400,128]{2,1,0:T(8,128)(2,1)S(1)} %slice.16), channel_id=1, source_target_pairs={{0,2},{1,3},{2,0},{3,1},{4,6},{5,7},{6,4},{7,5},{8,10},{9,11},{10,... | collective-permute-start | bytes 614408 | tf_op jit(solution)/shard_map/ppermute | solution.py:467
  111.6 11.4 %collective-permute-start.29 = (bf16[1,128,768]{2,1,0:T(8,128)(2,1)S(1)}, bf16[1,128,768]{2,1,0:T(8,128)(2,1)S(1)}, u32[]{:S(2)}, u32[]{:S(2)}) collective-permute-start(bf16[1,128,768]{2,1,0:T(8,128)(2,1)S(1)} %get-tuple-element.70), channel_id=1, source_target_pairs={{0,16},{4,20},{8,24},{12,28},{16,0},{20,4},{24,8},{28,12},{1,17},{... | collective-permute-start | bytes 589832 | tf_op jit(solution)/shard_map/ppermute | solution.py:470
  (21 other events, 142.1 us)

commit v7 on v4

--- a/solution.py
+++ b/solution.py
@@ -73,13 +73,13 @@
     rt, ct, half = nd * cs, nd * rs, rs // 2
 
     def body(rows_ref, cols_ref, count_ref, values_ref, tile_ref, turned_ref, acc):
-        i, j = lax.axis_index("row"), lax.axis_index("col")
+        i = lax.axis_index("row")
         z, c = i // 2, lax.rem(i, 2)
         acc[...] = jnp.zeros_like(acc)
 
         def add(s, carry):
             col = cols_ref[s]
-            row = rows_ref[s] ^ j
+            row = rows_ref[s]
             col = (z ^ (col // 2)) + half * (lax.rem(col, 2) ^ c)
             r = pl.multiple_of(row * nd, nd)
             c0 = pl.multiple_of(col * nd, nd)
@@ -107,20 +107,16 @@
     return jnp.concatenate([tile_ref[:, p * nd : (p + 1) * nd] for p in places], axis=1)
 
 
-def forward_first(tile, places, blocks, nd, cs, after):
+def forward_first(tile, places, blocks, nd, after):
     rt, ct = tile.shape
     width = blocks[0].shape[1]
 
     def body(*refs):
         tile_ref, feat_refs = refs[0], refs[1 : 1 + len(blocks)]
         sum_ref, mass_ref = refs[1 + len(blocks) :]
-        j = lax.axis_index("col")
         feats = jnp.concatenate([r[...] for r in feat_refs], axis=0)
         sum_ref[...] = mm(tile_columns(tile_ref, places, nd), feats)
-        ones = jnp.ones((8, ct), BF16)
-        for k in range(cs):
-            place = pl.multiple_of((j ^ k) * nd, nd)
-            mass_ref[:, pl.ds(place, nd)] = mm(ones, tile_ref[k * nd : (k + 1) * nd, :], 1, 1)
+        mass_ref[...] = mm(jnp.ones((8, ct), BF16), tile_ref[...], 1, 1)
 
     return call(
         body,
@@ -132,21 +128,25 @@
 
 
 def forward_parts(begun, tile, places, blocks, nd, cs, after):
+    rt = tile.shape[0]
     width = blocks[0].shape[1]
 
     def body(*refs):
         sum_ref, tile_ref, feat_refs = refs[0], refs[1], refs[2 : 2 + len(blocks)]
-        outs = refs[2 + len(blocks) :]
+        *outs, acc = refs[2 + len(blocks) :]
+        j = lax.axis_index("col")
         feats = jnp.concatenate([r[...] for r in feat_refs], axis=0)
-        parts = sum_ref[...] + mm(tile_columns(tile_ref, places, nd), feats)
+        acc[...] = sum_ref[...] + mm(tile_columns(tile_ref, places, nd), feats)
         for k in range(cs):
-            outs[k][...] = parts[k * nd : (k + 1) * nd].astype(outs[k].dtype)
+            start = pl.multiple_of((j ^ k) * nd, nd)
+            outs[k][...] = acc[pl.ds(start, nd), :].astype(outs[k].dtype)
 
     return call(
         body,
         [shape((nd, width), BF16 if k else F32) for k in range(cs)],
         [begun, tile, *blocks],
-        flops=2 * tile.shape[0] * len(places) * nd * width,
+        [pltpu.VMEM((rt, width), F32)],
+        flops=2 * rt * len(places) * nd * width,
         after=after,
     )
 
@@ -160,8 +160,7 @@
     def body(*refs):
         part_refs = refs[:cs]
         inv_ref, own_ref, feat_ref, w_ref, bias_ref, cot_ref = refs[cs : cs + 6]
-        out_ref, sum_ref, *packs = refs[cs + 6 : -1]
-        both = refs[-1]
+        out_ref, sum_ref, packs, both = refs[cs + 6 :]
         j = lax.axis_index("col")
         inv = inv_ref[pl.ds(pl.multiple_of(j * nd, nd), nd), :]
         total = sum(r[...].astype(F32) for r in part_refs)
@@ -175,21 +174,12 @@
         sum_ref[...] = jnp.broadcast_to(jnp.sum(grad, axis=0, keepdims=True), (8, hid))
         grad = grad.astype(BF16)
         for k in range(cs):
-            packs[k][:, :hid] = grad
-            target = j ^ k
-            if xw % LANES == 0:
-                start = pl.multiple_of(target * xw, LANES)
-                packs[k][:, hid:] = both[:, pl.ds(start, xw)]
-            else:
-                for d in range(cs):
-
-                    @pl.when(target == d)
-                    def _():
-                        packs[k][:, hid:] = both[:, d * xw : (d + 1) * xw]
-
-    return call(
-        body,
-        [shape((nd, hid), BF16), shape((8, hid), F32)] + [shape((nd, hid + xw), BF16)] * cs,
+            packs[k, :, :hid] = grad
+            packs[k, :, hid:] = both[:, k * xw : (k + 1) * xw]
+
+    return call(
+        body,
+        [shape((nd, hid), BF16), shape((8, hid), F32), shape((cs, nd, hid + xw), BF16)],
         [*parts, inverse, own, own_feat, w_neigh, bias, cotangent],
         [pltpu.VMEM((nd, 2 * depth), BF16)],
         flops=2 * own_feat.size * hid,
@@ -202,23 +192,21 @@
     return jnp.concatenate([high, total - high], axis=0)
 
 
-def weight_parts(packs, sums, rs, xr, nc, after):
-    cs = len(packs)
+def weight_parts(packs, sums, rs, xr, nc):
+    cs, nd, width = packs.shape
     hid = sums.shape[1]
-    nd, xw = packs[0].shape[0], packs[0].shape[1] - hid
+    xw = width - hid
     half = rs // 2
 
-    def body(*refs):
-        pack_refs = refs[:cs]
-        sum_ref, keep_ref, send_ref, acc = refs[cs:]
-        x_all = jnp.concatenate([r[:, hid:] for r in pack_refs], axis=0)
-        g_all = jnp.concatenate([r[:, :hid] for r in pack_refs], axis=0)
+    def body(pack_ref, sum_ref, *refs):
+        keep_ref, send_ref, acc = refs
+        x_all = jnp.concatenate([pack_ref[k, :, hid:] for k in range(cs)], axis=0)
+        g_all = jnp.concatenate([pack_ref[k, :, :hid] for k in range(cs)], axis=0)
         acc[...] = mm(x_all, g_all, 0, 0)
-        i = lax.axis_index("row")
-        z, c = i // 2, lax.rem(i, 2)
+        c = lax.rem(lax.axis_index("row"), 2)
         for k in range(half):
             for core, ref in ((c, keep_ref), (1 - c, send_ref)):
-                q = 2 * (z ^ k) + core
+                q = 2 * k + core
                 row = pl.multiple_of((q // nc) * xr, xr)
                 col = pl.multiple_of(lax.rem(q, nc) * LANES, LANES)
                 ref[k, :xr, :] = acc[pl.ds(row, xr), pl.ds(col, LANES)].astype(ref.dtype)
@@ -228,29 +216,21 @@
     return call(
         body,
         [shape(dims, F32), shape(dims, BF16)],
-        [*packs, sums],
+        [packs, sums],
         [pltpu.VMEM((xw, hid), F32)],
         flops=2 * cs * nd * xw * hid,
-        after=after,
-    )
-
-
-def scaled_parts(packs, first, inverse, turned_neigh, turned_self, cs, rs, after=()):
-    count = len(packs)
-    nd = packs[0].shape[0]
+    )
+
+
+def scaled_parts(packs, inverse, turned_neigh, turned_self, rs, after):
+    cs, nd, _ = packs.shape
     hid, depth = turned_neigh.shape
 
-    def body(neigh_ref, own_ref, inv_ref, *refs):
-        pack_refs, scaled_ref, self_ref = refs[:count], refs[count], refs[count + 1]
+    def body(pack_ref, neigh_ref, own_ref, inv_ref, scaled_ref, self_ref):
         i, j = lax.axis_index("row"), lax.axis_index("col")
-        grads = jnp.concatenate([r[:, :hid] for r in pack_refs], axis=0)
-        product = mm(grads, neigh_ref[...])
-        for r in range(count):
-            start = pl.multiple_of((j ^ (first + r)) * nd, nd)
-            inv = inv_ref[pl.ds(start, nd), :]
-            inv = jnp.concatenate([inv] * (depth // LANES), axis=1)
-            rows = slice(r * nd, (r + 1) * nd)
-            scaled_ref[rows, :] = (product[rows] * inv).astype(BF16)
+        grads = jnp.concatenate([pack_ref[k, :, :hid] for k in range(cs)], axis=0)
+        inv = jnp.concatenate([inv_ref[...]] * (depth // LANES), axis=1)
+        scaled_ref[...] = (mm(grads, neigh_ref[...]) * inv).astype(BF16)
 
         @pl.when(i * cs // rs == j)
         def _():
@@ -258,9 +238,9 @@
 
     return call(
         body,
-        [shape((count * nd, depth), BF16), shape((count * nd, depth), F32)],
-        [turned_neigh, turned_self, inverse, *packs],
-        flops=4 * count * nd * hid * depth,
+        [shape((cs * nd, depth), BF16), shape((cs * nd, depth), F32)],
+        [packs, turned_neigh, turned_self, inverse],
+        flops=4 * cs * nd * hid * depth,
         after=after,
     )
 
@@ -274,26 +254,21 @@
     return order
 
 
-def back_parts(turned, scaled, self_parts, nd, cs, rs, after):
-    depth = scaled[0].shape[1]
+def back_parts(turned, scaled, self_part, nd, cs, rs, after):
+    depth = scaled.shape[1]
     half = rs // 2
-    count = len(scaled)
-    each = cs // count
-
-    def body(tile_ref, *refs):
-        scaled_refs, self_refs = refs[:count], refs[count : 2 * count]
-        keep_ref, send_ref, acc = refs[2 * count :]
+
+    def body(tile_ref, scaled_ref, self_ref, keep_ref, send_ref, acc):
         i, j = lax.axis_index("row"), lax.axis_index("col")
         z, c = i // 2, lax.rem(i, 2)
-        acc[...] = mm(tile_ref[...], jnp.concatenate([r[...] for r in scaled_refs], axis=0))
+        acc[...] = mm(tile_ref[...], scaled_ref[...])
 
         @pl.when(i * cs // rs == j)
         def _():
             for r in range(cs):
-                q = i * cs - j * rs + (j ^ r)
+                q = i * cs - j * rs + r
                 place = ((z ^ (q // 2)) + half * (lax.rem(q, 2) ^ c)) * nd
-                rows = slice(r % each * nd, (r % each + 1) * nd)
-                acc[pl.ds(pl.multiple_of(place, nd), nd), :] += self_refs[r // each][rows]
+                acc[pl.ds(pl.multiple_of(place, nd), nd), :] += self_ref[r * nd : (r + 1) * nd]
 
         for ref, base in ((send_ref, half), (keep_ref, 0)):
             for k, distance in enumerate(halving_order(half)):
@@ -304,7 +279,7 @@
     return call(
         body,
         [shape(dims, F32), shape(dims, BF16)],
-        [turned, *scaled, *self_parts],
+        [turned, scaled, self_part],
         [pltpu.VMEM((rs * nd, depth), F32)],
         flops=2 * turned.size * depth,
         after=after,
@@ -333,35 +308,27 @@
     half, rows, width = keep.shape
     main = rows - EXTRA
 
-    def body(keep_ref, came_ref, *outs):
+    def body(keep_ref, came_ref, out_ref):
         for k in range(half):
             total = keep_ref[k] + came_ref[k].astype(F32)
-            dtype = outs[k].dtype
-            outs[k][:main, :] = total[:main].astype(dtype)
+            out_ref[k, :main, :] = total[:main].astype(BF16)
             merged = total[main : main + 8] + total[main + 8 :]
-            outs[k][main:, :] = split_pair(merged).astype(dtype)
-
-    return call(
-        body,
-        [shape((rows, width), BF16 if k else F32) for k in range(half)],
-        [keep, came],
-    )
-
-
-def last_sum(parts):
-    rows, width = parts[0].shape
+            out_ref[k, main:, :] = split_pair(merged).astype(BF16)
+
+    return call(body, [shape(keep.shape, BF16)], [keep, came])[0]
+
+
+def last_sum(came):
+    half, rows, width = came.shape
     main = rows - EXTRA
 
-    def body(*refs):
-        out_ref = refs[-1]
-        total = refs[0][...]
-        for ref in refs[1:-1]:
-            total = total + ref[...].astype(F32)
+    def body(came_ref, out_ref):
+        total = sum(came_ref[k].astype(F32) for k in range(half))
         out_ref[:main, :] = total[:main].astype(BF16)
         merged = total[main : main + 8] + total[main + 8 :]
         out_ref[main:, :] = split_pair(merged).astype(BF16)
 
-    return call(body, [shape((rows, width), BF16)], parts)[0]
+    return call(body, [shape((rows, width), BF16)], [came])[0]
 
 
 def assemble(pieces, mine, begun, depth, hid, xr, nc, cs, factors, after):
@@ -515,40 +482,41 @@
         return places, [*mine.values(), *theirs.values()]
 
     begun, mass = forward_first(
-        tile, *placed(mine_first, theirs_first), nd, cs, [own_feats[1]]
+        tile, *placed(mine_first, theirs_first), nd, [own_feats[1]]
     )
     evens = [x for d, x in own_feats.items() if d and d % 2 == 0]
     parts = forward_parts(begun, tile, *placed(mine_last, theirs_last), nd, cs, evens)
     own_feat = sum(list(own_feats.values())[1:], own_feats[0])
     degree = mass
-    step = 1
-    while step < cs:
-        degree = degree + along_col(degree, step)
-        step *= 2
+    for k in range(1, cs):
+        degree = degree + along_col(mass, k)
     inverse = 1.0 / (degree[0] + 1.0)
     inverse = jnp.broadcast_to(inverse[:, None], (rt, LANES))
     own = jnp.dot(own_feat, w_self, preferred_element_type=F32).astype(BF16)
 
-    turned_neigh, turned_self = turn([w_neigh, w_self], [parts[0]])
+    turned_neigh, turned_self = turn([w_neigh, w_self], parts[:1])
     parts = [parts[0]] + [along_col(parts[k], k) for k in range(1, cs)]
-    output, sums, *packs = activation(
-        parts, inverse, own, own_feat, w_neigh, bias[None, :], cotangent, [turned_neigh]
-    )
-    packs = [packs[0]] + [along_col(packs[k], k) for k in range(1, cs)]
-
-    mid = cs // 2
-    scaled_args = (inverse, turned_neigh, turned_self, cs, rs)
-    early = scaled_parts(packs[:mid], 0, *scaled_args)
-    keep, send = weight_parts(packs, sums, rs, xr, nc, early[:1])
+    output, sums, packs = activation(
+        parts,
+        inverse,
+        own,
+        own_feat,
+        w_neigh,
+        bias[None, :],
+        cotangent,
+        [turned_neigh],
+    )
+    packs = lax.all_to_all(packs, "col", 0, 0)
+
+    keep, send = weight_parts(packs, sums, rs, xr, nc)
     came = other_core(send)
-    late = scaled_parts(packs[mid:], mid, *scaled_args, [keep])
-    scaled, self_parts = zip(early, late)
+    scaled, self_part = scaled_parts(packs, inverse, turned_neigh, turned_self, rs, [keep])
     chunks = pair_sum(keep, came)
-    back_after = [chunks[1]]
-    chunks = [chunks[0]] + [along_chips(chunks[k], k) for k in range(1, half)]
-    line = gather_chips(last_sum(chunks))
-
-    keep, send = back_parts(turned, scaled, self_parts, nd, cs, rs, back_after)
+    groups = [[2 * z + core for z in range(half)] for core in range(2)]
+    arrived = lax.all_to_all(chunks, "row", 0, 0, axis_index_groups=groups)
+    line = gather_chips(last_sum(arrived))
+
+    keep, send = back_parts(turned, scaled, self_part, nd, cs, rs, [chunks])
     keep, send = fold(keep, other_core(send), line[1:])
     line = stack(line, [send])
     step = 1

time: 117 us -> 126 us (1.077)
  blocking collectives: 0 us -> 21.6 us
  waiting for transfers between devices: 60.7 us -> 41.9 us
  local copies, waits for them, and re-layouts: 2.63 us -> 7.99 us
  Pallas kernels: 16.4 us -> 19.5 us
  starting transfers between devices: 34.4 us -> 32.1 us
    all_to_all x0 -> x1, blocking collectives: none -> 21.6 us  [local(): packs = lax.all_to_all(packs, 'col', 0, 0)]
    ppermute x12 -> x10, waiting for transfers between devices: 23.1 us -> 4.02 us  [along_col(): return lax.ppermute(x, 'col', [(s, s ^ k) for s in range(cs)])]
    all_to_all x0 -> x1, waiting for transfers between devices: none -> 7.98 us  [local(): arrived = lax.all_to_all(chunks, 'row', 0, 0, axis_index_groups=groups)]
    ppermute x11 -> x8, waiting for transfers between devices: 34.8 us -> 27.5 us  [along_chips(): return lax.ppermute(x, 'row', [(s, s ^ 2 * k) for s in range(rs)])]
    unnamed x22 -> x30, local copies, waits for them, and re-layouts: 2.48 us -> 7.84 us
    ppermute x11 -> x8, starting transfers between devices: 11.4 us -> 7.47 us  [along_chips(): return lax.ppermute(x, 'row', [(s, s ^ 2 * k) for s in range(rs)])]
    all_to_all x0 -> x1, starting transfers between devices: none -> 3.46 us  [local(): arrived = lax.all_to_all(chunks, 'row', 0, 0, axis_index_groups=groups)]
    ppermute x12 -> x10, starting transfers between devices: 11.7 us -> 8.22 us  [along_col(): return lax.ppermute(x, 'col', [(s, s ^ k) for s in range(cs)])]
  transfers between devices with their start and end apart: 38 -> 34, of which waited for: 19 -> 12; matrix products, arithmetic and copies ran while one was open for 0% -> 0% of each run, Pallas kernels for 9% -> 11%
where the time goes in v7:
time: 126 us; the launch traced here: 125 us
  waiting for transfers between devices  41.9 us (33%)
  starting transfers between devices  32.1 us (25%)
  blocking collectives  21.6 us (17%)
  Pallas kernels  19.5 us (15%)
  local copies, waits for them, and re-layouts  7.99 us (6%)
  between operations  1.69 us (1%)
    ppermute x8, waiting for transfers between devices, along_chips(): return lax.ppermute(x, 'row', [(s, s ^ 2 * k) for s in range(rs)])  27.5 us
    all_to_all x1, blocking collectives, local(): packs = lax.all_to_all(packs, 'col', 0, 0)  21.6 us
    pallas_call x15, Pallas kernels, call(): pl.pallas_call(run, out_shape=outs, in_specs=[SMEM] * smem + [VMEM] * (co...  15.3 us
    ppermute x10, starting transfers between devices, along_col(): return lax.ppermute(x, 'col', [(s, s ^ k) for s in range(cs)])  8.22 us
    all_to_all x1, waiting for transfers between devices, local(): arrived = lax.all_to_all(chunks, 'row', 0, 0, axis_index_groups=groups)  7.98 us
    ppermute x4, starting transfers between devices, send_own(): return lax.ppermute(block, ('row', 'col'), pairs)  7.9 us
    unnamed x30, local copies, waits for them, and re-layouts  7.84 us
    ppermute x8, starting transfers between devices, along_chips(): return lax.ppermute(x, 'row', [(s, s ^ 2 * k) for s in range(rs)])  7.47 us
  transfers between devices with their start and end apart: 34, of which 12 were waited for; matrix products, arithmetic and copies ran while one was open for 0% of the time, Pallas kernels for 11%

profile of v7, /device:TPU:0, one launch (start us, length us, event | category | flops | bytes accessed | tf_op | source)
XLA Modules:
  0.0 125.4 jit_solution(17624743139845883466)
XLA Ops:
  0.6 3.1 %collective-permute-start = (bf16[128,768]{1,0:T(8,128)(2,1)}, bf16[128,768]{1,0:T(8,128)(2,1)S(1)}, u32[]{:S(2)}, u32[]{:S(2)}) collective-permute-start(bf16[128,768]{1,0:T(8,128)(2,1)} %refs_1_.2), channel_id=1, source_target_pairs={{0,8},{4,12},{8,0},{12,4},{16,24},{20,28},{24,16},{28,20},{1,9},{5... | collective-permute-start | bytes 589832 | tf_op jit(solution)/shard_map/ppermute | solution.py:422
  3.7 1.6 %collective-permute-start.2 = (bf16[128,768]{1,0:T(8,128)(2,1)}, bf16[128,768]{1,0:T(8,128)(2,1)S(1)}, u32[]{:S(2)}, u32[]{:S(2)}) collective-permute-start(bf16[128,768]{1,0:T(8,128)(2,1)} %refs_1_.2), channel_id=1, source_target_pairs={{0,0},{4,1},{9,10},{13,11},{18,20},{22,21},{27,30},{31,31}} | collective-permute-start | bytes 589832 | tf_op jit(solution)/shard_map/ppermute | solution.py:444
  5.3 2.0 %collective-permute-start.1 = (bf16[128,768]{1,0:T(8,128)(2,1)}, bf16[128,768]{1,0:T(8,128)(2,1)S(1)}, u32[]{:S(2)}, u32[]{:S(2)}) collective-permute-start(bf16[128,768]{1,0:T(8,128)(2,1)} %refs_1_.2), channel_id=1, source_target_pairs={{0,4},{4,0},{8,12},{12,8},{16,20},{20,16},{24,28},{28,24},{1,5},{5... | collective-permute-start | bytes 589832 | tf_op jit(solution)/shard_map/ppermute | solution.py:425
  7.3 1.5 %collective-permute-done.refs_4_.refs_2_ = bf16[128,768]{1,0:T(8,128)(2,1)S(1)} collective-permute-done((bf16[128,768]{1,0:T(8,128)(2,1)}, bf16[128,768]{1,0:T(8,128)(2,1)S(1)}, u32[]{:S(2)}, u32[]{:S(2)}) %collective-permute-start) | collective-permute-done | bytes 196640 | tf_op jit(solution)/shard_map/ppermute | solution.py:422
  9.5 3.6 %collective-permute-start.6 = (bf16[128,768]{1,0:T(8,128)(2,1)S(1)}, bf16[128,768]{1,0:T(8,128)(2,1)S(1)}, u32[]{:S(2)}, u32[]{:S(2)}) collective-permute-start(bf16[128,768]{1,0:T(8,128)(2,1)S(1)} %collective-permute-done.refs_4_.refs_2_), channel_id=1, source_target_pairs={{0,2},{4,3},{9,8},{13,9},{18,22},{22,23},{27,28},{31,29}} | collective-permute-start | bytes 589832 | tf_op jit(solution)/shard_map/ppermute | solution.py:444
  15.6 1.6 %shard_map.128 = (bf16[512,1024]{1,0:T(8,128)(2,1)S(1)}, bf16[1024,512]{1,0:T(8,128)(2,1)S(1)}) custom-call(s32[24]{0:T(128)S(1)} %bitcast.12, s32[24]{0:T(128)S(1)} %bitcast.13, s32[1]{0:T(128)} %bitcast.9.refs_2_, bf16[24,128,128]{2,1,0:T(8,128)(2,1)S(1)} %bitcast.10, bf16[128,768]{1,0:T(8,128)(2,1)S(1)} %collective-permute-done.refs_4_.refs_2_, ...), custom_call_target="tpu_custom_call" | custom-call | flops 524288 | bytes 2883780 | tf_op jit(solution)/shard_map/pallas_call | solution.py:27
  18.9 1.8 %collective-permute-start.5 = (bf16[128,768]{1,0:T(8,128)(2,1)S(1)}, bf16[128,768]{1,0:T(8,128)(2,1)S(1)}, u32[]{:S(2)}, u32[]{:S(2)}) collective-permute-start(bf16[128,768]{1,0:T(8,128)(2,1)S(1)} %shard_map.129.refs_3_), channel_id=1, source_target_pairs={{0,4},{4,0},{8,12},{12,8},{16,20},{20,16},{24,28},{28,24},{1,5},{5... | collective-permute-start | bytes 589832 | tf_op jit(solution)/shard_map/ppermute | solution.py:425
  23.3 3.1 %collective-permute-start.13 = (f32[8,512]{1,0:T(8,128)S(1)}, f32[8,512]{1,0:T(8,128)S(1)}, u32[]{:S(2)}, u32[]{:S(2)}) collective-permute-start(f32[8,512]{1,0:T(8,128)S(1)} %get-tuple-element.40), channel_id=1, source_target_pairs={{0,1},{1,0},{2,3},{3,2},{4,5},{5,4},{6,7},{7,6},{8,9},{9,8},{10,11... | collective-permute-start | bytes 49160 | tf_op jit(solution)/shard_map/ppermute | solution.py:419
  31.3 3.4 %collective-permute-start.12 = (bf16[128,768]{1,0:T(8,128)(2,1)S(1)}, bf16[128,768]{1,0:T(8,128)(2,1)S(1)}, u32[]{:S(2)}, u32[]{:S(2)}) collective-permute-start(bf16[128,768]{1,0:T(8,128)(2,1)S(1)} %get-tuple-element.39), channel_id=1, source_target_pairs={{0,3},{1,2},{2,1},{3,0},{4,7},{5,6},{6,5},{7,4},{8,11},{9,10},{10,... | collective-permute-start | bytes 589832 | tf_op jit(solution)/shard_map/ppermute | solution.py:419
  34.7 2.4 %shard_map.132 = (bf16[1024,768]{1,0:T(8,128)(2,1)S(1)}, bf16[1024,768]{1,0:T(8,128)(2,1)S(1)}) custom-call(bf16[768,1024]{1,0:T(8,128)(2,1)S(1)} %copy-done, bf16[768,1024]{1,0:T(8,128)(2,1)} %refs_1_.3, f32[128,768]{1,0:T(8,128)S(1)} %get-tuple-element.36.refs_2_.refs_0_), custom_call_target="tpu_custom_call" | custom-call | bytes 6291456 | tf_op jit(solution)/shard_map/pallas_call | solution.py:27
  39.0 3.8 %collective-permute-done.11.refs_2_ = bf16[128,768]{1,0:T(8,128)(2,1)S(1)} collective-permute-done((bf16[128,768]{1,0:T(8,128)(2,1)S(1)}, bf16[128,768]{1,0:T(8,128)(2,1)S(1)}, u32[]{:S(2)}, u32[]{:S(2)}) %collective-permute-start.11) | collective-permute-done | bytes 196640 | tf_op jit(solution)/shard_map/ppermute | solution.py:419
  44.2 21.6 %all_to_all.10.refs_0_ = bf16[4,128,1408]{2,1,0:T(8,128)(2,1)S(1)} all-to-all(bf16[4,128,1408]{2,1,0:T(8,128)(2,1)S(1)} %get-tuple-element.44), channel_id=1, replica_groups=mesh['row'=8,'col'=4] {'col'}, dimensions={0} | all-to-all | bytes 2883584 | tf_op jit(solution)/shard_map/all_to_all | solution.py:509
  66.7 3.8 %shard_map.135 = (bf16[512,768]{1,0:T(8,128)(2,1)S(1)}, f32[512,768]{1,0:T(8,128)S(1)}) custom-call(bf16[4,128,1408]{2,1,0:T(8,128)(2,1)S(1)} %all_to_all.10.refs_0_, bf16[1024,768]{1,0:T(8,128)(2,1)} %copy-done.1, bf16[1024,768]{1,0:T(8,128)(2,1)} %copy-done.13, f32[512,128]{1,0:T(8,128)S(1)} %broadcast_in_dim.4.refs_4_.refs_3_, ...), custom_call_target="tpu_custom_call" | custom-call | flops 1610612736 | bytes 7208960 | tf_op jit(solution)/shard_map/pallas_call | solution.py:27
  72.2 3.5 %all-to-all-start.1 = ((bf16[4,400,128]{2,1,0:T(8,128)(2,1)}), bf16[4,400,128]{2,1,0:T(8,128)(2,1)S(1)}, u32[]{:S(2)}, u32[]{:S(2)}) async-start(bf16[4,400,128]{2,1,0:T(8,128)(2,1)} %shard_map.136.refs_3_), calls=%async_computation.1 | async-start | bytes 819200 | tf_op jit(solution)/shard_map/all_to_all | solution.py:516
  78.0 2.1 %shard_map.137 = (f32[4,128,768]{2,1,0:T(8,128)S(1)}, bf16[4,128,768]{2,1,0:T(8,128)(2,1)}) custom-call(bf16[1024,512]{1,0:T(8,128)(2,1)S(1)} %copy-done.3, bf16[512,768]{1,0:T(8,128)(2,1)S(1)} %copy-done.6, f32[512,768]{1,0:T(8,128)S(1)} %get-tuple-element.49.refs_2_, bf16[4,400,128]{2,1,0:T(8,128)(2,1)} %shard_map.136.refs_3_), custom_call_target="tpu_custom_call" | custom-call | flops 805306368 | bytes 5767168 | tf_op jit(solution)/shard_map/pallas_call | solution.py:27
  80.6 8.0 %all-to-all-done.1.refs_0_ = bf16[4,400,128]{2,1,0:T(8,128)(2,1)S(1)} async-done(((bf16[4,400,128]{2,1,0:T(8,128)(2,1)}), bf16[4,400,128]{2,1,0:T(8,128)(2,1)S(1)}, u32[]{:S(2)}, u32[]{:S(2)}) %all-to-all-start.1) | async-done | bytes 409632 | tf_op jit(solution)/shard_map/all_to_all | solution.py:516
  88.8 2.0 %collective-permute-start.19 = (bf16[400,128]{1,0:T(8,128)(2,1)S(1)}, bf16[400,128]{1,0:T(8,128)(2,1)S(1)}, u32[]{:S(2)}, u32[]{:S(2)}) collective-permute-start(bf16[400,128]{1,0:T(8,128)(2,1)S(1)} %shard_map.138.refs_0_), channel_id=1, source_target_pairs={{0,8},{4,12},{8,0},{12,4},{16,24},{20,28},{24,16},{28,20},{1,9},{5... | collective-permute-start | bytes 307208 | tf_op jit(solution)/shard_map/ppermute | solution.py:422
  90.8 4.6 %collective-permute-done.20.refs_3_.refs_2_ = bf16[400,128]{1,0:T(8,128)(2,1)S(1)} collective-permute-done((bf16[400,128]{1,0:T(8,128)(2,1)S(1)}, bf16[400,128]{1,0:T(8,128)(2,1)S(1)}, u32[]{:S(2)}, u32[]{:S(2)}) %collective-permute-start.20) | collective-permute-done | bytes 102432 | tf_op jit(solution)/shard_map/ppermute | solution.py:422
  95.5 4.5 %collective-permute-done.21.refs_4_.refs_3_ = bf16[400,128]{1,0:T(8,128)(2,1)S(1)} collective-permute-done((bf16[400,128]{1,0:T(8,128)(2,1)S(1)}, bf16[400,128]{1,0:T(8,128)(2,1)S(1)}, u32[]{:S(2)}, u32[]{:S(2)}) %collective-permute-start.21) | collective-permute-done | bytes 102432 | tf_op jit(solution)/shard_map/ppermute | solution.py:422
  100.9 9.0 %collective-permute-done.22.refs_1_ = bf16[2,128,768]{2,1,0:T(8,128)(2,1)S(1)} collective-permute-done((bf16[2,128,768]{2,1,0:T(8,128)(2,1)S(1)}, bf16[2,128,768]{2,1,0:T(8,128)(2,1)S(1)}, u32[]{:S(2)}, u32[]{:S(2)}) %collective-permute-start.22) | collective-permute-done | bytes 393248 | tf_op jit(solution)/shard_map/ppermute | solution.py:422
  110.0 2.0 %collective-permute-start.23 = (bf16[1,128,768]{2,1,0:T(8,128)(2,1)S(1)}, bf16[1,128,768]{2,1,0:T(8,128)(2,1)S(1)}, u32[]{:S(2)}, u32[]{:S(2)}) collective-permute-start(bf16[1,128,768]{2,1,0:T(8,128)(2,1)S(1)} %get-tuple-element.56), channel_id=1, source_target_pairs={{0,16},{4,20},{8,24},{12,28},{16,0},{20,4},{24,8},{28,12},{1,17},{... | collective-permute-start | bytes 589832 | tf_op jit(solution)/shard_map/ppermute | solution.py:422
  112.8 7.0 %collective-permute-done.23.refs_1_ = bf16[1,128,768]{2,1,0:T(8,128)(2,1)S(1)} collective-permute-done((bf16[1,128,768]{2,1,0:T(8,128)(2,1)S(1)}, bf16[1,128,768]{2,1,0:T(8,128)(2,1)S(1)}, u32[]{:S(2)}, u32[]{:S(2)}) %collective-permute-start.23) | collective-permute-done | bytes 196640 | tf_op jit(solution)/shard_map/ppermute | solution.py:422
  121.1 1.8 %shard_map.143 = (f32[768,1024]{1,0:T(8,128)}, f32[768,1024]{1,0:T(8,128)}, f32[1,1024]{1,0:T(1,128)S(1)}) custom-call(bf16[4,400,128]{2,1,0:T(8,128)(2,1)S(1)} %shard_map.142.refs_0_, bf16[4,400,128]{2,1,0:T(8,128)(2,1)S(1)} %collective-permute-done.25.refs_1_, bf16[4,400,128]{2,1,0:T(8,128)(2,1)S(1)} %collective-permute-done.27.refs_2_, ...), custom_call_target="tpu_custom_call" | custom-call | bytes 9437184 | tf_op jit(solution)/shard_map/pallas_call | solution.py:387
  123.0 2.4 %shard_map.144 = (f32[768,1024]{1,0:T(8,128)}, f32[768,1024]{1,0:T(8,128)}, f32[1,1024]{1,0:T(1,128)}) custom-call(bf16[4,400,128]{2,1,0:T(8,128)(2,1)S(1)} %collective-permute-done.24.refs_0_, bf16[4,400,128]{2,1,0:T(8,128)(2,1)S(1)} %collective-permute-done.26.refs_1_, ...), custom_call_target="tpu_custom_call", output_to_operand_aliasing={{0}: (5, {}), {1}: (6, {})} | custom-call | bytes 9437184 | tf_op jit(solution)/shard_map/pallas_call | solution.py:387
  (98 shorter events, 23.5 us)
Async XLA Ops:
  0.6 8.2 %collective-permute-start = (bf16[128,768]{1,0:T(8,128)(2,1)}, bf16[128,768]{1,0:T(8,128)(2,1)S(1)}, u32[]{:S(2)}, u32[]{:S(2)}) collective-permute-start(bf16[128,768]{1,0:T(8,128)(2,1)} %refs_1_.2), channel_id=1, source_target_pairs={{0,8},{4,12},{8,0},{12,4},{16,24},{20,28},{24,16},{28,20},{1,9},{5... | collective-permute-start | bytes 589832 | tf_op jit(solution)/shard_map/ppermute | solution.py:422
  3.7 9.4 %collective-permute-start.2 = (bf16[128,768]{1,0:T(8,128)(2,1)}, bf16[128,768]{1,0:T(8,128)(2,1)S(1)}, u32[]{:S(2)}, u32[]{:S(2)}) collective-permute-start(bf16[128,768]{1,0:T(8,128)(2,1)} %refs_1_.2), channel_id=1, source_target_pairs={{0,0},{4,1},{9,10},{13,11},{18,20},{22,21},{27,30},{31,31}} | collective-permute-start | bytes 589832 | tf_op jit(solution)/shard_map/ppermute | solution.py:444
  5.3 7.8 %collective-permute-start.1 = (bf16[128,768]{1,0:T(8,128)(2,1)}, bf16[128,768]{1,0:T(8,128)(2,1)S(1)}, u32[]{:S(2)}, u32[]{:S(2)}) collective-permute-start(bf16[128,768]{1,0:T(8,128)(2,1)} %refs_1_.2), channel_id=1, source_target_pairs={{0,4},{4,0},{8,12},{12,8},{16,20},{20,16},{24,28},{28,24},{1,5},{5... | collective-permute-start | bytes 589832 | tf_op jit(solution)/shard_map/ppermute | solution.py:425
  7.3 11.6 %collective-permute-start.3 = (bf16[128,768]{1,0:T(8,128)(2,1)}, bf16[128,768]{1,0:T(8,128)(2,1)S(1)}, u32[]{:S(2)}, u32[]{:S(2)}) collective-permute-start(bf16[128,768]{1,0:T(8,128)(2,1)} %refs_1_.2), channel_id=1, source_target_pairs={{0,16},{4,20},{8,24},{12,28},{16,0},{20,4},{24,8},{28,12},{1,17},{... | collective-permute-start | bytes 589832 | tf_op jit(solution)/shard_map/ppermute | solution.py:422
  8.8 10.1 %collective-permute-start.4 = (bf16[128,768]{1,0:T(8,128)(2,1)S(1)}, bf16[128,768]{1,0:T(8,128)(2,1)S(1)}, u32[]{:S(2)}, u32[]{:S(2)}) collective-permute-start(bf16[128,768]{1,0:T(8,128)(2,1)S(1)} %collective-permute-done.refs_4_.refs_2_), channel_id=1, source_target_pairs={{0,4},{4,0},{8,12},{12,8},{16,20},{20,16},{24,28},{28,24},{1,5},{5... | collective-permute-start | bytes 589832 | tf_op jit(solution)/shard_map/ppermute | solution.py:425
  9.5 11.3 %collective-permute-start.6 = (bf16[128,768]{1,0:T(8,128)(2,1)S(1)}, bf16[128,768]{1,0:T(8,128)(2,1)S(1)}, u32[]{:S(2)}, u32[]{:S(2)}) collective-permute-start(bf16[128,768]{1,0:T(8,128)(2,1)S(1)} %collective-permute-done.refs_4_.refs_2_), channel_id=1, source_target_pairs={{0,2},{4,3},{9,8},{13,9},{18,22},{22,23},{27,28},{31,29}} | collective-permute-start | bytes 589832 | tf_op jit(solution)/shard_map/ppermute | solution.py:444
  20.8 7.1 %collective-permute-start.7 = (bf16[128,768]{1,0:T(8,128)(2,1)S(1)}, bf16[128,768]{1,0:T(8,128)(2,1)S(1)}, u32[]{:S(2)}, u32[]{:S(2)}) collective-permute-start(bf16[128,768]{1,0:T(8,128)(2,1)S(1)} %shard_map.129.refs_3_), channel_id=1, source_target_pairs={{0,8},{4,12},{8,0},{12,4},{16,24},{20,28},{24,16},{28,20},{1,9},{5... | collective-permute-start | bytes 589832 | tf_op jit(solution)/shard_map/ppermute | solution.py:422
  22.9 6.3 %collective-permute-start.14 = (f32[8,512]{1,0:T(8,128)S(1)}, f32[8,512]{1,0:T(8,128)S(1)}, u32[]{:S(2)}, u32[]{:S(2)}) collective-permute-start(f32[8,512]{1,0:T(8,128)S(1)} %get-tuple-element.40), channel_id=1, source_target_pairs={{0,2},{1,3},{2,0},{3,1},{4,6},{5,7},{6,4},{7,5},{8,10},{9,11},{10,... | collective-permute-start | bytes 49160 | tf_op jit(solution)/shard_map/ppermute | solution.py:419
  27.8 10.4 %collective-permute-start.16 = (bf16[128,768]{1,0:T(8,128)(2,1)S(1)}, bf16[128,768]{1,0:T(8,128)(2,1)S(1)}, u32[]{:S(2)}, u32[]{:S(2)}) collective-permute-start(bf16[128,768]{1,0:T(8,128)(2,1)S(1)} %collective-permute-done.7.refs_2_), channel_id=1, source_target_pairs={{0,6},{4,7},{9,12},{13,13},{18,18},{22,19},{27,24},{31,25}} | collective-permute-start | bytes 589832 | tf_op jit(solution)/shard_map/ppermute | solution.py:444
  31.2 7.8 %collective-permute-start.10 = (bf16[128,768]{1,0:T(8,128)(2,1)S(1)}, bf16[128,768]{1,0:T(8,128)(2,1)S(1)}, u32[]{:S(2)}, u32[]{:S(2)}) collective-permute-start(bf16[128,768]{1,0:T(8,128)(2,1)S(1)} %get-tuple-element.37), channel_id=1, source_target_pairs={{0,1},{1,0},{2,3},{3,2},{4,5},{5,4},{6,7},{7,6},{8,9},{9,8},{10,11... | collective-permute-start | bytes 589832 | tf_op jit(solution)/shard_map/ppermute | solution.py:419
  31.3 11.5 %collective-permute-start.11 = (bf16[128,768]{1,0:T(8,128)(2,1)S(1)}, bf16[128,768]{1,0:T(8,128)(2,1)S(1)}, u32[]{:S(2)}, u32[]{:S(2)}) collective-permute-start(bf16[128,768]{1,0:T(8,128)(2,1)S(1)} %get-tuple-element.38), channel_id=1, source_target_pairs={{0,2},{1,3},{2,0},{3,1},{4,6},{5,7},{6,4},{7,5},{8,10},{9,11},{10,... | collective-permute-start | bytes 589832 | tf_op jit(solution)/shard_map/ppermute | solution.py:419
  31.3 11.4 %collective-permute-start.12 = (bf16[128,768]{1,0:T(8,128)(2,1)S(1)}, bf16[128,768]{1,0:T(8,128)(2,1)S(1)}, u32[]{:S(2)}, u32[]{:S(2)}) collective-permute-start(bf16[128,768]{1,0:T(8,128)(2,1)S(1)} %get-tuple-element.39), channel_id=1, source_target_pairs={{0,3},{1,2},{2,1},{3,0},{4,7},{5,6},{6,5},{7,4},{8,11},{9,10},{10,... | collective-permute-start | bytes 589832 | tf_op jit(solution)/shard_map/ppermute | solution.py:419
  72.2 16.4 %all-to-all-start.1 = ((bf16[4,400,128]{2,1,0:T(8,128)(2,1)}), bf16[4,400,128]{2,1,0:T(8,128)(2,1)S(1)}, u32[]{:S(2)}, u32[]{:S(2)}) async-start(bf16[4,400,128]{2,1,0:T(8,128)(2,1)} %shard_map.136.refs_3_), calls=%async_computation.1 | async-start | bytes 819200 | tf_op jit(solution)/shard_map/all_to_all | solution.py:516
  80.1 15.4 %collective-permute-start.18 = (bf16[4,128,768]{2,1,0:T(8,128)(2,1)}, bf16[4,128,768]{2,1,0:T(8,128)(2,1)S(1)}, u32[]{:S(2)}, u32[]{:S(2)}) collective-permute-start(bf16[4,128,768]{2,1,0:T(8,128)(2,1)} %get-tuple-element.52), channel_id=1, source_target_pairs={{0,4},{4,0},{8,12},{12,8},{16,20},{20,16},{24,28},{28,24},{1,5},{5... | collective-permute-start | bytes 2359304 | tf_op jit(solution)/shard_map/ppermute | solution.py:425
  88.7 6.7 %collective-permute-start.20 = (bf16[400,128]{1,0:T(8,128)(2,1)S(1)}, bf16[400,128]{1,0:T(8,128)(2,1)S(1)}, u32[]{:S(2)}, u32[]{:S(2)}) collective-permute-start(bf16[400,128]{1,0:T(8,128)(2,1)S(1)} %shard_map.138.refs_0_), channel_id=1, source_target_pairs={{0,16},{4,20},{8,24},{12,28},{16,0},{20,4},{24,8},{28,12},{1,17},{... | collective-permute-start | bytes 307208 | tf_op jit(solution)/shard_map/ppermute | solution.py:422
  88.8 6.8 %collective-permute-start.19 = (bf16[400,128]{1,0:T(8,128)(2,1)S(1)}, bf16[400,128]{1,0:T(8,128)(2,1)S(1)}, u32[]{:S(2)}, u32[]{:S(2)}) collective-permute-start(bf16[400,128]{1,0:T(8,128)(2,1)S(1)} %shard_map.138.refs_0_), channel_id=1, source_target_pairs={{0,8},{4,12},{8,0},{12,4},{16,24},{20,28},{24,16},{28,20},{1,9},{5... | collective-permute-start | bytes 307208 | tf_op jit(solution)/shard_map/ppermute | solution.py:422
  100.1 9.8 %collective-permute-start.22 = (bf16[2,128,768]{2,1,0:T(8,128)(2,1)S(1)}, bf16[2,128,768]{2,1,0:T(8,128)(2,1)S(1)}, u32[]{:S(2)}, u32[]{:S(2)}) collective-permute-start(bf16[2,128,768]{2,1,0:T(8,128)(2,1)S(1)} %get-tuple-element.54.refs_4_), channel_id=1, source_target_pairs={{0,8},{4,12},{8,0},{12,4},{16,24},{20,28},{24,16},{28,20},{1,9},{5... | collective-permute-start | bytes 1179656 | tf_op jit(solution)/shard_map/ppermute | solution.py:422
  100.5 11.5 %collective-permute-start.27 = (bf16[4,400,128]{2,1,0:T(8,128)(2,1)S(1)}, bf16[4,400,128]{2,1,0:T(8,128)(2,1)S(1)}, u32[]{:S(2)}, u32[]{:S(2)}) collective-permute-start(bf16[4,400,128]{2,1,0:T(8,128)(2,1)S(1)} %shard_map.142.refs_0_), channel_id=1, source_target_pairs={{0,2},{1,3},{2,0},{3,1},{4,6},{5,7},{6,4},{7,5},{8,10},{9,11},{10,... | collective-permute-start | bytes 1228808 | tf_op jit(solution)/shard_map/ppermute | solution.py:419
  100.6 11.4 %collective-permute-start.25 = (bf16[4,400,128]{2,1,0:T(8,128)(2,1)S(1)}, bf16[4,400,128]{2,1,0:T(8,128)(2,1)S(1)}, u32[]{:S(2)}, u32[]{:S(2)}) collective-permute-start(bf16[4,400,128]{2,1,0:T(8,128)(2,1)S(1)} %shard_map.142.refs_0_), channel_id=1, source_target_pairs={{0,1},{1,0},{2,3},{3,2},{4,5},{5,4},{6,7},{7,6},{8,9},{9,8},{10,11... | collective-permute-start | bytes 1228808 | tf_op jit(solution)/shard_map/ppermute | solution.py:419
  110.0 9.8 %collective-permute-start.23 = (bf16[1,128,768]{2,1,0:T(8,128)(2,1)S(1)}, bf16[1,128,768]{2,1,0:T(8,128)(2,1)S(1)}, u32[]{:S(2)}, u32[]{:S(2)}) collective-permute-start(bf16[1,128,768]{2,1,0:T(8,128)(2,1)S(1)} %get-tuple-element.56), channel_id=1, source_target_pairs={{0,16},{4,20},{8,24},{12,28},{16,0},{20,4},{24,8},{28,12},{1,17},{... | collective-permute-start | bytes 589832 | tf_op jit(solution)/shard_map/ppermute | solution.py:422
  112.0 10.9 %collective-permute-start.24 = (bf16[4,400,128]{2,1,0:T(8,128)(2,1)S(1)}, bf16[4,400,128]{2,1,0:T(8,128)(2,1)S(1)}, u32[]{:S(2)}, u32[]{:S(2)}) collective-permute-start(bf16[4,400,128]{2,1,0:T(8,128)(2,1)S(1)} %shard_map.142.refs_0_), channel_id=1, source_target_pairs={{0,4},{4,0},{8,12},{12,8},{16,20},{20,16},{24,28},{28,24},{1,5},{5... | collective-permute-start | bytes 1228808 | tf_op jit(solution)/shard_map/ppermute | solution.py:425
  112.0 7.8 %collective-permute-start.31 = (bf16[2,400,128]{2,1,0:T(8,128)(2,1)S(1)}, bf16[2,400,128]{2,1,0:T(8,128)(2,1)S(1)}, u32[]{:S(2)}, u32[]{:S(2)}) collective-permute-start(bf16[2,400,128]{2,1,0:T(8,128)(2,1)S(1)} %slice.17), channel_id=1, source_target_pairs={{0,1},{1,0},{2,3},{3,2},{4,5},{5,4},{6,7},{7,6},{8,9},{9,8},{10,11... | collective-permute-start | bytes 614408 | tf_op jit(solution)/shard_map/ppermute | solution.py:419
  112.1 8.2 %collective-permute-start.29 = (bf16[2,400,128]{2,1,0:T(8,128)(2,1)S(1)}, bf16[2,400,128]{2,1,0:T(8,128)(2,1)S(1)}, u32[]{:S(2)}, u32[]{:S(2)}) collective-permute-start(bf16[2,400,128]{2,1,0:T(8,128)(2,1)S(1)} %slice.16), channel_id=1, source_target_pairs={{0,2},{1,3},{2,0},{3,1},{4,6},{5,7},{6,4},{7,5},{8,10},{9,11},{10,... | collective-permute-start | bytes 614408 | tf_op jit(solution)/shard_map/ppermute | solution.py:419
  112.8 10.2 %collective-permute-start.28 = (bf16[4,400,128]{2,1,0:T(8,128)(2,1)S(1)}, bf16[4,400,128]{2,1,0:T(8,128)(2,1)S(1)}, u32[]{:S(2)}, u32[]{:S(2)}) collective-permute-start(bf16[4,400,128]{2,1,0:T(8,128)(2,1)S(1)} %collective-permute-done.27.refs_2_), channel_id=1, source_target_pairs={{0,4},{4,0},{8,12},{12,8},{16,20},{20,16},{24,28},{28,24},{1,5},{5... | collective-permute-start | bytes 1228808 | tf_op jit(solution)/shard_map/ppermute | solution.py:425
  (25 other events, 75.5 us)

commit v8 on v5

--- a/solution.py
+++ b/solution.py
@@ -113,7 +113,7 @@
     return jnp.concatenate([tile_ref[:, p * nd : (p + 1) * nd] for p in places], axis=1)
 
 
-def row_sums(tile, nd, cs, after):
+def row_sums(tile, nd, cs):
     rt, ct = tile.shape
 
     def body(tile_ref, mass_ref):
@@ -123,7 +123,7 @@
             place = pl.multiple_of((j ^ k) * nd, nd)
             mass_ref[:, pl.ds(place, nd)] = mm(ones, tile_ref[k * nd : (k + 1) * nd, :], 1, 1)
 
-    return call(body, [shape((8, rt), F32)], [tile], flops=16 * tile.size, after=after)[0]
+    return call(body, [shape((8, rt), F32)], [tile], flops=16 * tile.size)[0]
 
 
 def forward_first(tile, places, blocks, nd, after):
@@ -145,7 +145,7 @@
     )[0]
 
 
-def forward_parts(begun, tile, places, blocks, nd, cs, after=()):
+def forward_parts(begun, tile, places, blocks, nd, cs, after):
     width = blocks[0].shape[1]
 
     def body(*refs):
@@ -165,7 +165,7 @@
     )
 
 
-def activation(parts, inverse, own, own_feat, w_neigh, bias, cotangent):
+def activation(parts, masses, own, own_feat, w_neigh, bias, cotangent, after):
     cs = len(parts)
     nd, hid = own.shape
     depth = own_feat.shape[1]
@@ -173,11 +173,14 @@
 
     def body(*refs):
         part_refs = refs[:cs]
-        inv_ref, own_ref, feat_ref, w_ref, bias_ref, cot_ref = refs[cs : cs + 6]
-        out_ref, sum_ref, *packs = refs[cs + 6 : -1]
+        mass_refs = refs[cs : cs + 2]
+        own_ref, feat_ref, w_ref, bias_ref, cot_ref = refs[cs + 2 : cs + 7]
+        out_ref, sum_ref, *packs = refs[cs + 7 : -1]
         both = refs[-1]
         j = lax.axis_index("col")
-        inv = inv_ref[pl.ds(pl.multiple_of(j * nd, nd), nd), :]
+        here = pl.ds(pl.multiple_of(j * nd, nd), nd)
+        inv = 1.0 / (mass_refs[0][:, here] + mass_refs[1][:, here] + 1.0)
+        inv = jnp.broadcast_to(inv.T[:, :1], (nd, LANES))
         total = sum(r[...].astype(F32) for r in part_refs)
         mean = (total * jnp.concatenate([inv] * (depth // LANES), axis=1)).astype(BF16)
         both[:, :depth] = feat_ref[...]
@@ -204,9 +207,10 @@
     return call(
         body,
         [shape((nd, hid), BF16), shape((8, hid), F32)] + [shape((nd, hid + xw), BF16)] * cs,
-        [*parts, inverse, own, own_feat, w_neigh, bias, cotangent],
+        [*parts, *masses, own, own_feat, w_neigh, bias, cotangent],
         [pltpu.VMEM((nd, 2 * depth), BF16)],
         flops=2 * own_feat.size * hid,
+        after=after,
     )
 
 
@@ -471,12 +475,7 @@
         return lax.ppermute(x, "row", [(s, s ^ 1) for s in range(rs)])
 
     def gather_chips(x):
-        found = {0: x}
-        step = half // 2
-        while step:
-            found.update({d + step: along_chips(found[d], step) for d in list(found)})
-            step //= 2
-        return [found[d] for d in range(half)]
+        return [x] + [along_chips(x, k) for k in range(1, half)]
 
     if rs == 2 * cs:
 
@@ -504,7 +503,6 @@
         step //= 2
     theirs_first = {0: other_core(features), 1: other_core(near)}
     own_feats = {0: send_own(features, 0)}
-    turned_neigh, turned_self = turn([w_neigh, w_self], [theirs_first[0]])
     tile, turned = densify(
         block_rows.reshape(-1),
         block_cols.reshape(-1),
@@ -513,15 +511,12 @@
         nd,
         rs,
         cs,
-        [near, turned_neigh, own_feats[0]],
-    )
-    mine_first.update(
-        {d: follow(x, [tile, theirs_first[1]]) for d, x in mine_first.items() if d > 1}
+        [],
     )
     mine_last = {d + 1: along_chips(x, 1) for d, x in mine_first.items() if d > 1}
     theirs_first.update({d: other_core(x) for d, x in mine_first.items() if d > 1})
     theirs_last = {d: other_core(x) for d, x in mine_last.items()}
-    own_feats.update({d: send_own(x, d) for d, x in mine_first.items() if d})
+    own_feats[1] = send_own(near, 1)
 
     def placed(mine, theirs):
         places = list(mine) + [half + d for d in theirs]
@@ -530,21 +525,25 @@
     begun = forward_first(
         tile, *placed(mine_first, theirs_first), nd, [own_feats[0], own_feats[1]]
     )
-    evens = [x for d, x in own_feats.items() if d and d % 2 == 0]
-    parts = forward_parts(begun, tile, *placed(mine_last, theirs_last), nd, cs, evens)
-    own_feats.update({d: send_own(follow(x, parts[:1]), d) for d, x in mine_last.items()})
+    degree = row_sums(tile, nd, cs)
+    step = 1
+    while step < cs:
+        masses = [degree, along_col(degree, step)]
+        degree = masses[0] + masses[1]
+        step *= 2
+    evens = {d: send_own(follow(x, [begun, masses[0]]), d) for d, x in mine_first.items() if d > 1}
+    own_feats.update(evens)
+    own_feats.update({d: send_own(x, d) for d, x in mine_last.items()})
+    parts = forward_parts(begun, tile, *placed(mine_last, theirs_last), nd, cs, list(evens.values()))
     own_feat = sum(list(own_feats.values())[1:], own_feats[0])
-    mass = row_sums(tile, nd, cs, parts[1:2])
-    degree = mass
-    for k in range(1, cs):
-        degree = degree + along_col(mass, k)
-    inverse = 1.0 / (degree[:1] + 1.0)
-    inverse = jnp.broadcast_to(inverse[0][:, None], (rt, LANES))
+    inverse = 1.0 / (degree[0] + 1.0)
+    inverse = jnp.broadcast_to(inverse[:, None], (rt, LANES))
     own = jnp.dot(own_feat, w_self, preferred_element_type=F32).astype(BF16)
 
+    turned_neigh, turned_self = turn([w_neigh, w_self], [parts[0]])
     parts = [parts[0]] + [along_col(parts[k], k) for k in range(1, cs)]
     output, sums, *packs = activation(
-        parts, inverse, own, own_feat, w_neigh, bias[None, :], cotangent
+        parts, masses, own, own_feat, w_neigh, bias[None, :], cotangent, [turned_neigh]
     )
     packs = [packs[0]] + [along_col(packs[k], k) for k in range(1, cs)]
 
@@ -556,48 +555,37 @@
     late = scaled_parts(packs[mid:], mid, *scaled_args, [keep])
     scaled, self_parts = zip(early, late)
     chunks = pair_sum(keep, came)
-    back_after = [chunks[1]]
     chunks = [chunks[0]] + [along_chips(chunks[k], k) for k in range(1, half)]
-    chunk = last_sum(chunks)
-    line = gather_chips(chunk)
-
-    keep, send = back_parts(turned, scaled, self_parts, nd, cs, rs, back_after)
-    keep, send = fold(keep, other_core(send), [chunk])
-    keep, send = fold(keep, along_chips(send, 1))
+    line = gather_chips(last_sum(chunks))
+
+    keep, send = back_parts(turned, scaled, self_parts, nd, cs, rs, chunks[1:])
+    keep, send = fold(keep, other_core(send), line[1:])
     line = stack(line, after=[send])
-    step = 2
+    step = 1
     while step < half:
         folded = fold(keep, along_chips(send, step))
         keep, send = folded if 2 * step < half else (folded, None)
         step *= 2
     grad_input = keep
 
-    def at(where, k):
-        return [(d, k) for d in where]
-
-    distances = list(range(half))
+    def piece(array, first, column, mine):
+        return array, [(first + t, column) for t in range(array.shape[0])], mine
+
+    mid = half // 2
+    if cs == 4 and mid:
+        first, second = along_col(line, 1), along_col(line, 2)
+        near = [(line, 0, 0), (first, 0, 1), (second, 0, 2)]
+        rest = [(along_col(first[:mid], 2), 0, 3), (along_col(second[mid:], 1), mid, 3)]
+    else:
+        near = [(line, 0, 0)] + [(along_col(line, k), 0, k) for k in range(1, cs - 1)]
+        rest = [(along_col(line, cs - 1), 0, cs - 1)]
     factor = 1.0 / math.sqrt(nd * rs * cs)
     sizes = (depth, hid, xr, nc, cs, (factor, 32.0 * factor))
-
-    def both_cores(array, where):
-        return [(array, where, True), (other_core(array), where, False)]
-
-    if cs == 4:
-        first, second = along_col(line, 1), along_col(line, 2)
-        near = [line, first, second]
-    else:
-        near = [line] + [along_col(line, k) for k in range(1, cs - 1)]
-    near = stack(near, joined=True, after=[grad_input])
-    near_where = sum((at(distances, k) for k in range(cs - 1)), [])
-    begun = assemble(both_cores(near, near_where), (), *sizes, ())
-    if cs == 4:
-        mid = half // 2
-        rest = [along_col(first[:mid], 2), along_col(second[mid:], 1)]
-    else:
-        rest = [along_col(line, cs - 1)]
-    rest = stack(rest, joined=True, after=begun[2:])
-    pieces = both_cores(rest, at(distances, cs - 1))
-    total_self, total_neigh, total_bias = assemble(pieces, begun, *sizes, ())
+    begun = assemble([piece(*x, True) for x in near], (), *sizes, ())
+    pieces = [piece(*x, True) for x in rest]
+    near = [(follow(x, [begun[2]]) if n == 1 else x, *where) for n, (x, *where) in enumerate(near)]
+    pieces += [piece(other_core(x), *where, False) for x, *where in near + rest]
+    total_self, total_neigh, total_bias = assemble(pieces, begun, *sizes, [grad_input])
     return output, grad_input, total_self, total_neigh, total_bias.reshape(-1)
 
 

time: 124 us -> 119 us (0.960)
  starting transfers between devices: 46.3 us -> 39.5 us
  local copies, waits for them, and re-layouts: 2.52 us -> 4.69 us
    ppermute x4, waiting for transfers between devices: 7.18 us -> 0.01 us  [send_own(): return lax.ppermute(block, ('row', 'col'), pairs)]
    ppermute x13 -> x12, waiting for transfers between devices: 15.2 us -> 19.4 us  [along_col(): return lax.ppermute(x, 'col', [(s, s ^ k) for s in range(cs)])]
    ppermute x11, waiting for transfers between devices: 30.9 us -> 33.5 us  [along_chips(): return lax.ppermute(x, 'row', [(s, s ^ 2 * k) for s in range(rs)])]
    ppermute x4, starting transfers between devices: 9.87 us -> 7.42 us  [send_own(): return lax.ppermute(block, ('row', 'col'), pairs)]
    ppermute x13 -> x12, starting transfers between devices: 14.8 us -> 12.6 us  [along_col(): return lax.ppermute(x, 'col', [(s, s ^ k) for s in range(cs)])]
    unnamed x20 -> x22, local copies, waits for them, and re-layouts: 2.37 us -> 4.54 us
    ppermute x11, starting transfers between devices: 18.9 us -> 17.1 us  [along_chips(): return lax.ppermute(x, 'row', [(s, s ^ 2 * k) for s in range(rs)])]
    ppermute x8 -> x11, waiting for transfers between devices: 3.31 us -> 2.78 us  [other_core(): return lax.ppermute(x, 'row', [(s, s ^ 1) for s in range(rs)])]
  transfers between devices with their start and end apart: 36 -> 38, of which waited for: 18 -> 14; matrix products, arithmetic and copies ran while one was open for 0% -> 0% of each run, Pallas kernels for 8% -> 8%
where the time goes in v8:
time: 119 us; the launch traced here: 118 us
  waiting for transfers between devices  55.7 us (47%)
  starting transfers between devices  39.5 us (33%)
  Pallas kernels  16.4 us (14%)
  local copies, waits for them, and re-layouts  4.69 us (4%)
  between operations  1.64 us (1%)
    ppermute x11, waiting for transfers between devices, along_chips(): return lax.ppermute(x, 'row', [(s, s ^ 2 * k) for s in range(rs)])  33.5 us
    ppermute x12, waiting for transfers between devices, along_col(): return lax.ppermute(x, 'col', [(s, s ^ k) for s in range(cs)])  19.4 us
    ppermute x11, starting transfers between devices, along_chips(): return lax.ppermute(x, 'row', [(s, s ^ 2 * k) for s in range(rs)])  17.1 us
    ppermute x12, starting transfers between devices, along_col(): return lax.ppermute(x, 'col', [(s, s ^ k) for s in range(cs)])  12.6 us
    pallas_call x18, Pallas kernels, call(): pl.pallas_call(run, out_shape=outs, in_specs=[SMEM] * smem + [VMEM] * (co...  12.2 us
    ppermute x4, starting transfers between devices, send_own(): return lax.ppermute(block, ('row', 'col'), pairs)  7.42 us
    unnamed x22, local copies, waits for them, and re-layouts  4.54 us
    pallas_call x2, Pallas kernels, assemble(): pl.pallas_call(run, out_shape=[weight, weight, shape((1, hid), F32)], in_...  4.2 us
  transfers between devices with their start and end apart: 38, of which 14 were waited for; matrix products, arithmetic and copies ran while one was open for 0% of the time, Pallas kernels for 8%

profile of v8, /device:TPU:0, one launch (start us, length us, event | category | flops | bytes accessed | tf_op | source)
XLA Modules:
  0.0 118.4 jit_solution(7615880914726694655)
XLA Ops:
  0.6 4.1 %collective-permute-start.1 = (bf16[128,768]{1,0:T(8,128)(2,1)}, bf16[128,768]{1,0:T(8,128)(2,1)S(1)}, u32[]{:S(2)}, u32[]{:S(2)}) collective-permute-start(bf16[128,768]{1,0:T(8,128)(2,1)} %refs_1_.2), channel_id=1, source_target_pairs={{0,16},{4,20},{8,24},{12,28},{16,0},{20,4},{24,8},{28,12},{1,17},{... | collective-permute-start | bytes 589832 | tf_op jit(solution)/shard_map/ppermute | solution.py:472
  4.7 1.6 %collective-permute-start = (bf16[128,768]{1,0:T(8,128)(2,1)}, bf16[128,768]{1,0:T(8,128)(2,1)S(1)}, u32[]{:S(2)}, u32[]{:S(2)}) collective-permute-start(bf16[128,768]{1,0:T(8,128)(2,1)} %refs_1_.2), channel_id=1, source_target_pairs={{0,8},{4,12},{8,0},{12,4},{16,24},{20,28},{24,16},{28,20},{1,9},{5... | collective-permute-start | bytes 589832 | tf_op jit(solution)/shard_map/ppermute | solution.py:472
  15.4 3.0 %collective-permute-start.6 = (bf16[128,768]{1,0:T(8,128)(2,1)S(1)}, bf16[128,768]{1,0:T(8,128)(2,1)S(1)}, u32[]{:S(2)}, u32[]{:S(2)}) collective-permute-start(bf16[128,768]{1,0:T(8,128)(2,1)S(1)} %collective-permute-done.refs_2_), channel_id=1, source_target_pairs={{0,2},{4,3},{9,8},{13,9},{18,22},{22,23},{27,28},{31,29}} | collective-permute-start | bytes 589832 | tf_op jit(solution)/shard_map/ppermute | solution.py:489
  19.5 2.3 %collective-permute-done.7.refs_2_ = bf16[128,768]{1,0:T(8,128)(2,1)S(1)} collective-permute-done((bf16[128,768]{1,0:T(8,128)(2,1)S(1)}, bf16[128,768]{1,0:T(8,128)(2,1)S(1)}, u32[]{:S(2)}, u32[]{:S(2)}) %collective-permute-start.7) | collective-permute-done | bytes 196640 | tf_op jit(solution)/shard_map/ppermute | solution.py:472
  22.7 2.4 %collective-permute-start.10 = (bf16[128,768]{1,0:T(8,128)(2,1)S(1)}, bf16[128,768]{1,0:T(8,128)(2,1)S(1)}, u32[]{:S(2)}, u32[]{:S(2)}) collective-permute-start(bf16[128,768]{1,0:T(8,128)(2,1)S(1)} %shard_map.131), channel_id=1, source_target_pairs={{0,4},{4,5},{9,14},{13,15},{18,16},{22,17},{27,26},{31,27}} | collective-permute-start | bytes 589832 | tf_op jit(solution)/shard_map/ppermute | solution.py:489
  27.0 1.7 %collective-permute-start.11 = (bf16[128,768]{1,0:T(8,128)(2,1)S(1)}, bf16[128,768]{1,0:T(8,128)(2,1)S(1)}, u32[]{:S(2)}, u32[]{:S(2)}) collective-permute-start(bf16[128,768]{1,0:T(8,128)(2,1)S(1)} %get-tuple-element.43), channel_id=1, source_target_pairs={{0,1},{1,0},{2,3},{3,2},{4,5},{5,4},{6,7},{7,6},{8,9},{9,8},{10,11... | collective-permute-start | bytes 589832 | tf_op jit(solution)/shard_map/ppermute | solution.py:469
  31.0 2.3 %shard_map.133 = (bf16[1024,768]{1,0:T(8,128)(2,1)S(1)}, bf16[1024,768]{1,0:T(8,128)(2,1)S(1)}) custom-call(bf16[768,1024]{1,0:T(8,128)(2,1)S(1)} %copy-done.2, bf16[768,1024]{1,0:T(8,128)(2,1)} %refs_1_.3, f32[128,768]{1,0:T(8,128)S(1)} %get-tuple-element.42.refs_2_.refs_0_), custom_call_target="tpu_custom_call" | custom-call | bytes 6291456 | tf_op jit(solution)/shard_map/pallas_call | solution.py:27
  34.5 5.5 %collective-permute-done.12.refs_2_ = bf16[128,768]{1,0:T(8,128)(2,1)S(1)} collective-permute-done((bf16[128,768]{1,0:T(8,128)(2,1)S(1)}, bf16[128,768]{1,0:T(8,128)(2,1)S(1)}, u32[]{:S(2)}, u32[]{:S(2)}) %collective-permute-start.12) | collective-permute-done | bytes 196640 | tf_op jit(solution)/shard_map/ppermute | solution.py:469
  43.2 1.7 %collective-permute-start.18 = (bf16[128,1408]{1,0:T(8,128)(2,1)S(1)}, bf16[128,1408]{1,0:T(8,128)(2,1)S(1)}, u32[]{:S(2)}, u32[]{:S(2)}) collective-permute-start(bf16[128,1408]{1,0:T(8,128)(2,1)S(1)} %get-tuple-element.54), channel_id=1, source_target_pairs={{0,3},{1,2},{2,1},{3,0},{4,7},{5,6},{6,5},{7,4},{8,11},{9,10},{10,... | collective-permute-start | bytes 1081352 | tf_op jit(solution)/shard_map/ppermute | solution.py:469
  44.9 7.7 %collective-permute-done.16.refs_4_.refs_1_ = bf16[128,1408]{1,0:T(8,128)(2,1)S(1)} collective-permute-done((bf16[128,1408]{1,0:T(8,128)(2,1)S(1)}, bf16[128,1408]{1,0:T(8,128)(2,1)S(1)}, u32[]{:S(2)}, u32[]{:S(2)}) %collective-permute-start.16) | collective-permute-done | bytes 360480 | tf_op jit(solution)/shard_map/ppermute | solution.py:469
  53.9 6.2 %collective-permute-done.17.refs_2_.refs_3_ = bf16[128,1408]{1,0:T(8,128)(2,1)S(1)} collective-permute-done((bf16[128,1408]{1,0:T(8,128)(2,1)S(1)}, bf16[128,1408]{1,0:T(8,128)(2,1)S(1)}, u32[]{:S(2)}, u32[]{:S(2)}) %collective-permute-start.17) | collective-permute-done | bytes 360480 | tf_op jit(solution)/shard_map/ppermute | solution.py:469
  61.0 1.7 %collective-permute-done.19.refs_1_ = bf16[4,400,128]{2,1,0:T(8,128)(2,1)S(1)} collective-permute-done((bf16[4,400,128]{2,1,0:T(8,128)(2,1)S(1)}, bf16[4,400,128]{2,1,0:T(8,128)(2,1)S(1)}, u32[]{:S(2)}, u32[]{:S(2)}) %collective-permute-start.19) | collective-permute-done | bytes 409632 | tf_op jit(solution)/shard_map/ppermute | solution.py:475
  62.8 2.5 %collective-permute-start.20 = (bf16[400,128]{1,0:T(8,128)(2,1)S(1)}, bf16[400,128]{1,0:T(8,128)(2,1)S(1)}, u32[]{:S(2)}, u32[]{:S(2)}) collective-permute-start(bf16[400,128]{1,0:T(8,128)(2,1)S(1)} %get-tuple-element.61), channel_id=1, source_target_pairs={{0,8},{4,12},{8,0},{12,4},{16,24},{20,28},{24,16},{28,20},{1,9},{5... | collective-permute-start | bytes 307208 | tf_op jit(solution)/shard_map/ppermute | solution.py:472
  66.2 1.5 %collective-permute-start.22 = (bf16[400,128]{1,0:T(8,128)(2,1)S(1)}, bf16[400,128]{1,0:T(8,128)(2,1)S(1)}, u32[]{:S(2)}, u32[]{:S(2)}) collective-permute-start(bf16[400,128]{1,0:T(8,128)(2,1)S(1)} %get-tuple-element.63), channel_id=1, source_target_pairs={{0,24},{4,28},{8,16},{12,20},{16,8},{20,12},{24,0},{28,4},{1,25},{... | collective-permute-start | bytes 307208 | tf_op jit(solution)/shard_map/ppermute | solution.py:472
  68.8 7.4 %collective-permute-done.21.refs_6_.refs_2_ = bf16[400,128]{1,0:T(8,128)(2,1)S(1)} collective-permute-done((bf16[400,128]{1,0:T(8,128)(2,1)S(1)}, bf16[400,128]{1,0:T(8,128)(2,1)S(1)}, u32[]{:S(2)}, u32[]{:S(2)}) %collective-permute-start.21) | collective-permute-done | bytes 102432 | tf_op jit(solution)/shard_map/ppermute | solution.py:472
  77.7 1.8 %collective-permute-start.26 = (bf16[400,128]{1,0:T(8,128)(2,1)S(1)}, bf16[400,128]{1,0:T(8,128)(2,1)S(1)}, u32[]{:S(2)}, u32[]{:S(2)}) collective-permute-start(bf16[400,128]{1,0:T(8,128)(2,1)S(1)} %shard_map.140.refs_0_), channel_id=1, source_target_pairs={{0,24},{4,28},{8,16},{12,20},{16,8},{20,12},{24,0},{28,4},{1,25},{... | collective-permute-start | bytes 307208 | tf_op jit(solution)/shard_map/ppermute | solution.py:472
  82.2 3.2 %collective-permute-done.26.refs_4_.refs_3_ = bf16[400,128]{1,0:T(8,128)(2,1)S(1)} collective-permute-done((bf16[400,128]{1,0:T(8,128)(2,1)S(1)}, bf16[400,128]{1,0:T(8,128)(2,1)S(1)}, u32[]{:S(2)}, u32[]{:S(2)}) %collective-permute-start.26) | collective-permute-done | bytes 102432 | tf_op jit(solution)/shard_map/ppermute | solution.py:472
  85.3 5.2 %collective-permute-done.25.refs_3_.refs_2_ = bf16[400,128]{1,0:T(8,128)(2,1)S(1)} collective-permute-done((bf16[400,128]{1,0:T(8,128)(2,1)S(1)}, bf16[400,128]{1,0:T(8,128)(2,1)S(1)}, u32[]{:S(2)}, u32[]{:S(2)}) %collective-permute-start.25) | collective-permute-done | bytes 102432 | tf_op jit(solution)/shard_map/ppermute | solution.py:472
  91.5 1.7 %collective-permute-start.29 = (bf16[4,400,128]{2,1,0:T(8,128)(2,1)S(1)}, bf16[4,400,128]{2,1,0:T(8,128)(2,1)S(1)}, u32[]{:S(2)}, u32[]{:S(2)}) collective-permute-start(bf16[4,400,128]{2,1,0:T(8,128)(2,1)S(1)} %shard_map.144.refs_0_), channel_id=1, source_target_pairs={{0,1},{1,0},{2,3},{3,2},{4,5},{5,4},{6,7},{7,6},{8,9},{9,8},{10,11... | collective-permute-start | bytes 1228808 | tf_op jit(solution)/shard_map/ppermute | solution.py:469
  93.2 8.3 %collective-permute-done.27.refs_1_ = bf16[2,128,768]{2,1,0:T(8,128)(2,1)S(1)} collective-permute-done((bf16[2,128,768]{2,1,0:T(8,128)(2,1)S(1)}, bf16[2,128,768]{2,1,0:T(8,128)(2,1)S(1)}, u32[]{:S(2)}, u32[]{:S(2)}) %collective-permute-start.27) | collective-permute-done | bytes 393248 | tf_op jit(solution)/shard_map/ppermute | solution.py:472
  103.2 1.5 %collective-permute-start.30 = (bf16[2,400,128]{2,1,0:T(8,128)(2,1)S(1)}, bf16[2,400,128]{2,1,0:T(8,128)(2,1)S(1)}, u32[]{:S(2)}, u32[]{:S(2)}) collective-permute-start(bf16[2,400,128]{2,1,0:T(8,128)(2,1)S(1)} %slice.14), channel_id=1, source_target_pairs={{0,2},{1,3},{2,0},{3,1},{4,6},{5,7},{6,4},{7,5},{8,10},{9,11},{10,... | collective-permute-start | bytes 614408 | tf_op jit(solution)/shard_map/ppermute | solution.py:469
  104.7 1.5 %shard_map.145 = (f32[768,1024]{1,0:T(8,128)}, f32[768,1024]{1,0:T(8,128)}, f32[1,1024]{1,0:T(1,128)S(1)}) custom-call(bf16[4,400,128]{2,1,0:T(8,128)(2,1)S(1)} %shard_map.144.refs_0_, bf16[4,400,128]{2,1,0:T(8,128)(2,1)S(1)} %collective-permute-done.29.refs_1_.refs_0_, bf16[4,400,128]{2,1,0:T(8,128)(2,1)S(1)} %collective-permute-done.31.refs_2_), custom_call_target="tpu_custom_call" | custom-call | bytes 7077888 | tf_op jit(solution)/shard_map/pallas_call | solution.py:437
  106.3 6.1 %collective-permute-done.28.refs_1_ = bf16[1,128,768]{2,1,0:T(8,128)(2,1)S(1)} collective-permute-done((bf16[1,128,768]{2,1,0:T(8,128)(2,1)S(1)}, bf16[1,128,768]{2,1,0:T(8,128)(2,1)S(1)}, u32[]{:S(2)}, u32[]{:S(2)}) %collective-permute-start.28) | collective-permute-done | bytes 196640 | tf_op jit(solution)/shard_map/ppermute | solution.py:472
  115.7 2.7 %shard_map.147 = (f32[768,1024]{1,0:T(8,128)}, f32[768,1024]{1,0:T(8,128)}, f32[1,1024]{1,0:T(1,128)}) custom-call(bf16[2,400,128]{2,1,0:T(8,128)(2,1)S(1)} %collective-permute-done.30.refs_0_, bf16[2,400,128]{2,1,0:T(8,128)(2,1)S(1)} %collective-permute-done.32.refs_1_, ...), custom_call_target="tpu_custom_call", output_to_operand_aliasing={{0}: (7, {}), {1}: (8, {})} | custom-call | bytes 11796480 | tf_op jit(solution)/shard_map/pallas_call | solution.py:437
  (101 shorter events, 33.0 us)
Async XLA Ops:
  0.6 13.5 %collective-permute-start.1 = (bf16[128,768]{1,0:T(8,128)(2,1)}, bf16[128,768]{1,0:T(8,128)(2,1)S(1)}, u32[]{:S(2)}, u32[]{:S(2)}) collective-permute-start(bf16[128,768]{1,0:T(8,128)(2,1)} %refs_1_.2), channel_id=1, source_target_pairs={{0,16},{4,20},{8,24},{12,28},{16,0},{20,4},{24,8},{28,12},{1,17},{... | collective-permute-start | bytes 589832 | tf_op jit(solution)/shard_map/ppermute | solution.py:472
  4.7 10.7 %collective-permute-start = (bf16[128,768]{1,0:T(8,128)(2,1)}, bf16[128,768]{1,0:T(8,128)(2,1)S(1)}, u32[]{:S(2)}, u32[]{:S(2)}) collective-permute-start(bf16[128,768]{1,0:T(8,128)(2,1)} %refs_1_.2), channel_id=1, source_target_pairs={{0,8},{4,12},{8,0},{12,4},{16,24},{20,28},{24,16},{28,20},{1,9},{5... | collective-permute-start | bytes 589832 | tf_op jit(solution)/shard_map/ppermute | solution.py:472
  6.3 12.1 %collective-permute-start.2 = (bf16[128,768]{1,0:T(8,128)(2,1)}, bf16[128,768]{1,0:T(8,128)(2,1)S(1)}, u32[]{:S(2)}, u32[]{:S(2)}) collective-permute-start(bf16[128,768]{1,0:T(8,128)(2,1)} %refs_1_.2), channel_id=1, source_target_pairs={{0,4},{4,0},{8,12},{12,8},{16,20},{20,16},{24,28},{28,24},{1,5},{5... | collective-permute-start | bytes 589832 | tf_op jit(solution)/shard_map/ppermute | solution.py:475
  12.5 9.3 %collective-permute-start.5 = (bf16[128,768]{1,0:T(8,128)(2,1)S(1)}, bf16[128,768]{1,0:T(8,128)(2,1)S(1)}, u32[]{:S(2)}, u32[]{:S(2)}) collective-permute-start(bf16[128,768]{1,0:T(8,128)(2,1)S(1)} %copy-done.6), channel_id=1, source_target_pairs={{0,0},{4,1},{9,10},{13,11},{18,20},{22,21},{27,30},{31,31}} | collective-permute-start | bytes 589832 | tf_op jit(solution)/shard_map/ppermute | solution.py:489
  26.5 8.0 %collective-permute-start.14 = (f32[8,512]{1,0:T(8,128)S(1)}, f32[8,512]{1,0:T(8,128)S(1)}, u32[]{:S(2)}, u32[]{:S(2)}) collective-permute-start(f32[8,512]{1,0:T(8,128)S(1)} %add.23.refs_2_.refs_4_), channel_id=1, source_target_pairs={{0,2},{1,3},{2,0},{3,1},{4,6},{5,7},{6,4},{7,5},{8,10},{9,11},{10,... | collective-permute-start | bytes 49160 | tf_op jit(solution)/shard_map/ppermute | solution.py:469
  28.6 11.3 %collective-permute-start.12 = (bf16[128,768]{1,0:T(8,128)(2,1)S(1)}, bf16[128,768]{1,0:T(8,128)(2,1)S(1)}, u32[]{:S(2)}, u32[]{:S(2)}) collective-permute-start(bf16[128,768]{1,0:T(8,128)(2,1)S(1)} %get-tuple-element.44), channel_id=1, source_target_pairs={{0,2},{1,3},{2,0},{3,1},{4,6},{5,7},{6,4},{7,5},{8,10},{9,11},{10,... | collective-permute-start | bytes 589832 | tf_op jit(solution)/shard_map/ppermute | solution.py:469
  29.1 10.8 %collective-permute-start.13 = (bf16[128,768]{1,0:T(8,128)(2,1)S(1)}, bf16[128,768]{1,0:T(8,128)(2,1)S(1)}, u32[]{:S(2)}, u32[]{:S(2)}) collective-permute-start(bf16[128,768]{1,0:T(8,128)(2,1)S(1)} %get-tuple-element.45), channel_id=1, source_target_pairs={{0,3},{1,2},{2,1},{3,0},{4,7},{5,6},{6,5},{7,4},{8,11},{9,10},{10,... | collective-permute-start | bytes 589832 | tf_op jit(solution)/shard_map/ppermute | solution.py:469
  41.4 11.2 %collective-permute-start.16 = (bf16[128,1408]{1,0:T(8,128)(2,1)S(1)}, bf16[128,1408]{1,0:T(8,128)(2,1)S(1)}, u32[]{:S(2)}, u32[]{:S(2)}) collective-permute-start(bf16[128,1408]{1,0:T(8,128)(2,1)S(1)} %get-tuple-element.51), channel_id=1, source_target_pairs={{0,1},{1,0},{2,3},{3,2},{4,5},{5,4},{6,7},{7,6},{8,9},{9,8},{10,11... | collective-permute-start | bytes 1081352 | tf_op jit(solution)/shard_map/ppermute | solution.py:469
  41.8 18.2 %collective-permute-start.17 = (bf16[128,1408]{1,0:T(8,128)(2,1)S(1)}, bf16[128,1408]{1,0:T(8,128)(2,1)S(1)}, u32[]{:S(2)}, u32[]{:S(2)}) collective-permute-start(bf16[128,1408]{1,0:T(8,128)(2,1)S(1)} %get-tuple-element.53), channel_id=1, source_target_pairs={{0,2},{1,3},{2,0},{3,1},{4,6},{5,7},{6,4},{7,5},{8,10},{9,11},{10,... | collective-permute-start | bytes 1081352 | tf_op jit(solution)/shard_map/ppermute | solution.py:469
  43.2 16.9 %collective-permute-start.18 = (bf16[128,1408]{1,0:T(8,128)(2,1)S(1)}, bf16[128,1408]{1,0:T(8,128)(2,1)S(1)}, u32[]{:S(2)}, u32[]{:S(2)}) collective-permute-start(bf16[128,1408]{1,0:T(8,128)(2,1)S(1)} %get-tuple-element.54), channel_id=1, source_target_pairs={{0,3},{1,2},{2,1},{3,0},{4,7},{5,6},{6,5},{7,4},{8,11},{9,10},{10,... | collective-permute-start | bytes 1081352 | tf_op jit(solution)/shard_map/ppermute | solution.py:469
  65.2 11.0 %collective-permute-start.21 = (bf16[400,128]{1,0:T(8,128)(2,1)S(1)}, bf16[400,128]{1,0:T(8,128)(2,1)S(1)}, u32[]{:S(2)}, u32[]{:S(2)}) collective-permute-start(bf16[400,128]{1,0:T(8,128)(2,1)S(1)} %get-tuple-element.62), channel_id=1, source_target_pairs={{0,16},{4,20},{8,24},{12,28},{16,0},{20,4},{24,8},{28,12},{1,17},{... | collective-permute-start | bytes 307208 | tf_op jit(solution)/shard_map/ppermute | solution.py:472
  66.2 10.1 %collective-permute-start.22 = (bf16[400,128]{1,0:T(8,128)(2,1)S(1)}, bf16[400,128]{1,0:T(8,128)(2,1)S(1)}, u32[]{:S(2)}, u32[]{:S(2)}) collective-permute-start(bf16[400,128]{1,0:T(8,128)(2,1)S(1)} %get-tuple-element.63), channel_id=1, source_target_pairs={{0,24},{4,28},{8,16},{12,20},{16,8},{20,12},{24,0},{28,4},{1,25},{... | collective-permute-start | bytes 307208 | tf_op jit(solution)/shard_map/ppermute | solution.py:472
  77.6 13.0 %collective-permute-start.23 = (bf16[4,128,768]{2,1,0:T(8,128)(2,1)S(1)}, bf16[4,128,768]{2,1,0:T(8,128)(2,1)S(1)}, u32[]{:S(2)}, u32[]{:S(2)}) collective-permute-start(bf16[4,128,768]{2,1,0:T(8,128)(2,1)S(1)} %get-tuple-element.65), channel_id=1, source_target_pairs={{0,4},{4,0},{8,12},{12,8},{16,20},{20,16},{24,28},{28,24},{1,5},{5... | collective-permute-start | bytes 2359304 | tf_op jit(solution)/shard_map/ppermute | solution.py:475
  77.7 7.6 %collective-permute-start.26 = (bf16[400,128]{1,0:T(8,128)(2,1)S(1)}, bf16[400,128]{1,0:T(8,128)(2,1)S(1)}, u32[]{:S(2)}, u32[]{:S(2)}) collective-permute-start(bf16[400,128]{1,0:T(8,128)(2,1)S(1)} %shard_map.140.refs_0_), channel_id=1, source_target_pairs={{0,24},{4,28},{8,16},{12,20},{16,8},{20,12},{24,0},{28,4},{1,25},{... | collective-permute-start | bytes 307208 | tf_op jit(solution)/shard_map/ppermute | solution.py:472
  79.5 11.0 %collective-permute-start.25 = (bf16[400,128]{1,0:T(8,128)(2,1)S(1)}, bf16[400,128]{1,0:T(8,128)(2,1)S(1)}, u32[]{:S(2)}, u32[]{:S(2)}) collective-permute-start(bf16[400,128]{1,0:T(8,128)(2,1)S(1)} %shard_map.140.refs_0_), channel_id=1, source_target_pairs={{0,16},{4,20},{8,24},{12,28},{16,0},{20,4},{24,8},{28,12},{1,17},{... | collective-permute-start | bytes 307208 | tf_op jit(solution)/shard_map/ppermute | solution.py:472
  80.7 9.8 %collective-permute-start.24 = (bf16[400,128]{1,0:T(8,128)(2,1)S(1)}, bf16[400,128]{1,0:T(8,128)(2,1)S(1)}, u32[]{:S(2)}, u32[]{:S(2)}) collective-permute-start(bf16[400,128]{1,0:T(8,128)(2,1)S(1)} %shard_map.140.refs_0_), channel_id=1, source_target_pairs={{0,8},{4,12},{8,0},{12,4},{16,24},{20,28},{24,16},{28,20},{1,9},{5... | collective-permute-start | bytes 307208 | tf_op jit(solution)/shard_map/ppermute | solution.py:472
  90.7 10.8 %collective-permute-start.27 = (bf16[2,128,768]{2,1,0:T(8,128)(2,1)S(1)}, bf16[2,128,768]{2,1,0:T(8,128)(2,1)S(1)}, u32[]{:S(2)}, u32[]{:S(2)}) collective-permute-start(bf16[2,128,768]{2,1,0:T(8,128)(2,1)S(1)} %get-tuple-element.68.refs_4_), channel_id=1, source_target_pairs={{0,8},{4,12},{8,0},{12,4},{16,24},{20,28},{24,16},{28,20},{1,9},{5... | collective-permute-start | bytes 1179656 | tf_op jit(solution)/shard_map/ppermute | solution.py:472
  90.8 12.1 %collective-permute-start.31 = (bf16[4,400,128]{2,1,0:T(8,128)(2,1)S(1)}, bf16[4,400,128]{2,1,0:T(8,128)(2,1)S(1)}, u32[]{:S(2)}, u32[]{:S(2)}) collective-permute-start(bf16[4,400,128]{2,1,0:T(8,128)(2,1)S(1)} %shard_map.144.refs_0_), channel_id=1, source_target_pairs={{0,2},{1,3},{2,0},{3,1},{4,6},{5,7},{6,4},{7,5},{8,10},{9,11},{10,... | collective-permute-start | bytes 1228808 | tf_op jit(solution)/shard_map/ppermute | solution.py:469
  91.5 11.8 %collective-permute-start.29 = (bf16[4,400,128]{2,1,0:T(8,128)(2,1)S(1)}, bf16[4,400,128]{2,1,0:T(8,128)(2,1)S(1)}, u32[]{:S(2)}, u32[]{:S(2)}) collective-permute-start(bf16[4,400,128]{2,1,0:T(8,128)(2,1)S(1)} %shard_map.144.refs_0_), channel_id=1, source_target_pairs={{0,1},{1,0},{2,3},{3,2},{4,5},{5,4},{6,7},{7,6},{8,9},{9,8},{10,11... | collective-permute-start | bytes 1228808 | tf_op jit(solution)/shard_map/ppermute | solution.py:469
  101.6 10.8 %collective-permute-start.28 = (bf16[1,128,768]{2,1,0:T(8,128)(2,1)S(1)}, bf16[1,128,768]{2,1,0:T(8,128)(2,1)S(1)}, u32[]{:S(2)}, u32[]{:S(2)}) collective-permute-start(bf16[1,128,768]{2,1,0:T(8,128)(2,1)S(1)} %get-tuple-element.70), channel_id=1, source_target_pairs={{0,16},{4,20},{8,24},{12,28},{16,0},{20,4},{24,8},{28,12},{1,17},{... | collective-permute-start | bytes 589832 | tf_op jit(solution)/shard_map/ppermute | solution.py:472
  102.9 10.8 %collective-permute-start.33 = (bf16[4,400,128]{2,1,0:T(8,128)(2,1)S(1)}, bf16[4,400,128]{2,1,0:T(8,128)(2,1)S(1)}, u32[]{:S(2)}, u32[]{:S(2)}) collective-permute-start(bf16[4,400,128]{2,1,0:T(8,128)(2,1)S(1)} %shard_map.144.refs_0_), channel_id=1, source_target_pairs={{0,4},{4,0},{8,12},{12,8},{16,20},{20,16},{24,28},{28,24},{1,5},{5... | collective-permute-start | bytes 1228808 | tf_op jit(solution)/shard_map/ppermute | solution.py:475
  102.9 9.5 %collective-permute-start.32 = (bf16[2,400,128]{2,1,0:T(8,128)(2,1)S(1)}, bf16[2,400,128]{2,1,0:T(8,128)(2,1)S(1)}, u32[]{:S(2)}, u32[]{:S(2)}) collective-permute-start(bf16[2,400,128]{2,1,0:T(8,128)(2,1)S(1)} %slice.15), channel_id=1, source_target_pairs={{0,1},{1,0},{2,3},{3,2},{4,5},{5,4},{6,7},{7,6},{8,9},{9,8},{10,11... | collective-permute-start | bytes 614408 | tf_op jit(solution)/shard_map/ppermute | solution.py:469
  103.2 9.7 %collective-permute-start.30 = (bf16[2,400,128]{2,1,0:T(8,128)(2,1)S(1)}, bf16[2,400,128]{2,1,0:T(8,128)(2,1)S(1)}, u32[]{:S(2)}, u32[]{:S(2)}) collective-permute-start(bf16[2,400,128]{2,1,0:T(8,128)(2,1)S(1)} %slice.14), channel_id=1, source_target_pairs={{0,2},{1,3},{2,0},{3,1},{4,6},{5,7},{6,4},{7,5},{8,10},{9,11},{10,... | collective-permute-start | bytes 614408 | tf_op jit(solution)/shard_map/ppermute | solution.py:469
  104.7 9.7 %collective-permute-start.35 = (bf16[4,400,128]{2,1,0:T(8,128)(2,1)S(1)}, bf16[4,400,128]{2,1,0:T(8,128)(2,1)S(1)}, u32[]{:S(2)}, u32[]{:S(2)}) collective-permute-start(bf16[4,400,128]{2,1,0:T(8,128)(2,1)S(1)} %collective-permute-done.31.refs_2_), channel_id=1, source_target_pairs={{0,4},{4,0},{8,12},{12,8},{16,20},{20,16},{24,28},{28,24},{1,5},{5... | collective-permute-start | bytes 1228808 | tf_op jit(solution)/shard_map/ppermute | solution.py:475
  (25 other events, 113.9 us)

commit v9 on v8

--- a/solution.py
+++ b/solution.py
@@ -475,7 +475,12 @@
         return lax.ppermute(x, "row", [(s, s ^ 1) for s in range(rs)])
 
     def gather_chips(x):
-        return [x] + [along_chips(x, k) for k in range(1, half)]
+        found = {0: x}
+        step = half // 2
+        while step:
+            found.update({d + step: along_chips(found[d], step) for d in list(found)})
+            step //= 2
+        return [found[d] for d in range(half)]
 
     if rs == 2 * cs:
 
@@ -581,10 +586,8 @@
         rest = [(along_col(line, cs - 1), 0, cs - 1)]
     factor = 1.0 / math.sqrt(nd * rs * cs)
     sizes = (depth, hid, xr, nc, cs, (factor, 32.0 * factor))
-    begun = assemble([piece(*x, True) for x in near], (), *sizes, ())
-    pieces = [piece(*x, True) for x in rest]
-    near = [(follow(x, [begun[2]]) if n == 1 else x, *where) for n, (x, *where) in enumerate(near)]
-    pieces += [piece(other_core(x), *where, False) for x, *where in near + rest]
+    begun = assemble([piece(*x, True) for x in near + rest], (), *sizes, ())
+    pieces = [piece(other_core(x), *where, False) for x, *where in near + rest]
     total_self, total_neigh, total_bias = assemble(pieces, begun, *sizes, [grad_input])
     return output, grad_input, total_self, total_neigh, total_bias.reshape(-1)
 

time: 119 us -> 116 us (0.975)
  starting transfers between devices: 39.5 us -> 37.3 us
    ppermute x11, starting transfers between devices: 17.1 us -> 14.3 us  [along_chips(): return lax.ppermute(x, 'row', [(s, s ^ 2 * k) for s in range(rs)])]
    ppermute x11, waiting for transfers between devices: 33.5 us -> 34.8 us  [along_chips(): return lax.ppermute(x, 'row', [(s, s ^ 2 * k) for s in range(rs)])]
    pallas_call x18 -> x17, Pallas kernels: 12.2 us -> 12.3 us  [call(): pl.pallas_call(run, out_shape=outs, in_specs=[SMEM] * smem + [VMEM] * (co...]
  transfers between devices with their start and end apart: 38 -> 38, of which waited for: 14 -> 13; matrix products, arithmetic and copies ran while one was open for 0% -> 1% of each run, Pallas kernels for 8% -> 9%
where the time goes in v9:
time: 116 us
  waiting for transfers between devices  56.2 us (48%)
  starting transfers between devices  37.3 us (32%)
  Pallas kernels  16.5 us (14%)
  local copies, waits for them, and re-layouts  3.76 us (3%)
  between operations  1.63 us (1%)
    ppermute x11, waiting for transfers between devices, along_chips(): return lax.ppermute(x, 'row', [(s, s ^ 2 * k) for s in range(rs)])  34.8 us
    ppermute x12, waiting for transfers between devices, along_col(): return lax.ppermute(x, 'col', [(s, s ^ k) for s in range(cs)])  19.6 us
    ppermute x11, starting transfers between devices, along_chips(): return lax.ppermute(x, 'row', [(s, s ^ 2 * k) for s in range(rs)])  14.3 us
    ppermute x12, starting transfers between devices, along_col(): return lax.ppermute(x, 'col', [(s, s ^ k) for s in range(cs)])  13.3 us
    pallas_call x17, Pallas kernels, call(): pl.pallas_call(run, out_shape=outs, in_specs=[SMEM] * smem + [VMEM] * (co...  12.3 us
    ppermute x4, starting transfers between devices, send_own(): return lax.ppermute(block, ('row', 'col'), pairs)  7.28 us
    pallas_call x2, Pallas kernels, assemble(): pl.pallas_call(run, out_shape=[weight, weight, shape((1, hid), F32)], in_...  4.22 us
    unnamed x22, local copies, waits for them, and re-layouts  3.61 us
  transfers between devices with their start and end apart: 38, of which 13 were waited for; matrix products, arithmetic and copies ran while one was open for 1% of the time, Pallas kernels for 9%

profile of v9, /device:TPU:0, one launch (start us, length us, event | category | flops | bytes accessed | tf_op | source)
XLA Modules:
  0.0 115.8 jit_solution(11859864808034670232)
XLA Ops:
  0.6 4.1 %collective-permute-start.1 = (bf16[128,768]{1,0:T(8,128)(2,1)}, bf16[128,768]{1,0:T(8,128)(2,1)S(1)}, u32[]{:S(2)}, u32[]{:S(2)}) collective-permute-start(bf16[128,768]{1,0:T(8,128)(2,1)} %refs_1_.2), channel_id=1, source_target_pairs={{0,16},{4,20},{8,24},{12,28},{16,0},{20,4},{24,8},{28,12},{1,17},{... | collective-permute-start | bytes 589832 | tf_op jit(solution)/shard_map/ppermute | solution.py:472
  4.7 1.6 %collective-permute-start = (bf16[128,768]{1,0:T(8,128)(2,1)}, bf16[128,768]{1,0:T(8,128)(2,1)S(1)}, u32[]{:S(2)}, u32[]{:S(2)}) collective-permute-start(bf16[128,768]{1,0:T(8,128)(2,1)} %refs_1_.2), channel_id=1, source_target_pairs={{0,8},{4,12},{8,0},{12,4},{16,24},{20,28},{24,16},{28,20},{1,9},{5... | collective-permute-start | bytes 589832 | tf_op jit(solution)/shard_map/ppermute | solution.py:472
  15.5 2.9 %collective-permute-start.6 = (bf16[128,768]{1,0:T(8,128)(2,1)S(1)}, bf16[128,768]{1,0:T(8,128)(2,1)S(1)}, u32[]{:S(2)}, u32[]{:S(2)}) collective-permute-start(bf16[128,768]{1,0:T(8,128)(2,1)S(1)} %collective-permute-done.refs_2_), channel_id=1, source_target_pairs={{0,2},{4,3},{9,8},{13,9},{18,22},{22,23},{27,28},{31,29}} | collective-permute-start | bytes 589832 | tf_op jit(solution)/shard_map/ppermute | solution.py:494
  19.5 2.1 %collective-permute-done.7.refs_2_ = bf16[128,768]{1,0:T(8,128)(2,1)S(1)} collective-permute-done((bf16[128,768]{1,0:T(8,128)(2,1)S(1)}, bf16[128,768]{1,0:T(8,128)(2,1)S(1)}, u32[]{:S(2)}, u32[]{:S(2)}) %collective-permute-start.7) | collective-permute-done | bytes 196640 | tf_op jit(solution)/shard_map/ppermute | solution.py:472
  22.6 2.4 %collective-permute-start.10 = (bf16[128,768]{1,0:T(8,128)(2,1)S(1)}, bf16[128,768]{1,0:T(8,128)(2,1)S(1)}, u32[]{:S(2)}, u32[]{:S(2)}) collective-permute-start(bf16[128,768]{1,0:T(8,128)(2,1)S(1)} %shard_map.131), channel_id=1, source_target_pairs={{0,4},{4,5},{9,14},{13,15},{18,16},{22,17},{27,26},{31,27}} | collective-permute-start | bytes 589832 | tf_op jit(solution)/shard_map/ppermute | solution.py:494
  26.9 1.9 %collective-permute-start.11 = (bf16[128,768]{1,0:T(8,128)(2,1)S(1)}, bf16[128,768]{1,0:T(8,128)(2,1)S(1)}, u32[]{:S(2)}, u32[]{:S(2)}) collective-permute-start(bf16[128,768]{1,0:T(8,128)(2,1)S(1)} %get-tuple-element.43), channel_id=1, source_target_pairs={{0,1},{1,0},{2,3},{3,2},{4,5},{5,4},{6,7},{7,6},{8,9},{9,8},{10,11... | collective-permute-start | bytes 589832 | tf_op jit(solution)/shard_map/ppermute | solution.py:469
  30.9 2.3 %shard_map.133 = (bf16[1024,768]{1,0:T(8,128)(2,1)S(1)}, bf16[1024,768]{1,0:T(8,128)(2,1)S(1)}) custom-call(bf16[768,1024]{1,0:T(8,128)(2,1)S(1)} %copy-done.2, bf16[768,1024]{1,0:T(8,128)(2,1)} %refs_1_.3, f32[128,768]{1,0:T(8,128)S(1)} %get-tuple-element.42.refs_2_.refs_0_), custom_call_target="tpu_custom_call" | custom-call | bytes 6291456 | tf_op jit(solution)/shard_map/pallas_call | solution.py:27
  35.9 4.1 %collective-permute-done.13.refs_3_ = bf16[128,768]{1,0:T(8,128)(2,1)S(1)} collective-permute-done((bf16[128,768]{1,0:T(8,128)(2,1)S(1)}, bf16[128,768]{1,0:T(8,128)(2,1)S(1)}, u32[]{:S(2)}, u32[]{:S(2)}) %collective-permute-start.13) | collective-permute-done | bytes 196640 | tf_op jit(solution)/shard_map/ppermute | solution.py:469
  41.6 1.8 %collective-permute-start.17 = (bf16[128,1408]{1,0:T(8,128)(2,1)S(1)}, bf16[128,1408]{1,0:T(8,128)(2,1)S(1)}, u32[]{:S(2)}, u32[]{:S(2)}) collective-permute-start(bf16[128,1408]{1,0:T(8,128)(2,1)S(1)} %get-tuple-element.53), channel_id=1, source_target_pairs={{0,2},{1,3},{2,0},{3,1},{4,6},{5,7},{6,4},{7,5},{8,10},{9,11},{10,... | collective-permute-start | bytes 1081352 | tf_op jit(solution)/shard_map/ppermute | solution.py:469
  44.8 7.8 %collective-permute-done.16.refs_4_.refs_1_ = bf16[128,1408]{1,0:T(8,128)(2,1)S(1)} collective-permute-done((bf16[128,1408]{1,0:T(8,128)(2,1)S(1)}, bf16[128,1408]{1,0:T(8,128)(2,1)S(1)}, u32[]{:S(2)}, u32[]{:S(2)}) %collective-permute-start.16) | collective-permute-done | bytes 360480 | tf_op jit(solution)/shard_map/ppermute | solution.py:469
  53.9 6.1 %collective-permute-done.17.refs_2_.refs_3_ = bf16[128,1408]{1,0:T(8,128)(2,1)S(1)} collective-permute-done((bf16[128,1408]{1,0:T(8,128)(2,1)S(1)}, bf16[128,1408]{1,0:T(8,128)(2,1)S(1)}, u32[]{:S(2)}, u32[]{:S(2)}) %collective-permute-start.17) | collective-permute-done | bytes 360480 | tf_op jit(solution)/shard_map/ppermute | solution.py:469
  60.9 1.7 %collective-permute-done.19.refs_1_ = bf16[4,400,128]{2,1,0:T(8,128)(2,1)S(1)} collective-permute-done((bf16[4,400,128]{2,1,0:T(8,128)(2,1)S(1)}, bf16[4,400,128]{2,1,0:T(8,128)(2,1)S(1)}, u32[]{:S(2)}, u32[]{:S(2)}) %collective-permute-start.19) | collective-permute-done | bytes 409632 | tf_op jit(solution)/shard_map/ppermute | solution.py:475
  62.7 2.5 %collective-permute-start.20 = (bf16[400,128]{1,0:T(8,128)(2,1)S(1)}, bf16[400,128]{1,0:T(8,128)(2,1)S(1)}, u32[]{:S(2)}, u32[]{:S(2)}) collective-permute-start(bf16[400,128]{1,0:T(8,128)(2,1)S(1)} %get-tuple-element.61), channel_id=1, source_target_pairs={{0,8},{4,12},{8,0},{12,4},{16,24},{20,28},{24,16},{28,20},{1,9},{5... | collective-permute-start | bytes 307208 | tf_op jit(solution)/shard_map/ppermute | solution.py:472
  66.2 1.5 %collective-permute-start.22 = (bf16[400,128]{1,0:T(8,128)(2,1)S(1)}, bf16[400,128]{1,0:T(8,128)(2,1)S(1)}, u32[]{:S(2)}, u32[]{:S(2)}) collective-permute-start(bf16[400,128]{1,0:T(8,128)(2,1)S(1)} %get-tuple-element.63), channel_id=1, source_target_pairs={{0,24},{4,28},{8,16},{12,20},{16,8},{20,12},{24,0},{28,4},{1,25},{... | collective-permute-start | bytes 307208 | tf_op jit(solution)/shard_map/ppermute | solution.py:472
  68.8 7.4 %collective-permute-done.21.refs_6_.refs_2_ = bf16[400,128]{1,0:T(8,128)(2,1)S(1)} collective-permute-done((bf16[400,128]{1,0:T(8,128)(2,1)S(1)}, bf16[400,128]{1,0:T(8,128)(2,1)S(1)}, u32[]{:S(2)}, u32[]{:S(2)}) %collective-permute-start.21) | collective-permute-done | bytes 102432 | tf_op jit(solution)/shard_map/ppermute | solution.py:472
  77.7 2.4 %collective-permute-start.25 = (bf16[400,128]{1,0:T(8,128)(2,1)S(1)}, bf16[400,128]{1,0:T(8,128)(2,1)S(1)}, u32[]{:S(2)}, u32[]{:S(2)}) collective-permute-start(bf16[400,128]{1,0:T(8,128)(2,1)S(1)} %shard_map.140.refs_0_), channel_id=1, source_target_pairs={{0,16},{4,20},{8,24},{12,28},{16,0},{20,4},{24,8},{28,12},{1,17},{... | collective-permute-start | bytes 307208 | tf_op jit(solution)/shard_map/ppermute | solution.py:472
  80.1 6.1 %collective-permute-done.25.refs_3_.refs_2_ = bf16[400,128]{1,0:T(8,128)(2,1)S(1)} collective-permute-done((bf16[400,128]{1,0:T(8,128)(2,1)S(1)}, bf16[400,128]{1,0:T(8,128)(2,1)S(1)}, u32[]{:S(2)}, u32[]{:S(2)}) %collective-permute-start.25) | collective-permute-done | bytes 102432 | tf_op jit(solution)/shard_map/ppermute | solution.py:472
  86.3 4.6 %collective-permute-done.26.refs_4_.refs_3_ = bf16[400,128]{1,0:T(8,128)(2,1)S(1)} collective-permute-done((bf16[400,128]{1,0:T(8,128)(2,1)S(1)}, bf16[400,128]{1,0:T(8,128)(2,1)S(1)}, u32[]{:S(2)}, u32[]{:S(2)}) %collective-permute-start.26) | collective-permute-done | bytes 102432 | tf_op jit(solution)/shard_map/ppermute | solution.py:472
  91.5 1.7 %collective-permute-start.30 = (bf16[4,400,128]{2,1,0:T(8,128)(2,1)S(1)}, bf16[4,400,128]{2,1,0:T(8,128)(2,1)S(1)}, u32[]{:S(2)}, u32[]{:S(2)}) collective-permute-start(bf16[4,400,128]{2,1,0:T(8,128)(2,1)S(1)} %shard_map.144.refs_0_), channel_id=1, source_target_pairs={{0,1},{1,0},{2,3},{3,2},{4,5},{5,4},{6,7},{7,6},{8,9},{9,8},{10,11... | collective-permute-start | bytes 1228808 | tf_op jit(solution)/shard_map/ppermute | solution.py:469
  93.2 7.4 %collective-permute-done.27.refs_1_ = bf16[2,128,768]{2,1,0:T(8,128)(2,1)S(1)} collective-permute-done((bf16[2,128,768]{2,1,0:T(8,128)(2,1)S(1)}, bf16[2,128,768]{2,1,0:T(8,128)(2,1)S(1)}, u32[]{:S(2)}, u32[]{:S(2)}) %collective-permute-start.27) | collective-permute-done | bytes 393248 | tf_op jit(solution)/shard_map/ppermute | solution.py:472
  101.9 2.2 %collective-permute-start.34 = (bf16[2,400,128]{2,1,0:T(8,128)(2,1)S(1)}, bf16[2,400,128]{2,1,0:T(8,128)(2,1)S(1)}, u32[]{:S(2)}, u32[]{:S(2)}) collective-permute-start(bf16[2,400,128]{2,1,0:T(8,128)(2,1)S(1)} %slice.14), channel_id=1, source_target_pairs={{0,2},{1,3},{2,0},{3,1},{4,6},{5,7},{6,4},{7,5},{8,10},{9,11},{10,... | collective-permute-start | bytes 614408 | tf_op jit(solution)/shard_map/ppermute | solution.py:469
  104.1 6.1 %collective-permute-done.28.refs_1_ = bf16[1,128,768]{2,1,0:T(8,128)(2,1)S(1)} collective-permute-done((bf16[1,128,768]{2,1,0:T(8,128)(2,1)S(1)}, bf16[1,128,768]{2,1,0:T(8,128)(2,1)S(1)}, u32[]{:S(2)}, u32[]{:S(2)}) %collective-permute-start.28) | collective-permute-done | bytes 196640 | tf_op jit(solution)/shard_map/ppermute | solution.py:472
  111.5 1.8 %shard_map.145 = (f32[768,1024]{1,0:T(8,128)}, f32[768,1024]{1,0:T(8,128)}, f32[1,1024]{1,0:T(1,128)S(1)}) custom-call(bf16[4,400,128]{2,1,0:T(8,128)(2,1)S(1)} %shard_map.144.refs_0_, bf16[4,400,128]{2,1,0:T(8,128)(2,1)S(1)} %collective-permute-done.30.refs_1_, bf16[4,400,128]{2,1,0:T(8,128)(2,1)S(1)} %collective-permute-done.32.refs_2_, ...), custom_call_target="tpu_custom_call" | custom-call | bytes 9437184 | tf_op jit(solution)/shard_map/pallas_call | solution.py:437
  113.4 2.4 %shard_map.146 = (f32[768,1024]{1,0:T(8,128)}, f32[768,1024]{1,0:T(8,128)}, f32[1,1024]{1,0:T(1,128)}) custom-call(bf16[4,400,128]{2,1,0:T(8,128)(2,1)S(1)} %collective-permute-done.29.refs_0_, bf16[4,400,128]{2,1,0:T(8,128)(2,1)S(1)} %collective-permute-done.31.refs_1_, ...), custom_call_target="tpu_custom_call", output_to_operand_aliasing={{0}: (5, {}), {1}: (6, {})} | custom-call | bytes 9437184 | tf_op jit(solution)/shard_map/pallas_call | solution.py:437
  (100 shorter events, 29.2 us)
Async XLA Ops:
  0.6 13.5 %collective-permute-start.1 = (bf16[128,768]{1,0:T(8,128)(2,1)}, bf16[128,768]{1,0:T(8,128)(2,1)S(1)}, u32[]{:S(2)}, u32[]{:S(2)}) collective-permute-start(bf16[128,768]{1,0:T(8,128)(2,1)} %refs_1_.2), channel_id=1, source_target_pairs={{0,16},{4,20},{8,24},{12,28},{16,0},{20,4},{24,8},{28,12},{1,17},{... | collective-permute-start | bytes 589832 | tf_op jit(solution)/shard_map/ppermute | solution.py:472
  4.7 10.8 %collective-permute-start = (bf16[128,768]{1,0:T(8,128)(2,1)}, bf16[128,768]{1,0:T(8,128)(2,1)S(1)}, u32[]{:S(2)}, u32[]{:S(2)}) collective-permute-start(bf16[128,768]{1,0:T(8,128)(2,1)} %refs_1_.2), channel_id=1, source_target_pairs={{0,8},{4,12},{8,0},{12,4},{16,24},{20,28},{24,16},{28,20},{1,9},{5... | collective-permute-start | bytes 589832 | tf_op jit(solution)/shard_map/ppermute | solution.py:472
  6.3 12.1 %collective-permute-start.2 = (bf16[128,768]{1,0:T(8,128)(2,1)}, bf16[128,768]{1,0:T(8,128)(2,1)S(1)}, u32[]{:S(2)}, u32[]{:S(2)}) collective-permute-start(bf16[128,768]{1,0:T(8,128)(2,1)} %refs_1_.2), channel_id=1, source_target_pairs={{0,4},{4,0},{8,12},{12,8},{16,20},{20,16},{24,28},{28,24},{1,5},{5... | collective-permute-start | bytes 589832 | tf_op jit(solution)/shard_map/ppermute | solution.py:475
  12.5 9.2 %collective-permute-start.5 = (bf16[128,768]{1,0:T(8,128)(2,1)S(1)}, bf16[128,768]{1,0:T(8,128)(2,1)S(1)}, u32[]{:S(2)}, u32[]{:S(2)}) collective-permute-start(bf16[128,768]{1,0:T(8,128)(2,1)S(1)} %copy-done.6), channel_id=1, source_target_pairs={{0,0},{4,1},{9,10},{13,11},{18,20},{22,21},{27,30},{31,31}} | collective-permute-start | bytes 589832 | tf_op jit(solution)/shard_map/ppermute | solution.py:494
  14.2 7.5 %collective-permute-start.7 = (bf16[128,768]{1,0:T(8,128)(2,1)S(1)}, bf16[128,768]{1,0:T(8,128)(2,1)S(1)}, u32[]{:S(2)}, u32[]{:S(2)}) collective-permute-start(bf16[128,768]{1,0:T(8,128)(2,1)S(1)} %collective-permute-done.1.refs_3_.refs_0_), channel_id=1, source_target_pairs={{0,8},{4,12},{8,0},{12,4},{16,24},{20,28},{24,16},{28,20},{1,9},{5... | collective-permute-start | bytes 589832 | tf_op jit(solution)/shard_map/ppermute | solution.py:472
  26.4 8.0 %collective-permute-start.14 = (f32[8,512]{1,0:T(8,128)S(1)}, f32[8,512]{1,0:T(8,128)S(1)}, u32[]{:S(2)}, u32[]{:S(2)}) collective-permute-start(f32[8,512]{1,0:T(8,128)S(1)} %add.23.refs_2_.refs_4_), channel_id=1, source_target_pairs={{0,2},{1,3},{2,0},{3,1},{4,6},{5,7},{6,4},{7,5},{8,10},{9,11},{10,... | collective-permute-start | bytes 49160 | tf_op jit(solution)/shard_map/ppermute | solution.py:469
  26.9 7.5 %collective-permute-start.11 = (bf16[128,768]{1,0:T(8,128)(2,1)S(1)}, bf16[128,768]{1,0:T(8,128)(2,1)S(1)}, u32[]{:S(2)}, u32[]{:S(2)}) collective-permute-start(bf16[128,768]{1,0:T(8,128)(2,1)S(1)} %get-tuple-element.43), channel_id=1, source_target_pairs={{0,1},{1,0},{2,3},{3,2},{4,5},{5,4},{6,7},{7,6},{8,9},{9,8},{10,11... | collective-permute-start | bytes 589832 | tf_op jit(solution)/shard_map/ppermute | solution.py:469
  28.7 7.1 %collective-permute-start.12 = (bf16[128,768]{1,0:T(8,128)(2,1)S(1)}, bf16[128,768]{1,0:T(8,128)(2,1)S(1)}, u32[]{:S(2)}, u32[]{:S(2)}) collective-permute-start(bf16[128,768]{1,0:T(8,128)(2,1)S(1)} %get-tuple-element.44), channel_id=1, source_target_pairs={{0,2},{1,3},{2,0},{3,1},{4,6},{5,7},{6,4},{7,5},{8,10},{9,11},{10,... | collective-permute-start | bytes 589832 | tf_op jit(solution)/shard_map/ppermute | solution.py:469
  29.0 10.9 %collective-permute-start.13 = (bf16[128,768]{1,0:T(8,128)(2,1)S(1)}, bf16[128,768]{1,0:T(8,128)(2,1)S(1)}, u32[]{:S(2)}, u32[]{:S(2)}) collective-permute-start(bf16[128,768]{1,0:T(8,128)(2,1)S(1)} %get-tuple-element.45), channel_id=1, source_target_pairs={{0,3},{1,2},{2,1},{3,0},{4,7},{5,6},{6,5},{7,4},{8,11},{9,10},{10,... | collective-permute-start | bytes 589832 | tf_op jit(solution)/shard_map/ppermute | solution.py:469
  41.3 11.3 %collective-permute-start.16 = (bf16[128,1408]{1,0:T(8,128)(2,1)S(1)}, bf16[128,1408]{1,0:T(8,128)(2,1)S(1)}, u32[]{:S(2)}, u32[]{:S(2)}) collective-permute-start(bf16[128,1408]{1,0:T(8,128)(2,1)S(1)} %get-tuple-element.51), channel_id=1, source_target_pairs={{0,1},{1,0},{2,3},{3,2},{4,5},{5,4},{6,7},{7,6},{8,9},{9,8},{10,11... | collective-permute-start | bytes 1081352 | tf_op jit(solution)/shard_map/ppermute | solution.py:469
  41.6 18.4 %collective-permute-start.17 = (bf16[128,1408]{1,0:T(8,128)(2,1)S(1)}, bf16[128,1408]{1,0:T(8,128)(2,1)S(1)}, u32[]{:S(2)}, u32[]{:S(2)}) collective-permute-start(bf16[128,1408]{1,0:T(8,128)(2,1)S(1)} %get-tuple-element.53), channel_id=1, source_target_pairs={{0,2},{1,3},{2,0},{3,1},{4,6},{5,7},{6,4},{7,5},{8,10},{9,11},{10,... | collective-permute-start | bytes 1081352 | tf_op jit(solution)/shard_map/ppermute | solution.py:469
  43.4 16.6 %collective-permute-start.18 = (bf16[128,1408]{1,0:T(8,128)(2,1)S(1)}, bf16[128,1408]{1,0:T(8,128)(2,1)S(1)}, u32[]{:S(2)}, u32[]{:S(2)}) collective-permute-start(bf16[128,1408]{1,0:T(8,128)(2,1)S(1)} %get-tuple-element.54), channel_id=1, source_target_pairs={{0,3},{1,2},{2,1},{3,0},{4,7},{5,6},{6,5},{7,4},{8,11},{9,10},{10,... | collective-permute-start | bytes 1081352 | tf_op jit(solution)/shard_map/ppermute | solution.py:469
  65.2 11.0 %collective-permute-start.21 = (bf16[400,128]{1,0:T(8,128)(2,1)S(1)}, bf16[400,128]{1,0:T(8,128)(2,1)S(1)}, u32[]{:S(2)}, u32[]{:S(2)}) collective-permute-start(bf16[400,128]{1,0:T(8,128)(2,1)S(1)} %get-tuple-element.62), channel_id=1, source_target_pairs={{0,16},{4,20},{8,24},{12,28},{16,0},{20,4},{24,8},{28,12},{1,17},{... | collective-permute-start | bytes 307208 | tf_op jit(solution)/shard_map/ppermute | solution.py:472
  66.2 10.1 %collective-permute-start.22 = (bf16[400,128]{1,0:T(8,128)(2,1)S(1)}, bf16[400,128]{1,0:T(8,128)(2,1)S(1)}, u32[]{:S(2)}, u32[]{:S(2)}) collective-permute-start(bf16[400,128]{1,0:T(8,128)(2,1)S(1)} %get-tuple-element.63), channel_id=1, source_target_pairs={{0,24},{4,28},{8,16},{12,20},{16,8},{20,12},{24,0},{28,4},{1,25},{... | collective-permute-start | bytes 307208 | tf_op jit(solution)/shard_map/ppermute | solution.py:472
  77.6 13.4 %collective-permute-start.23 = (bf16[4,128,768]{2,1,0:T(8,128)(2,1)S(1)}, bf16[4,128,768]{2,1,0:T(8,128)(2,1)S(1)}, u32[]{:S(2)}, u32[]{:S(2)}) collective-permute-start(bf16[4,128,768]{2,1,0:T(8,128)(2,1)S(1)} %get-tuple-element.65), channel_id=1, source_target_pairs={{0,4},{4,0},{8,12},{12,8},{16,20},{20,16},{24,28},{28,24},{1,5},{5... | collective-permute-start | bytes 2359304 | tf_op jit(solution)/shard_map/ppermute | solution.py:475
  77.7 8.5 %collective-permute-start.25 = (bf16[400,128]{1,0:T(8,128)(2,1)S(1)}, bf16[400,128]{1,0:T(8,128)(2,1)S(1)}, u32[]{:S(2)}, u32[]{:S(2)}) collective-permute-start(bf16[400,128]{1,0:T(8,128)(2,1)S(1)} %shard_map.140.refs_0_), channel_id=1, source_target_pairs={{0,16},{4,20},{8,24},{12,28},{16,0},{20,4},{24,8},{28,12},{1,17},{... | collective-permute-start | bytes 307208 | tf_op jit(solution)/shard_map/ppermute | solution.py:472
  91.1 9.5 %collective-permute-start.27 = (bf16[2,128,768]{2,1,0:T(8,128)(2,1)S(1)}, bf16[2,128,768]{2,1,0:T(8,128)(2,1)S(1)}, u32[]{:S(2)}, u32[]{:S(2)}) collective-permute-start(bf16[2,128,768]{2,1,0:T(8,128)(2,1)S(1)} %get-tuple-element.68.refs_4_), channel_id=1, source_target_pairs={{0,8},{4,12},{8,0},{12,4},{16,24},{20,28},{24,16},{28,20},{1,9},{5... | collective-permute-start | bytes 1179656 | tf_op jit(solution)/shard_map/ppermute | solution.py:472
  91.2 10.0 %collective-permute-start.32 = (bf16[4,400,128]{2,1,0:T(8,128)(2,1)S(1)}, bf16[4,400,128]{2,1,0:T(8,128)(2,1)S(1)}, u32[]{:S(2)}, u32[]{:S(2)}) collective-permute-start(bf16[4,400,128]{2,1,0:T(8,128)(2,1)S(1)} %shard_map.144.refs_0_), channel_id=1, source_target_pairs={{0,2},{1,3},{2,0},{3,1},{4,6},{5,7},{6,4},{7,5},{8,10},{9,11},{10,... | collective-permute-start | bytes 1228808 | tf_op jit(solution)/shard_map/ppermute | solution.py:469
  91.5 10.4 %collective-permute-start.30 = (bf16[4,400,128]{2,1,0:T(8,128)(2,1)S(1)}, bf16[4,400,128]{2,1,0:T(8,128)(2,1)S(1)}, u32[]{:S(2)}, u32[]{:S(2)}) collective-permute-start(bf16[4,400,128]{2,1,0:T(8,128)(2,1)S(1)} %shard_map.144.refs_0_), channel_id=1, source_target_pairs={{0,1},{1,0},{2,3},{3,2},{4,5},{5,4},{6,7},{7,6},{8,9},{9,8},{10,11... | collective-permute-start | bytes 1228808 | tf_op jit(solution)/shard_map/ppermute | solution.py:469
  100.7 9.5 %collective-permute-start.28 = (bf16[1,128,768]{2,1,0:T(8,128)(2,1)S(1)}, bf16[1,128,768]{2,1,0:T(8,128)(2,1)S(1)}, u32[]{:S(2)}, u32[]{:S(2)}) collective-permute-start(bf16[1,128,768]{2,1,0:T(8,128)(2,1)S(1)} %get-tuple-element.70), channel_id=1, source_target_pairs={{0,16},{4,20},{8,24},{12,28},{16,0},{20,4},{24,8},{28,12},{1,17},{... | collective-permute-start | bytes 589832 | tf_op jit(solution)/shard_map/ppermute | solution.py:472
  101.2 12.1 %collective-permute-start.29 = (bf16[4,400,128]{2,1,0:T(8,128)(2,1)S(1)}, bf16[4,400,128]{2,1,0:T(8,128)(2,1)S(1)}, u32[]{:S(2)}, u32[]{:S(2)}) collective-permute-start(bf16[4,400,128]{2,1,0:T(8,128)(2,1)S(1)} %shard_map.144.refs_0_), channel_id=1, source_target_pairs={{0,4},{4,0},{8,12},{12,8},{16,20},{20,16},{24,28},{28,24},{1,5},{5... | collective-permute-start | bytes 1228808 | tf_op jit(solution)/shard_map/ppermute | solution.py:475
  101.2 9.0 %collective-permute-start.36 = (bf16[2,400,128]{2,1,0:T(8,128)(2,1)S(1)}, bf16[2,400,128]{2,1,0:T(8,128)(2,1)S(1)}, u32[]{:S(2)}, u32[]{:S(2)}) collective-permute-start(bf16[2,400,128]{2,1,0:T(8,128)(2,1)S(1)} %slice.15), channel_id=1, source_target_pairs={{0,1},{1,0},{2,3},{3,2},{4,5},{5,4},{6,7},{7,6},{8,9},{9,8},{10,11... | collective-permute-start | bytes 614408 | tf_op jit(solution)/shard_map/ppermute | solution.py:469
  101.9 8.8 %collective-permute-start.34 = (bf16[2,400,128]{2,1,0:T(8,128)(2,1)S(1)}, bf16[2,400,128]{2,1,0:T(8,128)(2,1)S(1)}, u32[]{:S(2)}, u32[]{:S(2)}) collective-permute-start(bf16[2,400,128]{2,1,0:T(8,128)(2,1)S(1)} %slice.14), channel_id=1, source_target_pairs={{0,2},{1,3},{2,0},{3,1},{4,6},{5,7},{6,4},{7,5},{8,10},{9,11},{10,... | collective-permute-start | bytes 614408 | tf_op jit(solution)/shard_map/ppermute | solution.py:469
  104.1 9.2 %collective-permute-start.33 = (bf16[4,400,128]{2,1,0:T(8,128)(2,1)S(1)}, bf16[4,400,128]{2,1,0:T(8,128)(2,1)S(1)}, u32[]{:S(2)}, u32[]{:S(2)}) collective-permute-start(bf16[4,400,128]{2,1,0:T(8,128)(2,1)S(1)} %collective-permute-done.32.refs_2_), channel_id=1, source_target_pairs={{0,4},{4,0},{8,12},{12,8},{16,20},{20,16},{24,28},{28,24},{1,5},{5... | collective-permute-start | bytes 1228808 | tf_op jit(solution)/shard_map/ppermute | solution.py:475
  (25 other events, 113.1 us)

commit v10 on v9

--- a/solution.py
+++ b/solution.py
@@ -13,13 +13,18 @@
 EXTRA = 16
 VMEM = pl.BlockSpec(memory_space=pltpu.VMEM)
 SMEM = pl.BlockSpec(memory_space=pltpu.SMEM)
-PARAMS = pltpu.CompilerParams(vmem_limit_bytes=48 * 1024 * 1024)
+MIB = 1024 * 1024
+
+
+def limits(arrays, scratch=0):
+    held = sum(math.prod(a.shape) * a.dtype.itemsize for a in arrays) + scratch
+    return pltpu.CompilerParams(vmem_limit_bytes=min(56 * MIB, 2 * held + 12 * MIB))
 
 
 def call(body, outs, args, scratch=(), smem=0, flops=0, after=()):
     count = len(args)
-    moved = sum(math.prod(o.shape) * o.dtype.itemsize for o in outs)
-    moved += sum(a.size * a.dtype.itemsize for a in args)
+    moved = sum(math.prod(a.shape) * a.dtype.itemsize for a in (*outs, *args))
+    held = sum(math.prod(x.shape) * x.dtype.itemsize for x in scratch)
 
     def run(*refs):
         body(*refs[:count], *refs[count + len(after) :])
@@ -32,7 +37,7 @@
         + [pl.BlockSpec(memory_space=pl.ANY)] * len(after),
         out_specs=[VMEM] * len(outs),
         scratch_shapes=list(scratch),
-        compiler_params=PARAMS,
+        compiler_params=limits([*outs, *args], held),
         cost_estimate=pl.CostEstimate(flops=flops, bytes_accessed=moved, transcendentals=0),
     )(*args, *after)
 
@@ -446,7 +451,7 @@
             pltpu.SemaphoreType.DMA((copies,)),
         ],
         input_output_aliases={len(arrays): 0, len(arrays) + 1: 1} if begun else {},
-        compiler_params=PARAMS,
+        compiler_params=limits(arrays, copies * xr * LANES * 4),
         cost_estimate=pl.CostEstimate(flops=0, bytes_accessed=moved, transcendentals=0),
     )(*inputs, *after)
 
@@ -563,8 +568,8 @@
     chunks = [chunks[0]] + [along_chips(chunks[k], k) for k in range(1, half)]
     line = gather_chips(last_sum(chunks))
 
-    keep, send = back_parts(turned, scaled, self_parts, nd, cs, rs, chunks[1:])
-    keep, send = fold(keep, other_core(send), line[1:])
+    keep, send = back_parts(turned, scaled, self_parts, nd, cs, rs, [keep])
+    keep, send = fold(keep, other_core(follow(send, chunks[1:])), line[1:])
     line = stack(line, after=[send])
     step = 1
     while step < half:

time: 116 us -> 115 us (level)
  Pallas kernels: 16.5 us -> 15.2 us
    ppermute x12, waiting for transfers between devices: 19.6 us -> 22.4 us  [along_col(): return lax.ppermute(x, 'col', [(s, s ^ k) for s in range(cs)])]
    ppermute x11, waiting for transfers between devices: 34.8 us -> 32.8 us  [along_chips(): return lax.ppermute(x, 'row', [(s, s ^ 2 * k) for s in range(rs)])]
    pallas_call x17 -> x18, Pallas kernels: 12.3 us -> 11 us  [call(): pl.pallas_call(run, out_shape=outs, in_specs=[SMEM] * smem + [VMEM] * (co...]
    unnamed x22 -> x18, local copies, waits for them, and re-layouts: 3.61 us -> 2.47 us
where the time goes in v10:
time: 115 us
  waiting for transfers between devices  56.9 us (49%)
  starting transfers between devices  37.8 us (33%)
  Pallas kernels  15.2 us (13%)
  local copies, waits for them, and re-layouts  2.62 us (2%)
  between operations  1.65 us (1%)
    ppermute x11, waiting for transfers between devices, along_chips(): return lax.ppermute(x, 'row', [(s, s ^ 2 * k) for s in range(rs)])  32.8 us
    ppermute x12, waiting for transfers between devices, along_col(): return lax.ppermute(x, 'col', [(s, s ^ k) for s in range(cs)])  22.4 us
    ppermute x11, starting transfers between devices, along_chips(): return lax.ppermute(x, 'row', [(s, s ^ 2 * k) for s in range(rs)])  14.5 us
    ppermute x12, starting transfers between devices, along_col(): return lax.ppermute(x, 'col', [(s, s ^ k) for s in range(cs)])  13.4 us
    pallas_call x18, Pallas kernels, call(): pl.pallas_call(run, out_shape=outs, in_specs=[SMEM] * smem + [VMEM] * (co...  11 us
    ppermute x4, starting transfers between devices, send_own(): return lax.ppermute(block, ('row', 'col'), pairs)  7.23 us
    pallas_call x2, Pallas kernels, assemble(): pl.pallas_call(run, out_shape=[weight, weight, shape((1, hid), F32)], in_...  4.22 us
    ppermute x11, starting transfers between devices, other_core(): return lax.ppermute(x, 'row', [(s, s ^ 1) for s in range(rs)])  2.67 us
  transfers between devices with their start and end apart: 38, of which 13 were waited for; matrix products, arithmetic and copies ran while one was open for 1% of the time, Pallas kernels for 9%

profile of v10, /device:TPU:0, one launch (start us, length us, event | category | flops | bytes accessed | tf_op | source)
XLA Modules:
  0.0 114.6 jit_solution(6381047479855195450)
XLA Ops:
  0.6 4.1 %collective-permute-start.1 = (bf16[128,768]{1,0:T(8,128)(2,1)}, bf16[128,768]{1,0:T(8,128)(2,1)S(1)}, u32[]{:S(2)}, u32[]{:S(2)}) collective-permute-start(bf16[128,768]{1,0:T(8,128)(2,1)} %refs_1_.2), channel_id=1, source_target_pairs={{0,16},{4,20},{8,24},{12,28},{16,0},{20,4},{24,8},{28,12},{1,17},{... | collective-permute-start | bytes 589832 | tf_op jit(solution)/shard_map/ppermute | solution.py:477
  4.7 1.6 %collective-permute-start = (bf16[128,768]{1,0:T(8,128)(2,1)}, bf16[128,768]{1,0:T(8,128)(2,1)S(1)}, u32[]{:S(2)}, u32[]{:S(2)}) collective-permute-start(bf16[128,768]{1,0:T(8,128)(2,1)} %refs_1_.2), channel_id=1, source_target_pairs={{0,8},{4,12},{8,0},{12,4},{16,24},{20,28},{24,16},{28,20},{1,9},{5... | collective-permute-start | bytes 589832 | tf_op jit(solution)/shard_map/ppermute | solution.py:477
  15.6 2.8 %collective-permute-start.6 = (bf16[128,768]{1,0:T(8,128)(2,1)S(1)}, bf16[128,768]{1,0:T(8,128)(2,1)S(1)}, u32[]{:S(2)}, u32[]{:S(2)}) collective-permute-start(bf16[128,768]{1,0:T(8,128)(2,1)S(1)} %collective-permute-done.refs_2_), channel_id=1, source_target_pairs={{0,2},{4,3},{9,8},{13,9},{18,22},{22,23},{27,28},{31,29}} | collective-permute-start | bytes 589832 | tf_op jit(solution)/shard_map/ppermute | solution.py:499
  19.7 1.9 %collective-permute-done.7.refs_2_ = bf16[128,768]{1,0:T(8,128)(2,1)S(1)} collective-permute-done((bf16[128,768]{1,0:T(8,128)(2,1)S(1)}, bf16[128,768]{1,0:T(8,128)(2,1)S(1)}, u32[]{:S(2)}, u32[]{:S(2)}) %collective-permute-start.7) | collective-permute-done | bytes 196640 | tf_op jit(solution)/shard_map/ppermute | solution.py:477
  22.6 2.5 %collective-permute-start.10 = (bf16[128,768]{1,0:T(8,128)(2,1)S(1)}, bf16[128,768]{1,0:T(8,128)(2,1)S(1)}, u32[]{:S(2)}, u32[]{:S(2)}) collective-permute-start(bf16[128,768]{1,0:T(8,128)(2,1)S(1)} %shard_map.131), channel_id=1, source_target_pairs={{0,4},{4,5},{9,14},{13,15},{18,16},{22,17},{27,26},{31,27}} | collective-permute-start | bytes 589832 | tf_op jit(solution)/shard_map/ppermute | solution.py:499
  26.9 2.0 %collective-permute-start.11 = (bf16[128,768]{1,0:T(8,128)(2,1)S(1)}, bf16[128,768]{1,0:T(8,128)(2,1)S(1)}, u32[]{:S(2)}, u32[]{:S(2)}) collective-permute-start(bf16[128,768]{1,0:T(8,128)(2,1)S(1)} %get-tuple-element.43), channel_id=1, source_target_pairs={{0,1},{1,0},{2,3},{3,2},{4,5},{5,4},{6,7},{7,6},{8,9},{9,8},{10,11... | collective-permute-start | bytes 589832 | tf_op jit(solution)/shard_map/ppermute | solution.py:474
  31.9 1.9 %collective-permute-done.11.refs_1_ = bf16[128,768]{1,0:T(8,128)(2,1)S(1)} collective-permute-done((bf16[128,768]{1,0:T(8,128)(2,1)S(1)}, bf16[128,768]{1,0:T(8,128)(2,1)S(1)}, u32[]{:S(2)}, u32[]{:S(2)}) %collective-permute-start.11) | collective-permute-done | bytes 196640 | tf_op jit(solution)/shard_map/ppermute | solution.py:474
  33.8 6.4 %collective-permute-done.12.refs_2_ = bf16[128,768]{1,0:T(8,128)(2,1)S(1)} collective-permute-done((bf16[128,768]{1,0:T(8,128)(2,1)S(1)}, bf16[128,768]{1,0:T(8,128)(2,1)S(1)}, u32[]{:S(2)}, u32[]{:S(2)}) %collective-permute-start.12) | collective-permute-done | bytes 196640 | tf_op jit(solution)/shard_map/ppermute | solution.py:474
  41.6 1.8 %collective-permute-start.17 = (bf16[128,1408]{1,0:T(8,128)(2,1)S(1)}, bf16[128,1408]{1,0:T(8,128)(2,1)S(1)}, u32[]{:S(2)}, u32[]{:S(2)}) collective-permute-start(bf16[128,1408]{1,0:T(8,128)(2,1)S(1)} %get-tuple-element.53), channel_id=1, source_target_pairs={{0,2},{1,3},{2,0},{3,1},{4,6},{5,7},{6,4},{7,5},{8,10},{9,11},{10,... | collective-permute-start | bytes 1081352 | tf_op jit(solution)/shard_map/ppermute | solution.py:474
  43.4 1.7 %collective-permute-start.18 = (bf16[128,1408]{1,0:T(8,128)(2,1)S(1)}, bf16[128,1408]{1,0:T(8,128)(2,1)S(1)}, u32[]{:S(2)}, u32[]{:S(2)}) collective-permute-start(bf16[128,1408]{1,0:T(8,128)(2,1)S(1)} %get-tuple-element.54), channel_id=1, source_target_pairs={{0,3},{1,2},{2,1},{3,0},{4,7},{5,6},{6,5},{7,4},{8,11},{9,10},{10,... | collective-permute-start | bytes 1081352 | tf_op jit(solution)/shard_map/ppermute | solution.py:474
  45.1 7.7 %collective-permute-done.16.refs_4_.refs_1_ = bf16[128,1408]{1,0:T(8,128)(2,1)S(1)} collective-permute-done((bf16[128,1408]{1,0:T(8,128)(2,1)S(1)}, bf16[128,1408]{1,0:T(8,128)(2,1)S(1)}, u32[]{:S(2)}, u32[]{:S(2)}) %collective-permute-start.16) | collective-permute-done | bytes 360480 | tf_op jit(solution)/shard_map/ppermute | solution.py:474
  54.1 6.1 %collective-permute-done.17.refs_2_.refs_3_ = bf16[128,1408]{1,0:T(8,128)(2,1)S(1)} collective-permute-done((bf16[128,1408]{1,0:T(8,128)(2,1)S(1)}, bf16[128,1408]{1,0:T(8,128)(2,1)S(1)}, u32[]{:S(2)}, u32[]{:S(2)}) %collective-permute-start.17) | collective-permute-done | bytes 360480 | tf_op jit(solution)/shard_map/ppermute | solution.py:474
  61.1 1.7 %collective-permute-done.19.refs_1_ = bf16[4,400,128]{2,1,0:T(8,128)(2,1)S(1)} collective-permute-done((bf16[4,400,128]{2,1,0:T(8,128)(2,1)S(1)}, bf16[4,400,128]{2,1,0:T(8,128)(2,1)S(1)}, u32[]{:S(2)}, u32[]{:S(2)}) %collective-permute-start.19) | collective-permute-done | bytes 409632 | tf_op jit(solution)/shard_map/ppermute | solution.py:480
  63.0 2.3 %collective-permute-start.20 = (bf16[400,128]{1,0:T(8,128)(2,1)S(1)}, bf16[400,128]{1,0:T(8,128)(2,1)S(1)}, u32[]{:S(2)}, u32[]{:S(2)}) collective-permute-start(bf16[400,128]{1,0:T(8,128)(2,1)S(1)} %get-tuple-element.63), channel_id=1, source_target_pairs={{0,8},{4,12},{8,0},{12,4},{16,24},{20,28},{24,16},{28,20},{1,9},{5... | collective-permute-start | bytes 307208 | tf_op jit(solution)/shard_map/ppermute | solution.py:477
  70.2 6.1 %collective-permute-done.21.refs_2_ = bf16[400,128]{1,0:T(8,128)(2,1)S(1)} collective-permute-done((bf16[400,128]{1,0:T(8,128)(2,1)S(1)}, bf16[400,128]{1,0:T(8,128)(2,1)S(1)}, u32[]{:S(2)}, u32[]{:S(2)}) %collective-permute-start.21) | collective-permute-done | bytes 102432 | tf_op jit(solution)/shard_map/ppermute | solution.py:477
  76.5 2.6 %collective-permute-start.25 = (bf16[400,128]{1,0:T(8,128)(2,1)S(1)}, bf16[400,128]{1,0:T(8,128)(2,1)S(1)}, u32[]{:S(2)}, u32[]{:S(2)}) collective-permute-start(bf16[400,128]{1,0:T(8,128)(2,1)S(1)} %shard_map.141.refs_0_), channel_id=1, source_target_pairs={{0,16},{4,20},{8,24},{12,28},{16,0},{20,4},{24,8},{28,12},{1,17},{... | collective-permute-start | bytes 307208 | tf_op jit(solution)/shard_map/ppermute | solution.py:477
  79.1 6.0 %collective-permute-done.25.refs_3_.refs_2_ = bf16[400,128]{1,0:T(8,128)(2,1)S(1)} collective-permute-done((bf16[400,128]{1,0:T(8,128)(2,1)S(1)}, bf16[400,128]{1,0:T(8,128)(2,1)S(1)}, u32[]{:S(2)}, u32[]{:S(2)}) %collective-permute-start.25) | collective-permute-done | bytes 102432 | tf_op jit(solution)/shard_map/ppermute | solution.py:477
  85.1 4.7 %collective-permute-done.26.refs_4_.refs_3_ = bf16[400,128]{1,0:T(8,128)(2,1)S(1)} collective-permute-done((bf16[400,128]{1,0:T(8,128)(2,1)S(1)}, bf16[400,128]{1,0:T(8,128)(2,1)S(1)}, u32[]{:S(2)}, u32[]{:S(2)}) %collective-permute-start.26) | collective-permute-done | bytes 102432 | tf_op jit(solution)/shard_map/ppermute | solution.py:477
  90.4 1.7 %collective-permute-start.30 = (bf16[4,400,128]{2,1,0:T(8,128)(2,1)S(1)}, bf16[4,400,128]{2,1,0:T(8,128)(2,1)S(1)}, u32[]{:S(2)}, u32[]{:S(2)}) collective-permute-start(bf16[4,400,128]{2,1,0:T(8,128)(2,1)S(1)} %shard_map.145.refs_0_), channel_id=1, source_target_pairs={{0,1},{1,0},{2,3},{3,2},{4,5},{5,4},{6,7},{7,6},{8,9},{9,8},{10,11... | collective-permute-start | bytes 1228808 | tf_op jit(solution)/shard_map/ppermute | solution.py:474
  92.1 7.3 %collective-permute-done.27.refs_1_ = bf16[2,128,768]{2,1,0:T(8,128)(2,1)S(1)} collective-permute-done((bf16[2,128,768]{2,1,0:T(8,128)(2,1)S(1)}, bf16[2,128,768]{2,1,0:T(8,128)(2,1)S(1)}, u32[]{:S(2)}, u32[]{:S(2)}) %collective-permute-start.27) | collective-permute-done | bytes 393248 | tf_op jit(solution)/shard_map/ppermute | solution.py:477
  100.8 2.0 %collective-permute-start.34 = (bf16[2,400,128]{2,1,0:T(8,128)(2,1)S(1)}, bf16[2,400,128]{2,1,0:T(8,128)(2,1)S(1)}, u32[]{:S(2)}, u32[]{:S(2)}) collective-permute-start(bf16[2,400,128]{2,1,0:T(8,128)(2,1)S(1)} %slice.14), channel_id=1, source_target_pairs={{0,2},{1,3},{2,0},{3,1},{4,6},{5,7},{6,4},{7,5},{8,10},{9,11},{10,... | collective-permute-start | bytes 614408 | tf_op jit(solution)/shard_map/ppermute | solution.py:474
  102.9 6.1 %collective-permute-done.28.refs_1_ = bf16[1,128,768]{2,1,0:T(8,128)(2,1)S(1)} collective-permute-done((bf16[1,128,768]{2,1,0:T(8,128)(2,1)S(1)}, bf16[1,128,768]{2,1,0:T(8,128)(2,1)S(1)}, u32[]{:S(2)}, u32[]{:S(2)}) %collective-permute-start.28) | collective-permute-done | bytes 196640 | tf_op jit(solution)/shard_map/ppermute | solution.py:477
  110.3 1.8 %shard_map.146 = (f32[768,1024]{1,0:T(8,128)}, f32[768,1024]{1,0:T(8,128)}, f32[1,1024]{1,0:T(1,128)S(1)}) custom-call(bf16[4,400,128]{2,1,0:T(8,128)(2,1)S(1)} %shard_map.145.refs_0_, bf16[4,400,128]{2,1,0:T(8,128)(2,1)S(1)} %collective-permute-done.30.refs_1_, bf16[4,400,128]{2,1,0:T(8,128)(2,1)S(1)} %collective-permute-done.32.refs_2_, ...), custom_call_target="tpu_custom_call" | custom-call | bytes 9437184 | tf_op jit(solution)/shard_map/pallas_call | solution.py:442
  112.2 2.4 %shard_map.147 = (f32[768,1024]{1,0:T(8,128)}, f32[768,1024]{1,0:T(8,128)}, f32[1,1024]{1,0:T(1,128)}) custom-call(bf16[4,400,128]{2,1,0:T(8,128)(2,1)S(1)} %collective-permute-done.29.refs_0_, bf16[4,400,128]{2,1,0:T(8,128)(2,1)S(1)} %collective-permute-done.31.refs_1_, ...), custom_call_target="tpu_custom_call", output_to_operand_aliasing={{0}: (5, {}), {1}: (6, {})} | custom-call | bytes 9437184 | tf_op jit(solution)/shard_map/pallas_call | solution.py:442
  (97 shorter events, 27.8 us)
Async XLA Ops:
  0.6 13.5 %collective-permute-start.1 = (bf16[128,768]{1,0:T(8,128)(2,1)}, bf16[128,768]{1,0:T(8,128)(2,1)S(1)}, u32[]{:S(2)}, u32[]{:S(2)}) collective-permute-start(bf16[128,768]{1,0:T(8,128)(2,1)} %refs_1_.2), channel_id=1, source_target_pairs={{0,16},{4,20},{8,24},{12,28},{16,0},{20,4},{24,8},{28,12},{1,17},{... | collective-permute-start | bytes 589832 | tf_op jit(solution)/shard_map/ppermute | solution.py:477
  4.7 10.9 %collective-permute-start = (bf16[128,768]{1,0:T(8,128)(2,1)}, bf16[128,768]{1,0:T(8,128)(2,1)S(1)}, u32[]{:S(2)}, u32[]{:S(2)}) collective-permute-start(bf16[128,768]{1,0:T(8,128)(2,1)} %refs_1_.2), channel_id=1, source_target_pairs={{0,8},{4,12},{8,0},{12,4},{16,24},{20,28},{24,16},{28,20},{1,9},{5... | collective-permute-start | bytes 589832 | tf_op jit(solution)/shard_map/ppermute | solution.py:477
  6.3 12.1 %collective-permute-start.2 = (bf16[128,768]{1,0:T(8,128)(2,1)}, bf16[128,768]{1,0:T(8,128)(2,1)S(1)}, u32[]{:S(2)}, u32[]{:S(2)}) collective-permute-start(bf16[128,768]{1,0:T(8,128)(2,1)} %refs_1_.2), channel_id=1, source_target_pairs={{0,4},{4,0},{8,12},{12,8},{16,20},{20,16},{24,28},{28,24},{1,5},{5... | collective-permute-start | bytes 589832 | tf_op jit(solution)/shard_map/ppermute | solution.py:480
  12.8 9.0 %collective-permute-start.5 = (bf16[128,768]{1,0:T(8,128)(2,1)S(1)}, bf16[128,768]{1,0:T(8,128)(2,1)S(1)}, u32[]{:S(2)}, u32[]{:S(2)}) collective-permute-start(bf16[128,768]{1,0:T(8,128)(2,1)S(1)} %copy-done.5), channel_id=1, source_target_pairs={{0,0},{4,1},{9,10},{13,11},{18,20},{22,21},{27,30},{31,31}} | collective-permute-start | bytes 589832 | tf_op jit(solution)/shard_map/ppermute | solution.py:499
  14.2 7.5 %collective-permute-start.7 = (bf16[128,768]{1,0:T(8,128)(2,1)S(1)}, bf16[128,768]{1,0:T(8,128)(2,1)S(1)}, u32[]{:S(2)}, u32[]{:S(2)}) collective-permute-start(bf16[128,768]{1,0:T(8,128)(2,1)S(1)} %collective-permute-done.1.refs_3_.refs_0_), channel_id=1, source_target_pairs={{0,8},{4,12},{8,0},{12,4},{16,24},{20,28},{24,16},{28,20},{1,9},{5... | collective-permute-start | bytes 589832 | tf_op jit(solution)/shard_map/ppermute | solution.py:477
  26.9 6.8 %collective-permute-start.11 = (bf16[128,768]{1,0:T(8,128)(2,1)S(1)}, bf16[128,768]{1,0:T(8,128)(2,1)S(1)}, u32[]{:S(2)}, u32[]{:S(2)}) collective-permute-start(bf16[128,768]{1,0:T(8,128)(2,1)S(1)} %get-tuple-element.43), channel_id=1, source_target_pairs={{0,1},{1,0},{2,3},{3,2},{4,5},{5,4},{6,7},{7,6},{8,9},{9,8},{10,11... | collective-permute-start | bytes 589832 | tf_op jit(solution)/shard_map/ppermute | solution.py:474
  28.9 11.2 %collective-permute-start.12 = (bf16[128,768]{1,0:T(8,128)(2,1)S(1)}, bf16[128,768]{1,0:T(8,128)(2,1)S(1)}, u32[]{:S(2)}, u32[]{:S(2)}) collective-permute-start(bf16[128,768]{1,0:T(8,128)(2,1)S(1)} %get-tuple-element.44), channel_id=1, source_target_pairs={{0,2},{1,3},{2,0},{3,1},{4,6},{5,7},{6,4},{7,5},{8,10},{9,11},{10,... | collective-permute-start | bytes 589832 | tf_op jit(solution)/shard_map/ppermute | solution.py:474
  29.1 11.1 %collective-permute-start.13 = (bf16[128,768]{1,0:T(8,128)(2,1)S(1)}, bf16[128,768]{1,0:T(8,128)(2,1)S(1)}, u32[]{:S(2)}, u32[]{:S(2)}) collective-permute-start(bf16[128,768]{1,0:T(8,128)(2,1)S(1)} %get-tuple-element.45), channel_id=1, source_target_pairs={{0,3},{1,2},{2,1},{3,0},{4,7},{5,6},{6,5},{7,4},{8,11},{9,10},{10,... | collective-permute-start | bytes 589832 | tf_op jit(solution)/shard_map/ppermute | solution.py:474
  41.6 11.2 %collective-permute-start.16 = (bf16[128,1408]{1,0:T(8,128)(2,1)S(1)}, bf16[128,1408]{1,0:T(8,128)(2,1)S(1)}, u32[]{:S(2)}, u32[]{:S(2)}) collective-permute-start(bf16[128,1408]{1,0:T(8,128)(2,1)S(1)} %get-tuple-element.51), channel_id=1, source_target_pairs={{0,1},{1,0},{2,3},{3,2},{4,5},{5,4},{6,7},{7,6},{8,9},{9,8},{10,11... | collective-permute-start | bytes 1081352 | tf_op jit(solution)/shard_map/ppermute | solution.py:474
  41.6 18.6 %collective-permute-start.17 = (bf16[128,1408]{1,0:T(8,128)(2,1)S(1)}, bf16[128,1408]{1,0:T(8,128)(2,1)S(1)}, u32[]{:S(2)}, u32[]{:S(2)}) collective-permute-start(bf16[128,1408]{1,0:T(8,128)(2,1)S(1)} %get-tuple-element.53), channel_id=1, source_target_pairs={{0,2},{1,3},{2,0},{3,1},{4,6},{5,7},{6,4},{7,5},{8,10},{9,11},{10,... | collective-permute-start | bytes 1081352 | tf_op jit(solution)/shard_map/ppermute | solution.py:474
  43.4 16.8 %collective-permute-start.18 = (bf16[128,1408]{1,0:T(8,128)(2,1)S(1)}, bf16[128,1408]{1,0:T(8,128)(2,1)S(1)}, u32[]{:S(2)}, u32[]{:S(2)}) collective-permute-start(bf16[128,1408]{1,0:T(8,128)(2,1)S(1)} %get-tuple-element.54), channel_id=1, source_target_pairs={{0,3},{1,2},{2,1},{3,0},{4,7},{5,6},{6,5},{7,4},{8,11},{9,10},{10,... | collective-permute-start | bytes 1081352 | tf_op jit(solution)/shard_map/ppermute | solution.py:474
  63.0 7.2 %collective-permute-start.20 = (bf16[400,128]{1,0:T(8,128)(2,1)S(1)}, bf16[400,128]{1,0:T(8,128)(2,1)S(1)}, u32[]{:S(2)}, u32[]{:S(2)}) collective-permute-start(bf16[400,128]{1,0:T(8,128)(2,1)S(1)} %get-tuple-element.63), channel_id=1, source_target_pairs={{0,8},{4,12},{8,0},{12,4},{16,24},{20,28},{24,16},{28,20},{1,9},{5... | collective-permute-start | bytes 307208 | tf_op jit(solution)/shard_map/ppermute | solution.py:477
  65.3 11.0 %collective-permute-start.21 = (bf16[400,128]{1,0:T(8,128)(2,1)S(1)}, bf16[400,128]{1,0:T(8,128)(2,1)S(1)}, u32[]{:S(2)}, u32[]{:S(2)}) collective-permute-start(bf16[400,128]{1,0:T(8,128)(2,1)S(1)} %get-tuple-element.64), channel_id=1, source_target_pairs={{0,16},{4,20},{8,24},{12,28},{16,0},{20,4},{24,8},{28,12},{1,17},{... | collective-permute-start | bytes 307208 | tf_op jit(solution)/shard_map/ppermute | solution.py:477
  66.2 10.1 %collective-permute-start.22 = (bf16[400,128]{1,0:T(8,128)(2,1)S(1)}, bf16[400,128]{1,0:T(8,128)(2,1)S(1)}, u32[]{:S(2)}, u32[]{:S(2)}) collective-permute-start(bf16[400,128]{1,0:T(8,128)(2,1)S(1)} %get-tuple-element.65), channel_id=1, source_target_pairs={{0,24},{4,28},{8,16},{12,20},{16,8},{20,12},{24,0},{28,4},{1,25},{... | collective-permute-start | bytes 307208 | tf_op jit(solution)/shard_map/ppermute | solution.py:477
  76.4 13.4 %collective-permute-start.23 = (bf16[4,128,768]{2,1,0:T(8,128)(2,1)S(1)}, bf16[4,128,768]{2,1,0:T(8,128)(2,1)S(1)}, u32[]{:S(2)}, u32[]{:S(2)}) collective-permute-start(bf16[4,128,768]{2,1,0:T(8,128)(2,1)S(1)} %shard_map.140), channel_id=1, source_target_pairs={{0,4},{4,0},{8,12},{12,8},{16,20},{20,16},{24,28},{28,24},{1,5},{5... | collective-permute-start | bytes 2359304 | tf_op jit(solution)/shard_map/ppermute | solution.py:480
  76.5 8.5 %collective-permute-start.25 = (bf16[400,128]{1,0:T(8,128)(2,1)S(1)}, bf16[400,128]{1,0:T(8,128)(2,1)S(1)}, u32[]{:S(2)}, u32[]{:S(2)}) collective-permute-start(bf16[400,128]{1,0:T(8,128)(2,1)S(1)} %shard_map.141.refs_0_), channel_id=1, source_target_pairs={{0,16},{4,20},{8,24},{12,28},{16,0},{20,4},{24,8},{28,12},{1,17},{... | collective-permute-start | bytes 307208 | tf_op jit(solution)/shard_map/ppermute | solution.py:477
  89.8 9.5 %collective-permute-start.27 = (bf16[2,128,768]{2,1,0:T(8,128)(2,1)S(1)}, bf16[2,128,768]{2,1,0:T(8,128)(2,1)S(1)}, u32[]{:S(2)}, u32[]{:S(2)}) collective-permute-start(bf16[2,128,768]{2,1,0:T(8,128)(2,1)S(1)} %get-tuple-element.68.refs_4_), channel_id=1, source_target_pairs={{0,8},{4,12},{8,0},{12,4},{16,24},{20,28},{24,16},{28,20},{1,9},{5... | collective-permute-start | bytes 1179656 | tf_op jit(solution)/shard_map/ppermute | solution.py:477
  90.0 10.2 %collective-permute-start.32 = (bf16[4,400,128]{2,1,0:T(8,128)(2,1)S(1)}, bf16[4,400,128]{2,1,0:T(8,128)(2,1)S(1)}, u32[]{:S(2)}, u32[]{:S(2)}) collective-permute-start(bf16[4,400,128]{2,1,0:T(8,128)(2,1)S(1)} %shard_map.145.refs_0_), channel_id=1, source_target_pairs={{0,2},{1,3},{2,0},{3,1},{4,6},{5,7},{6,4},{7,5},{8,10},{9,11},{10,... | collective-permute-start | bytes 1228808 | tf_op jit(solution)/shard_map/ppermute | solution.py:474
  90.4 10.4 %collective-permute-start.30 = (bf16[4,400,128]{2,1,0:T(8,128)(2,1)S(1)}, bf16[4,400,128]{2,1,0:T(8,128)(2,1)S(1)}, u32[]{:S(2)}, u32[]{:S(2)}) collective-permute-start(bf16[4,400,128]{2,1,0:T(8,128)(2,1)S(1)} %shard_map.145.refs_0_), channel_id=1, source_target_pairs={{0,1},{1,0},{2,3},{3,2},{4,5},{5,4},{6,7},{7,6},{8,9},{9,8},{10,11... | collective-permute-start | bytes 1228808 | tf_op jit(solution)/shard_map/ppermute | solution.py:474
  99.5 9.5 %collective-permute-start.28 = (bf16[1,128,768]{2,1,0:T(8,128)(2,1)S(1)}, bf16[1,128,768]{2,1,0:T(8,128)(2,1)S(1)}, u32[]{:S(2)}, u32[]{:S(2)}) collective-permute-start(bf16[1,128,768]{2,1,0:T(8,128)(2,1)S(1)} %get-tuple-element.70), channel_id=1, source_target_pairs={{0,16},{4,20},{8,24},{12,28},{16,0},{20,4},{24,8},{28,12},{1,17},{... | collective-permute-start | bytes 589832 | tf_op jit(solution)/shard_map/ppermute | solution.py:477
  100.1 12.0 %collective-permute-start.29 = (bf16[4,400,128]{2,1,0:T(8,128)(2,1)S(1)}, bf16[4,400,128]{2,1,0:T(8,128)(2,1)S(1)}, u32[]{:S(2)}, u32[]{:S(2)}) collective-permute-start(bf16[4,400,128]{2,1,0:T(8,128)(2,1)S(1)} %shard_map.145.refs_0_), channel_id=1, source_target_pairs={{0,4},{4,0},{8,12},{12,8},{16,20},{20,16},{24,28},{28,24},{1,5},{5... | collective-permute-start | bytes 1228808 | tf_op jit(solution)/shard_map/ppermute | solution.py:480
  100.2 8.8 %collective-permute-start.36 = (bf16[2,400,128]{2,1,0:T(8,128)(2,1)S(1)}, bf16[2,400,128]{2,1,0:T(8,128)(2,1)S(1)}, u32[]{:S(2)}, u32[]{:S(2)}) collective-permute-start(bf16[2,400,128]{2,1,0:T(8,128)(2,1)S(1)} %slice.15), channel_id=1, source_target_pairs={{0,1},{1,0},{2,3},{3,2},{4,5},{5,4},{6,7},{7,6},{8,9},{9,8},{10,11... | collective-permute-start | bytes 614408 | tf_op jit(solution)/shard_map/ppermute | solution.py:474
  100.8 8.7 %collective-permute-start.34 = (bf16[2,400,128]{2,1,0:T(8,128)(2,1)S(1)}, bf16[2,400,128]{2,1,0:T(8,128)(2,1)S(1)}, u32[]{:S(2)}, u32[]{:S(2)}) collective-permute-start(bf16[2,400,128]{2,1,0:T(8,128)(2,1)S(1)} %slice.14), channel_id=1, source_target_pairs={{0,2},{1,3},{2,0},{3,1},{4,6},{5,7},{6,4},{7,5},{8,10},{9,11},{10,... | collective-permute-start | bytes 614408 | tf_op jit(solution)/shard_map/ppermute | solution.py:474
  102.8 9.3 %collective-permute-start.33 = (bf16[4,400,128]{2,1,0:T(8,128)(2,1)S(1)}, bf16[4,400,128]{2,1,0:T(8,128)(2,1)S(1)}, u32[]{:S(2)}, u32[]{:S(2)}) collective-permute-start(bf16[4,400,128]{2,1,0:T(8,128)(2,1)S(1)} %collective-permute-done.32.refs_2_), channel_id=1, source_target_pairs={{0,4},{4,0},{8,12},{12,8},{16,20},{20,16},{24,28},{28,24},{1,5},{5... | collective-permute-start | bytes 1228808 | tf_op jit(solution)/shard_map/ppermute | solution.py:480
  (23 other events, 99.0 us)

commit v11 on v10

--- a/solution.py
+++ b/solution.py
@@ -525,7 +525,6 @@
     )
     mine_last = {d + 1: along_chips(x, 1) for d, x in mine_first.items() if d > 1}
     theirs_first.update({d: other_core(x) for d, x in mine_first.items() if d > 1})
-    theirs_last = {d: other_core(x) for d, x in mine_last.items()}
     own_feats[1] = send_own(near, 1)
 
     def placed(mine, theirs):
@@ -541,6 +540,7 @@
         masses = [degree, along_col(degree, step)]
         degree = masses[0] + masses[1]
         step *= 2
+    theirs_last = {d: other_core(follow(x, [begun])) for d, x in mine_last.items()}
     evens = {d: send_own(follow(x, [begun, masses[0]]), d) for d, x in mine_first.items() if d > 1}
     own_feats.update(evens)
     own_feats.update({d: send_own(x, d) for d, x in mine_last.items()})
@@ -591,8 +591,10 @@
         rest = [(along_col(line, cs - 1), 0, cs - 1)]
     factor = 1.0 / math.sqrt(nd * rs * cs)
     sizes = (depth, hid, xr, nc, cs, (factor, 32.0 * factor))
-    begun = assemble([piece(*x, True) for x in near + rest], (), *sizes, ())
-    pieces = [piece(other_core(x), *where, False) for x, *where in near + rest]
+    begun = assemble([piece(*x, True) for x in near], (), *sizes, ())
+    pieces = [piece(*x, True) for x in rest]
+    sent = [(follow(x, begun[2:]) if n == 1 else x, *where) for n, (x, *where) in enumerate(near)]
+    pieces += [piece(other_core(x), *where, False) for x, *where in sent + rest]
     total_self, total_neigh, total_bias = assemble(pieces, begun, *sizes, [grad_input])
     return output, grad_input, total_self, total_neigh, total_bias.reshape(-1)
 

time: 115 us -> 117 us (1.017)
    ppermute x11, waiting for transfers between devices: 32.8 us -> 30.6 us  [along_chips(): return lax.ppermute(x, 'row', [(s, s ^ 2 * k) for s in range(rs)])]
    ppermute x4, waiting for transfers between devices: 0.01 us -> 2.01 us  [send_own(): return lax.ppermute(block, ('row', 'col'), pairs)]
    pallas_call x18 -> x20, Pallas kernels: 11 us -> 10.8 us  [call(): pl.pallas_call(run, out_shape=outs, in_specs=[SMEM] * smem + [VMEM] * (co...]
  transfers between devices with their start and end apart: 38 -> 38, of which waited for: 13 -> 16; matrix products, arithmetic and copies ran while one was open for 1% -> 0% of each run, Pallas kernels for 9% -> 8%
where the time goes in v11:
time: 117 us; the launch traced here: 116 us
  waiting for transfers between devices  57.3 us (49%)
  starting transfers between devices  38.4 us (33%)
  Pallas kernels  15 us (13%)
  local copies, waits for them, and re-layouts  3.54 us (3%)
  between operations  1.64 us (1%)
    ppermute x11, waiting for transfers between devices, along_chips(): return lax.ppermute(x, 'row', [(s, s ^ 2 * k) for s in range(rs)])  30.6 us
    ppermute x12, waiting for transfers between devices, along_col(): return lax.ppermute(x, 'col', [(s, s ^ k) for s in range(cs)])  21.9 us
    ppermute x11, starting transfers between devices, along_chips(): return lax.ppermute(x, 'row', [(s, s ^ 2 * k) for s in range(rs)])  14.7 us
    ppermute x12, starting transfers between devices, along_col(): return lax.ppermute(x, 'col', [(s, s ^ k) for s in range(cs)])  13.6 us
    pallas_call x20, Pallas kernels, call(): pl.pallas_call(run, out_shape=outs, in_specs=[SMEM] * smem + [VMEM] * (co...  10.8 us
    ppermute x4, starting transfers between devices, send_own(): return lax.ppermute(block, ('row', 'col'), pairs)  7.06 us
    pallas_call x2, Pallas kernels, assemble(): pl.pallas_call(run, out_shape=[weight, weight, shape((1, hid), F32)], in_...  4.2 us
    unnamed x18, local copies, waits for them, and re-layouts  3.39 us
  transfers between devices with their start and end apart: 38, of which 16 were waited for; matrix products, arithmetic and copies ran while one was open for 0% of the time, Pallas kernels for 8%

profile of v11, /device:TPU:0, one launch (start us, length us, event | category | flops | bytes accessed | tf_op | source)
XLA Modules:
  0.0 116.3 jit_solution(15373753735201005960)
XLA Ops:
  0.6 4.1 %collective-permute-start.1 = (bf16[128,768]{1,0:T(8,128)(2,1)}, bf16[128,768]{1,0:T(8,128)(2,1)S(1)}, u32[]{:S(2)}, u32[]{:S(2)}) collective-permute-start(bf16[128,768]{1,0:T(8,128)(2,1)} %refs_1_.2), channel_id=1, source_target_pairs={{0,16},{4,20},{8,24},{12,28},{16,0},{20,4},{24,8},{28,12},{1,17},{... | collective-permute-start | bytes 589832 | tf_op jit(solution)/shard_map/ppermute | solution.py:477
  4.7 1.6 %collective-permute-start = (bf16[128,768]{1,0:T(8,128)(2,1)}, bf16[128,768]{1,0:T(8,128)(2,1)S(1)}, u32[]{:S(2)}, u32[]{:S(2)}) collective-permute-start(bf16[128,768]{1,0:T(8,128)(2,1)} %refs_1_.2), channel_id=1, source_target_pairs={{0,8},{4,12},{8,0},{12,4},{16,24},{20,28},{24,16},{28,20},{1,9},{5... | collective-permute-start | bytes 589832 | tf_op jit(solution)/shard_map/ppermute | solution.py:477
  15.3 2.6 %collective-permute-start.6 = (bf16[128,768]{1,0:T(8,128)(2,1)S(1)}, bf16[128,768]{1,0:T(8,128)(2,1)S(1)}, u32[]{:S(2)}, u32[]{:S(2)}) collective-permute-start(bf16[128,768]{1,0:T(8,128)(2,1)S(1)} %collective-permute-done.refs_2_), channel_id=1, source_target_pairs={{0,2},{4,3},{9,8},{13,9},{18,22},{22,23},{27,28},{31,29}} | collective-permute-start | bytes 589832 | tf_op jit(solution)/shard_map/ppermute | solution.py:499
  19.0 2.0 %collective-permute-done.6.refs_8_ = bf16[128,768]{1,0:T(8,128)(2,1)S(1)} collective-permute-done((bf16[128,768]{1,0:T(8,128)(2,1)S(1)}, bf16[128,768]{1,0:T(8,128)(2,1)S(1)}, u32[]{:S(2)}, u32[]{:S(2)}) %collective-permute-start.6) | collective-permute-done | bytes 196640 | tf_op jit(solution)/shard_map/ppermute | solution.py:499
  21.8 4.1 %collective-permute-done.7.refs_0_.refs_2_ = bf16[128,768]{1,0:T(8,128)(2,1)S(1)} collective-permute-done((bf16[128,768]{1,0:T(8,128)(2,1)S(1)}, bf16[128,768]{1,0:T(8,128)(2,1)S(1)}, u32[]{:S(2)}, u32[]{:S(2)}) %collective-permute-start.7) | collective-permute-done | bytes 196640 | tf_op jit(solution)/shard_map/ppermute | solution.py:477
  26.0 2.5 %collective-permute-start.10 = (bf16[128,768]{1,0:T(8,128)(2,1)S(1)}, bf16[128,768]{1,0:T(8,128)(2,1)S(1)}, u32[]{:S(2)}, u32[]{:S(2)}) collective-permute-start(bf16[128,768]{1,0:T(8,128)(2,1)S(1)} %shard_map.132), channel_id=1, source_target_pairs={{0,4},{4,5},{9,14},{13,15},{18,16},{22,17},{27,26},{31,27}} | collective-permute-start | bytes 589832 | tf_op jit(solution)/shard_map/ppermute | solution.py:499
  30.4 2.1 %collective-permute-start.12 = (bf16[128,768]{1,0:T(8,128)(2,1)S(1)}, bf16[128,768]{1,0:T(8,128)(2,1)S(1)}, u32[]{:S(2)}, u32[]{:S(2)}) collective-permute-start(bf16[128,768]{1,0:T(8,128)(2,1)S(1)} %get-tuple-element.44), channel_id=1, source_target_pairs={{0,2},{1,3},{2,0},{3,1},{4,6},{5,7},{6,4},{7,5},{8,10},{9,11},{10,... | collective-permute-start | bytes 589832 | tf_op jit(solution)/shard_map/ppermute | solution.py:474
  35.2 2.3 %collective-permute-done.11.refs_1_ = bf16[128,768]{1,0:T(8,128)(2,1)S(1)} collective-permute-done((bf16[128,768]{1,0:T(8,128)(2,1)S(1)}, bf16[128,768]{1,0:T(8,128)(2,1)S(1)}, u32[]{:S(2)}, u32[]{:S(2)}) %collective-permute-start.11) | collective-permute-done | bytes 196640 | tf_op jit(solution)/shard_map/ppermute | solution.py:474
  37.8 4.7 %collective-permute-done.13.refs_3_ = bf16[128,768]{1,0:T(8,128)(2,1)S(1)} collective-permute-done((bf16[128,768]{1,0:T(8,128)(2,1)S(1)}, bf16[128,768]{1,0:T(8,128)(2,1)S(1)}, u32[]{:S(2)}, u32[]{:S(2)}) %collective-permute-start.13) | collective-permute-done | bytes 196640 | tf_op jit(solution)/shard_map/ppermute | solution.py:474
  45.5 2.1 %collective-permute-start.17 = (bf16[128,1408]{1,0:T(8,128)(2,1)S(1)}, bf16[128,1408]{1,0:T(8,128)(2,1)S(1)}, u32[]{:S(2)}, u32[]{:S(2)}) collective-permute-start(bf16[128,1408]{1,0:T(8,128)(2,1)S(1)} %get-tuple-element.53), channel_id=1, source_target_pairs={{0,2},{1,3},{2,0},{3,1},{4,6},{5,7},{6,4},{7,5},{8,10},{9,11},{10,... | collective-permute-start | bytes 1081352 | tf_op jit(solution)/shard_map/ppermute | solution.py:474
  47.6 7.7 %collective-permute-done.16.refs_4_.refs_1_ = bf16[128,1408]{1,0:T(8,128)(2,1)S(1)} collective-permute-done((bf16[128,1408]{1,0:T(8,128)(2,1)S(1)}, bf16[128,1408]{1,0:T(8,128)(2,1)S(1)}, u32[]{:S(2)}, u32[]{:S(2)}) %collective-permute-start.16) | collective-permute-done | bytes 360480 | tf_op jit(solution)/shard_map/ppermute | solution.py:474
  56.6 6.9 %collective-permute-done.17.refs_2_.refs_3_ = bf16[128,1408]{1,0:T(8,128)(2,1)S(1)} collective-permute-done((bf16[128,1408]{1,0:T(8,128)(2,1)S(1)}, bf16[128,1408]{1,0:T(8,128)(2,1)S(1)}, u32[]{:S(2)}, u32[]{:S(2)}) %collective-permute-start.17) | collective-permute-done | bytes 360480 | tf_op jit(solution)/shard_map/ppermute | solution.py:474
  64.3 1.7 %collective-permute-done.19.refs_1_ = bf16[4,400,128]{2,1,0:T(8,128)(2,1)S(1)} collective-permute-done((bf16[4,400,128]{2,1,0:T(8,128)(2,1)S(1)}, bf16[4,400,128]{2,1,0:T(8,128)(2,1)S(1)}, u32[]{:S(2)}, u32[]{:S(2)}) %collective-permute-start.19) | collective-permute-done | bytes 409632 | tf_op jit(solution)/shard_map/ppermute | solution.py:480
  67.5 3.1 %collective-permute-start.22 = (bf16[400,128]{1,0:T(8,128)(2,1)S(1)}, bf16[400,128]{1,0:T(8,128)(2,1)S(1)}, u32[]{:S(2)}, u32[]{:S(2)}) collective-permute-start(bf16[400,128]{1,0:T(8,128)(2,1)S(1)} %get-tuple-element.65), channel_id=1, source_target_pairs={{0,24},{4,28},{8,16},{12,20},{16,8},{20,12},{24,0},{28,4},{1,25},{... | collective-permute-start | bytes 307208 | tf_op jit(solution)/shard_map/ppermute | solution.py:477
  73.1 5.0 %collective-permute-done.21.refs_2_ = bf16[400,128]{1,0:T(8,128)(2,1)S(1)} collective-permute-done((bf16[400,128]{1,0:T(8,128)(2,1)S(1)}, bf16[400,128]{1,0:T(8,128)(2,1)S(1)}, u32[]{:S(2)}, u32[]{:S(2)}) %collective-permute-start.21) | collective-permute-done | bytes 102432 | tf_op jit(solution)/shard_map/ppermute | solution.py:477
  78.3 1.9 %collective-permute-start.25 = (bf16[400,128]{1,0:T(8,128)(2,1)S(1)}, bf16[400,128]{1,0:T(8,128)(2,1)S(1)}, u32[]{:S(2)}, u32[]{:S(2)}) collective-permute-start(bf16[400,128]{1,0:T(8,128)(2,1)S(1)} %shard_map.142.refs_0_), channel_id=1, source_target_pairs={{0,16},{4,20},{8,24},{12,28},{16,0},{20,4},{24,8},{28,12},{1,17},{... | collective-permute-start | bytes 307208 | tf_op jit(solution)/shard_map/ppermute | solution.py:477
  80.5 6.2 %collective-permute-done.25.refs_3_.refs_2_ = bf16[400,128]{1,0:T(8,128)(2,1)S(1)} collective-permute-done((bf16[400,128]{1,0:T(8,128)(2,1)S(1)}, bf16[400,128]{1,0:T(8,128)(2,1)S(1)}, u32[]{:S(2)}, u32[]{:S(2)}) %collective-permute-start.25) | collective-permute-done | bytes 102432 | tf_op jit(solution)/shard_map/ppermute | solution.py:477
  87.0 4.3 %collective-permute-done.26.refs_4_.refs_3_ = bf16[400,128]{1,0:T(8,128)(2,1)S(1)} collective-permute-done((bf16[400,128]{1,0:T(8,128)(2,1)S(1)}, bf16[400,128]{1,0:T(8,128)(2,1)S(1)}, u32[]{:S(2)}, u32[]{:S(2)}) %collective-permute-start.26) | collective-permute-done | bytes 102432 | tf_op jit(solution)/shard_map/ppermute | solution.py:477
  92.6 1.7 %collective-permute-start.29 = (bf16[4,400,128]{2,1,0:T(8,128)(2,1)S(1)}, bf16[4,400,128]{2,1,0:T(8,128)(2,1)S(1)}, u32[]{:S(2)}, u32[]{:S(2)}) collective-permute-start(bf16[4,400,128]{2,1,0:T(8,128)(2,1)S(1)} %shard_map.146.refs_0_), channel_id=1, source_target_pairs={{0,1},{1,0},{2,3},{3,2},{4,5},{5,4},{6,7},{7,6},{8,9},{9,8},{10,11... | collective-permute-start | bytes 1228808 | tf_op jit(solution)/shard_map/ppermute | solution.py:474
  94.3 6.7 %collective-permute-done.27.refs_1_ = bf16[2,128,768]{2,1,0:T(8,128)(2,1)S(1)} collective-permute-done((bf16[2,128,768]{2,1,0:T(8,128)(2,1)S(1)}, bf16[2,128,768]{2,1,0:T(8,128)(2,1)S(1)}, u32[]{:S(2)}, u32[]{:S(2)}) %collective-permute-start.27) | collective-permute-done | bytes 393248 | tf_op jit(solution)/shard_map/ppermute | solution.py:477
  101.1 1.6 %collective-permute-start.28 = (bf16[1,128,768]{2,1,0:T(8,128)(2,1)S(1)}, bf16[1,128,768]{2,1,0:T(8,128)(2,1)S(1)}, u32[]{:S(2)}, u32[]{:S(2)}) collective-permute-start(bf16[1,128,768]{2,1,0:T(8,128)(2,1)S(1)} %get-tuple-element.70), channel_id=1, source_target_pairs={{0,16},{4,20},{8,24},{12,28},{16,0},{20,4},{24,8},{28,12},{1,17},{... | collective-permute-start | bytes 589832 | tf_op jit(solution)/shard_map/ppermute | solution.py:477
  103.3 1.9 %collective-permute-start.30 = (bf16[2,400,128]{2,1,0:T(8,128)(2,1)S(1)}, bf16[2,400,128]{2,1,0:T(8,128)(2,1)S(1)}, u32[]{:S(2)}, u32[]{:S(2)}) collective-permute-start(bf16[2,400,128]{2,1,0:T(8,128)(2,1)S(1)} %slice.14), channel_id=1, source_target_pairs={{0,2},{1,3},{2,0},{3,1},{4,6},{5,7},{6,4},{7,5},{8,10},{9,11},{10,... | collective-permute-start | bytes 614408 | tf_op jit(solution)/shard_map/ppermute | solution.py:474
  106.8 3.6 %collective-permute-done.28.refs_1_ = bf16[1,128,768]{2,1,0:T(8,128)(2,1)S(1)} collective-permute-done((bf16[1,128,768]{2,1,0:T(8,128)(2,1)S(1)}, bf16[1,128,768]{2,1,0:T(8,128)(2,1)S(1)}, u32[]{:S(2)}, u32[]{:S(2)}) %collective-permute-start.28) | collective-permute-done | bytes 196640 | tf_op jit(solution)/shard_map/ppermute | solution.py:477
  113.6 2.7 %shard_map.149 = (f32[768,1024]{1,0:T(8,128)}, f32[768,1024]{1,0:T(8,128)}, f32[1,1024]{1,0:T(1,128)}) custom-call(bf16[2,400,128]{2,1,0:T(8,128)(2,1)S(1)} %collective-permute-done.30.refs_0_, bf16[2,400,128]{2,1,0:T(8,128)(2,1)S(1)} %collective-permute-done.32.refs_1_, ...), custom_call_target="tpu_custom_call", output_to_operand_aliasing={{0}: (7, {}), {1}: (8, {})} | custom-call | bytes 11796480 | tf_op jit(solution)/shard_map/pallas_call | solution.py:442
  (99 shorter events, 31.8 us)
Async XLA Ops:
  0.6 13.5 %collective-permute-start.1 = (bf16[128,768]{1,0:T(8,128)(2,1)}, bf16[128,768]{1,0:T(8,128)(2,1)S(1)}, u32[]{:S(2)}, u32[]{:S(2)}) collective-permute-start(bf16[128,768]{1,0:T(8,128)(2,1)} %refs_1_.2), channel_id=1, source_target_pairs={{0,16},{4,20},{8,24},{12,28},{16,0},{20,4},{24,8},{28,12},{1,17},{... | collective-permute-start | bytes 589832 | tf_op jit(solution)/shard_map/ppermute | solution.py:477
  4.7 10.5 %collective-permute-start = (bf16[128,768]{1,0:T(8,128)(2,1)}, bf16[128,768]{1,0:T(8,128)(2,1)S(1)}, u32[]{:S(2)}, u32[]{:S(2)}) collective-permute-start(bf16[128,768]{1,0:T(8,128)(2,1)} %refs_1_.2), channel_id=1, source_target_pairs={{0,8},{4,12},{8,0},{12,4},{16,24},{20,28},{24,16},{28,20},{1,9},{5... | collective-permute-start | bytes 589832 | tf_op jit(solution)/shard_map/ppermute | solution.py:477
  6.3 12.6 %collective-permute-start.2 = (bf16[128,768]{1,0:T(8,128)(2,1)}, bf16[128,768]{1,0:T(8,128)(2,1)S(1)}, u32[]{:S(2)}, u32[]{:S(2)}) collective-permute-start(bf16[128,768]{1,0:T(8,128)(2,1)} %refs_1_.2), channel_id=1, source_target_pairs={{0,4},{4,0},{8,12},{12,8},{16,20},{20,16},{24,28},{28,24},{1,5},{5... | collective-permute-start | bytes 589832 | tf_op jit(solution)/shard_map/ppermute | solution.py:480
  19.0 6.9 %collective-permute-start.7 = (bf16[128,768]{1,0:T(8,128)(2,1)S(1)}, bf16[128,768]{1,0:T(8,128)(2,1)S(1)}, u32[]{:S(2)}, u32[]{:S(2)}) collective-permute-start(bf16[128,768]{1,0:T(8,128)(2,1)S(1)} %collective-permute-done.1.refs_3_.refs_0_), channel_id=1, source_target_pairs={{0,8},{4,12},{8,0},{12,4},{16,24},{20,28},{24,16},{28,20},{1,9},{5... | collective-permute-start | bytes 589832 | tf_op jit(solution)/shard_map/ppermute | solution.py:477
  30.3 7.2 %collective-permute-start.11 = (bf16[128,768]{1,0:T(8,128)(2,1)S(1)}, bf16[128,768]{1,0:T(8,128)(2,1)S(1)}, u32[]{:S(2)}, u32[]{:S(2)}) collective-permute-start(bf16[128,768]{1,0:T(8,128)(2,1)S(1)} %get-tuple-element.43), channel_id=1, source_target_pairs={{0,1},{1,0},{2,3},{3,2},{4,5},{5,4},{6,7},{7,6},{8,9},{9,8},{10,11... | collective-permute-start | bytes 589832 | tf_op jit(solution)/shard_map/ppermute | solution.py:474
  30.4 7.4 %collective-permute-start.12 = (bf16[128,768]{1,0:T(8,128)(2,1)S(1)}, bf16[128,768]{1,0:T(8,128)(2,1)S(1)}, u32[]{:S(2)}, u32[]{:S(2)}) collective-permute-start(bf16[128,768]{1,0:T(8,128)(2,1)S(1)} %get-tuple-element.44), channel_id=1, source_target_pairs={{0,2},{1,3},{2,0},{3,1},{4,6},{5,7},{6,4},{7,5},{8,10},{9,11},{10,... | collective-permute-start | bytes 589832 | tf_op jit(solution)/shard_map/ppermute | solution.py:474
  32.5 10.1 %collective-permute-start.13 = (bf16[128,768]{1,0:T(8,128)(2,1)S(1)}, bf16[128,768]{1,0:T(8,128)(2,1)S(1)}, u32[]{:S(2)}, u32[]{:S(2)}) collective-permute-start(bf16[128,768]{1,0:T(8,128)(2,1)S(1)} %get-tuple-element.45), channel_id=1, source_target_pairs={{0,3},{1,2},{2,1},{3,0},{4,7},{5,6},{6,5},{7,4},{8,11},{9,10},{10,... | collective-permute-start | bytes 589832 | tf_op jit(solution)/shard_map/ppermute | solution.py:474
  44.0 11.3 %collective-permute-start.16 = (bf16[128,1408]{1,0:T(8,128)(2,1)S(1)}, bf16[128,1408]{1,0:T(8,128)(2,1)S(1)}, u32[]{:S(2)}, u32[]{:S(2)}) collective-permute-start(bf16[128,1408]{1,0:T(8,128)(2,1)S(1)} %get-tuple-element.51), channel_id=1, source_target_pairs={{0,1},{1,0},{2,3},{3,2},{4,5},{5,4},{6,7},{7,6},{8,9},{9,8},{10,11... | collective-permute-start | bytes 1081352 | tf_op jit(solution)/shard_map/ppermute | solution.py:474
  45.5 18.0 %collective-permute-start.17 = (bf16[128,1408]{1,0:T(8,128)(2,1)S(1)}, bf16[128,1408]{1,0:T(8,128)(2,1)S(1)}, u32[]{:S(2)}, u32[]{:S(2)}) collective-permute-start(bf16[128,1408]{1,0:T(8,128)(2,1)S(1)} %get-tuple-element.53), channel_id=1, source_target_pairs={{0,2},{1,3},{2,0},{3,1},{4,6},{5,7},{6,4},{7,5},{8,10},{9,11},{10,... | collective-permute-start | bytes 1081352 | tf_op jit(solution)/shard_map/ppermute | solution.py:474
  47.5 15.9 %collective-permute-start.18 = (bf16[128,1408]{1,0:T(8,128)(2,1)S(1)}, bf16[128,1408]{1,0:T(8,128)(2,1)S(1)}, u32[]{:S(2)}, u32[]{:S(2)}) collective-permute-start(bf16[128,1408]{1,0:T(8,128)(2,1)S(1)} %get-tuple-element.54), channel_id=1, source_target_pairs={{0,3},{1,2},{2,1},{3,0},{4,7},{5,6},{6,5},{7,4},{8,11},{9,10},{10,... | collective-permute-start | bytes 1081352 | tf_op jit(solution)/shard_map/ppermute | solution.py:474
  66.2 6.9 %collective-permute-start.20 = (bf16[400,128]{1,0:T(8,128)(2,1)S(1)}, bf16[400,128]{1,0:T(8,128)(2,1)S(1)}, u32[]{:S(2)}, u32[]{:S(2)}) collective-permute-start(bf16[400,128]{1,0:T(8,128)(2,1)S(1)} %get-tuple-element.63), channel_id=1, source_target_pairs={{0,8},{4,12},{8,0},{12,4},{16,24},{20,28},{24,16},{28,20},{1,9},{5... | collective-permute-start | bytes 307208 | tf_op jit(solution)/shard_map/ppermute | solution.py:477
  67.5 10.6 %collective-permute-start.21 = (bf16[400,128]{1,0:T(8,128)(2,1)S(1)}, bf16[400,128]{1,0:T(8,128)(2,1)S(1)}, u32[]{:S(2)}, u32[]{:S(2)}) collective-permute-start(bf16[400,128]{1,0:T(8,128)(2,1)S(1)} %get-tuple-element.64), channel_id=1, source_target_pairs={{0,16},{4,20},{8,24},{12,28},{16,0},{20,4},{24,8},{28,12},{1,17},{... | collective-permute-start | bytes 307208 | tf_op jit(solution)/shard_map/ppermute | solution.py:477
  67.5 10.5 %collective-permute-start.22 = (bf16[400,128]{1,0:T(8,128)(2,1)S(1)}, bf16[400,128]{1,0:T(8,128)(2,1)S(1)}, u32[]{:S(2)}, u32[]{:S(2)}) collective-permute-start(bf16[400,128]{1,0:T(8,128)(2,1)S(1)} %get-tuple-element.65), channel_id=1, source_target_pairs={{0,24},{4,28},{8,16},{12,20},{16,8},{20,12},{24,0},{28,4},{1,25},{... | collective-permute-start | bytes 307208 | tf_op jit(solution)/shard_map/ppermute | solution.py:477
  78.1 13.2 %collective-permute-start.23 = (bf16[4,128,768]{2,1,0:T(8,128)(2,1)S(1)}, bf16[4,128,768]{2,1,0:T(8,128)(2,1)S(1)}, u32[]{:S(2)}, u32[]{:S(2)}) collective-permute-start(bf16[4,128,768]{2,1,0:T(8,128)(2,1)S(1)} %shard_map.141), channel_id=1, source_target_pairs={{0,4},{4,0},{8,12},{12,8},{16,20},{20,16},{24,28},{28,24},{1,5},{5... | collective-permute-start | bytes 2359304 | tf_op jit(solution)/shard_map/ppermute | solution.py:480
  78.3 8.4 %collective-permute-start.25 = (bf16[400,128]{1,0:T(8,128)(2,1)S(1)}, bf16[400,128]{1,0:T(8,128)(2,1)S(1)}, u32[]{:S(2)}, u32[]{:S(2)}) collective-permute-start(bf16[400,128]{1,0:T(8,128)(2,1)S(1)} %shard_map.142.refs_0_), channel_id=1, source_target_pairs={{0,16},{4,20},{8,24},{12,28},{16,0},{20,4},{24,8},{28,12},{1,17},{... | collective-permute-start | bytes 307208 | tf_op jit(solution)/shard_map/ppermute | solution.py:477
  80.2 6.9 %collective-permute-start.24 = (bf16[400,128]{1,0:T(8,128)(2,1)S(1)}, bf16[400,128]{1,0:T(8,128)(2,1)S(1)}, u32[]{:S(2)}, u32[]{:S(2)}) collective-permute-start(bf16[400,128]{1,0:T(8,128)(2,1)S(1)} %shard_map.142.refs_0_), channel_id=1, source_target_pairs={{0,8},{4,12},{8,0},{12,4},{16,24},{20,28},{24,16},{28,20},{1,9},{5... | collective-permute-start | bytes 307208 | tf_op jit(solution)/shard_map/ppermute | solution.py:477
  91.5 9.5 %collective-permute-start.27 = (bf16[2,128,768]{2,1,0:T(8,128)(2,1)S(1)}, bf16[2,128,768]{2,1,0:T(8,128)(2,1)S(1)}, u32[]{:S(2)}, u32[]{:S(2)}) collective-permute-start(bf16[2,128,768]{2,1,0:T(8,128)(2,1)S(1)} %get-tuple-element.68.refs_4_), channel_id=1, source_target_pairs={{0,8},{4,12},{8,0},{12,4},{16,24},{20,28},{24,16},{28,20},{1,9},{5... | collective-permute-start | bytes 1179656 | tf_op jit(solution)/shard_map/ppermute | solution.py:477
  91.9 10.7 %collective-permute-start.31 = (bf16[4,400,128]{2,1,0:T(8,128)(2,1)S(1)}, bf16[4,400,128]{2,1,0:T(8,128)(2,1)S(1)}, u32[]{:S(2)}, u32[]{:S(2)}) collective-permute-start(bf16[4,400,128]{2,1,0:T(8,128)(2,1)S(1)} %shard_map.146.refs_0_), channel_id=1, source_target_pairs={{0,2},{1,3},{2,0},{3,1},{4,6},{5,7},{6,4},{7,5},{8,10},{9,11},{10,... | collective-permute-start | bytes 1228808 | tf_op jit(solution)/shard_map/ppermute | solution.py:474
  92.6 10.7 %collective-permute-start.29 = (bf16[4,400,128]{2,1,0:T(8,128)(2,1)S(1)}, bf16[4,400,128]{2,1,0:T(8,128)(2,1)S(1)}, u32[]{:S(2)}, u32[]{:S(2)}) collective-permute-start(bf16[4,400,128]{2,1,0:T(8,128)(2,1)S(1)} %shard_map.146.refs_0_), channel_id=1, source_target_pairs={{0,1},{1,0},{2,3},{3,2},{4,5},{5,4},{6,7},{7,6},{8,9},{9,8},{10,11... | collective-permute-start | bytes 1228808 | tf_op jit(solution)/shard_map/ppermute | solution.py:474
  101.1 9.3 %collective-permute-start.28 = (bf16[1,128,768]{2,1,0:T(8,128)(2,1)S(1)}, bf16[1,128,768]{2,1,0:T(8,128)(2,1)S(1)}, u32[]{:S(2)}, u32[]{:S(2)}) collective-permute-start(bf16[1,128,768]{2,1,0:T(8,128)(2,1)S(1)} %get-tuple-element.70), channel_id=1, source_target_pairs={{0,16},{4,20},{8,24},{12,28},{16,0},{20,4},{24,8},{28,12},{1,17},{... | collective-permute-start | bytes 589832 | tf_op jit(solution)/shard_map/ppermute | solution.py:477
  102.7 9.0 %collective-permute-start.33 = (bf16[4,400,128]{2,1,0:T(8,128)(2,1)S(1)}, bf16[4,400,128]{2,1,0:T(8,128)(2,1)S(1)}, u32[]{:S(2)}, u32[]{:S(2)}) collective-permute-start(bf16[4,400,128]{2,1,0:T(8,128)(2,1)S(1)} %shard_map.146.refs_0_), channel_id=1, source_target_pairs={{0,4},{4,0},{8,12},{12,8},{16,20},{20,16},{24,28},{28,24},{1,5},{5... | collective-permute-start | bytes 1228808 | tf_op jit(solution)/shard_map/ppermute | solution.py:480
  102.7 7.7 %collective-permute-start.32 = (bf16[2,400,128]{2,1,0:T(8,128)(2,1)S(1)}, bf16[2,400,128]{2,1,0:T(8,128)(2,1)S(1)}, u32[]{:S(2)}, u32[]{:S(2)}) collective-permute-start(bf16[2,400,128]{2,1,0:T(8,128)(2,1)S(1)} %slice.15), channel_id=1, source_target_pairs={{0,1},{1,0},{2,3},{3,2},{4,5},{5,4},{6,7},{7,6},{8,9},{9,8},{10,11... | collective-permute-start | bytes 614408 | tf_op jit(solution)/shard_map/ppermute | solution.py:474
  103.3 7.5 %collective-permute-start.30 = (bf16[2,400,128]{2,1,0:T(8,128)(2,1)S(1)}, bf16[2,400,128]{2,1,0:T(8,128)(2,1)S(1)}, u32[]{:S(2)}, u32[]{:S(2)}) collective-permute-start(bf16[2,400,128]{2,1,0:T(8,128)(2,1)S(1)} %slice.14), channel_id=1, source_target_pairs={{0,2},{1,3},{2,0},{3,1},{4,6},{5,7},{6,4},{7,5},{8,10},{9,11},{10,... | collective-permute-start | bytes 614408 | tf_op jit(solution)/shard_map/ppermute | solution.py:474
  105.3 7.2 %collective-permute-start.35 = (bf16[4,400,128]{2,1,0:T(8,128)(2,1)S(1)}, bf16[4,400,128]{2,1,0:T(8,128)(2,1)S(1)}, u32[]{:S(2)}, u32[]{:S(2)}) collective-permute-start(bf16[4,400,128]{2,1,0:T(8,128)(2,1)S(1)} %collective-permute-done.31.refs_2_), channel_id=1, source_target_pairs={{0,4},{4,0},{8,12},{12,8},{16,20},{20,16},{24,28},{28,24},{1,5},{5... | collective-permute-start | bytes 1228808 | tf_op jit(solution)/shard_map/ppermute | solution.py:480
  (23 other events, 93.2 us)

commit v12 on v10

--- a/solution.py
+++ b/solution.py
@@ -224,7 +224,7 @@
     return jnp.concatenate([high, total - high], axis=0)
 
 
-def weight_parts(packs, sums, rs, xr, nc, after):
+def weight_parts(packs, sums, rs, xr, nc):
     cs = len(packs)
     hid = sums.shape[1]
     nd, xw = packs[0].shape[0], packs[0].shape[1] - hid
@@ -253,23 +253,21 @@
         [*packs, sums],
         [pltpu.VMEM((xw, hid), F32)],
         flops=2 * cs * nd * xw * hid,
-        after=after,
-    )
-
-
-def scaled_parts(packs, first, inverse, turned_neigh, turned_self, cs, rs, after=()):
-    count = len(packs)
+    )
+
+
+def scaled_parts(packs, inverse, turned_neigh, turned_self, rs, after):
+    cs = len(packs)
     nd = packs[0].shape[0]
     hid, depth = turned_neigh.shape
 
     def body(neigh_ref, own_ref, inv_ref, *refs):
-        pack_refs, scaled_ref, self_ref = refs[:count], refs[count], refs[count + 1]
+        pack_refs, scaled_ref, self_ref = refs[:cs], refs[cs], refs[cs + 1]
         i, j = lax.axis_index("row"), lax.axis_index("col")
         grads = jnp.concatenate([r[:, :hid] for r in pack_refs], axis=0)
         product = mm(grads, neigh_ref[...])
-        for r in range(count):
-            start = pl.multiple_of((j ^ (first + r)) * nd, nd)
-            inv = inv_ref[pl.ds(start, nd), :]
+        for r in range(cs):
+            inv = inv_ref[pl.ds(pl.multiple_of((j ^ r) * nd, nd), nd), :]
             inv = jnp.concatenate([inv] * (depth // LANES), axis=1)
             rows = slice(r * nd, (r + 1) * nd)
             scaled_ref[rows, :] = (product[rows] * inv).astype(BF16)
@@ -280,9 +278,9 @@
 
     return call(
         body,
-        [shape((count * nd, depth), BF16), shape((count * nd, depth), F32)],
+        [shape((cs * nd, depth), BF16), shape((cs * nd, depth), F32)],
         [turned_neigh, turned_self, inverse, *packs],
-        flops=4 * count * nd * hid * depth,
+        flops=4 * cs * nd * hid * depth,
         after=after,
     )
 
@@ -296,26 +294,21 @@
     return order
 
 
-def back_parts(turned, scaled, self_parts, nd, cs, rs, after):
-    depth = scaled[0].shape[1]
+def back_parts(turned, scaled, self_part, nd, cs, rs, after):
+    depth = scaled.shape[1]
     half = rs // 2
-    count = len(scaled)
-    each = cs // count
-
-    def body(tile_ref, *refs):
-        scaled_refs, self_refs = refs[:count], refs[count : 2 * count]
-        keep_ref, send_ref, acc = refs[2 * count :]
+
+    def body(tile_ref, scaled_ref, self_ref, keep_ref, send_ref, acc):
         i, j = lax.axis_index("row"), lax.axis_index("col")
         z, c = i // 2, lax.rem(i, 2)
-        acc[...] = mm(tile_ref[...], jnp.concatenate([r[...] for r in scaled_refs], axis=0))
+        acc[...] = mm(tile_ref[...], scaled_ref[...])
 
         @pl.when(i * cs // rs == j)
         def _():
             for r in range(cs):
                 q = i * cs - j * rs + (j ^ r)
                 place = ((z ^ (q // 2)) + half * (lax.rem(q, 2) ^ c)) * nd
-                rows = slice(r % each * nd, (r % each + 1) * nd)
-                acc[pl.ds(pl.multiple_of(place, nd), nd), :] += self_refs[r // each][rows]
+                acc[pl.ds(pl.multiple_of(place, nd), nd), :] += self_ref[r * nd : (r + 1) * nd]
 
         for ref, base in ((send_ref, half), (keep_ref, 0)):
             for k, distance in enumerate(halving_order(half)):
@@ -326,7 +319,7 @@
     return call(
         body,
         [shape(dims, F32), shape(dims, BF16)],
-        [turned, *scaled, *self_parts],
+        [turned, scaled, self_part],
         [pltpu.VMEM((rs * nd, depth), F32)],
         flops=2 * turned.size * depth,
         after=after,
@@ -551,24 +544,21 @@
     own = jnp.dot(own_feat, w_self, preferred_element_type=F32).astype(BF16)
 
     turned_neigh, turned_self = turn([w_neigh, w_self], [parts[0]])
-    parts = [parts[0]] + [along_col(parts[k], k) for k in range(1, cs)]
+    parts = [parts[0]] + [along_col(parts[k], k) for k in range(cs - 1, 0, -1)]
     output, sums, *packs = activation(
         parts, masses, own, own_feat, w_neigh, bias[None, :], cotangent, [turned_neigh]
     )
-    packs = [packs[0]] + [along_col(packs[k], k) for k in range(1, cs)]
-
-    mid = cs // 2
-    scaled_args = (inverse, turned_neigh, turned_self, cs, rs)
-    early = scaled_parts(packs[:mid], 0, *scaled_args)
-    keep, send = weight_parts(packs, sums, rs, xr, nc, early[:1])
+    packs = [packs[0]] + [along_col(packs[k], k) for k in range(cs - 1, 0, -1)]
+
+    keep, send = weight_parts(packs, sums, rs, xr, nc)
+    packs = [packs[0]] + packs[:0:-1]
     came = other_core(send)
-    late = scaled_parts(packs[mid:], mid, *scaled_args, [keep])
-    scaled, self_parts = zip(early, late)
+    scaled, self_part = scaled_parts(packs, inverse, turned_neigh, turned_self, rs, [keep])
     chunks = pair_sum(keep, came)
-    chunks = [chunks[0]] + [along_chips(chunks[k], k) for k in range(1, half)]
+    chunks = [chunks[0]] + [along_chips(chunks[k], k) for k in range(half - 1, 0, -1)]
     line = gather_chips(last_sum(chunks))
 
-    keep, send = back_parts(turned, scaled, self_parts, nd, cs, rs, [keep])
+    keep, send = back_parts(turned, scaled, self_part, nd, cs, rs, [keep])
     keep, send = fold(keep, other_core(follow(send, chunks[1:])), line[1:])
     line = stack(line, after=[send])
     step = 1

time: 115 us -> 116 us (level)
  waiting for transfers between devices: 56.9 us -> 59.2 us
    ppermute x12, waiting for transfers between devices: 22.4 us -> 24.7 us  [along_col(): return lax.ppermute(x, 'col', [(s, s ^ k) for s in range(cs)])]
    pallas_call x18 -> x17, Pallas kernels: 11 us -> 10.7 us  [call(): pl.pallas_call(run, out_shape=outs, in_specs=[SMEM] * smem + [VMEM] * (co...]
  transfers between devices with their start and end apart: 38 -> 38, of which waited for: 13 -> 16; matrix products, arithmetic and copies ran while one was open for 1% -> 1% of each run, Pallas kernels for 9% -> 9%
where the time goes in v12:
time: 116 us
  waiting for transfers between devices  59.2 us (51%)
  starting transfers between devices  37 us (32%)
  Pallas kernels  15 us (13%)
  local copies, waits for them, and re-layouts  2.62 us (2%)
  between operations  1.65 us (1%)
    ppermute x11, waiting for transfers between devices, along_chips(): return lax.ppermute(x, 'row', [(s, s ^ 2 * k) for s in range(rs)])  32.7 us
    ppermute x12, waiting for transfers between devices, along_col(): return lax.ppermute(x, 'col', [(s, s ^ k) for s in range(cs)])  24.7 us
    ppermute x11, starting transfers between devices, along_chips(): return lax.ppermute(x, 'row', [(s, s ^ 2 * k) for s in range(rs)])  14.9 us
    ppermute x12, starting transfers between devices, along_col(): return lax.ppermute(x, 'col', [(s, s ^ k) for s in range(cs)])  12.5 us
    pallas_call x17, Pallas kernels, call(): pl.pallas_call(run, out_shape=outs, in_specs=[SMEM] * smem + [VMEM] * (co...  10.7 us
    ppermute x4, starting transfers between devices, send_own(): return lax.ppermute(block, ('row', 'col'), pairs)  7.02 us
    pallas_call x2, Pallas kernels, assemble(): pl.pallas_call(run, out_shape=[weight, weight, shape((1, hid), F32)], in_...  4.22 us
    ppermute x11, starting transfers between devices, other_core(): return lax.ppermute(x, 'row', [(s, s ^ 1) for s in range(rs)])  2.63 us
  transfers between devices with their start and end apart: 38, of which 16 were waited for; matrix products, arithmetic and copies ran while one was open for 1% of the time, Pallas kernels for 9%

profile of v12, /device:TPU:0, one launch (start us, length us, event | category | flops | bytes accessed | tf_op | source)
XLA Modules:
  0.0 115.8 jit_solution(16712324428698518262)
XLA Ops:
  0.6 4.1 %collective-permute-start.1 = (bf16[128,768]{1,0:T(8,128)(2,1)}, bf16[128,768]{1,0:T(8,128)(2,1)S(1)}, u32[]{:S(2)}, u32[]{:S(2)}) collective-permute-start(bf16[128,768]{1,0:T(8,128)(2,1)} %refs_1_.2), channel_id=1, source_target_pairs={{0,16},{4,20},{8,24},{12,28},{16,0},{20,4},{24,8},{28,12},{1,17},{... | collective-permute-start | bytes 589832 | tf_op jit(solution)/shard_map/ppermute | solution.py:470
  4.7 1.6 %collective-permute-start = (bf16[128,768]{1,0:T(8,128)(2,1)}, bf16[128,768]{1,0:T(8,128)(2,1)S(1)}, u32[]{:S(2)}, u32[]{:S(2)}) collective-permute-start(bf16[128,768]{1,0:T(8,128)(2,1)} %refs_1_.2), channel_id=1, source_target_pairs={{0,8},{4,12},{8,0},{12,4},{16,24},{20,28},{24,16},{28,20},{1,9},{5... | collective-permute-start | bytes 589832 | tf_op jit(solution)/shard_map/ppermute | solution.py:470
  9.4 1.6 %shard_map.128 = (bf16[512,1024]{1,0:T(8,128)(2,1)S(1)}, bf16[1024,512]{1,0:T(8,128)(2,1)S(1)}) custom-call(s32[24]{0:T(128)S(1)} %bitcast.12, s32[24]{0:T(128)S(1)} %bitcast.13, s32[1]{0:T(128)} %bitcast.9.refs_2_, bf16[24,128,128]{2,1,0:T(8,128)(2,1)S(1)} %bitcast.10), custom_call_target="tpu_custom_call" | custom-call | flops 524288 | bytes 2883780 | tf_op jit(solution)/shard_map/pallas_call | solution.py:32
  15.7 2.7 %collective-permute-start.6 = (bf16[128,768]{1,0:T(8,128)(2,1)S(1)}, bf16[128,768]{1,0:T(8,128)(2,1)S(1)}, u32[]{:S(2)}, u32[]{:S(2)}) collective-permute-start(bf16[128,768]{1,0:T(8,128)(2,1)S(1)} %collective-permute-done.refs_2_), channel_id=1, source_target_pairs={{0,2},{4,3},{9,8},{13,9},{18,22},{22,23},{27,28},{31,29}} | collective-permute-start | bytes 589832 | tf_op jit(solution)/shard_map/ppermute | solution.py:492
  19.6 2.0 %collective-permute-done.7.refs_2_ = bf16[128,768]{1,0:T(8,128)(2,1)S(1)} collective-permute-done((bf16[128,768]{1,0:T(8,128)(2,1)S(1)}, bf16[128,768]{1,0:T(8,128)(2,1)S(1)}, u32[]{:S(2)}, u32[]{:S(2)}) %collective-permute-start.7) | collective-permute-done | bytes 196640 | tf_op jit(solution)/shard_map/ppermute | solution.py:470
  22.6 2.4 %collective-permute-start.10 = (bf16[128,768]{1,0:T(8,128)(2,1)S(1)}, bf16[128,768]{1,0:T(8,128)(2,1)S(1)}, u32[]{:S(2)}, u32[]{:S(2)}) collective-permute-start(bf16[128,768]{1,0:T(8,128)(2,1)S(1)} %shard_map.131), channel_id=1, source_target_pairs={{0,4},{4,5},{9,14},{13,15},{18,16},{22,17},{27,26},{31,27}} | collective-permute-start | bytes 589832 | tf_op jit(solution)/shard_map/ppermute | solution.py:492
  28.3 2.0 %collective-permute-start.12 = (bf16[128,768]{1,0:T(8,128)(2,1)S(1)}, bf16[128,768]{1,0:T(8,128)(2,1)S(1)}, u32[]{:S(2)}, u32[]{:S(2)}) collective-permute-start(bf16[128,768]{1,0:T(8,128)(2,1)S(1)} %get-tuple-element.42), channel_id=1, source_target_pairs={{0,2},{1,3},{2,0},{3,1},{4,6},{5,7},{6,4},{7,5},{8,10},{9,11},{10,... | collective-permute-start | bytes 589832 | tf_op jit(solution)/shard_map/ppermute | solution.py:467
  31.7 3.3 %collective-permute-done.11.refs_1_ = bf16[128,768]{1,0:T(8,128)(2,1)S(1)} collective-permute-done((bf16[128,768]{1,0:T(8,128)(2,1)S(1)}, bf16[128,768]{1,0:T(8,128)(2,1)S(1)}, u32[]{:S(2)}, u32[]{:S(2)}) %collective-permute-start.11) | collective-permute-done | bytes 196640 | tf_op jit(solution)/shard_map/ppermute | solution.py:467
  35.0 4.7 %collective-permute-done.12.refs_2_ = bf16[128,768]{1,0:T(8,128)(2,1)S(1)} collective-permute-done((bf16[128,768]{1,0:T(8,128)(2,1)S(1)}, bf16[128,768]{1,0:T(8,128)(2,1)S(1)}, u32[]{:S(2)}, u32[]{:S(2)}) %collective-permute-start.12) | collective-permute-done | bytes 196640 | tf_op jit(solution)/shard_map/ppermute | solution.py:467
  41.5 1.6 %collective-permute-start.16 = (bf16[128,1408]{1,0:T(8,128)(2,1)S(1)}, bf16[128,1408]{1,0:T(8,128)(2,1)S(1)}, u32[]{:S(2)}, u32[]{:S(2)}) collective-permute-start(bf16[128,1408]{1,0:T(8,128)(2,1)S(1)} %get-tuple-element.49), channel_id=1, source_target_pairs={{0,1},{1,0},{2,3},{3,2},{4,5},{5,4},{6,7},{7,6},{8,9},{9,8},{10,11... | collective-permute-start | bytes 1081352 | tf_op jit(solution)/shard_map/ppermute | solution.py:467
  45.0 7.8 %collective-permute-done.16.refs_3_.refs_4_ = bf16[128,1408]{1,0:T(8,128)(2,1)S(1)} collective-permute-done((bf16[128,1408]{1,0:T(8,128)(2,1)S(1)}, bf16[128,1408]{1,0:T(8,128)(2,1)S(1)}, u32[]{:S(2)}, u32[]{:S(2)}) %collective-permute-start.16) | collective-permute-done | bytes 360480 | tf_op jit(solution)/shard_map/ppermute | solution.py:467
  52.8 8.2 %collective-permute-done.17.refs_2_.refs_5_ = bf16[128,1408]{1,0:T(8,128)(2,1)S(1)} collective-permute-done((bf16[128,1408]{1,0:T(8,128)(2,1)S(1)}, bf16[128,1408]{1,0:T(8,128)(2,1)S(1)}, u32[]{:S(2)}, u32[]{:S(2)}) %collective-permute-start.17) | collective-permute-done | bytes 360480 | tf_op jit(solution)/shard_map/ppermute | solution.py:467
  61.9 1.7 %collective-permute-done.19.refs_1_ = bf16[4,400,128]{2,1,0:T(8,128)(2,1)S(1)} collective-permute-done((bf16[4,400,128]{2,1,0:T(8,128)(2,1)S(1)}, bf16[4,400,128]{2,1,0:T(8,128)(2,1)S(1)}, u32[]{:S(2)}, u32[]{:S(2)}) %collective-permute-start.19) | collective-permute-done | bytes 409632 | tf_op jit(solution)/shard_map/ppermute | solution.py:473
  63.7 2.2 %collective-permute-start.20 = (bf16[400,128]{1,0:T(8,128)(2,1)S(1)}, bf16[400,128]{1,0:T(8,128)(2,1)S(1)}, u32[]{:S(2)}, u32[]{:S(2)}) collective-permute-start(bf16[400,128]{1,0:T(8,128)(2,1)S(1)} %get-tuple-element.59), channel_id=1, source_target_pairs={{0,24},{4,28},{8,16},{12,20},{16,8},{20,12},{24,0},{28,4},{1,25},{... | collective-permute-start | bytes 307208 | tf_op jit(solution)/shard_map/ppermute | solution.py:470
  68.3 2.0 %shard_map.136 = (bf16[512,768]{1,0:T(8,128)(2,1)S(1)}, f32[512,768]{1,0:T(8,128)S(1)}) custom-call(bf16[1024,768]{1,0:T(8,128)(2,1)S(1)} %get-tuple-element.44.refs_11_.refs_0_, bf16[1024,768]{1,0:T(8,128)(2,1)S(1)} %get-tuple-element.47.refs_1_, f32[512,128]{1,0:T(8,128)S(1)} %broadcast_in_dim.10.refs_2_, ...), custom_call_target="tpu_custom_call" | custom-call | flops 1610612736 | bytes 7208960 | tf_op jit(solution)/shard_map/pallas_call | solution.py:32
  71.6 4.6 %collective-permute-done.21.refs_2_ = bf16[400,128]{1,0:T(8,128)(2,1)S(1)} collective-permute-done((bf16[400,128]{1,0:T(8,128)(2,1)S(1)}, bf16[400,128]{1,0:T(8,128)(2,1)S(1)}, u32[]{:S(2)}, u32[]{:S(2)}) %collective-permute-start.21) | collective-permute-done | bytes 102432 | tf_op jit(solution)/shard_map/ppermute | solution.py:470
  76.5 3.0 %collective-permute-start.24 = (bf16[400,128]{1,0:T(8,128)(2,1)S(1)}, bf16[400,128]{1,0:T(8,128)(2,1)S(1)}, u32[]{:S(2)}, u32[]{:S(2)}) collective-permute-start(bf16[400,128]{1,0:T(8,128)(2,1)S(1)} %shard_map.140.refs_0_), channel_id=1, source_target_pairs={{0,8},{4,12},{8,0},{12,4},{16,24},{20,28},{24,16},{28,20},{1,9},{5... | collective-permute-start | bytes 307208 | tf_op jit(solution)/shard_map/ppermute | solution.py:470
  79.5 5.3 %collective-permute-done.25.refs_3_.refs_2_ = bf16[400,128]{1,0:T(8,128)(2,1)S(1)} collective-permute-done((bf16[400,128]{1,0:T(8,128)(2,1)S(1)}, bf16[400,128]{1,0:T(8,128)(2,1)S(1)}, u32[]{:S(2)}, u32[]{:S(2)}) %collective-permute-start.25) | collective-permute-done | bytes 102432 | tf_op jit(solution)/shard_map/ppermute | solution.py:470
  84.9 4.6 %collective-permute-done.26.refs_4_.refs_3_ = bf16[400,128]{1,0:T(8,128)(2,1)S(1)} collective-permute-done((bf16[400,128]{1,0:T(8,128)(2,1)S(1)}, bf16[400,128]{1,0:T(8,128)(2,1)S(1)}, u32[]{:S(2)}, u32[]{:S(2)}) %collective-permute-start.26) | collective-permute-done | bytes 102432 | tf_op jit(solution)/shard_map/ppermute | solution.py:470
  91.9 8.1 %collective-permute-done.27.refs_1_ = bf16[2,128,768]{2,1,0:T(8,128)(2,1)S(1)} collective-permute-done((bf16[2,128,768]{2,1,0:T(8,128)(2,1)S(1)}, bf16[2,128,768]{2,1,0:T(8,128)(2,1)S(1)}, u32[]{:S(2)}, u32[]{:S(2)}) %collective-permute-start.27) | collective-permute-done | bytes 393248 | tf_op jit(solution)/shard_map/ppermute | solution.py:470
  101.5 1.5 %collective-permute-start.34 = (bf16[2,400,128]{2,1,0:T(8,128)(2,1)S(1)}, bf16[2,400,128]{2,1,0:T(8,128)(2,1)S(1)}, u32[]{:S(2)}, u32[]{:S(2)}) collective-permute-start(bf16[2,400,128]{2,1,0:T(8,128)(2,1)S(1)} %slice.14), channel_id=1, source_target_pairs={{0,2},{1,3},{2,0},{3,1},{4,6},{5,7},{6,4},{7,5},{8,10},{9,11},{10,... | collective-permute-start | bytes 614408 | tf_op jit(solution)/shard_map/ppermute | solution.py:467
  103.0 7.2 %collective-permute-done.28.refs_1_ = bf16[1,128,768]{2,1,0:T(8,128)(2,1)S(1)} collective-permute-done((bf16[1,128,768]{2,1,0:T(8,128)(2,1)S(1)}, bf16[1,128,768]{2,1,0:T(8,128)(2,1)S(1)}, u32[]{:S(2)}, u32[]{:S(2)}) %collective-permute-start.28) | collective-permute-done | bytes 196640 | tf_op jit(solution)/shard_map/ppermute | solution.py:470
  111.5 1.8 %shard_map.145 = (f32[768,1024]{1,0:T(8,128)}, f32[768,1024]{1,0:T(8,128)}, f32[1,1024]{1,0:T(1,128)S(1)}) custom-call(bf16[4,400,128]{2,1,0:T(8,128)(2,1)S(1)} %shard_map.144.refs_0_, bf16[4,400,128]{2,1,0:T(8,128)(2,1)S(1)} %collective-permute-done.30.refs_1_, bf16[4,400,128]{2,1,0:T(8,128)(2,1)S(1)} %collective-permute-done.32.refs_2_, ...), custom_call_target="tpu_custom_call" | custom-call | bytes 9437184 | tf_op jit(solution)/shard_map/pallas_call | solution.py:435
  113.4 2.4 %shard_map.146 = (f32[768,1024]{1,0:T(8,128)}, f32[768,1024]{1,0:T(8,128)}, f32[1,1024]{1,0:T(1,128)}) custom-call(bf16[4,400,128]{2,1,0:T(8,128)(2,1)S(1)} %collective-permute-done.29.refs_0_, bf16[4,400,128]{2,1,0:T(8,128)(2,1)S(1)} %collective-permute-done.31.refs_1_, ...), custom_call_target="tpu_custom_call", output_to_operand_aliasing={{0}: (5, {}), {1}: (6, {})} | custom-call | bytes 9437184 | tf_op jit(solution)/shard_map/pallas_call | solution.py:435
  (96 shorter events, 27.9 us)
Async XLA Ops:
  0.6 13.5 %collective-permute-start.1 = (bf16[128,768]{1,0:T(8,128)(2,1)}, bf16[128,768]{1,0:T(8,128)(2,1)S(1)}, u32[]{:S(2)}, u32[]{:S(2)}) collective-permute-start(bf16[128,768]{1,0:T(8,128)(2,1)} %refs_1_.2), channel_id=1, source_target_pairs={{0,16},{4,20},{8,24},{12,28},{16,0},{20,4},{24,8},{28,12},{1,17},{... | collective-permute-start | bytes 589832 | tf_op jit(solution)/shard_map/ppermute | solution.py:470
  4.7 10.9 %collective-permute-start = (bf16[128,768]{1,0:T(8,128)(2,1)}, bf16[128,768]{1,0:T(8,128)(2,1)S(1)}, u32[]{:S(2)}, u32[]{:S(2)}) collective-permute-start(bf16[128,768]{1,0:T(8,128)(2,1)} %refs_1_.2), channel_id=1, source_target_pairs={{0,8},{4,12},{8,0},{12,4},{16,24},{20,28},{24,16},{28,20},{1,9},{5... | collective-permute-start | bytes 589832 | tf_op jit(solution)/shard_map/ppermute | solution.py:470
  6.3 12.0 %collective-permute-start.2 = (bf16[128,768]{1,0:T(8,128)(2,1)}, bf16[128,768]{1,0:T(8,128)(2,1)S(1)}, u32[]{:S(2)}, u32[]{:S(2)}) collective-permute-start(bf16[128,768]{1,0:T(8,128)(2,1)} %refs_1_.2), channel_id=1, source_target_pairs={{0,4},{4,0},{8,12},{12,8},{16,20},{20,16},{24,28},{28,24},{1,5},{5... | collective-permute-start | bytes 589832 | tf_op jit(solution)/shard_map/ppermute | solution.py:473
  12.7 9.0 %collective-permute-start.5 = (bf16[128,768]{1,0:T(8,128)(2,1)S(1)}, bf16[128,768]{1,0:T(8,128)(2,1)S(1)}, u32[]{:S(2)}, u32[]{:S(2)}) collective-permute-start(bf16[128,768]{1,0:T(8,128)(2,1)S(1)} %copy-done.5), channel_id=1, source_target_pairs={{0,0},{4,1},{9,10},{13,11},{18,20},{22,21},{27,30},{31,31}} | collective-permute-start | bytes 589832 | tf_op jit(solution)/shard_map/ppermute | solution.py:492
  26.8 8.2 %collective-permute-start.11 = (bf16[128,768]{1,0:T(8,128)(2,1)S(1)}, bf16[128,768]{1,0:T(8,128)(2,1)S(1)}, u32[]{:S(2)}, u32[]{:S(2)}) collective-permute-start(bf16[128,768]{1,0:T(8,128)(2,1)S(1)} %get-tuple-element.41), channel_id=1, source_target_pairs={{0,3},{1,2},{2,1},{3,0},{4,7},{5,6},{6,5},{7,4},{8,11},{9,10},{10,... | collective-permute-start | bytes 589832 | tf_op jit(solution)/shard_map/ppermute | solution.py:467
  28.3 11.4 %collective-permute-start.12 = (bf16[128,768]{1,0:T(8,128)(2,1)S(1)}, bf16[128,768]{1,0:T(8,128)(2,1)S(1)}, u32[]{:S(2)}, u32[]{:S(2)}) collective-permute-start(bf16[128,768]{1,0:T(8,128)(2,1)S(1)} %get-tuple-element.42), channel_id=1, source_target_pairs={{0,2},{1,3},{2,0},{3,1},{4,6},{5,7},{6,4},{7,5},{8,10},{9,11},{10,... | collective-permute-start | bytes 589832 | tf_op jit(solution)/shard_map/ppermute | solution.py:467
  30.3 9.8 %collective-permute-start.13 = (bf16[128,768]{1,0:T(8,128)(2,1)S(1)}, bf16[128,768]{1,0:T(8,128)(2,1)S(1)}, u32[]{:S(2)}, u32[]{:S(2)}) collective-permute-start(bf16[128,768]{1,0:T(8,128)(2,1)S(1)} %get-tuple-element.43), channel_id=1, source_target_pairs={{0,1},{1,0},{2,3},{3,2},{4,5},{5,4},{6,7},{7,6},{8,9},{9,8},{10,11... | collective-permute-start | bytes 589832 | tf_op jit(solution)/shard_map/ppermute | solution.py:467
  41.5 11.3 %collective-permute-start.16 = (bf16[128,1408]{1,0:T(8,128)(2,1)S(1)}, bf16[128,1408]{1,0:T(8,128)(2,1)S(1)}, u32[]{:S(2)}, u32[]{:S(2)}) collective-permute-start(bf16[128,1408]{1,0:T(8,128)(2,1)S(1)} %get-tuple-element.49), channel_id=1, source_target_pairs={{0,1},{1,0},{2,3},{3,2},{4,5},{5,4},{6,7},{7,6},{8,9},{9,8},{10,11... | collective-permute-start | bytes 1081352 | tf_op jit(solution)/shard_map/ppermute | solution.py:467
  43.1 17.8 %collective-permute-start.17 = (bf16[128,1408]{1,0:T(8,128)(2,1)S(1)}, bf16[128,1408]{1,0:T(8,128)(2,1)S(1)}, u32[]{:S(2)}, u32[]{:S(2)}) collective-permute-start(bf16[128,1408]{1,0:T(8,128)(2,1)S(1)} %get-tuple-element.50), channel_id=1, source_target_pairs={{0,2},{1,3},{2,0},{3,1},{4,6},{5,7},{6,4},{7,5},{8,10},{9,11},{10,... | collective-permute-start | bytes 1081352 | tf_op jit(solution)/shard_map/ppermute | solution.py:467
  44.1 16.9 %collective-permute-start.18 = (bf16[128,1408]{1,0:T(8,128)(2,1)S(1)}, bf16[128,1408]{1,0:T(8,128)(2,1)S(1)}, u32[]{:S(2)}, u32[]{:S(2)}) collective-permute-start(bf16[128,1408]{1,0:T(8,128)(2,1)S(1)} %get-tuple-element.51), channel_id=1, source_target_pairs={{0,3},{1,2},{2,1},{3,0},{4,7},{5,6},{6,5},{7,4},{8,11},{9,10},{10,... | collective-permute-start | bytes 1081352 | tf_op jit(solution)/shard_map/ppermute | solution.py:467
  63.7 7.9 %collective-permute-start.20 = (bf16[400,128]{1,0:T(8,128)(2,1)S(1)}, bf16[400,128]{1,0:T(8,128)(2,1)S(1)}, u32[]{:S(2)}, u32[]{:S(2)}) collective-permute-start(bf16[400,128]{1,0:T(8,128)(2,1)S(1)} %get-tuple-element.59), channel_id=1, source_target_pairs={{0,24},{4,28},{8,16},{12,20},{16,8},{20,12},{24,0},{28,4},{1,25},{... | collective-permute-start | bytes 307208 | tf_op jit(solution)/shard_map/ppermute | solution.py:470
  65.9 10.4 %collective-permute-start.21 = (bf16[400,128]{1,0:T(8,128)(2,1)S(1)}, bf16[400,128]{1,0:T(8,128)(2,1)S(1)}, u32[]{:S(2)}, u32[]{:S(2)}) collective-permute-start(bf16[400,128]{1,0:T(8,128)(2,1)S(1)} %get-tuple-element.60), channel_id=1, source_target_pairs={{0,16},{4,20},{8,24},{12,28},{16,0},{20,4},{24,8},{28,12},{1,17},{... | collective-permute-start | bytes 307208 | tf_op jit(solution)/shard_map/ppermute | solution.py:470
  66.7 9.5 %collective-permute-start.22 = (bf16[400,128]{1,0:T(8,128)(2,1)S(1)}, bf16[400,128]{1,0:T(8,128)(2,1)S(1)}, u32[]{:S(2)}, u32[]{:S(2)}) collective-permute-start(bf16[400,128]{1,0:T(8,128)(2,1)S(1)} %get-tuple-element.61), channel_id=1, source_target_pairs={{0,8},{4,12},{8,0},{12,4},{16,24},{20,28},{24,16},{28,20},{1,9},{5... | collective-permute-start | bytes 307208 | tf_op jit(solution)/shard_map/ppermute | solution.py:470
  76.3 13.3 %collective-permute-start.23 = (bf16[4,128,768]{2,1,0:T(8,128)(2,1)S(1)}, bf16[4,128,768]{2,1,0:T(8,128)(2,1)S(1)}, u32[]{:S(2)}, u32[]{:S(2)}) collective-permute-start(bf16[4,128,768]{2,1,0:T(8,128)(2,1)S(1)} %shard_map.139), channel_id=1, source_target_pairs={{0,4},{4,0},{8,12},{12,8},{16,20},{20,16},{24,28},{28,24},{1,5},{5... | collective-permute-start | bytes 2359304 | tf_op jit(solution)/shard_map/ppermute | solution.py:473
  76.4 8.3 %collective-permute-start.25 = (bf16[400,128]{1,0:T(8,128)(2,1)S(1)}, bf16[400,128]{1,0:T(8,128)(2,1)S(1)}, u32[]{:S(2)}, u32[]{:S(2)}) collective-permute-start(bf16[400,128]{1,0:T(8,128)(2,1)S(1)} %shard_map.140.refs_0_), channel_id=1, source_target_pairs={{0,16},{4,20},{8,24},{12,28},{16,0},{20,4},{24,8},{28,12},{1,17},{... | collective-permute-start | bytes 307208 | tf_op jit(solution)/shard_map/ppermute | solution.py:470
  76.5 8.4 %collective-permute-start.24 = (bf16[400,128]{1,0:T(8,128)(2,1)S(1)}, bf16[400,128]{1,0:T(8,128)(2,1)S(1)}, u32[]{:S(2)}, u32[]{:S(2)}) collective-permute-start(bf16[400,128]{1,0:T(8,128)(2,1)S(1)} %shard_map.140.refs_0_), channel_id=1, source_target_pairs={{0,8},{4,12},{8,0},{12,4},{16,24},{20,28},{24,16},{28,20},{1,9},{5... | collective-permute-start | bytes 307208 | tf_op jit(solution)/shard_map/ppermute | solution.py:470
  89.7 10.2 %collective-permute-start.27 = (bf16[2,128,768]{2,1,0:T(8,128)(2,1)S(1)}, bf16[2,128,768]{2,1,0:T(8,128)(2,1)S(1)}, u32[]{:S(2)}, u32[]{:S(2)}) collective-permute-start(bf16[2,128,768]{2,1,0:T(8,128)(2,1)S(1)} %get-tuple-element.64.refs_4_), channel_id=1, source_target_pairs={{0,8},{4,12},{8,0},{12,4},{16,24},{20,28},{24,16},{28,20},{1,9},{5... | collective-permute-start | bytes 1179656 | tf_op jit(solution)/shard_map/ppermute | solution.py:470
  90.1 10.6 %collective-permute-start.32 = (bf16[4,400,128]{2,1,0:T(8,128)(2,1)S(1)}, bf16[4,400,128]{2,1,0:T(8,128)(2,1)S(1)}, u32[]{:S(2)}, u32[]{:S(2)}) collective-permute-start(bf16[4,400,128]{2,1,0:T(8,128)(2,1)S(1)} %shard_map.144.refs_0_), channel_id=1, source_target_pairs={{0,2},{1,3},{2,0},{3,1},{4,6},{5,7},{6,4},{7,5},{8,10},{9,11},{10,... | collective-permute-start | bytes 1228808 | tf_op jit(solution)/shard_map/ppermute | solution.py:467
  90.4 11.1 %collective-permute-start.30 = (bf16[4,400,128]{2,1,0:T(8,128)(2,1)S(1)}, bf16[4,400,128]{2,1,0:T(8,128)(2,1)S(1)}, u32[]{:S(2)}, u32[]{:S(2)}) collective-permute-start(bf16[4,400,128]{2,1,0:T(8,128)(2,1)S(1)} %shard_map.144.refs_0_), channel_id=1, source_target_pairs={{0,1},{1,0},{2,3},{3,2},{4,5},{5,4},{6,7},{7,6},{8,9},{9,8},{10,11... | collective-permute-start | bytes 1228808 | tf_op jit(solution)/shard_map/ppermute | solution.py:467
  100.0 10.2 %collective-permute-start.28 = (bf16[1,128,768]{2,1,0:T(8,128)(2,1)S(1)}, bf16[1,128,768]{2,1,0:T(8,128)(2,1)S(1)}, u32[]{:S(2)}, u32[]{:S(2)}) collective-permute-start(bf16[1,128,768]{2,1,0:T(8,128)(2,1)S(1)} %get-tuple-element.66), channel_id=1, source_target_pairs={{0,16},{4,20},{8,24},{12,28},{16,0},{20,4},{24,8},{28,12},{1,17},{... | collective-permute-start | bytes 589832 | tf_op jit(solution)/shard_map/ppermute | solution.py:470
  100.6 12.7 %collective-permute-start.29 = (bf16[4,400,128]{2,1,0:T(8,128)(2,1)S(1)}, bf16[4,400,128]{2,1,0:T(8,128)(2,1)S(1)}, u32[]{:S(2)}, u32[]{:S(2)}) collective-permute-start(bf16[4,400,128]{2,1,0:T(8,128)(2,1)S(1)} %shard_map.144.refs_0_), channel_id=1, source_target_pairs={{0,4},{4,0},{8,12},{12,8},{16,20},{20,16},{24,28},{28,24},{1,5},{5... | collective-permute-start | bytes 1228808 | tf_op jit(solution)/shard_map/ppermute | solution.py:473
  100.7 9.5 %collective-permute-start.36 = (bf16[2,400,128]{2,1,0:T(8,128)(2,1)S(1)}, bf16[2,400,128]{2,1,0:T(8,128)(2,1)S(1)}, u32[]{:S(2)}, u32[]{:S(2)}) collective-permute-start(bf16[2,400,128]{2,1,0:T(8,128)(2,1)S(1)} %slice.15), channel_id=1, source_target_pairs={{0,1},{1,0},{2,3},{3,2},{4,5},{5,4},{6,7},{7,6},{8,9},{9,8},{10,11... | collective-permute-start | bytes 614408 | tf_op jit(solution)/shard_map/ppermute | solution.py:467
  101.5 9.3 %collective-permute-start.34 = (bf16[2,400,128]{2,1,0:T(8,128)(2,1)S(1)}, bf16[2,400,128]{2,1,0:T(8,128)(2,1)S(1)}, u32[]{:S(2)}, u32[]{:S(2)}) collective-permute-start(bf16[2,400,128]{2,1,0:T(8,128)(2,1)S(1)} %slice.14), channel_id=1, source_target_pairs={{0,2},{1,3},{2,0},{3,1},{4,6},{5,7},{6,4},{7,5},{8,10},{9,11},{10,... | collective-permute-start | bytes 614408 | tf_op jit(solution)/shard_map/ppermute | solution.py:467
  103.0 10.4 %collective-permute-start.33 = (bf16[4,400,128]{2,1,0:T(8,128)(2,1)S(1)}, bf16[4,400,128]{2,1,0:T(8,128)(2,1)S(1)}, u32[]{:S(2)}, u32[]{:S(2)}) collective-permute-start(bf16[4,400,128]{2,1,0:T(8,128)(2,1)S(1)} %collective-permute-done.32.refs_2_), channel_id=1, source_target_pairs={{0,4},{4,0},{8,12},{12,8},{16,20},{20,16},{24,28},{28,24},{1,5},{5... | collective-permute-start | bytes 1228808 | tf_op jit(solution)/shard_map/ppermute | solution.py:473
  (23 other events, 100.1 us)

commit v13 on v10

--- a/solution.py
+++ b/solution.py
@@ -339,14 +339,9 @@
 
     def body(keep_ref, came_ref, *outs):
         total = keep_ref[...] + came_ref[...].astype(F32)
-        if count == 1:
-            outs[0][...] = total[0].astype(BF16)
-        else:
-            outs[0][...] = total[:half]
-            outs[1][...] = total[half:].astype(BF16)
-
-    if count == 1:
-        return call(body, [shape((rows, width), BF16)], [keep, came], after=after)[0]
+        outs[0][...] = total[:half]
+        outs[1][...] = total[half:].astype(BF16)
+
     dims = (half, rows, width)
     return call(body, [shape(dims, F32), shape(dims, BF16)], [keep, came], after=after)
 
@@ -386,21 +381,21 @@
     return call(body, [shape((rows, width), BF16)], parts)[0]
 
 
-def assemble(pieces, begun, depth, hid, xr, nc, cs, factors, after):
+def assemble(pieces, begun, depth, hid, xr, nc, cs, factors, after, adds=()):
     xw = 2 * depth // cs
     side = cs // 2
     copies = sum(len(where) for _, where, _ in pieces)
     arrays = [array for array, _, _ in pieces]
-    inputs = arrays + list(begun)
+    inputs = arrays + list(begun) + list(adds)
     weight = shape((depth, hid), F32)
 
     def body(*refs):
         piece_refs = refs[: len(pieces)]
-        self_ref, neigh_ref, bias_ref, staged, sems = refs[-5:]
+        self_ref, neigh_ref, bias_ref, *sum_ref, staged, sems = refs[len(inputs) :]
         i, j = lax.axis_index("row"), lax.axis_index("col")
         z, c = i // 2, lax.rem(i, 2)
         if begun:
-            bias_ref[...] = refs[len(inputs) - 1][...]
+            bias_ref[...] = refs[len(arrays) + 2][...]
         else:
             bias_ref[...] = jnp.zeros_like(bias_ref)
         waits = []
@@ -431,6 +426,9 @@
                     bias_ref[:, pl.ds(col, LANES)] += total
 
                 at += 1
+        if adds:
+            keep_ref, came_ref = refs[len(inputs) - 2 : len(inputs)]
+            sum_ref[0][...] = (keep_ref[0] + came_ref[0].astype(F32)).astype(BF16)
         for here, copy in waits:
             pl.when(here)(copy.wait)
 
@@ -438,14 +436,16 @@
         body(*refs[: len(inputs)], *refs[len(inputs) + len(after) :])
 
     somewhere = pl.BlockSpec(memory_space=pl.ANY)
+    sums = [shape(adds[0].shape[1:], BF16)] if adds else []
     moved = 2 * copies * xr * LANES * 6
     return pl.pallas_call(
         run,
-        out_shape=[weight, weight, shape((1, hid), F32)],
+        out_shape=[weight, weight, shape((1, hid), F32), *sums],
         in_specs=[VMEM] * len(arrays)
         + ([somewhere, somewhere, VMEM] if begun else [])
+        + [VMEM] * len(adds)
         + [somewhere] * len(after),
-        out_specs=[somewhere, somewhere, VMEM],
+        out_specs=[somewhere, somewhere, VMEM] + [VMEM] * len(sums),
         scratch_shapes=[
             pltpu.VMEM((copies, xr, LANES), F32),
             pltpu.SemaphoreType.DMA((copies,)),
@@ -565,18 +565,17 @@
     late = scaled_parts(packs[mid:], mid, *scaled_args, [keep])
     scaled, self_parts = zip(early, late)
     chunks = pair_sum(keep, came)
-    chunks = [chunks[0]] + [along_chips(chunks[k], k) for k in range(1, half)]
+    chunks = [chunks[0]] + [along_chips(chunks[k], k) for k in range(half - 1, 0, -1)]
     line = gather_chips(last_sum(chunks))
 
     keep, send = back_parts(turned, scaled, self_parts, nd, cs, rs, [keep])
     keep, send = fold(keep, other_core(follow(send, chunks[1:])), line[1:])
     line = stack(line, after=[send])
     step = 1
-    while step < half:
-        folded = fold(keep, along_chips(send, step))
-        keep, send = folded if 2 * step < half else (folded, None)
+    while 2 * step < half:
+        keep, send = fold(keep, along_chips(send, step))
         step *= 2
-    grad_input = keep
+    last = (keep, along_chips(send, step))
 
     def piece(array, first, column, mine):
         return array, [(first + t, column) for t in range(array.shape[0])], mine
@@ -591,9 +590,10 @@
         rest = [(along_col(line, cs - 1), 0, cs - 1)]
     factor = 1.0 / math.sqrt(nd * rs * cs)
     sizes = (depth, hid, xr, nc, cs, (factor, 32.0 * factor))
-    begun = assemble([piece(*x, True) for x in near + rest], (), *sizes, ())
+    pieces = [piece(*x, True) for x in near + rest]
+    *begun, grad_input = assemble(pieces, (), *sizes, (), last)
     pieces = [piece(other_core(x), *where, False) for x, *where in near + rest]
-    total_self, total_neigh, total_bias = assemble(pieces, begun, *sizes, [grad_input])
+    total_self, total_neigh, total_bias = assemble(pieces, begun, *sizes, ())
     return output, grad_input, total_self, total_neigh, total_bias.reshape(-1)
 
 

time: 115 us -> 115 us (level)
    ppermute x11, waiting for transfers between devices: 32.8 us -> 34 us  [along_chips(): return lax.ppermute(x, 'row', [(s, s ^ 2 * k) for s in range(rs)])]
    pallas_call x18 -> x17, Pallas kernels: 11 us -> 10.1 us  [call(): pl.pallas_call(run, out_shape=outs, in_specs=[SMEM] * smem + [VMEM] * (co...]
    unnamed x18 -> x16, local copies, waits for them, and re-layouts: 2.47 us -> 2.46 us
  transfers between devices with their start and end apart: 38 -> 38, of which waited for: 13 -> 14; matrix products, arithmetic and copies ran while one was open for 1% -> 1% of each run, Pallas kernels for 9% -> 9%
where the time goes in v13:
time: 115 us
  waiting for transfers between devices  57.7 us (50%)
  starting transfers between devices  37.1 us (32%)
  Pallas kernels  15 us (13%)
  local copies, waits for them, and re-layouts  2.61 us (2%)
  between operations  1.64 us (1%)
    ppermute x11, waiting for transfers between devices, along_chips(): return lax.ppermute(x, 'row', [(s, s ^ 2 * k) for s in range(rs)])  34 us
    ppermute x12, waiting for transfers between devices, along_col(): return lax.ppermute(x, 'col', [(s, s ^ k) for s in range(cs)])  22 us
    ppermute x11, starting transfers between devices, along_chips(): return lax.ppermute(x, 'row', [(s, s ^ 2 * k) for s in range(rs)])  14.9 us
    ppermute x12, starting transfers between devices, along_col(): return lax.ppermute(x, 'col', [(s, s ^ k) for s in range(cs)])  12.5 us
    pallas_call x17, Pallas kernels, call(): pl.pallas_call(run, out_shape=outs, in_specs=[SMEM] * smem + [VMEM] * (co...  10.1 us
    ppermute x4, starting transfers between devices, send_own(): return lax.ppermute(block, ('row', 'col'), pairs)  7.56 us
    pallas_call x2, Pallas kernels, assemble(): pl.pallas_call(run, out_shape=[weight, weight, shape((1, hid), F32), *sum...  4.89 us
    unnamed x16, local copies, waits for them, and re-layouts  2.46 us
  transfers between devices with their start and end apart: 38, of which 14 were waited for; matrix products, arithmetic and copies ran while one was open for 1% of the time, Pallas kernels for 9%

profile of v13, /device:TPU:0, one launch (start us, length us, event | category | flops | bytes accessed | tf_op | source)
XLA Modules:
  0.0 114.6 jit_solution(2935684989522557140)
XLA Ops:
  0.6 4.1 %collective-permute-start.1 = (bf16[128,768]{1,0:T(8,128)(2,1)}, bf16[128,768]{1,0:T(8,128)(2,1)S(1)}, u32[]{:S(2)}, u32[]{:S(2)}) collective-permute-start(bf16[128,768]{1,0:T(8,128)(2,1)} %refs_1_.2), channel_id=1, source_target_pairs={{0,16},{4,20},{8,24},{12,28},{16,0},{20,4},{24,8},{28,12},{1,17},{... | collective-permute-start | bytes 589832 | tf_op jit(solution)/shard_map/ppermute | solution.py:477
  4.7 1.6 %collective-permute-start = (bf16[128,768]{1,0:T(8,128)(2,1)}, bf16[128,768]{1,0:T(8,128)(2,1)S(1)}, u32[]{:S(2)}, u32[]{:S(2)}) collective-permute-start(bf16[128,768]{1,0:T(8,128)(2,1)} %refs_1_.2), channel_id=1, source_target_pairs={{0,8},{4,12},{8,0},{12,4},{16,24},{20,28},{24,16},{28,20},{1,9},{5... | collective-permute-start | bytes 589832 | tf_op jit(solution)/shard_map/ppermute | solution.py:477
  15.4 3.2 %collective-permute-start.6 = (bf16[128,768]{1,0:T(8,128)(2,1)S(1)}, bf16[128,768]{1,0:T(8,128)(2,1)S(1)}, u32[]{:S(2)}, u32[]{:S(2)}) collective-permute-start(bf16[128,768]{1,0:T(8,128)(2,1)S(1)} %collective-permute-done.refs_2_), channel_id=1, source_target_pairs={{0,2},{4,3},{9,8},{13,9},{18,22},{22,23},{27,28},{31,29}} | collective-permute-start | bytes 589832 | tf_op jit(solution)/shard_map/ppermute | solution.py:499
  19.5 2.3 %collective-permute-done.7.refs_2_ = bf16[128,768]{1,0:T(8,128)(2,1)S(1)} collective-permute-done((bf16[128,768]{1,0:T(8,128)(2,1)S(1)}, bf16[128,768]{1,0:T(8,128)(2,1)S(1)}, u32[]{:S(2)}, u32[]{:S(2)}) %collective-permute-start.7) | collective-permute-done | bytes 196640 | tf_op jit(solution)/shard_map/ppermute | solution.py:477
  22.8 2.4 %collective-permute-start.10 = (bf16[128,768]{1,0:T(8,128)(2,1)S(1)}, bf16[128,768]{1,0:T(8,128)(2,1)S(1)}, u32[]{:S(2)}, u32[]{:S(2)}) collective-permute-start(bf16[128,768]{1,0:T(8,128)(2,1)S(1)} %shard_map.131), channel_id=1, source_target_pairs={{0,4},{4,5},{9,14},{13,15},{18,16},{22,17},{27,26},{31,27}} | collective-permute-start | bytes 589832 | tf_op jit(solution)/shard_map/ppermute | solution.py:499
  27.0 1.6 %collective-permute-start.11 = (bf16[128,768]{1,0:T(8,128)(2,1)S(1)}, bf16[128,768]{1,0:T(8,128)(2,1)S(1)}, u32[]{:S(2)}, u32[]{:S(2)}) collective-permute-start(bf16[128,768]{1,0:T(8,128)(2,1)S(1)} %get-tuple-element.44), channel_id=1, source_target_pairs={{0,1},{1,0},{2,3},{3,2},{4,5},{5,4},{6,7},{7,6},{8,9},{9,8},{10,11... | collective-permute-start | bytes 589832 | tf_op jit(solution)/shard_map/ppermute | solution.py:474
  31.9 1.9 %collective-permute-done.11.refs_1_ = bf16[128,768]{1,0:T(8,128)(2,1)S(1)} collective-permute-done((bf16[128,768]{1,0:T(8,128)(2,1)S(1)}, bf16[128,768]{1,0:T(8,128)(2,1)S(1)}, u32[]{:S(2)}, u32[]{:S(2)}) %collective-permute-start.11) | collective-permute-done | bytes 196640 | tf_op jit(solution)/shard_map/ppermute | solution.py:474
  33.8 5.9 %collective-permute-done.12.refs_2_ = bf16[128,768]{1,0:T(8,128)(2,1)S(1)} collective-permute-done((bf16[128,768]{1,0:T(8,128)(2,1)S(1)}, bf16[128,768]{1,0:T(8,128)(2,1)S(1)}, u32[]{:S(2)}, u32[]{:S(2)}) %collective-permute-start.12) | collective-permute-done | bytes 196640 | tf_op jit(solution)/shard_map/ppermute | solution.py:474
  41.7 1.5 %collective-permute-start.17 = (bf16[128,1408]{1,0:T(8,128)(2,1)S(1)}, bf16[128,1408]{1,0:T(8,128)(2,1)S(1)}, u32[]{:S(2)}, u32[]{:S(2)}) collective-permute-start(bf16[128,1408]{1,0:T(8,128)(2,1)S(1)} %get-tuple-element.51), channel_id=1, source_target_pairs={{0,2},{1,3},{2,0},{3,1},{4,6},{5,7},{6,4},{7,5},{8,10},{9,11},{10,... | collective-permute-start | bytes 1081352 | tf_op jit(solution)/shard_map/ppermute | solution.py:474
  43.2 1.5 %collective-permute-start.18 = (bf16[128,1408]{1,0:T(8,128)(2,1)S(1)}, bf16[128,1408]{1,0:T(8,128)(2,1)S(1)}, u32[]{:S(2)}, u32[]{:S(2)}) collective-permute-start(bf16[128,1408]{1,0:T(8,128)(2,1)S(1)} %get-tuple-element.52), channel_id=1, source_target_pairs={{0,3},{1,2},{2,1},{3,0},{4,7},{5,6},{6,5},{7,4},{8,11},{9,10},{10,... | collective-permute-start | bytes 1081352 | tf_op jit(solution)/shard_map/ppermute | solution.py:474
  44.7 7.8 %collective-permute-done.16.refs_4_.refs_1_ = bf16[128,1408]{1,0:T(8,128)(2,1)S(1)} collective-permute-done((bf16[128,1408]{1,0:T(8,128)(2,1)S(1)}, bf16[128,1408]{1,0:T(8,128)(2,1)S(1)}, u32[]{:S(2)}, u32[]{:S(2)}) %collective-permute-start.16) | collective-permute-done | bytes 360480 | tf_op jit(solution)/shard_map/ppermute | solution.py:474
  53.8 6.3 %collective-permute-done.17.refs_2_.refs_3_ = bf16[128,1408]{1,0:T(8,128)(2,1)S(1)} collective-permute-done((bf16[128,1408]{1,0:T(8,128)(2,1)S(1)}, bf16[128,1408]{1,0:T(8,128)(2,1)S(1)}, u32[]{:S(2)}, u32[]{:S(2)}) %collective-permute-start.17) | collective-permute-done | bytes 360480 | tf_op jit(solution)/shard_map/ppermute | solution.py:474
  61.0 1.7 %collective-permute-done.19.refs_1_ = bf16[4,400,128]{2,1,0:T(8,128)(2,1)S(1)} collective-permute-done((bf16[4,400,128]{2,1,0:T(8,128)(2,1)S(1)}, bf16[4,400,128]{2,1,0:T(8,128)(2,1)S(1)}, u32[]{:S(2)}, u32[]{:S(2)}) %collective-permute-start.19) | collective-permute-done | bytes 409632 | tf_op jit(solution)/shard_map/ppermute | solution.py:480
  64.1 2.6 %collective-permute-start.21 = (bf16[400,128]{1,0:T(8,128)(2,1)S(1)}, bf16[400,128]{1,0:T(8,128)(2,1)S(1)}, u32[]{:S(2)}, u32[]{:S(2)}) collective-permute-start(bf16[400,128]{1,0:T(8,128)(2,1)S(1)} %get-tuple-element.60), channel_id=1, source_target_pairs={{0,16},{4,20},{8,24},{12,28},{16,0},{20,4},{24,8},{28,12},{1,17},{... | collective-permute-start | bytes 307208 | tf_op jit(solution)/shard_map/ppermute | solution.py:477
  69.9 6.3 %collective-permute-done.21.refs_2_ = bf16[400,128]{1,0:T(8,128)(2,1)S(1)} collective-permute-done((bf16[400,128]{1,0:T(8,128)(2,1)S(1)}, bf16[400,128]{1,0:T(8,128)(2,1)S(1)}, u32[]{:S(2)}, u32[]{:S(2)}) %collective-permute-start.21) | collective-permute-done | bytes 102432 | tf_op jit(solution)/shard_map/ppermute | solution.py:477
  76.5 1.8 %collective-permute-start.23 = (bf16[400,128]{1,0:T(8,128)(2,1)S(1)}, bf16[400,128]{1,0:T(8,128)(2,1)S(1)}, u32[]{:S(2)}, u32[]{:S(2)}) collective-permute-start(bf16[400,128]{1,0:T(8,128)(2,1)S(1)} %shard_map.138.refs_0_), channel_id=1, source_target_pairs={{0,8},{4,12},{8,0},{12,4},{16,24},{20,28},{24,16},{28,20},{1,9},{5... | collective-permute-start | bytes 307208 | tf_op jit(solution)/shard_map/ppermute | solution.py:477
  78.2 5.3 %collective-permute-done.24.refs_3_.refs_2_ = bf16[400,128]{1,0:T(8,128)(2,1)S(1)} collective-permute-done((bf16[400,128]{1,0:T(8,128)(2,1)S(1)}, bf16[400,128]{1,0:T(8,128)(2,1)S(1)}, u32[]{:S(2)}, u32[]{:S(2)}) %collective-permute-start.24) | collective-permute-done | bytes 102432 | tf_op jit(solution)/shard_map/ppermute | solution.py:477
  84.0 4.3 %collective-permute-done.25.refs_4_.refs_3_ = bf16[400,128]{1,0:T(8,128)(2,1)S(1)} collective-permute-done((bf16[400,128]{1,0:T(8,128)(2,1)S(1)}, bf16[400,128]{1,0:T(8,128)(2,1)S(1)}, u32[]{:S(2)}, u32[]{:S(2)}) %collective-permute-start.25) | collective-permute-done | bytes 102432 | tf_op jit(solution)/shard_map/ppermute | solution.py:477
  88.9 1.5 %collective-permute-start.28 = (bf16[4,400,128]{2,1,0:T(8,128)(2,1)S(1)}, bf16[4,400,128]{2,1,0:T(8,128)(2,1)S(1)}, u32[]{:S(2)}, u32[]{:S(2)}) collective-permute-start(bf16[4,400,128]{2,1,0:T(8,128)(2,1)S(1)} %shard_map.143.refs_0_), channel_id=1, source_target_pairs={{0,2},{1,3},{2,0},{3,1},{4,6},{5,7},{6,4},{7,5},{8,10},{9,11},{10,... | collective-permute-start | bytes 1228808 | tf_op jit(solution)/shard_map/ppermute | solution.py:474
  91.0 7.8 %collective-permute-done.31.refs_1_ = bf16[2,128,768]{2,1,0:T(8,128)(2,1)S(1)} collective-permute-done((bf16[2,128,768]{2,1,0:T(8,128)(2,1)S(1)}, bf16[2,128,768]{2,1,0:T(8,128)(2,1)S(1)}, u32[]{:S(2)}, u32[]{:S(2)}) %collective-permute-start.31) | collective-permute-done | bytes 393248 | tf_op jit(solution)/shard_map/ppermute | solution.py:477
  98.8 1.8 %collective-permute-start.32 = (bf16[1,128,768]{2,1,0:T(8,128)(2,1)S(1)}, bf16[1,128,768]{2,1,0:T(8,128)(2,1)S(1)}, u32[]{:S(2)}, u32[]{:S(2)}) collective-permute-start(bf16[1,128,768]{2,1,0:T(8,128)(2,1)S(1)} %get-tuple-element.71), channel_id=1, source_target_pairs={{0,16},{4,20},{8,24},{12,28},{16,0},{20,4},{24,8},{28,12},{1,17},{... | collective-permute-start | bytes 589832 | tf_op jit(solution)/shard_map/ppermute | solution.py:477
  102.5 6.5 %collective-permute-done.32.refs_6_ = bf16[1,128,768]{2,1,0:T(8,128)(2,1)S(1)} collective-permute-done((bf16[1,128,768]{2,1,0:T(8,128)(2,1)S(1)}, bf16[1,128,768]{2,1,0:T(8,128)(2,1)S(1)}, u32[]{:S(2)}, u32[]{:S(2)}) %collective-permute-start.32) | collective-permute-done | bytes 196640 | tf_op jit(solution)/shard_map/ppermute | solution.py:477
  109.6 2.5 %shard_map.145 = (f32[768,1024]{1,0:T(8,128)}, f32[768,1024]{1,0:T(8,128)}, f32[1,1024]{1,0:T(1,128)S(1)}, bf16[128,768]{1,0:T(8,128)(2,1)}) custom-call(bf16[4,400,128]{2,1,0:T(8,128)(2,1)S(1)} %shard_map.143.refs_0_, bf16[4,400,128]{2,1,0:T(8,128)(2,1)S(1)} %collective-permute-done.27.refs_1_, bf16[4,400,128]{2,1,0:T(8,128)(2,1)S(1)} %collective-permute-done.28.refs_2_, ...), custom_call_target="tpu_custom_call" | custom-call | bytes 9437184 | tf_op jit(solution)/shard_map/pallas_call | solution.py:441
  112.2 2.4 %shard_map.146 = (f32[768,1024]{1,0:T(8,128)}, f32[768,1024]{1,0:T(8,128)}, f32[1,1024]{1,0:T(1,128)}) custom-call(bf16[4,400,128]{2,1,0:T(8,128)(2,1)S(1)} %collective-permute-done.33.refs_0_, bf16[4,400,128]{2,1,0:T(8,128)(2,1)S(1)} %collective-permute-done.34.refs_1_, ...), custom_call_target="tpu_custom_call", output_to_operand_aliasing={{0}: (5, {}), {1}: (6, {})} | custom-call | bytes 9437184 | tf_op jit(solution)/shard_map/pallas_call | solution.py:441
  (94 shorter events, 28.4 us)
Async XLA Ops:
  0.6 13.5 %collective-permute-start.1 = (bf16[128,768]{1,0:T(8,128)(2,1)}, bf16[128,768]{1,0:T(8,128)(2,1)S(1)}, u32[]{:S(2)}, u32[]{:S(2)}) collective-permute-start(bf16[128,768]{1,0:T(8,128)(2,1)} %refs_1_.2), channel_id=1, source_target_pairs={{0,16},{4,20},{8,24},{12,28},{16,0},{20,4},{24,8},{28,12},{1,17},{... | collective-permute-start | bytes 589832 | tf_op jit(solution)/shard_map/ppermute | solution.py:477
  4.7 10.6 %collective-permute-start = (bf16[128,768]{1,0:T(8,128)(2,1)}, bf16[128,768]{1,0:T(8,128)(2,1)S(1)}, u32[]{:S(2)}, u32[]{:S(2)}) collective-permute-start(bf16[128,768]{1,0:T(8,128)(2,1)} %refs_1_.2), channel_id=1, source_target_pairs={{0,8},{4,12},{8,0},{12,4},{16,24},{20,28},{24,16},{28,20},{1,9},{5... | collective-permute-start | bytes 589832 | tf_op jit(solution)/shard_map/ppermute | solution.py:477
  6.3 12.2 %collective-permute-start.2 = (bf16[128,768]{1,0:T(8,128)(2,1)}, bf16[128,768]{1,0:T(8,128)(2,1)S(1)}, u32[]{:S(2)}, u32[]{:S(2)}) collective-permute-start(bf16[128,768]{1,0:T(8,128)(2,1)} %refs_1_.2), channel_id=1, source_target_pairs={{0,4},{4,0},{8,12},{12,8},{16,20},{20,16},{24,28},{28,24},{1,5},{5... | collective-permute-start | bytes 589832 | tf_op jit(solution)/shard_map/ppermute | solution.py:480
  12.5 9.4 %collective-permute-start.5 = (bf16[128,768]{1,0:T(8,128)(2,1)S(1)}, bf16[128,768]{1,0:T(8,128)(2,1)S(1)}, u32[]{:S(2)}, u32[]{:S(2)}) collective-permute-start(bf16[128,768]{1,0:T(8,128)(2,1)S(1)} %copy-done.4), channel_id=1, source_target_pairs={{0,0},{4,1},{9,10},{13,11},{18,20},{22,21},{27,30},{31,31}} | collective-permute-start | bytes 589832 | tf_op jit(solution)/shard_map/ppermute | solution.py:499
  14.2 7.6 %collective-permute-start.7 = (bf16[128,768]{1,0:T(8,128)(2,1)S(1)}, bf16[128,768]{1,0:T(8,128)(2,1)S(1)}, u32[]{:S(2)}, u32[]{:S(2)}) collective-permute-start(bf16[128,768]{1,0:T(8,128)(2,1)S(1)} %collective-permute-done.1.refs_3_.refs_0_), channel_id=1, source_target_pairs={{0,8},{4,12},{8,0},{12,4},{16,24},{20,28},{24,16},{28,20},{1,9},{5... | collective-permute-start | bytes 589832 | tf_op jit(solution)/shard_map/ppermute | solution.py:477
  28.7 11.1 %collective-permute-start.12 = (bf16[128,768]{1,0:T(8,128)(2,1)S(1)}, bf16[128,768]{1,0:T(8,128)(2,1)S(1)}, u32[]{:S(2)}, u32[]{:S(2)}) collective-permute-start(bf16[128,768]{1,0:T(8,128)(2,1)S(1)} %get-tuple-element.45), channel_id=1, source_target_pairs={{0,2},{1,3},{2,0},{3,1},{4,6},{5,7},{6,4},{7,5},{8,10},{9,11},{10,... | collective-permute-start | bytes 589832 | tf_op jit(solution)/shard_map/ppermute | solution.py:474
  29.2 10.6 %collective-permute-start.13 = (bf16[128,768]{1,0:T(8,128)(2,1)S(1)}, bf16[128,768]{1,0:T(8,128)(2,1)S(1)}, u32[]{:S(2)}, u32[]{:S(2)}) collective-permute-start(bf16[128,768]{1,0:T(8,128)(2,1)S(1)} %get-tuple-element.46), channel_id=1, source_target_pairs={{0,3},{1,2},{2,1},{3,0},{4,7},{5,6},{6,5},{7,4},{8,11},{9,10},{10,... | collective-permute-start | bytes 589832 | tf_op jit(solution)/shard_map/ppermute | solution.py:474
  41.2 11.3 %collective-permute-start.16 = (bf16[128,1408]{1,0:T(8,128)(2,1)S(1)}, bf16[128,1408]{1,0:T(8,128)(2,1)S(1)}, u32[]{:S(2)}, u32[]{:S(2)}) collective-permute-start(bf16[128,1408]{1,0:T(8,128)(2,1)S(1)} %get-tuple-element.50), channel_id=1, source_target_pairs={{0,1},{1,0},{2,3},{3,2},{4,5},{5,4},{6,7},{7,6},{8,9},{9,8},{10,11... | collective-permute-start | bytes 1081352 | tf_op jit(solution)/shard_map/ppermute | solution.py:474
  41.7 18.4 %collective-permute-start.17 = (bf16[128,1408]{1,0:T(8,128)(2,1)S(1)}, bf16[128,1408]{1,0:T(8,128)(2,1)S(1)}, u32[]{:S(2)}, u32[]{:S(2)}) collective-permute-start(bf16[128,1408]{1,0:T(8,128)(2,1)S(1)} %get-tuple-element.51), channel_id=1, source_target_pairs={{0,2},{1,3},{2,0},{3,1},{4,6},{5,7},{6,4},{7,5},{8,10},{9,11},{10,... | collective-permute-start | bytes 1081352 | tf_op jit(solution)/shard_map/ppermute | solution.py:474
  43.2 16.9 %collective-permute-start.18 = (bf16[128,1408]{1,0:T(8,128)(2,1)S(1)}, bf16[128,1408]{1,0:T(8,128)(2,1)S(1)}, u32[]{:S(2)}, u32[]{:S(2)}) collective-permute-start(bf16[128,1408]{1,0:T(8,128)(2,1)S(1)} %get-tuple-element.52), channel_id=1, source_target_pairs={{0,3},{1,2},{2,1},{3,0},{4,7},{5,6},{6,5},{7,4},{8,11},{9,10},{10,... | collective-permute-start | bytes 1081352 | tf_op jit(solution)/shard_map/ppermute | solution.py:474
  62.8 7.1 %collective-permute-start.20 = (bf16[400,128]{1,0:T(8,128)(2,1)S(1)}, bf16[400,128]{1,0:T(8,128)(2,1)S(1)}, u32[]{:S(2)}, u32[]{:S(2)}) collective-permute-start(bf16[400,128]{1,0:T(8,128)(2,1)S(1)} %get-tuple-element.59), channel_id=1, source_target_pairs={{0,24},{4,28},{8,16},{12,20},{16,8},{20,12},{24,0},{28,4},{1,25},{... | collective-permute-start | bytes 307208 | tf_op jit(solution)/shard_map/ppermute | solution.py:477
  64.1 12.1 %collective-permute-start.21 = (bf16[400,128]{1,0:T(8,128)(2,1)S(1)}, bf16[400,128]{1,0:T(8,128)(2,1)S(1)}, u32[]{:S(2)}, u32[]{:S(2)}) collective-permute-start(bf16[400,128]{1,0:T(8,128)(2,1)S(1)} %get-tuple-element.60), channel_id=1, source_target_pairs={{0,16},{4,20},{8,24},{12,28},{16,0},{20,4},{24,8},{28,12},{1,17},{... | collective-permute-start | bytes 307208 | tf_op jit(solution)/shard_map/ppermute | solution.py:477
  66.7 9.5 %collective-permute-start.22 = (bf16[400,128]{1,0:T(8,128)(2,1)S(1)}, bf16[400,128]{1,0:T(8,128)(2,1)S(1)}, u32[]{:S(2)}, u32[]{:S(2)}) collective-permute-start(bf16[400,128]{1,0:T(8,128)(2,1)S(1)} %get-tuple-element.61), channel_id=1, source_target_pairs={{0,8},{4,12},{8,0},{12,4},{16,24},{20,28},{24,16},{28,20},{1,9},{5... | collective-permute-start | bytes 307208 | tf_op jit(solution)/shard_map/ppermute | solution.py:477
  76.2 12.1 %collective-permute-start.26 = (bf16[4,128,768]{2,1,0:T(8,128)(2,1)S(1)}, bf16[4,128,768]{2,1,0:T(8,128)(2,1)S(1)}, u32[]{:S(2)}, u32[]{:S(2)}) collective-permute-start(bf16[4,128,768]{2,1,0:T(8,128)(2,1)S(1)} %shard_map.141), channel_id=1, source_target_pairs={{0,4},{4,0},{8,12},{12,8},{16,20},{20,16},{24,28},{28,24},{1,5},{5... | collective-permute-start | bytes 2359304 | tf_op jit(solution)/shard_map/ppermute | solution.py:480
  76.4 7.1 %collective-permute-start.24 = (bf16[400,128]{1,0:T(8,128)(2,1)S(1)}, bf16[400,128]{1,0:T(8,128)(2,1)S(1)}, u32[]{:S(2)}, u32[]{:S(2)}) collective-permute-start(bf16[400,128]{1,0:T(8,128)(2,1)S(1)} %shard_map.138.refs_0_), channel_id=1, source_target_pairs={{0,16},{4,20},{8,24},{12,28},{16,0},{20,4},{24,8},{28,12},{1,17},{... | collective-permute-start | bytes 307208 | tf_op jit(solution)/shard_map/ppermute | solution.py:477
  76.5 7.5 %collective-permute-start.23 = (bf16[400,128]{1,0:T(8,128)(2,1)S(1)}, bf16[400,128]{1,0:T(8,128)(2,1)S(1)}, u32[]{:S(2)}, u32[]{:S(2)}) collective-permute-start(bf16[400,128]{1,0:T(8,128)(2,1)S(1)} %shard_map.138.refs_0_), channel_id=1, source_target_pairs={{0,8},{4,12},{8,0},{12,4},{16,24},{20,28},{24,16},{28,20},{1,9},{5... | collective-permute-start | bytes 307208 | tf_op jit(solution)/shard_map/ppermute | solution.py:477
  88.5 10.2 %collective-permute-start.31 = (bf16[2,128,768]{2,1,0:T(8,128)(2,1)S(1)}, bf16[2,128,768]{2,1,0:T(8,128)(2,1)S(1)}, u32[]{:S(2)}, u32[]{:S(2)}) collective-permute-start(bf16[2,128,768]{2,1,0:T(8,128)(2,1)S(1)} %get-tuple-element.68.refs_4_), channel_id=1, source_target_pairs={{0,8},{4,12},{8,0},{12,4},{16,24},{20,28},{24,16},{28,20},{1,9},{5... | collective-permute-start | bytes 1179656 | tf_op jit(solution)/shard_map/ppermute | solution.py:477
  88.9 11.8 %collective-permute-start.28 = (bf16[4,400,128]{2,1,0:T(8,128)(2,1)S(1)}, bf16[4,400,128]{2,1,0:T(8,128)(2,1)S(1)}, u32[]{:S(2)}, u32[]{:S(2)}) collective-permute-start(bf16[4,400,128]{2,1,0:T(8,128)(2,1)S(1)} %shard_map.143.refs_0_), channel_id=1, source_target_pairs={{0,2},{1,3},{2,0},{3,1},{4,6},{5,7},{6,4},{7,5},{8,10},{9,11},{10,... | collective-permute-start | bytes 1228808 | tf_op jit(solution)/shard_map/ppermute | solution.py:474
  90.3 11.0 %collective-permute-start.27 = (bf16[4,400,128]{2,1,0:T(8,128)(2,1)S(1)}, bf16[4,400,128]{2,1,0:T(8,128)(2,1)S(1)}, u32[]{:S(2)}, u32[]{:S(2)}) collective-permute-start(bf16[4,400,128]{2,1,0:T(8,128)(2,1)S(1)} %shard_map.143.refs_0_), channel_id=1, source_target_pairs={{0,1},{1,0},{2,3},{3,2},{4,5},{5,4},{6,7},{7,6},{8,9},{9,8},{10,11... | collective-permute-start | bytes 1228808 | tf_op jit(solution)/shard_map/ppermute | solution.py:474
  98.8 10.2 %collective-permute-start.32 = (bf16[1,128,768]{2,1,0:T(8,128)(2,1)S(1)}, bf16[1,128,768]{2,1,0:T(8,128)(2,1)S(1)}, u32[]{:S(2)}, u32[]{:S(2)}) collective-permute-start(bf16[1,128,768]{2,1,0:T(8,128)(2,1)S(1)} %get-tuple-element.71), channel_id=1, source_target_pairs={{0,16},{4,20},{8,24},{12,28},{16,0},{20,4},{24,8},{28,12},{1,17},{... | collective-permute-start | bytes 589832 | tf_op jit(solution)/shard_map/ppermute | solution.py:477
  100.6 11.5 %collective-permute-start.33 = (bf16[4,400,128]{2,1,0:T(8,128)(2,1)S(1)}, bf16[4,400,128]{2,1,0:T(8,128)(2,1)S(1)}, u32[]{:S(2)}, u32[]{:S(2)}) collective-permute-start(bf16[4,400,128]{2,1,0:T(8,128)(2,1)S(1)} %shard_map.143.refs_0_), channel_id=1, source_target_pairs={{0,4},{4,0},{8,12},{12,8},{16,20},{20,16},{24,28},{28,24},{1,5},{5... | collective-permute-start | bytes 1228808 | tf_op jit(solution)/shard_map/ppermute | solution.py:480
  100.6 8.4 %collective-permute-start.30 = (bf16[2,400,128]{2,1,0:T(8,128)(2,1)S(1)}, bf16[2,400,128]{2,1,0:T(8,128)(2,1)S(1)}, u32[]{:S(2)}, u32[]{:S(2)}) collective-permute-start(bf16[2,400,128]{2,1,0:T(8,128)(2,1)S(1)} %slice.15), channel_id=1, source_target_pairs={{0,1},{1,0},{2,3},{3,2},{4,5},{5,4},{6,7},{7,6},{8,9},{9,8},{10,11... | collective-permute-start | bytes 614408 | tf_op jit(solution)/shard_map/ppermute | solution.py:474
  101.3 8.2 %collective-permute-start.29 = (bf16[2,400,128]{2,1,0:T(8,128)(2,1)S(1)}, bf16[2,400,128]{2,1,0:T(8,128)(2,1)S(1)}, u32[]{:S(2)}, u32[]{:S(2)}) collective-permute-start(bf16[2,400,128]{2,1,0:T(8,128)(2,1)S(1)} %slice.14), channel_id=1, source_target_pairs={{0,2},{1,3},{2,0},{3,1},{4,6},{5,7},{6,4},{7,5},{8,10},{9,11},{10,... | collective-permute-start | bytes 614408 | tf_op jit(solution)/shard_map/ppermute | solution.py:474
  102.5 9.6 %collective-permute-start.35 = (bf16[4,400,128]{2,1,0:T(8,128)(2,1)S(1)}, bf16[4,400,128]{2,1,0:T(8,128)(2,1)S(1)}, u32[]{:S(2)}, u32[]{:S(2)}) collective-permute-start(bf16[4,400,128]{2,1,0:T(8,128)(2,1)S(1)} %collective-permute-done.28.refs_2_), channel_id=1, source_target_pairs={{0,4},{4,0},{8,12},{12,8},{16,20},{20,16},{24,28},{28,24},{1,5},{5... | collective-permute-start | bytes 1228808 | tf_op jit(solution)/shard_map/ppermute | solution.py:480
  (22 other events, 97.2 us)

commit v14 on v13

--- a/solution.py
+++ b/solution.py
@@ -11,6 +11,7 @@
 BF16 = jnp.bfloat16
 LANES = 128
 EXTRA = 16
+SPARE = 16
 VMEM = pl.BlockSpec(memory_space=pltpu.VMEM)
 SMEM = pl.BlockSpec(memory_space=pltpu.SMEM)
 MIB = 1024 * 1024
@@ -63,6 +64,19 @@
             out_ref[...] = ref[...].T
 
     return call(body, [shape(w.shape[::-1], w.dtype) for w in weights], weights, after=after)
+
+
+def join(parts, after=()):
+    counts = [x.shape[0] for x in parts]
+
+    def body(*refs):
+        at = 0
+        for count, ref in zip(counts, refs):
+            refs[-1][at : at + count] = ref[...]
+            at += count
+
+    out = shape((sum(counts), *parts[0].shape[1:]), parts[0].dtype)
+    return call(body, [out], parts, after=after)[0]
 
 
 def stack(parts, joined=False, after=()):
@@ -333,17 +347,19 @@
     )
 
 
-def fold(keep, came, after=()):
+def fold(keep, came, after=(), spare=0):
     count, rows, width = keep.shape
     half = count // 2
 
-    def body(keep_ref, came_ref, *outs):
+    def body(keep_ref, came_ref, kept_ref, send_ref):
         total = keep_ref[...] + came_ref[...].astype(F32)
-        outs[0][...] = total[:half]
-        outs[1][...] = total[half:].astype(BF16)
-
-    dims = (half, rows, width)
-    return call(body, [shape(dims, F32), shape(dims, BF16)], [keep, came], after=after)
+        kept_ref[...] = total[:half]
+        send_ref[:, :rows, :] = total[half:].astype(BF16)
+        if spare:
+            send_ref[:, rows:, :] = jnp.zeros((half, spare, width), BF16)
+
+    outs = [shape((half, rows, width), F32), shape((half, rows + spare, width), BF16)]
+    return call(body, outs, [keep, came], after=after)
 
 
 def pair_sum(keep, came):
@@ -428,7 +444,8 @@
                 at += 1
         if adds:
             keep_ref, came_ref = refs[len(inputs) - 2 : len(inputs)]
-            sum_ref[0][...] = (keep_ref[0] + came_ref[0].astype(F32)).astype(BF16)
+            came = came_ref[0, : keep_ref.shape[1], :].astype(F32)
+            sum_ref[0][...] = (keep_ref[0] + came).astype(BF16)
         for here, copy in waits:
             pl.when(here)(copy.wait)
 
@@ -573,7 +590,8 @@
     line = stack(line, after=[send])
     step = 1
     while 2 * step < half:
-        keep, send = fold(keep, along_chips(send, step))
+        spare = SPARE if 4 * step == half else 0
+        keep, send = fold(keep, along_chips(send, step), (), spare)
         step *= 2
     last = (keep, along_chips(send, step))
 
@@ -590,10 +608,13 @@
         rest = [(along_col(line, cs - 1), 0, cs - 1)]
     factor = 1.0 / math.sqrt(nd * rs * cs)
     sizes = (depth, hid, xr, nc, cs, (factor, 32.0 * factor))
-    pieces = [piece(*x, True) for x in near + rest]
-    *begun, grad_input = assemble(pieces, (), *sizes, (), last)
-    pieces = [piece(other_core(x), *where, False) for x, *where in near + rest]
-    total_self, total_neigh, total_bias = assemble(pieces, begun, *sizes, ())
+    where = [(d, k) for k in range(cs - 1) for d in range(half)]
+    near = join([x for x, *_ in near], [keep])
+    begun = assemble([(near, where, True), (other_core(near), where, False)], (), *sizes, ())
+    rest[-1] = (follow(rest[-1][0], begun[2:]), *rest[-1][1:])
+    pieces = [piece(*x, True) for x in rest]
+    pieces += [piece(other_core(x), *where, False) for x, *where in rest]
+    total_self, total_neigh, total_bias, grad_input = assemble(pieces, begun, *sizes, (), last)
     return output, grad_input, total_self, total_neigh, total_bias.reshape(-1)
 
 

time: 115 us -> 118 us (1.026)
  waiting for transfers between devices: 57.7 us -> 61 us
    ppermute x12, waiting for transfers between devices: 22 us -> 25.9 us  [along_col(): return lax.ppermute(x, 'col', [(s, s ^ k) for s in range(cs)])]
    pallas_call x17 -> x19, Pallas kernels: 10.1 us -> 10.4 us  [call(): pl.pallas_call(run, out_shape=outs, in_specs=[SMEM] * smem + [VMEM] * (co...]
    ppermute x11 -> x9, starting transfers between devices: 2.23 us -> 2.4 us  [other_core(): return lax.ppermute(x, 'row', [(s, s ^ 1) for s in range(rs)])]
  transfers between devices with their start and end apart: 38 -> 36, of which waited for: 14 -> 17; matrix products, arithmetic and copies ran while one was open for 1% -> 1% of each run, Pallas kernels for 9% -> 9%
where the time goes in v14:
time: 118 us; the launch traced here: 117 us
  waiting for transfers between devices  61 us (52%)
  starting transfers between devices  37.1 us (31%)
  Pallas kernels  14.7 us (12%)
  local copies, waits for them, and re-layouts  2.61 us (2%)
  between operations  1.62 us (1%)
    ppermute x11, waiting for transfers between devices, along_chips(): return lax.ppermute(x, 'row', [(s, s ^ 2 * k) for s in range(rs)])  33.4 us
    ppermute x12, waiting for transfers between devices, along_col(): return lax.ppermute(x, 'col', [(s, s ^ k) for s in range(cs)])  25.9 us
    ppermute x11, starting transfers between devices, along_chips(): return lax.ppermute(x, 'row', [(s, s ^ 2 * k) for s in range(rs)])  14.7 us
    ppermute x12, starting transfers between devices, along_col(): return lax.ppermute(x, 'col', [(s, s ^ k) for s in range(cs)])  12.7 us
    pallas_call x19, Pallas kernels, call(): pl.pallas_call(run, out_shape=outs, in_specs=[SMEM] * smem + [VMEM] * (co...  10.4 us
    ppermute x4, starting transfers between devices, send_own(): return lax.ppermute(block, ('row', 'col'), pairs)  7.2 us
    pallas_call x2, Pallas kernels, assemble(): pl.pallas_call(run, out_shape=[weight, weight, shape((1, hid), F32), *sum...  4.29 us
    unnamed x16, local copies, waits for them, and re-layouts  2.46 us
  transfers between devices with their start and end apart: 36, of which 17 were waited for; matrix products, arithmetic and copies ran while one was open for 1% of the time, Pallas kernels for 9%

profile of v14, /device:TPU:0, one launch (start us, length us, event | category | flops | bytes accessed | tf_op | source)
XLA Modules:
  0.0 117.5 jit_solution(5571078540498944512)
XLA Ops:
  0.6 4.1 %collective-permute-start.1 = (bf16[128,768]{1,0:T(8,128)(2,1)}, bf16[128,768]{1,0:T(8,128)(2,1)S(1)}, u32[]{:S(2)}, u32[]{:S(2)}) collective-permute-start(bf16[128,768]{1,0:T(8,128)(2,1)} %refs_1_.2), channel_id=1, source_target_pairs={{0,16},{4,20},{8,24},{12,28},{16,0},{20,4},{24,8},{28,12},{1,17},{... | collective-permute-start | bytes 589832 | tf_op jit(solution)/shard_map/ppermute | solution.py:494
  9.4 1.6 %shard_map.128 = (bf16[512,1024]{1,0:T(8,128)(2,1)S(1)}, bf16[1024,512]{1,0:T(8,128)(2,1)S(1)}) custom-call(s32[24]{0:T(128)S(1)} %bitcast.12, s32[24]{0:T(128)S(1)} %bitcast.13, s32[1]{0:T(128)} %bitcast.9.refs_2_, bf16[24,128,128]{2,1,0:T(8,128)(2,1)S(1)} %bitcast.10), custom_call_target="tpu_custom_call" | custom-call | flops 524288 | bytes 2883780 | tf_op jit(solution)/shard_map/pallas_call | solution.py:33
  15.7 2.9 %collective-permute-start.6 = (bf16[128,768]{1,0:T(8,128)(2,1)S(1)}, bf16[128,768]{1,0:T(8,128)(2,1)S(1)}, u32[]{:S(2)}, u32[]{:S(2)}) collective-permute-start(bf16[128,768]{1,0:T(8,128)(2,1)S(1)} %collective-permute-done.refs_2_), channel_id=1, source_target_pairs={{0,2},{4,3},{9,8},{13,9},{18,22},{22,23},{27,28},{31,29}} | collective-permute-start | bytes 589832 | tf_op jit(solution)/shard_map/ppermute | solution.py:516
  19.5 2.1 %collective-permute-done.7.refs_2_ = bf16[128,768]{1,0:T(8,128)(2,1)S(1)} collective-permute-done((bf16[128,768]{1,0:T(8,128)(2,1)S(1)}, bf16[128,768]{1,0:T(8,128)(2,1)S(1)}, u32[]{:S(2)}, u32[]{:S(2)}) %collective-permute-start.7) | collective-permute-done | bytes 196640 | tf_op jit(solution)/shard_map/ppermute | solution.py:494
  22.6 2.4 %collective-permute-start.10 = (bf16[128,768]{1,0:T(8,128)(2,1)S(1)}, bf16[128,768]{1,0:T(8,128)(2,1)S(1)}, u32[]{:S(2)}, u32[]{:S(2)}) collective-permute-start(bf16[128,768]{1,0:T(8,128)(2,1)S(1)} %shard_map.131), channel_id=1, source_target_pairs={{0,4},{4,5},{9,14},{13,15},{18,16},{22,17},{27,26},{31,27}} | collective-permute-start | bytes 589832 | tf_op jit(solution)/shard_map/ppermute | solution.py:516
  27.0 1.7 %collective-permute-start.11 = (bf16[128,768]{1,0:T(8,128)(2,1)S(1)}, bf16[128,768]{1,0:T(8,128)(2,1)S(1)}, u32[]{:S(2)}, u32[]{:S(2)}) collective-permute-start(bf16[128,768]{1,0:T(8,128)(2,1)S(1)} %get-tuple-element.44), channel_id=1, source_target_pairs={{0,1},{1,0},{2,3},{3,2},{4,5},{5,4},{6,7},{7,6},{8,9},{9,8},{10,11... | collective-permute-start | bytes 589832 | tf_op jit(solution)/shard_map/ppermute | solution.py:491
  31.9 1.9 %collective-permute-done.11.refs_1_ = bf16[128,768]{1,0:T(8,128)(2,1)S(1)} collective-permute-done((bf16[128,768]{1,0:T(8,128)(2,1)S(1)}, bf16[128,768]{1,0:T(8,128)(2,1)S(1)}, u32[]{:S(2)}, u32[]{:S(2)}) %collective-permute-start.11) | collective-permute-done | bytes 196640 | tf_op jit(solution)/shard_map/ppermute | solution.py:491
  33.7 1.9 %collective-permute-done.12.refs_2_ = bf16[128,768]{1,0:T(8,128)(2,1)S(1)} collective-permute-done((bf16[128,768]{1,0:T(8,128)(2,1)S(1)}, bf16[128,768]{1,0:T(8,128)(2,1)S(1)}, u32[]{:S(2)}, u32[]{:S(2)}) %collective-permute-start.12) | collective-permute-done | bytes 196640 | tf_op jit(solution)/shard_map/ppermute | solution.py:491
  35.6 4.3 %collective-permute-done.13.refs_3_ = bf16[128,768]{1,0:T(8,128)(2,1)S(1)} collective-permute-done((bf16[128,768]{1,0:T(8,128)(2,1)S(1)}, bf16[128,768]{1,0:T(8,128)(2,1)S(1)}, u32[]{:S(2)}, u32[]{:S(2)}) %collective-permute-start.13) | collective-permute-done | bytes 196640 | tf_op jit(solution)/shard_map/ppermute | solution.py:491
  41.6 1.8 %collective-permute-start.17 = (bf16[128,1408]{1,0:T(8,128)(2,1)S(1)}, bf16[128,1408]{1,0:T(8,128)(2,1)S(1)}, u32[]{:S(2)}, u32[]{:S(2)}) collective-permute-start(bf16[128,1408]{1,0:T(8,128)(2,1)S(1)} %get-tuple-element.51), channel_id=1, source_target_pairs={{0,2},{1,3},{2,0},{3,1},{4,6},{5,7},{6,4},{7,5},{8,10},{9,11},{10,... | collective-permute-start | bytes 1081352 | tf_op jit(solution)/shard_map/ppermute | solution.py:491
  44.8 7.7 %collective-permute-done.16.refs_4_.refs_1_ = bf16[128,1408]{1,0:T(8,128)(2,1)S(1)} collective-permute-done((bf16[128,1408]{1,0:T(8,128)(2,1)S(1)}, bf16[128,1408]{1,0:T(8,128)(2,1)S(1)}, u32[]{:S(2)}, u32[]{:S(2)}) %collective-permute-start.16) | collective-permute-done | bytes 360480 | tf_op jit(solution)/shard_map/ppermute | solution.py:491
  53.8 6.3 %collective-permute-done.17.refs_2_.refs_3_ = bf16[128,1408]{1,0:T(8,128)(2,1)S(1)} collective-permute-done((bf16[128,1408]{1,0:T(8,128)(2,1)S(1)}, bf16[128,1408]{1,0:T(8,128)(2,1)S(1)}, u32[]{:S(2)}, u32[]{:S(2)}) %collective-permute-start.17) | collective-permute-done | bytes 360480 | tf_op jit(solution)/shard_map/ppermute | solution.py:491
  61.0 1.7 %collective-permute-done.19.refs_1_ = bf16[4,400,128]{2,1,0:T(8,128)(2,1)S(1)} collective-permute-done((bf16[4,400,128]{2,1,0:T(8,128)(2,1)S(1)}, bf16[4,400,128]{2,1,0:T(8,128)(2,1)S(1)}, u32[]{:S(2)}, u32[]{:S(2)}) %collective-permute-start.19) | collective-permute-done | bytes 409632 | tf_op jit(solution)/shard_map/ppermute | solution.py:497
  64.1 2.7 %collective-permute-start.21 = (bf16[400,128]{1,0:T(8,128)(2,1)S(1)}, bf16[400,128]{1,0:T(8,128)(2,1)S(1)}, u32[]{:S(2)}, u32[]{:S(2)}) collective-permute-start(bf16[400,128]{1,0:T(8,128)(2,1)S(1)} %get-tuple-element.60), channel_id=1, source_target_pairs={{0,16},{4,20},{8,24},{12,28},{16,0},{20,4},{24,8},{28,12},{1,17},{... | collective-permute-start | bytes 307208 | tf_op jit(solution)/shard_map/ppermute | solution.py:494
  69.9 6.3 %collective-permute-done.21.refs_2_ = bf16[400,128]{1,0:T(8,128)(2,1)S(1)} collective-permute-done((bf16[400,128]{1,0:T(8,128)(2,1)S(1)}, bf16[400,128]{1,0:T(8,128)(2,1)S(1)}, u32[]{:S(2)}, u32[]{:S(2)}) %collective-permute-start.21) | collective-permute-done | bytes 102432 | tf_op jit(solution)/shard_map/ppermute | solution.py:494
  76.5 1.8 %collective-permute-start.23 = (bf16[400,128]{1,0:T(8,128)(2,1)S(1)}, bf16[400,128]{1,0:T(8,128)(2,1)S(1)}, u32[]{:S(2)}, u32[]{:S(2)}) collective-permute-start(bf16[400,128]{1,0:T(8,128)(2,1)S(1)} %shard_map.138.refs_0_), channel_id=1, source_target_pairs={{0,8},{4,12},{8,0},{12,4},{16,24},{20,28},{24,16},{28,20},{1,9},{5... | collective-permute-start | bytes 307208 | tf_op jit(solution)/shard_map/ppermute | solution.py:494
  78.2 5.3 %collective-permute-done.24.refs_3_.refs_2_ = bf16[400,128]{1,0:T(8,128)(2,1)S(1)} collective-permute-done((bf16[400,128]{1,0:T(8,128)(2,1)S(1)}, bf16[400,128]{1,0:T(8,128)(2,1)S(1)}, u32[]{:S(2)}, u32[]{:S(2)}) %collective-permute-start.24) | collective-permute-done | bytes 102432 | tf_op jit(solution)/shard_map/ppermute | solution.py:494
  84.0 4.3 %collective-permute-done.25.refs_4_.refs_3_ = bf16[400,128]{1,0:T(8,128)(2,1)S(1)} collective-permute-done((bf16[400,128]{1,0:T(8,128)(2,1)S(1)}, bf16[400,128]{1,0:T(8,128)(2,1)S(1)}, u32[]{:S(2)}, u32[]{:S(2)}) %collective-permute-start.25) | collective-permute-done | bytes 102432 | tf_op jit(solution)/shard_map/ppermute | solution.py:494
  90.9 9.3 %collective-permute-done.31.refs_1_ = bf16[2,128,768]{2,1,0:T(8,128)(2,1)S(1)} collective-permute-done((bf16[2,128,768]{2,1,0:T(8,128)(2,1)S(1)}, bf16[2,128,768]{2,1,0:T(8,128)(2,1)S(1)}, u32[]{:S(2)}, u32[]{:S(2)}) %collective-permute-start.31) | collective-permute-done | bytes 393248 | tf_op jit(solution)/shard_map/ppermute | solution.py:494
  102.7 1.8 %collective-permute-start.35 = (bf16[1,144,768]{2,1,0:T(8,128)(2,1)S(1)}, bf16[1,144,768]{2,1,0:T(8,128)(2,1)S(1)}, u32[]{:S(2)}, u32[]{:S(2)}) collective-permute-start(bf16[1,144,768]{2,1,0:T(8,128)(2,1)S(1)} %get-tuple-element.74), channel_id=1, source_target_pairs={{0,16},{4,20},{8,24},{12,28},{16,0},{20,4},{24,8},{28,12},{1,17},{... | collective-permute-start | bytes 663560 | tf_op jit(solution)/shard_map/ppermute | solution.py:494
  104.4 3.6 %collective-permute-done.28.refs_0_ = bf16[2,400,128]{2,1,0:T(8,128)(2,1)S(1)} collective-permute-done((bf16[2,400,128]{2,1,0:T(8,128)(2,1)S(1)}, bf16[2,400,128]{2,1,0:T(8,128)(2,1)S(1)}, u32[]{:S(2)}, u32[]{:S(2)}) %collective-permute-start.28) | collective-permute-done | bytes 204832 | tf_op jit(solution)/shard_map/ppermute | solution.py:491
  108.0 2.4 %shard_map.146 = (f32[768,1024]{1,0:T(8,128)}, f32[768,1024]{1,0:T(8,128)}, f32[1,1024]{1,0:T(1,128)S(1)}) custom-call(bf16[12,400,128]{2,1,0:T(8,128)(2,1)S(1)} %shard_map.145.refs_0_, bf16[12,400,128]{2,1,0:T(8,128)(2,1)S(1)} %collective-permute-done.32.refs_1_), custom_call_target="tpu_custom_call" | custom-call | bytes 14155776 | tf_op jit(solution)/shard_map/pallas_call | solution.py:458
  111.0 4.5 %collective-permute-done.35.refs_8_ = bf16[1,144,768]{2,1,0:T(8,128)(2,1)S(1)} collective-permute-done((bf16[1,144,768]{2,1,0:T(8,128)(2,1)S(1)}, bf16[1,144,768]{2,1,0:T(8,128)(2,1)S(1)}, u32[]{:S(2)}, u32[]{:S(2)}) %collective-permute-start.35) | collective-permute-done | bytes 221216 | tf_op jit(solution)/shard_map/ppermute | solution.py:494
  115.6 1.9 %shard_map.148 = (f32[768,1024]{1,0:T(8,128)}, f32[768,1024]{1,0:T(8,128)}, f32[1,1024]{1,0:T(1,128)}, bf16[128,768]{1,0:T(8,128)(2,1)}) custom-call(bf16[2,400,128]{2,1,0:T(8,128)(2,1)S(1)} %collective-permute-done.28.refs_0_, bf16[2,400,128]{2,1,0:T(8,128)(2,1)S(1)} %shard_map.147.refs_1_, ...), custom_call_target="tpu_custom_call", output_to_operand_aliasing={{0}: (4, {}), {1}: (5, {})} | custom-call | bytes 4718592 | tf_op jit(solution)/shard_map/pallas_call | solution.py:458
  (92 shorter events, 31.7 us)
Async XLA Ops:
  0.6 13.5 %collective-permute-start.1 = (bf16[128,768]{1,0:T(8,128)(2,1)}, bf16[128,768]{1,0:T(8,128)(2,1)S(1)}, u32[]{:S(2)}, u32[]{:S(2)}) collective-permute-start(bf16[128,768]{1,0:T(8,128)(2,1)} %refs_1_.2), channel_id=1, source_target_pairs={{0,16},{4,20},{8,24},{12,28},{16,0},{20,4},{24,8},{28,12},{1,17},{... | collective-permute-start | bytes 589832 | tf_op jit(solution)/shard_map/ppermute | solution.py:494
  4.7 10.9 %collective-permute-start = (bf16[128,768]{1,0:T(8,128)(2,1)}, bf16[128,768]{1,0:T(8,128)(2,1)S(1)}, u32[]{:S(2)}, u32[]{:S(2)}) collective-permute-start(bf16[128,768]{1,0:T(8,128)(2,1)} %refs_1_.2), channel_id=1, source_target_pairs={{0,8},{4,12},{8,0},{12,4},{16,24},{20,28},{24,16},{28,20},{1,9},{5... | collective-permute-start | bytes 589832 | tf_op jit(solution)/shard_map/ppermute | solution.py:494
  6.3 12.2 %collective-permute-start.2 = (bf16[128,768]{1,0:T(8,128)(2,1)}, bf16[128,768]{1,0:T(8,128)(2,1)S(1)}, u32[]{:S(2)}, u32[]{:S(2)}) collective-permute-start(bf16[128,768]{1,0:T(8,128)(2,1)} %refs_1_.2), channel_id=1, source_target_pairs={{0,4},{4,0},{8,12},{12,8},{16,20},{20,16},{24,28},{28,24},{1,5},{5... | collective-permute-start | bytes 589832 | tf_op jit(solution)/shard_map/ppermute | solution.py:497
  12.6 9.1 %collective-permute-start.5 = (bf16[128,768]{1,0:T(8,128)(2,1)S(1)}, bf16[128,768]{1,0:T(8,128)(2,1)S(1)}, u32[]{:S(2)}, u32[]{:S(2)}) collective-permute-start(bf16[128,768]{1,0:T(8,128)(2,1)S(1)} %copy-done.4), channel_id=1, source_target_pairs={{0,0},{4,1},{9,10},{13,11},{18,20},{22,21},{27,30},{31,31}} | collective-permute-start | bytes 589832 | tf_op jit(solution)/shard_map/ppermute | solution.py:516
  14.2 7.4 %collective-permute-start.7 = (bf16[128,768]{1,0:T(8,128)(2,1)S(1)}, bf16[128,768]{1,0:T(8,128)(2,1)S(1)}, u32[]{:S(2)}, u32[]{:S(2)}) collective-permute-start(bf16[128,768]{1,0:T(8,128)(2,1)S(1)} %collective-permute-done.1.refs_3_.refs_0_), channel_id=1, source_target_pairs={{0,8},{4,12},{8,0},{12,4},{16,24},{20,28},{24,16},{28,20},{1,9},{5... | collective-permute-start | bytes 589832 | tf_op jit(solution)/shard_map/ppermute | solution.py:494
  28.7 6.9 %collective-permute-start.12 = (bf16[128,768]{1,0:T(8,128)(2,1)S(1)}, bf16[128,768]{1,0:T(8,128)(2,1)S(1)}, u32[]{:S(2)}, u32[]{:S(2)}) collective-permute-start(bf16[128,768]{1,0:T(8,128)(2,1)S(1)} %get-tuple-element.45), channel_id=1, source_target_pairs={{0,2},{1,3},{2,0},{3,1},{4,6},{5,7},{6,4},{7,5},{8,10},{9,11},{10,... | collective-permute-start | bytes 589832 | tf_op jit(solution)/shard_map/ppermute | solution.py:491
  29.0 10.9 %collective-permute-start.13 = (bf16[128,768]{1,0:T(8,128)(2,1)S(1)}, bf16[128,768]{1,0:T(8,128)(2,1)S(1)}, u32[]{:S(2)}, u32[]{:S(2)}) collective-permute-start(bf16[128,768]{1,0:T(8,128)(2,1)S(1)} %get-tuple-element.46), channel_id=1, source_target_pairs={{0,3},{1,2},{2,1},{3,0},{4,7},{5,6},{6,5},{7,4},{8,11},{9,10},{10,... | collective-permute-start | bytes 589832 | tf_op jit(solution)/shard_map/ppermute | solution.py:491
  41.3 11.2 %collective-permute-start.16 = (bf16[128,1408]{1,0:T(8,128)(2,1)S(1)}, bf16[128,1408]{1,0:T(8,128)(2,1)S(1)}, u32[]{:S(2)}, u32[]{:S(2)}) collective-permute-start(bf16[128,1408]{1,0:T(8,128)(2,1)S(1)} %get-tuple-element.50), channel_id=1, source_target_pairs={{0,1},{1,0},{2,3},{3,2},{4,5},{5,4},{6,7},{7,6},{8,9},{9,8},{10,11... | collective-permute-start | bytes 1081352 | tf_op jit(solution)/shard_map/ppermute | solution.py:491
  41.6 18.5 %collective-permute-start.17 = (bf16[128,1408]{1,0:T(8,128)(2,1)S(1)}, bf16[128,1408]{1,0:T(8,128)(2,1)S(1)}, u32[]{:S(2)}, u32[]{:S(2)}) collective-permute-start(bf16[128,1408]{1,0:T(8,128)(2,1)S(1)} %get-tuple-element.51), channel_id=1, source_target_pairs={{0,2},{1,3},{2,0},{3,1},{4,6},{5,7},{6,4},{7,5},{8,10},{9,11},{10,... | collective-permute-start | bytes 1081352 | tf_op jit(solution)/shard_map/ppermute | solution.py:491
  43.4 16.7 %collective-permute-start.18 = (bf16[128,1408]{1,0:T(8,128)(2,1)S(1)}, bf16[128,1408]{1,0:T(8,128)(2,1)S(1)}, u32[]{:S(2)}, u32[]{:S(2)}) collective-permute-start(bf16[128,1408]{1,0:T(8,128)(2,1)S(1)} %get-tuple-element.52), channel_id=1, source_target_pairs={{0,3},{1,2},{2,1},{3,0},{4,7},{5,6},{6,5},{7,4},{8,11},{9,10},{10,... | collective-permute-start | bytes 1081352 | tf_op jit(solution)/shard_map/ppermute | solution.py:491
  62.8 7.0 %collective-permute-start.20 = (bf16[400,128]{1,0:T(8,128)(2,1)S(1)}, bf16[400,128]{1,0:T(8,128)(2,1)S(1)}, u32[]{:S(2)}, u32[]{:S(2)}) collective-permute-start(bf16[400,128]{1,0:T(8,128)(2,1)S(1)} %get-tuple-element.59), channel_id=1, source_target_pairs={{0,24},{4,28},{8,16},{12,20},{16,8},{20,12},{24,0},{28,4},{1,25},{... | collective-permute-start | bytes 307208 | tf_op jit(solution)/shard_map/ppermute | solution.py:494
  64.1 12.1 %collective-permute-start.21 = (bf16[400,128]{1,0:T(8,128)(2,1)S(1)}, bf16[400,128]{1,0:T(8,128)(2,1)S(1)}, u32[]{:S(2)}, u32[]{:S(2)}) collective-permute-start(bf16[400,128]{1,0:T(8,128)(2,1)S(1)} %get-tuple-element.60), channel_id=1, source_target_pairs={{0,16},{4,20},{8,24},{12,28},{16,0},{20,4},{24,8},{28,12},{1,17},{... | collective-permute-start | bytes 307208 | tf_op jit(solution)/shard_map/ppermute | solution.py:494
  66.7 9.4 %collective-permute-start.22 = (bf16[400,128]{1,0:T(8,128)(2,1)S(1)}, bf16[400,128]{1,0:T(8,128)(2,1)S(1)}, u32[]{:S(2)}, u32[]{:S(2)}) collective-permute-start(bf16[400,128]{1,0:T(8,128)(2,1)S(1)} %get-tuple-element.61), channel_id=1, source_target_pairs={{0,8},{4,12},{8,0},{12,4},{16,24},{20,28},{24,16},{28,20},{1,9},{5... | collective-permute-start | bytes 307208 | tf_op jit(solution)/shard_map/ppermute | solution.py:494
  76.2 12.1 %collective-permute-start.26 = (bf16[4,128,768]{2,1,0:T(8,128)(2,1)S(1)}, bf16[4,128,768]{2,1,0:T(8,128)(2,1)S(1)}, u32[]{:S(2)}, u32[]{:S(2)}) collective-permute-start(bf16[4,128,768]{2,1,0:T(8,128)(2,1)S(1)} %shard_map.141), channel_id=1, source_target_pairs={{0,4},{4,0},{8,12},{12,8},{16,20},{20,16},{24,28},{28,24},{1,5},{5... | collective-permute-start | bytes 2359304 | tf_op jit(solution)/shard_map/ppermute | solution.py:497
  76.4 7.1 %collective-permute-start.24 = (bf16[400,128]{1,0:T(8,128)(2,1)S(1)}, bf16[400,128]{1,0:T(8,128)(2,1)S(1)}, u32[]{:S(2)}, u32[]{:S(2)}) collective-permute-start(bf16[400,128]{1,0:T(8,128)(2,1)S(1)} %shard_map.138.refs_0_), channel_id=1, source_target_pairs={{0,16},{4,20},{8,24},{12,28},{16,0},{20,4},{24,8},{28,12},{1,17},{... | collective-permute-start | bytes 307208 | tf_op jit(solution)/shard_map/ppermute | solution.py:494
  76.5 7.5 %collective-permute-start.23 = (bf16[400,128]{1,0:T(8,128)(2,1)S(1)}, bf16[400,128]{1,0:T(8,128)(2,1)S(1)}, u32[]{:S(2)}, u32[]{:S(2)}) collective-permute-start(bf16[400,128]{1,0:T(8,128)(2,1)S(1)} %shard_map.138.refs_0_), channel_id=1, source_target_pairs={{0,8},{4,12},{8,0},{12,4},{16,24},{20,28},{24,16},{28,20},{1,9},{5... | collective-permute-start | bytes 307208 | tf_op jit(solution)/shard_map/ppermute | solution.py:494
  88.5 11.8 %collective-permute-start.29 = (bf16[4,400,128]{2,1,0:T(8,128)(2,1)S(1)}, bf16[4,400,128]{2,1,0:T(8,128)(2,1)S(1)}, u32[]{:S(2)}, u32[]{:S(2)}) collective-permute-start(bf16[4,400,128]{2,1,0:T(8,128)(2,1)S(1)} %shard_map.143.refs_0_), channel_id=1, source_target_pairs={{0,2},{1,3},{2,0},{3,1},{4,6},{5,7},{6,4},{7,5},{8,10},{9,11},{10,... | collective-permute-start | bytes 1228808 | tf_op jit(solution)/shard_map/ppermute | solution.py:491
  90.0 10.3 %collective-permute-start.27 = (bf16[4,400,128]{2,1,0:T(8,128)(2,1)S(1)}, bf16[4,400,128]{2,1,0:T(8,128)(2,1)S(1)}, u32[]{:S(2)}, u32[]{:S(2)}) collective-permute-start(bf16[4,400,128]{2,1,0:T(8,128)(2,1)S(1)} %shard_map.143.refs_0_), channel_id=1, source_target_pairs={{0,1},{1,0},{2,3},{3,2},{4,5},{5,4},{6,7},{7,6},{8,9},{9,8},{10,11... | collective-permute-start | bytes 1228808 | tf_op jit(solution)/shard_map/ppermute | solution.py:491
  90.6 9.6 %collective-permute-start.31 = (bf16[2,128,768]{2,1,0:T(8,128)(2,1)S(1)}, bf16[2,128,768]{2,1,0:T(8,128)(2,1)S(1)}, u32[]{:S(2)}, u32[]{:S(2)}) collective-permute-start(bf16[2,128,768]{2,1,0:T(8,128)(2,1)S(1)} %get-tuple-element.68.refs_4_), channel_id=1, source_target_pairs={{0,8},{4,12},{8,0},{12,4},{16,24},{20,28},{24,16},{28,20},{1,9},{5... | collective-permute-start | bytes 1179656 | tf_op jit(solution)/shard_map/ppermute | solution.py:494
  100.4 7.6 %collective-permute-start.32 = (bf16[12,400,128]{2,1,0:T(8,128)(2,1)S(1)}, bf16[12,400,128]{2,1,0:T(8,128)(2,1)S(1)}, u32[]{:S(2)}, u32[]{:S(2)}) collective-permute-start(bf16[12,400,128]{2,1,0:T(8,128)(2,1)S(1)} %shard_map.145.refs_0_), channel_id=1, source_target_pairs={{0,4},{4,0},{8,12},{12,8},{16,20},{20,16},{24,28},{28,24},{1,5},{5... | collective-permute-start | bytes 3686408 | tf_op jit(solution)/shard_map/ppermute | solution.py:497
  100.5 7.5 %collective-permute-start.28 = (bf16[2,400,128]{2,1,0:T(8,128)(2,1)S(1)}, bf16[2,400,128]{2,1,0:T(8,128)(2,1)S(1)}, u32[]{:S(2)}, u32[]{:S(2)}) collective-permute-start(bf16[2,400,128]{2,1,0:T(8,128)(2,1)S(1)} %slice.14), channel_id=1, source_target_pairs={{0,2},{1,3},{2,0},{3,1},{4,6},{5,7},{6,4},{7,5},{8,10},{9,11},{10,... | collective-permute-start | bytes 614408 | tf_op jit(solution)/shard_map/ppermute | solution.py:491
  102.0 8.5 %collective-permute-start.30 = (bf16[2,400,128]{2,1,0:T(8,128)(2,1)S(1)}, bf16[2,400,128]{2,1,0:T(8,128)(2,1)S(1)}, u32[]{:S(2)}, u32[]{:S(2)}) collective-permute-start(bf16[2,400,128]{2,1,0:T(8,128)(2,1)S(1)} %slice.15), channel_id=1, source_target_pairs={{0,1},{1,0},{2,3},{3,2},{4,5},{5,4},{6,7},{7,6},{8,9},{9,8},{10,11... | collective-permute-start | bytes 614408 | tf_op jit(solution)/shard_map/ppermute | solution.py:491
  102.7 12.9 %collective-permute-start.35 = (bf16[1,144,768]{2,1,0:T(8,128)(2,1)S(1)}, bf16[1,144,768]{2,1,0:T(8,128)(2,1)S(1)}, u32[]{:S(2)}, u32[]{:S(2)}) collective-permute-start(bf16[1,144,768]{2,1,0:T(8,128)(2,1)S(1)} %get-tuple-element.74), channel_id=1, source_target_pairs={{0,16},{4,20},{8,24},{12,28},{16,0},{20,4},{24,8},{28,12},{1,17},{... | collective-permute-start | bytes 663560 | tf_op jit(solution)/shard_map/ppermute | solution.py:494
  108.0 7.5 %collective-permute-start.33 = (bf16[2,400,128]{2,1,0:T(8,128)(2,1)S(1)}, bf16[2,400,128]{2,1,0:T(8,128)(2,1)S(1)}, u32[]{:S(2)}, u32[]{:S(2)}) collective-permute-start(bf16[2,400,128]{2,1,0:T(8,128)(2,1)S(1)} %collective-permute-done.28.refs_0_), channel_id=1, source_target_pairs={{0,4},{4,0},{8,12},{12,8},{16,20},{20,16},{24,28},{28,24},{1,5},{5... | collective-permute-start | bytes 614408 | tf_op jit(solution)/shard_map/ppermute | solution.py:497
  (20 other events, 93.6 us)

commit v15 on v13

--- a/solution.py
+++ b/solution.py
@@ -365,20 +365,22 @@
     )
 
 
-def last_sum(parts):
+def last_sum(parts, passed):
     rows, width = parts[0].shape
     main = rows - EXTRA
 
     def body(*refs):
-        out_ref = refs[-1]
-        total = refs[0][...]
-        for ref in refs[1:-1]:
+        *part_refs, passed_ref, out_ref, again_ref = refs
+        total = part_refs[0][...]
+        for ref in part_refs[1:]:
             total = total + ref[...].astype(F32)
         out_ref[:main, :] = total[:main].astype(BF16)
         merged = total[main : main + 8] + total[main + 8 :]
         out_ref[main:, :] = split_pair(merged).astype(BF16)
-
-    return call(body, [shape((rows, width), BF16)], parts)[0]
+        again_ref[...] = passed_ref[...]
+
+    outs = [shape((rows, width), BF16), shape(passed.shape, passed.dtype)]
+    return call(body, outs, [*parts, passed])
 
 
 def assemble(pieces, begun, depth, hid, xr, nc, cs, factors, after, adds=()):
@@ -566,10 +568,10 @@
     scaled, self_parts = zip(early, late)
     chunks = pair_sum(keep, came)
     chunks = [chunks[0]] + [along_chips(chunks[k], k) for k in range(half - 1, 0, -1)]
-    line = gather_chips(last_sum(chunks))
-
     keep, send = back_parts(turned, scaled, self_parts, nd, cs, rs, [keep])
-    keep, send = fold(keep, other_core(follow(send, chunks[1:])), line[1:])
+    chunk, send = last_sum(chunks, send)
+    line = gather_chips(chunk)
+    keep, send = fold(keep, other_core(send), line[1:])
     line = stack(line, after=[send])
     step = 1
     while 2 * step < half:

time: 115 us -> 115 us (level)
    pallas_call x17 -> x16, Pallas kernels: 10.1 us -> 10.2 us  [call(): pl.pallas_call(run, out_shape=outs, in_specs=[SMEM] * smem + [VMEM] * (co...]
  transfers between devices with their start and end apart: 38 -> 38, of which waited for: 14 -> 15; matrix products, arithmetic and copies ran while one was open for 1% -> 1% of each run, Pallas kernels for 9% -> 9%
where the time goes in v15:
time: 115 us; the launch traced here: 114 us
  waiting for transfers between devices  57 us (50%)
  starting transfers between devices  37.7 us (33%)
  Pallas kernels  15.1 us (13%)
  local copies, waits for them, and re-layouts  2.61 us (2%)
  between operations  1.63 us (1%)
    ppermute x11, waiting for transfers between devices, along_chips(): return lax.ppermute(x, 'row', [(s, s ^ 2 * k) for s in range(rs)])  33 us
    ppermute x12, waiting for transfers between devices, along_col(): return lax.ppermute(x, 'col', [(s, s ^ k) for s in range(cs)])  22.2 us
    ppermute x11, starting transfers between devices, along_chips(): return lax.ppermute(x, 'row', [(s, s ^ 2 * k) for s in range(rs)])  14.8 us
    ppermute x12, starting transfers between devices, along_col(): return lax.ppermute(x, 'col', [(s, s ^ k) for s in range(cs)])  13 us
    pallas_call x16, Pallas kernels, call(): pl.pallas_call(run, out_shape=outs, in_specs=[SMEM] * smem + [VMEM] * (co...  10.2 us
    ppermute x4, starting transfers between devices, send_own(): return lax.ppermute(block, ('row', 'col'), pairs)  7.22 us
    pallas_call x2, Pallas kernels, assemble(): pl.pallas_call(run, out_shape=[weight, weight, shape((1, hid), F32), *sum...  4.89 us
    ppermute x11, starting transfers between devices, other_core(): return lax.ppermute(x, 'row', [(s, s ^ 1) for s in range(rs)])  2.6 us
  transfers between devices with their start and end apart: 38, of which 15 were waited for; matrix products, arithmetic and copies ran while one was open for 1% of the time, Pallas kernels for 9%

profile of v15, /device:TPU:0, one launch (start us, length us, event | category | flops | bytes accessed | tf_op | source)
XLA Modules:
  0.0 114.5 jit_solution(15566625723497378345)
XLA Ops:
  0.6 4.1 %collective-permute-start.1 = (bf16[128,768]{1,0:T(8,128)(2,1)}, bf16[128,768]{1,0:T(8,128)(2,1)S(1)}, u32[]{:S(2)}, u32[]{:S(2)}) collective-permute-start(bf16[128,768]{1,0:T(8,128)(2,1)} %refs_1_.2), channel_id=1, source_target_pairs={{0,16},{4,20},{8,24},{12,28},{16,0},{20,4},{24,8},{28,12},{1,17},{... | collective-permute-start | bytes 589832 | tf_op jit(solution)/shard_map/ppermute | solution.py:479
  4.7 1.6 %collective-permute-start = (bf16[128,768]{1,0:T(8,128)(2,1)}, bf16[128,768]{1,0:T(8,128)(2,1)S(1)}, u32[]{:S(2)}, u32[]{:S(2)}) collective-permute-start(bf16[128,768]{1,0:T(8,128)(2,1)} %refs_1_.2), channel_id=1, source_target_pairs={{0,8},{4,12},{8,0},{12,4},{16,24},{20,28},{24,16},{28,20},{1,9},{5... | collective-permute-start | bytes 589832 | tf_op jit(solution)/shard_map/ppermute | solution.py:479
  9.4 1.5 %shard_map.128 = (bf16[512,1024]{1,0:T(8,128)(2,1)S(1)}, bf16[1024,512]{1,0:T(8,128)(2,1)S(1)}) custom-call(s32[24]{0:T(128)S(1)} %bitcast.12, s32[24]{0:T(128)S(1)} %bitcast.13, s32[1]{0:T(128)} %bitcast.9.refs_2_, bf16[24,128,128]{2,1,0:T(8,128)(2,1)S(1)} %bitcast.10), custom_call_target="tpu_custom_call" | custom-call | flops 524288 | bytes 2883780 | tf_op jit(solution)/shard_map/pallas_call | solution.py:32
  11.3 1.7 %collective-permute-start.9 = (f32[8,512]{1,0:T(8,128)S(1)}, f32[8,512]{1,0:T(8,128)S(1)}, u32[]{:S(2)}, u32[]{:S(2)}) collective-permute-start(f32[8,512]{1,0:T(8,128)S(1)} %shard_map.130), channel_id=1, source_target_pairs={{0,1},{1,0},{2,3},{3,2},{4,5},{5,4},{6,7},{7,6},{8,9},{9,8},{10,11... | collective-permute-start | bytes 49160 | tf_op jit(solution)/shard_map/ppermute | solution.py:476
  15.5 2.8 %collective-permute-start.6 = (bf16[128,768]{1,0:T(8,128)(2,1)S(1)}, bf16[128,768]{1,0:T(8,128)(2,1)S(1)}, u32[]{:S(2)}, u32[]{:S(2)}) collective-permute-start(bf16[128,768]{1,0:T(8,128)(2,1)S(1)} %collective-permute-done.refs_2_), channel_id=1, source_target_pairs={{0,2},{4,3},{9,8},{13,9},{18,22},{22,23},{27,28},{31,29}} | collective-permute-start | bytes 589832 | tf_op jit(solution)/shard_map/ppermute | solution.py:501
  19.6 2.0 %collective-permute-done.7.refs_2_ = bf16[128,768]{1,0:T(8,128)(2,1)S(1)} collective-permute-done((bf16[128,768]{1,0:T(8,128)(2,1)S(1)}, bf16[128,768]{1,0:T(8,128)(2,1)S(1)}, u32[]{:S(2)}, u32[]{:S(2)}) %collective-permute-start.7) | collective-permute-done | bytes 196640 | tf_op jit(solution)/shard_map/ppermute | solution.py:479
  22.6 2.4 %collective-permute-start.10 = (bf16[128,768]{1,0:T(8,128)(2,1)S(1)}, bf16[128,768]{1,0:T(8,128)(2,1)S(1)}, u32[]{:S(2)}, u32[]{:S(2)}) collective-permute-start(bf16[128,768]{1,0:T(8,128)(2,1)S(1)} %shard_map.131), channel_id=1, source_target_pairs={{0,4},{4,5},{9,14},{13,15},{18,16},{22,17},{27,26},{31,27}} | collective-permute-start | bytes 589832 | tf_op jit(solution)/shard_map/ppermute | solution.py:501
  26.9 1.9 %collective-permute-start.11 = (bf16[128,768]{1,0:T(8,128)(2,1)S(1)}, bf16[128,768]{1,0:T(8,128)(2,1)S(1)}, u32[]{:S(2)}, u32[]{:S(2)}) collective-permute-start(bf16[128,768]{1,0:T(8,128)(2,1)S(1)} %get-tuple-element.46), channel_id=1, source_target_pairs={{0,1},{1,0},{2,3},{3,2},{4,5},{5,4},{6,7},{7,6},{8,9},{9,8},{10,11... | collective-permute-start | bytes 589832 | tf_op jit(solution)/shard_map/ppermute | solution.py:476
  31.8 1.9 %collective-permute-done.11.refs_1_ = bf16[128,768]{1,0:T(8,128)(2,1)S(1)} collective-permute-done((bf16[128,768]{1,0:T(8,128)(2,1)S(1)}, bf16[128,768]{1,0:T(8,128)(2,1)S(1)}, u32[]{:S(2)}, u32[]{:S(2)}) %collective-permute-start.11) | collective-permute-done | bytes 196640 | tf_op jit(solution)/shard_map/ppermute | solution.py:476
  33.7 6.5 %collective-permute-done.12.refs_2_ = bf16[128,768]{1,0:T(8,128)(2,1)S(1)} collective-permute-done((bf16[128,768]{1,0:T(8,128)(2,1)S(1)}, bf16[128,768]{1,0:T(8,128)(2,1)S(1)}, u32[]{:S(2)}, u32[]{:S(2)}) %collective-permute-start.12) | collective-permute-done | bytes 196640 | tf_op jit(solution)/shard_map/ppermute | solution.py:476
  41.7 2.3 %collective-permute-start.17 = (bf16[128,1408]{1,0:T(8,128)(2,1)S(1)}, bf16[128,1408]{1,0:T(8,128)(2,1)S(1)}, u32[]{:S(2)}, u32[]{:S(2)}) collective-permute-start(bf16[128,1408]{1,0:T(8,128)(2,1)S(1)} %get-tuple-element.53), channel_id=1, source_target_pairs={{0,2},{1,3},{2,0},{3,1},{4,6},{5,7},{6,4},{7,5},{8,10},{9,11},{10,... | collective-permute-start | bytes 1081352 | tf_op jit(solution)/shard_map/ppermute | solution.py:476
  45.2 7.7 %collective-permute-done.16.refs_4_.refs_1_ = bf16[128,1408]{1,0:T(8,128)(2,1)S(1)} collective-permute-done((bf16[128,1408]{1,0:T(8,128)(2,1)S(1)}, bf16[128,1408]{1,0:T(8,128)(2,1)S(1)}, u32[]{:S(2)}, u32[]{:S(2)}) %collective-permute-start.16) | collective-permute-done | bytes 360480 | tf_op jit(solution)/shard_map/ppermute | solution.py:476
  54.2 5.9 %collective-permute-done.17.refs_2_.refs_3_ = bf16[128,1408]{1,0:T(8,128)(2,1)S(1)} collective-permute-done((bf16[128,1408]{1,0:T(8,128)(2,1)S(1)}, bf16[128,1408]{1,0:T(8,128)(2,1)S(1)}, u32[]{:S(2)}, u32[]{:S(2)}) %collective-permute-start.17) | collective-permute-done | bytes 360480 | tf_op jit(solution)/shard_map/ppermute | solution.py:476
  61.0 1.7 %collective-permute-done.19.refs_1_ = bf16[4,400,128]{2,1,0:T(8,128)(2,1)S(1)} collective-permute-done((bf16[4,400,128]{2,1,0:T(8,128)(2,1)S(1)}, bf16[4,400,128]{2,1,0:T(8,128)(2,1)S(1)}, u32[]{:S(2)}, u32[]{:S(2)}) %collective-permute-start.19) | collective-permute-done | bytes 409632 | tf_op jit(solution)/shard_map/ppermute | solution.py:482
  64.1 2.7 %collective-permute-start.21 = (bf16[400,128]{1,0:T(8,128)(2,1)S(1)}, bf16[400,128]{1,0:T(8,128)(2,1)S(1)}, u32[]{:S(2)}, u32[]{:S(2)}) collective-permute-start(bf16[400,128]{1,0:T(8,128)(2,1)S(1)} %get-tuple-element.62), channel_id=1, source_target_pairs={{0,16},{4,20},{8,24},{12,28},{16,0},{20,4},{24,8},{28,12},{1,17},{... | collective-permute-start | bytes 307208 | tf_op jit(solution)/shard_map/ppermute | solution.py:479
  69.9 6.3 %collective-permute-done.21.refs_2_ = bf16[400,128]{1,0:T(8,128)(2,1)S(1)} collective-permute-done((bf16[400,128]{1,0:T(8,128)(2,1)S(1)}, bf16[400,128]{1,0:T(8,128)(2,1)S(1)}, u32[]{:S(2)}, u32[]{:S(2)}) %collective-permute-start.21) | collective-permute-done | bytes 102432 | tf_op jit(solution)/shard_map/ppermute | solution.py:479
  76.5 1.7 %collective-permute-start.23 = (bf16[400,128]{1,0:T(8,128)(2,1)S(1)}, bf16[400,128]{1,0:T(8,128)(2,1)S(1)}, u32[]{:S(2)}, u32[]{:S(2)}) collective-permute-start(bf16[400,128]{1,0:T(8,128)(2,1)S(1)} %get-tuple-element.69.refs_0_), channel_id=1, source_target_pairs={{0,8},{4,12},{8,0},{12,4},{16,24},{20,28},{24,16},{28,20},{1,9},{5... | collective-permute-start | bytes 307208 | tf_op jit(solution)/shard_map/ppermute | solution.py:479
  78.2 5.2 %collective-permute-done.24.refs_3_.refs_2_ = bf16[400,128]{1,0:T(8,128)(2,1)S(1)} collective-permute-done((bf16[400,128]{1,0:T(8,128)(2,1)S(1)}, bf16[400,128]{1,0:T(8,128)(2,1)S(1)}, u32[]{:S(2)}, u32[]{:S(2)}) %collective-permute-start.24) | collective-permute-done | bytes 102432 | tf_op jit(solution)/shard_map/ppermute | solution.py:479
  83.9 4.3 %collective-permute-done.25.refs_4_.refs_3_ = bf16[400,128]{1,0:T(8,128)(2,1)S(1)} collective-permute-done((bf16[400,128]{1,0:T(8,128)(2,1)S(1)}, bf16[400,128]{1,0:T(8,128)(2,1)S(1)}, u32[]{:S(2)}, u32[]{:S(2)}) %collective-permute-start.25) | collective-permute-done | bytes 102432 | tf_op jit(solution)/shard_map/ppermute | solution.py:479
  90.9 7.8 %collective-permute-done.31.refs_1_ = bf16[2,128,768]{2,1,0:T(8,128)(2,1)S(1)} collective-permute-done((bf16[2,128,768]{2,1,0:T(8,128)(2,1)S(1)}, bf16[2,128,768]{2,1,0:T(8,128)(2,1)S(1)}, u32[]{:S(2)}, u32[]{:S(2)}) %collective-permute-start.31) | collective-permute-done | bytes 393248 | tf_op jit(solution)/shard_map/ppermute | solution.py:479
  98.7 1.8 %collective-permute-start.32 = (bf16[1,128,768]{2,1,0:T(8,128)(2,1)S(1)}, bf16[1,128,768]{2,1,0:T(8,128)(2,1)S(1)}, u32[]{:S(2)}, u32[]{:S(2)}) collective-permute-start(bf16[1,128,768]{2,1,0:T(8,128)(2,1)S(1)} %get-tuple-element.75), channel_id=1, source_target_pairs={{0,16},{4,20},{8,24},{12,28},{16,0},{20,4},{24,8},{28,12},{1,17},{... | collective-permute-start | bytes 589832 | tf_op jit(solution)/shard_map/ppermute | solution.py:479
  102.8 6.2 %collective-permute-done.32.refs_6_ = bf16[1,128,768]{2,1,0:T(8,128)(2,1)S(1)} collective-permute-done((bf16[1,128,768]{2,1,0:T(8,128)(2,1)S(1)}, bf16[1,128,768]{2,1,0:T(8,128)(2,1)S(1)}, u32[]{:S(2)}, u32[]{:S(2)}) %collective-permute-start.32) | collective-permute-done | bytes 196640 | tf_op jit(solution)/shard_map/ppermute | solution.py:479
  109.5 2.5 %shard_map.144 = (f32[768,1024]{1,0:T(8,128)}, f32[768,1024]{1,0:T(8,128)}, f32[1,1024]{1,0:T(1,128)S(1)}, bf16[128,768]{1,0:T(8,128)(2,1)}) custom-call(bf16[4,400,128]{2,1,0:T(8,128)(2,1)S(1)} %shard_map.142.refs_0_, bf16[4,400,128]{2,1,0:T(8,128)(2,1)S(1)} %collective-permute-done.27.refs_1_, bf16[4,400,128]{2,1,0:T(8,128)(2,1)S(1)} %collective-permute-done.28.refs_2_, ...), custom_call_target="tpu_custom_call" | custom-call | bytes 9437184 | tf_op jit(solution)/shard_map/pallas_call | solution.py:443
  112.1 2.4 %shard_map.145 = (f32[768,1024]{1,0:T(8,128)}, f32[768,1024]{1,0:T(8,128)}, f32[1,1024]{1,0:T(1,128)}) custom-call(bf16[4,400,128]{2,1,0:T(8,128)(2,1)S(1)} %collective-permute-done.33.refs_0_, bf16[4,400,128]{2,1,0:T(8,128)(2,1)S(1)} %collective-permute-done.34.refs_1_, ...), custom_call_target="tpu_custom_call", output_to_operand_aliasing={{0}: (5, {}), {1}: (6, {})} | custom-call | bytes 9437184 | tf_op jit(solution)/shard_map/pallas_call | solution.py:443
  (93 shorter events, 27.7 us)
Async XLA Ops:
  0.6 13.5 %collective-permute-start.1 = (bf16[128,768]{1,0:T(8,128)(2,1)}, bf16[128,768]{1,0:T(8,128)(2,1)S(1)}, u32[]{:S(2)}, u32[]{:S(2)}) collective-permute-start(bf16[128,768]{1,0:T(8,128)(2,1)} %refs_1_.2), channel_id=1, source_target_pairs={{0,16},{4,20},{8,24},{12,28},{16,0},{20,4},{24,8},{28,12},{1,17},{... | collective-permute-start | bytes 589832 | tf_op jit(solution)/shard_map/ppermute | solution.py:479
  4.7 10.8 %collective-permute-start = (bf16[128,768]{1,0:T(8,128)(2,1)}, bf16[128,768]{1,0:T(8,128)(2,1)S(1)}, u32[]{:S(2)}, u32[]{:S(2)}) collective-permute-start(bf16[128,768]{1,0:T(8,128)(2,1)} %refs_1_.2), channel_id=1, source_target_pairs={{0,8},{4,12},{8,0},{12,4},{16,24},{20,28},{24,16},{28,20},{1,9},{5... | collective-permute-start | bytes 589832 | tf_op jit(solution)/shard_map/ppermute | solution.py:479
  6.3 12.0 %collective-permute-start.2 = (bf16[128,768]{1,0:T(8,128)(2,1)}, bf16[128,768]{1,0:T(8,128)(2,1)S(1)}, u32[]{:S(2)}, u32[]{:S(2)}) collective-permute-start(bf16[128,768]{1,0:T(8,128)(2,1)} %refs_1_.2), channel_id=1, source_target_pairs={{0,4},{4,0},{8,12},{12,8},{16,20},{20,16},{24,28},{28,24},{1,5},{5... | collective-permute-start | bytes 589832 | tf_op jit(solution)/shard_map/ppermute | solution.py:482
  13.0 8.8 %collective-permute-start.5 = (bf16[128,768]{1,0:T(8,128)(2,1)S(1)}, bf16[128,768]{1,0:T(8,128)(2,1)S(1)}, u32[]{:S(2)}, u32[]{:S(2)}) collective-permute-start(bf16[128,768]{1,0:T(8,128)(2,1)S(1)} %copy-done.4), channel_id=1, source_target_pairs={{0,0},{4,1},{9,10},{13,11},{18,20},{22,21},{27,30},{31,31}} | collective-permute-start | bytes 589832 | tf_op jit(solution)/shard_map/ppermute | solution.py:501
  14.2 7.5 %collective-permute-start.7 = (bf16[128,768]{1,0:T(8,128)(2,1)S(1)}, bf16[128,768]{1,0:T(8,128)(2,1)S(1)}, u32[]{:S(2)}, u32[]{:S(2)}) collective-permute-start(bf16[128,768]{1,0:T(8,128)(2,1)S(1)} %collective-permute-done.1.refs_3_.refs_0_), channel_id=1, source_target_pairs={{0,8},{4,12},{8,0},{12,4},{16,24},{20,28},{24,16},{28,20},{1,9},{5... | collective-permute-start | bytes 589832 | tf_op jit(solution)/shard_map/ppermute | solution.py:479
  28.8 11.4 %collective-permute-start.12 = (bf16[128,768]{1,0:T(8,128)(2,1)S(1)}, bf16[128,768]{1,0:T(8,128)(2,1)S(1)}, u32[]{:S(2)}, u32[]{:S(2)}) collective-permute-start(bf16[128,768]{1,0:T(8,128)(2,1)S(1)} %get-tuple-element.47), channel_id=1, source_target_pairs={{0,2},{1,3},{2,0},{3,1},{4,6},{5,7},{6,4},{7,5},{8,10},{9,11},{10,... | collective-permute-start | bytes 589832 | tf_op jit(solution)/shard_map/ppermute | solution.py:476
  29.0 11.2 %collective-permute-start.13 = (bf16[128,768]{1,0:T(8,128)(2,1)S(1)}, bf16[128,768]{1,0:T(8,128)(2,1)S(1)}, u32[]{:S(2)}, u32[]{:S(2)}) collective-permute-start(bf16[128,768]{1,0:T(8,128)(2,1)S(1)} %get-tuple-element.48), channel_id=1, source_target_pairs={{0,3},{1,2},{2,1},{3,0},{4,7},{5,6},{6,5},{7,4},{8,11},{9,10},{10,... | collective-permute-start | bytes 589832 | tf_op jit(solution)/shard_map/ppermute | solution.py:476
  41.7 11.2 %collective-permute-start.16 = (bf16[128,1408]{1,0:T(8,128)(2,1)S(1)}, bf16[128,1408]{1,0:T(8,128)(2,1)S(1)}, u32[]{:S(2)}, u32[]{:S(2)}) collective-permute-start(bf16[128,1408]{1,0:T(8,128)(2,1)S(1)} %get-tuple-element.52), channel_id=1, source_target_pairs={{0,1},{1,0},{2,3},{3,2},{4,5},{5,4},{6,7},{7,6},{8,9},{9,8},{10,11... | collective-permute-start | bytes 1081352 | tf_op jit(solution)/shard_map/ppermute | solution.py:476
  41.7 18.4 %collective-permute-start.17 = (bf16[128,1408]{1,0:T(8,128)(2,1)S(1)}, bf16[128,1408]{1,0:T(8,128)(2,1)S(1)}, u32[]{:S(2)}, u32[]{:S(2)}) collective-permute-start(bf16[128,1408]{1,0:T(8,128)(2,1)S(1)} %get-tuple-element.53), channel_id=1, source_target_pairs={{0,2},{1,3},{2,0},{3,1},{4,6},{5,7},{6,4},{7,5},{8,10},{9,11},{10,... | collective-permute-start | bytes 1081352 | tf_op jit(solution)/shard_map/ppermute | solution.py:476
  44.0 16.1 %collective-permute-start.18 = (bf16[128,1408]{1,0:T(8,128)(2,1)S(1)}, bf16[128,1408]{1,0:T(8,128)(2,1)S(1)}, u32[]{:S(2)}, u32[]{:S(2)}) collective-permute-start(bf16[128,1408]{1,0:T(8,128)(2,1)S(1)} %get-tuple-element.54), channel_id=1, source_target_pairs={{0,3},{1,2},{2,1},{3,0},{4,7},{5,6},{6,5},{7,4},{8,11},{9,10},{10,... | collective-permute-start | bytes 1081352 | tf_op jit(solution)/shard_map/ppermute | solution.py:476
  62.8 7.1 %collective-permute-start.20 = (bf16[400,128]{1,0:T(8,128)(2,1)S(1)}, bf16[400,128]{1,0:T(8,128)(2,1)S(1)}, u32[]{:S(2)}, u32[]{:S(2)}) collective-permute-start(bf16[400,128]{1,0:T(8,128)(2,1)S(1)} %get-tuple-element.61), channel_id=1, source_target_pairs={{0,24},{4,28},{8,16},{12,20},{16,8},{20,12},{24,0},{28,4},{1,25},{... | collective-permute-start | bytes 307208 | tf_op jit(solution)/shard_map/ppermute | solution.py:479
  64.1 12.1 %collective-permute-start.21 = (bf16[400,128]{1,0:T(8,128)(2,1)S(1)}, bf16[400,128]{1,0:T(8,128)(2,1)S(1)}, u32[]{:S(2)}, u32[]{:S(2)}) collective-permute-start(bf16[400,128]{1,0:T(8,128)(2,1)S(1)} %get-tuple-element.62), channel_id=1, source_target_pairs={{0,16},{4,20},{8,24},{12,28},{16,0},{20,4},{24,8},{28,12},{1,17},{... | collective-permute-start | bytes 307208 | tf_op jit(solution)/shard_map/ppermute | solution.py:479
  66.7 9.5 %collective-permute-start.22 = (bf16[400,128]{1,0:T(8,128)(2,1)S(1)}, bf16[400,128]{1,0:T(8,128)(2,1)S(1)}, u32[]{:S(2)}, u32[]{:S(2)}) collective-permute-start(bf16[400,128]{1,0:T(8,128)(2,1)S(1)} %get-tuple-element.63), channel_id=1, source_target_pairs={{0,8},{4,12},{8,0},{12,4},{16,24},{20,28},{24,16},{28,20},{1,9},{5... | collective-permute-start | bytes 307208 | tf_op jit(solution)/shard_map/ppermute | solution.py:479
  76.3 11.9 %collective-permute-start.26 = (bf16[4,128,768]{2,1,0:T(8,128)(2,1)S(1)}, bf16[4,128,768]{2,1,0:T(8,128)(2,1)S(1)}, u32[]{:S(2)}, u32[]{:S(2)}) collective-permute-start(bf16[4,128,768]{2,1,0:T(8,128)(2,1)S(1)} %get-tuple-element.71), channel_id=1, source_target_pairs={{0,4},{4,0},{8,12},{12,8},{16,20},{20,16},{24,28},{28,24},{1,5},{5... | collective-permute-start | bytes 2359304 | tf_op jit(solution)/shard_map/ppermute | solution.py:482
  76.4 7.0 %collective-permute-start.24 = (bf16[400,128]{1,0:T(8,128)(2,1)S(1)}, bf16[400,128]{1,0:T(8,128)(2,1)S(1)}, u32[]{:S(2)}, u32[]{:S(2)}) collective-permute-start(bf16[400,128]{1,0:T(8,128)(2,1)S(1)} %get-tuple-element.69.refs_0_), channel_id=1, source_target_pairs={{0,16},{4,20},{8,24},{12,28},{16,0},{20,4},{24,8},{28,12},{1,17},{... | collective-permute-start | bytes 307208 | tf_op jit(solution)/shard_map/ppermute | solution.py:479
  76.5 7.4 %collective-permute-start.23 = (bf16[400,128]{1,0:T(8,128)(2,1)S(1)}, bf16[400,128]{1,0:T(8,128)(2,1)S(1)}, u32[]{:S(2)}, u32[]{:S(2)}) collective-permute-start(bf16[400,128]{1,0:T(8,128)(2,1)S(1)} %get-tuple-element.69.refs_0_), channel_id=1, source_target_pairs={{0,8},{4,12},{8,0},{12,4},{16,24},{20,28},{24,16},{28,20},{1,9},{5... | collective-permute-start | bytes 307208 | tf_op jit(solution)/shard_map/ppermute | solution.py:479
  88.4 10.2 %collective-permute-start.31 = (bf16[2,128,768]{2,1,0:T(8,128)(2,1)S(1)}, bf16[2,128,768]{2,1,0:T(8,128)(2,1)S(1)}, u32[]{:S(2)}, u32[]{:S(2)}) collective-permute-start(bf16[2,128,768]{2,1,0:T(8,128)(2,1)S(1)} %get-tuple-element.72.refs_4_), channel_id=1, source_target_pairs={{0,8},{4,12},{8,0},{12,4},{16,24},{20,28},{24,16},{28,20},{1,9},{5... | collective-permute-start | bytes 1179656 | tf_op jit(solution)/shard_map/ppermute | solution.py:479
  88.8 11.8 %collective-permute-start.28 = (bf16[4,400,128]{2,1,0:T(8,128)(2,1)S(1)}, bf16[4,400,128]{2,1,0:T(8,128)(2,1)S(1)}, u32[]{:S(2)}, u32[]{:S(2)}) collective-permute-start(bf16[4,400,128]{2,1,0:T(8,128)(2,1)S(1)} %shard_map.142.refs_0_), channel_id=1, source_target_pairs={{0,2},{1,3},{2,0},{3,1},{4,6},{5,7},{6,4},{7,5},{8,10},{9,11},{10,... | collective-permute-start | bytes 1228808 | tf_op jit(solution)/shard_map/ppermute | solution.py:476
  90.2 11.0 %collective-permute-start.27 = (bf16[4,400,128]{2,1,0:T(8,128)(2,1)S(1)}, bf16[4,400,128]{2,1,0:T(8,128)(2,1)S(1)}, u32[]{:S(2)}, u32[]{:S(2)}) collective-permute-start(bf16[4,400,128]{2,1,0:T(8,128)(2,1)S(1)} %shard_map.142.refs_0_), channel_id=1, source_target_pairs={{0,1},{1,0},{2,3},{3,2},{4,5},{5,4},{6,7},{7,6},{8,9},{9,8},{10,11... | collective-permute-start | bytes 1228808 | tf_op jit(solution)/shard_map/ppermute | solution.py:476
  98.7 10.2 %collective-permute-start.32 = (bf16[1,128,768]{2,1,0:T(8,128)(2,1)S(1)}, bf16[1,128,768]{2,1,0:T(8,128)(2,1)S(1)}, u32[]{:S(2)}, u32[]{:S(2)}) collective-permute-start(bf16[1,128,768]{2,1,0:T(8,128)(2,1)S(1)} %get-tuple-element.75), channel_id=1, source_target_pairs={{0,16},{4,20},{8,24},{12,28},{16,0},{20,4},{24,8},{28,12},{1,17},{... | collective-permute-start | bytes 589832 | tf_op jit(solution)/shard_map/ppermute | solution.py:479
  100.6 11.5 %collective-permute-start.33 = (bf16[4,400,128]{2,1,0:T(8,128)(2,1)S(1)}, bf16[4,400,128]{2,1,0:T(8,128)(2,1)S(1)}, u32[]{:S(2)}, u32[]{:S(2)}) collective-permute-start(bf16[4,400,128]{2,1,0:T(8,128)(2,1)S(1)} %shard_map.142.refs_0_), channel_id=1, source_target_pairs={{0,4},{4,0},{8,12},{12,8},{16,20},{20,16},{24,28},{28,24},{1,5},{5... | collective-permute-start | bytes 1228808 | tf_op jit(solution)/shard_map/ppermute | solution.py:482
  100.6 8.4 %collective-permute-start.30 = (bf16[2,400,128]{2,1,0:T(8,128)(2,1)S(1)}, bf16[2,400,128]{2,1,0:T(8,128)(2,1)S(1)}, u32[]{:S(2)}, u32[]{:S(2)}) collective-permute-start(bf16[2,400,128]{2,1,0:T(8,128)(2,1)S(1)} %slice.15), channel_id=1, source_target_pairs={{0,1},{1,0},{2,3},{3,2},{4,5},{5,4},{6,7},{7,6},{8,9},{9,8},{10,11... | collective-permute-start | bytes 614408 | tf_op jit(solution)/shard_map/ppermute | solution.py:476
  101.3 8.2 %collective-permute-start.29 = (bf16[2,400,128]{2,1,0:T(8,128)(2,1)S(1)}, bf16[2,400,128]{2,1,0:T(8,128)(2,1)S(1)}, u32[]{:S(2)}, u32[]{:S(2)}) collective-permute-start(bf16[2,400,128]{2,1,0:T(8,128)(2,1)S(1)} %slice.14), channel_id=1, source_target_pairs={{0,2},{1,3},{2,0},{3,1},{4,6},{5,7},{6,4},{7,5},{8,10},{9,11},{10,... | collective-permute-start | bytes 614408 | tf_op jit(solution)/shard_map/ppermute | solution.py:476
  102.8 9.3 %collective-permute-start.35 = (bf16[4,400,128]{2,1,0:T(8,128)(2,1)S(1)}, bf16[4,400,128]{2,1,0:T(8,128)(2,1)S(1)}, u32[]{:S(2)}, u32[]{:S(2)}) collective-permute-start(bf16[4,400,128]{2,1,0:T(8,128)(2,1)S(1)} %collective-permute-done.28.refs_2_), channel_id=1, source_target_pairs={{0,4},{4,0},{8,12},{12,8},{16,20},{20,16},{24,28},{28,24},{1,5},{5... | collective-permute-start | bytes 1228808 | tf_op jit(solution)/shard_map/ppermute | solution.py:482
  (22 other events, 98.4 us)

commit v16 on v15

--- a/solution.py
+++ b/solution.py
@@ -571,7 +571,7 @@
     keep, send = back_parts(turned, scaled, self_parts, nd, cs, rs, [keep])
     chunk, send = last_sum(chunks, send)
     line = gather_chips(chunk)
-    keep, send = fold(keep, other_core(send), line[1:])
+    keep, send = fold(keep, other_core(send))
     line = stack(line, after=[send])
     step = 1
     while 2 * step < half:

time: 115 us -> 120 us (1.043)
  waiting for transfers between devices: 57 us -> 63.7 us
  starting transfers between devices: 37.7 us -> 35.9 us
    ppermute x12, waiting for transfers between devices: 22.2 us -> 35 us  [along_col(): return lax.ppermute(x, 'col', [(s, s ^ k) for s in range(cs)])]
    ppermute x11, waiting for transfers between devices: 33 us -> 24.8 us  [along_chips(): return lax.ppermute(x, 'row', [(s, s ^ 2 * k) for s in range(rs)])]
    ppermute x11, waiting for transfers between devices: 1.76 us -> 3.95 us  [other_core(): return lax.ppermute(x, 'row', [(s, s ^ 1) for s in range(rs)])]
    ppermute x11, starting transfers between devices: 14.8 us -> 13.1 us  [along_chips(): return lax.ppermute(x, 'row', [(s, s ^ 2 * k) for s in range(rs)])]
  transfers between devices with their start and end apart: 38 -> 38, of which waited for: 15 -> 17; matrix products, arithmetic and copies ran while one was open for 1% -> 0% of each run, Pallas kernels for 9% -> 9%
where the time goes in v16:
time: 120 us; the launch traced here: 119 us
  waiting for transfers between devices  63.7 us (53%)
  starting transfers between devices  35.9 us (30%)
  Pallas kernels  15 us (12%)
  local copies, waits for them, and re-layouts  2.61 us (2%)
  between operations  1.63 us (1%)
    ppermute x12, waiting for transfers between devices, along_col(): return lax.ppermute(x, 'col', [(s, s ^ k) for s in range(cs)])  35 us
    ppermute x11, waiting for transfers between devices, along_chips(): return lax.ppermute(x, 'row', [(s, s ^ 2 * k) for s in range(rs)])  24.8 us
    ppermute x11, starting transfers between devices, along_chips(): return lax.ppermute(x, 'row', [(s, s ^ 2 * k) for s in range(rs)])  13.1 us
    ppermute x12, starting transfers between devices, along_col(): return lax.ppermute(x, 'col', [(s, s ^ k) for s in range(cs)])  12.9 us
    pallas_call x16, Pallas kernels, call(): pl.pallas_call(run, out_shape=outs, in_specs=[SMEM] * smem + [VMEM] * (co...  10.1 us
    ppermute x4, starting transfers between devices, send_own(): return lax.ppermute(block, ('row', 'col'), pairs)  7.47 us
    pallas_call x2, Pallas kernels, assemble(): pl.pallas_call(run, out_shape=[weight, weight, shape((1, hid), F32), *sum...  4.89 us
    ppermute x11, waiting for transfers between devices, other_core(): return lax.ppermute(x, 'row', [(s, s ^ 1) for s in range(rs)])  3.95 us
  transfers between devices with their start and end apart: 38, of which 17 were waited for; matrix products, arithmetic and copies ran while one was open for 0% of the time, Pallas kernels for 9%

profile of v16, /device:TPU:0, one launch (start us, length us, event | category | flops | bytes accessed | tf_op | source)
XLA Modules:
  0.0 119.3 jit_solution(2956290392376407626)
XLA Ops:
  0.6 4.1 %collective-permute-start.1 = (bf16[128,768]{1,0:T(8,128)(2,1)}, bf16[128,768]{1,0:T(8,128)(2,1)S(1)}, u32[]{:S(2)}, u32[]{:S(2)}) collective-permute-start(bf16[128,768]{1,0:T(8,128)(2,1)} %refs_1_.2), channel_id=1, source_target_pairs={{0,16},{4,20},{8,24},{12,28},{16,0},{20,4},{24,8},{28,12},{1,17},{... | collective-permute-start | bytes 589832 | tf_op jit(solution)/shard_map/ppermute | solution.py:479
  4.7 1.6 %collective-permute-start = (bf16[128,768]{1,0:T(8,128)(2,1)}, bf16[128,768]{1,0:T(8,128)(2,1)S(1)}, u32[]{:S(2)}, u32[]{:S(2)}) collective-permute-start(bf16[128,768]{1,0:T(8,128)(2,1)} %refs_1_.2), channel_id=1, source_target_pairs={{0,8},{4,12},{8,0},{12,4},{16,24},{20,28},{24,16},{28,20},{1,9},{5... | collective-permute-start | bytes 589832 | tf_op jit(solution)/shard_map/ppermute | solution.py:479
  15.5 3.1 %collective-permute-start.6 = (bf16[128,768]{1,0:T(8,128)(2,1)S(1)}, bf16[128,768]{1,0:T(8,128)(2,1)S(1)}, u32[]{:S(2)}, u32[]{:S(2)}) collective-permute-start(bf16[128,768]{1,0:T(8,128)(2,1)S(1)} %collective-permute-done.refs_2_), channel_id=1, source_target_pairs={{0,2},{4,3},{9,8},{13,9},{18,22},{22,23},{27,28},{31,29}} | collective-permute-start | bytes 589832 | tf_op jit(solution)/shard_map/ppermute | solution.py:501
  19.5 2.2 %collective-permute-done.7.refs_2_ = bf16[128,768]{1,0:T(8,128)(2,1)S(1)} collective-permute-done((bf16[128,768]{1,0:T(8,128)(2,1)S(1)}, bf16[128,768]{1,0:T(8,128)(2,1)S(1)}, u32[]{:S(2)}, u32[]{:S(2)}) %collective-permute-start.7) | collective-permute-done | bytes 196640 | tf_op jit(solution)/shard_map/ppermute | solution.py:479
  22.7 2.4 %collective-permute-start.10 = (bf16[128,768]{1,0:T(8,128)(2,1)S(1)}, bf16[128,768]{1,0:T(8,128)(2,1)S(1)}, u32[]{:S(2)}, u32[]{:S(2)}) collective-permute-start(bf16[128,768]{1,0:T(8,128)(2,1)S(1)} %shard_map.131), channel_id=1, source_target_pairs={{0,4},{4,5},{9,14},{13,15},{18,16},{22,17},{27,26},{31,27}} | collective-permute-start | bytes 589832 | tf_op jit(solution)/shard_map/ppermute | solution.py:501
  27.0 1.7 %collective-permute-start.11 = (bf16[128,768]{1,0:T(8,128)(2,1)S(1)}, bf16[128,768]{1,0:T(8,128)(2,1)S(1)}, u32[]{:S(2)}, u32[]{:S(2)}) collective-permute-start(bf16[128,768]{1,0:T(8,128)(2,1)S(1)} %get-tuple-element.46), channel_id=1, source_target_pairs={{0,1},{1,0},{2,3},{3,2},{4,5},{5,4},{6,7},{7,6},{8,9},{9,8},{10,11... | collective-permute-start | bytes 589832 | tf_op jit(solution)/shard_map/ppermute | solution.py:476
  31.9 2.0 %collective-permute-done.11.refs_1_ = bf16[128,768]{1,0:T(8,128)(2,1)S(1)} collective-permute-done((bf16[128,768]{1,0:T(8,128)(2,1)S(1)}, bf16[128,768]{1,0:T(8,128)(2,1)S(1)}, u32[]{:S(2)}, u32[]{:S(2)}) %collective-permute-start.11) | collective-permute-done | bytes 196640 | tf_op jit(solution)/shard_map/ppermute | solution.py:476
  33.9 6.1 %collective-permute-done.12.refs_2_ = bf16[128,768]{1,0:T(8,128)(2,1)S(1)} collective-permute-done((bf16[128,768]{1,0:T(8,128)(2,1)S(1)}, bf16[128,768]{1,0:T(8,128)(2,1)S(1)}, u32[]{:S(2)}, u32[]{:S(2)}) %collective-permute-start.12) | collective-permute-done | bytes 196640 | tf_op jit(solution)/shard_map/ppermute | solution.py:476
  43.2 1.7 %collective-permute-start.18 = (bf16[128,1408]{1,0:T(8,128)(2,1)S(1)}, bf16[128,1408]{1,0:T(8,128)(2,1)S(1)}, u32[]{:S(2)}, u32[]{:S(2)}) collective-permute-start(bf16[128,1408]{1,0:T(8,128)(2,1)S(1)} %get-tuple-element.54), channel_id=1, source_target_pairs={{0,3},{1,2},{2,1},{3,0},{4,7},{5,6},{6,5},{7,4},{8,11},{9,10},{10,... | collective-permute-start | bytes 1081352 | tf_op jit(solution)/shard_map/ppermute | solution.py:476
  44.9 7.7 %collective-permute-done.16.refs_4_.refs_1_ = bf16[128,1408]{1,0:T(8,128)(2,1)S(1)} collective-permute-done((bf16[128,1408]{1,0:T(8,128)(2,1)S(1)}, bf16[128,1408]{1,0:T(8,128)(2,1)S(1)}, u32[]{:S(2)}, u32[]{:S(2)}) %collective-permute-start.16) | collective-permute-done | bytes 360480 | tf_op jit(solution)/shard_map/ppermute | solution.py:476
  53.9 6.2 %collective-permute-done.17.refs_2_.refs_3_ = bf16[128,1408]{1,0:T(8,128)(2,1)S(1)} collective-permute-done((bf16[128,1408]{1,0:T(8,128)(2,1)S(1)}, bf16[128,1408]{1,0:T(8,128)(2,1)S(1)}, u32[]{:S(2)}, u32[]{:S(2)}) %collective-permute-start.17) | collective-permute-done | bytes 360480 | tf_op jit(solution)/shard_map/ppermute | solution.py:476
  61.0 1.7 %collective-permute-done.19.refs_1_ = bf16[4,400,128]{2,1,0:T(8,128)(2,1)S(1)} collective-permute-done((bf16[4,400,128]{2,1,0:T(8,128)(2,1)S(1)}, bf16[4,400,128]{2,1,0:T(8,128)(2,1)S(1)}, u32[]{:S(2)}, u32[]{:S(2)}) %collective-permute-start.19) | collective-permute-done | bytes 409632 | tf_op jit(solution)/shard_map/ppermute | solution.py:482
  64.1 2.7 %collective-permute-start.21 = (bf16[400,128]{1,0:T(8,128)(2,1)S(1)}, bf16[400,128]{1,0:T(8,128)(2,1)S(1)}, u32[]{:S(2)}, u32[]{:S(2)}) collective-permute-start(bf16[400,128]{1,0:T(8,128)(2,1)S(1)} %get-tuple-element.62), channel_id=1, source_target_pairs={{0,16},{4,20},{8,24},{12,28},{16,0},{20,4},{24,8},{28,12},{1,17},{... | collective-permute-start | bytes 307208 | tf_op jit(solution)/shard_map/ppermute | solution.py:479
  69.8 6.4 %collective-permute-done.21.refs_2_ = bf16[400,128]{1,0:T(8,128)(2,1)S(1)} collective-permute-done((bf16[400,128]{1,0:T(8,128)(2,1)S(1)}, bf16[400,128]{1,0:T(8,128)(2,1)S(1)}, u32[]{:S(2)}, u32[]{:S(2)}) %collective-permute-start.21) | collective-permute-done | bytes 102432 | tf_op jit(solution)/shard_map/ppermute | solution.py:479
  76.4 2.2 %collective-permute-done.26.refs_1_ = bf16[4,128,768]{2,1,0:T(8,128)(2,1)S(1)} collective-permute-done((bf16[4,128,768]{2,1,0:T(8,128)(2,1)S(1)}, bf16[4,128,768]{2,1,0:T(8,128)(2,1)S(1)}, u32[]{:S(2)}, u32[]{:S(2)}) %collective-permute-start.26) | collective-permute-done | bytes 786464 | tf_op jit(solution)/shard_map/ppermute | solution.py:482
  78.8 2.0 %collective-permute-start.23 = (bf16[400,128]{1,0:T(8,128)(2,1)S(1)}, bf16[400,128]{1,0:T(8,128)(2,1)S(1)}, u32[]{:S(2)}, u32[]{:S(2)}) collective-permute-start(bf16[400,128]{1,0:T(8,128)(2,1)S(1)} %get-tuple-element.69.refs_0_), channel_id=1, source_target_pairs={{0,8},{4,12},{8,0},{12,4},{16,24},{20,28},{24,16},{28,20},{1,9},{5... | collective-permute-start | bytes 307208 | tf_op jit(solution)/shard_map/ppermute | solution.py:479
  80.8 2.6 %collective-permute-done.24.refs_2_ = bf16[400,128]{1,0:T(8,128)(2,1)S(1)} collective-permute-done((bf16[400,128]{1,0:T(8,128)(2,1)S(1)}, bf16[400,128]{1,0:T(8,128)(2,1)S(1)}, u32[]{:S(2)}, u32[]{:S(2)}) %collective-permute-start.24) | collective-permute-done | bytes 102432 | tf_op jit(solution)/shard_map/ppermute | solution.py:479
  83.4 10.6 %collective-permute-done.23.refs_1_ = bf16[400,128]{1,0:T(8,128)(2,1)S(1)} collective-permute-done((bf16[400,128]{1,0:T(8,128)(2,1)S(1)}, bf16[400,128]{1,0:T(8,128)(2,1)S(1)}, u32[]{:S(2)}, u32[]{:S(2)}) %collective-permute-start.23) | collective-permute-done | bytes 102432 | tf_op jit(solution)/shard_map/ppermute | solution.py:479
  94.0 2.1 %collective-permute-done.25.refs_3_ = bf16[400,128]{1,0:T(8,128)(2,1)S(1)} collective-permute-done((bf16[400,128]{1,0:T(8,128)(2,1)S(1)}, bf16[400,128]{1,0:T(8,128)(2,1)S(1)}, u32[]{:S(2)}, u32[]{:S(2)}) %collective-permute-start.25) | collective-permute-done | bytes 102432 | tf_op jit(solution)/shard_map/ppermute | solution.py:479
  98.5 9.1 %collective-permute-done.28.refs_2_ = bf16[4,400,128]{2,1,0:T(8,128)(2,1)S(1)} collective-permute-done((bf16[4,400,128]{2,1,0:T(8,128)(2,1)S(1)}, bf16[4,400,128]{2,1,0:T(8,128)(2,1)S(1)}, u32[]{:S(2)}, u32[]{:S(2)}) %collective-permute-start.28) | collective-permute-done | bytes 409632 | tf_op jit(solution)/shard_map/ppermute | solution.py:476
  108.3 1.5 %collective-permute-start.29 = (bf16[2,400,128]{2,1,0:T(8,128)(2,1)S(1)}, bf16[2,400,128]{2,1,0:T(8,128)(2,1)S(1)}, u32[]{:S(2)}, u32[]{:S(2)}) collective-permute-start(bf16[2,400,128]{2,1,0:T(8,128)(2,1)S(1)} %slice.14), channel_id=1, source_target_pairs={{0,2},{1,3},{2,0},{3,1},{4,6},{5,7},{6,4},{7,5},{8,10},{9,11},{10,... | collective-permute-start | bytes 614408 | tf_op jit(solution)/shard_map/ppermute | solution.py:476
  110.3 3.5 %collective-permute-done.30.refs_4_ = bf16[2,400,128]{2,1,0:T(8,128)(2,1)S(1)} collective-permute-done((bf16[2,400,128]{2,1,0:T(8,128)(2,1)S(1)}, bf16[2,400,128]{2,1,0:T(8,128)(2,1)S(1)}, u32[]{:S(2)}, u32[]{:S(2)}) %collective-permute-start.30) | collective-permute-done | bytes 204832 | tf_op jit(solution)/shard_map/ppermute | solution.py:476
  114.4 2.5 %shard_map.144 = (f32[768,1024]{1,0:T(8,128)}, f32[768,1024]{1,0:T(8,128)}, f32[1,1024]{1,0:T(1,128)S(1)}, bf16[128,768]{1,0:T(8,128)(2,1)}) custom-call(bf16[4,400,128]{2,1,0:T(8,128)(2,1)S(1)} %shard_map.142.refs_0_, bf16[4,400,128]{2,1,0:T(8,128)(2,1)S(1)} %collective-permute-done.27.refs_1_, bf16[4,400,128]{2,1,0:T(8,128)(2,1)S(1)} %collective-permute-done.28.refs_2_, ...), custom_call_target="tpu_custom_call" | custom-call | bytes 9437184 | tf_op jit(solution)/shard_map/pallas_call | solution.py:443
  116.9 2.4 %shard_map.145 = (f32[768,1024]{1,0:T(8,128)}, f32[768,1024]{1,0:T(8,128)}, f32[1,1024]{1,0:T(1,128)}) custom-call(bf16[4,400,128]{2,1,0:T(8,128)(2,1)S(1)} %collective-permute-done.33.refs_0_, bf16[4,400,128]{2,1,0:T(8,128)(2,1)S(1)} %collective-permute-done.34.refs_1_, ...), custom_call_target="tpu_custom_call", output_to_operand_aliasing={{0}: (5, {}), {1}: (6, {})} | custom-call | bytes 9437184 | tf_op jit(solution)/shard_map/pallas_call | solution.py:443
  (93 shorter events, 29.6 us)
Async XLA Ops:
  0.6 13.5 %collective-permute-start.1 = (bf16[128,768]{1,0:T(8,128)(2,1)}, bf16[128,768]{1,0:T(8,128)(2,1)S(1)}, u32[]{:S(2)}, u32[]{:S(2)}) collective-permute-start(bf16[128,768]{1,0:T(8,128)(2,1)} %refs_1_.2), channel_id=1, source_target_pairs={{0,16},{4,20},{8,24},{12,28},{16,0},{20,4},{24,8},{28,12},{1,17},{... | collective-permute-start | bytes 589832 | tf_op jit(solution)/shard_map/ppermute | solution.py:479
  4.7 10.7 %collective-permute-start = (bf16[128,768]{1,0:T(8,128)(2,1)}, bf16[128,768]{1,0:T(8,128)(2,1)S(1)}, u32[]{:S(2)}, u32[]{:S(2)}) collective-permute-start(bf16[128,768]{1,0:T(8,128)(2,1)} %refs_1_.2), channel_id=1, source_target_pairs={{0,8},{4,12},{8,0},{12,4},{16,24},{20,28},{24,16},{28,20},{1,9},{5... | collective-permute-start | bytes 589832 | tf_op jit(solution)/shard_map/ppermute | solution.py:479
  6.3 12.2 %collective-permute-start.2 = (bf16[128,768]{1,0:T(8,128)(2,1)}, bf16[128,768]{1,0:T(8,128)(2,1)S(1)}, u32[]{:S(2)}, u32[]{:S(2)}) collective-permute-start(bf16[128,768]{1,0:T(8,128)(2,1)} %refs_1_.2), channel_id=1, source_target_pairs={{0,4},{4,0},{8,12},{12,8},{16,20},{20,16},{24,28},{28,24},{1,5},{5... | collective-permute-start | bytes 589832 | tf_op jit(solution)/shard_map/ppermute | solution.py:482
  12.7 9.1 %collective-permute-start.5 = (bf16[128,768]{1,0:T(8,128)(2,1)S(1)}, bf16[128,768]{1,0:T(8,128)(2,1)S(1)}, u32[]{:S(2)}, u32[]{:S(2)}) collective-permute-start(bf16[128,768]{1,0:T(8,128)(2,1)S(1)} %copy-done.4), channel_id=1, source_target_pairs={{0,0},{4,1},{9,10},{13,11},{18,20},{22,21},{27,30},{31,31}} | collective-permute-start | bytes 589832 | tf_op jit(solution)/shard_map/ppermute | solution.py:501
  14.2 7.5 %collective-permute-start.7 = (bf16[128,768]{1,0:T(8,128)(2,1)S(1)}, bf16[128,768]{1,0:T(8,128)(2,1)S(1)}, u32[]{:S(2)}, u32[]{:S(2)}) collective-permute-start(bf16[128,768]{1,0:T(8,128)(2,1)S(1)} %collective-permute-done.1.refs_3_.refs_0_), channel_id=1, source_target_pairs={{0,8},{4,12},{8,0},{12,4},{16,24},{20,28},{24,16},{28,20},{1,9},{5... | collective-permute-start | bytes 589832 | tf_op jit(solution)/shard_map/ppermute | solution.py:479
  27.0 6.9 %collective-permute-start.11 = (bf16[128,768]{1,0:T(8,128)(2,1)S(1)}, bf16[128,768]{1,0:T(8,128)(2,1)S(1)}, u32[]{:S(2)}, u32[]{:S(2)}) collective-permute-start(bf16[128,768]{1,0:T(8,128)(2,1)S(1)} %get-tuple-element.46), channel_id=1, source_target_pairs={{0,1},{1,0},{2,3},{3,2},{4,5},{5,4},{6,7},{7,6},{8,9},{9,8},{10,11... | collective-permute-start | bytes 589832 | tf_op jit(solution)/shard_map/ppermute | solution.py:476
  28.7 11.3 %collective-permute-start.12 = (bf16[128,768]{1,0:T(8,128)(2,1)S(1)}, bf16[128,768]{1,0:T(8,128)(2,1)S(1)}, u32[]{:S(2)}, u32[]{:S(2)}) collective-permute-start(bf16[128,768]{1,0:T(8,128)(2,1)S(1)} %get-tuple-element.47), channel_id=1, source_target_pairs={{0,2},{1,3},{2,0},{3,1},{4,6},{5,7},{6,4},{7,5},{8,10},{9,11},{10,... | collective-permute-start | bytes 589832 | tf_op jit(solution)/shard_map/ppermute | solution.py:476
  29.1 10.9 %collective-permute-start.13 = (bf16[128,768]{1,0:T(8,128)(2,1)S(1)}, bf16[128,768]{1,0:T(8,128)(2,1)S(1)}, u32[]{:S(2)}, u32[]{:S(2)}) collective-permute-start(bf16[128,768]{1,0:T(8,128)(2,1)S(1)} %get-tuple-element.48), channel_id=1, source_target_pairs={{0,3},{1,2},{2,1},{3,0},{4,7},{5,6},{6,5},{7,4},{8,11},{9,10},{10,... | collective-permute-start | bytes 589832 | tf_op jit(solution)/shard_map/ppermute | solution.py:476
  41.4 11.2 %collective-permute-start.16 = (bf16[128,1408]{1,0:T(8,128)(2,1)S(1)}, bf16[128,1408]{1,0:T(8,128)(2,1)S(1)}, u32[]{:S(2)}, u32[]{:S(2)}) collective-permute-start(bf16[128,1408]{1,0:T(8,128)(2,1)S(1)} %get-tuple-element.52), channel_id=1, source_target_pairs={{0,1},{1,0},{2,3},{3,2},{4,5},{5,4},{6,7},{7,6},{8,9},{9,8},{10,11... | collective-permute-start | bytes 1081352 | tf_op jit(solution)/shard_map/ppermute | solution.py:476
  41.8 18.3 %collective-permute-start.17 = (bf16[128,1408]{1,0:T(8,128)(2,1)S(1)}, bf16[128,1408]{1,0:T(8,128)(2,1)S(1)}, u32[]{:S(2)}, u32[]{:S(2)}) collective-permute-start(bf16[128,1408]{1,0:T(8,128)(2,1)S(1)} %get-tuple-element.53), channel_id=1, source_target_pairs={{0,2},{1,3},{2,0},{3,1},{4,6},{5,7},{6,4},{7,5},{8,10},{9,11},{10,... | collective-permute-start | bytes 1081352 | tf_op jit(solution)/shard_map/ppermute | solution.py:476
  43.2 16.9 %collective-permute-start.18 = (bf16[128,1408]{1,0:T(8,128)(2,1)S(1)}, bf16[128,1408]{1,0:T(8,128)(2,1)S(1)}, u32[]{:S(2)}, u32[]{:S(2)}) collective-permute-start(bf16[128,1408]{1,0:T(8,128)(2,1)S(1)} %get-tuple-element.54), channel_id=1, source_target_pairs={{0,3},{1,2},{2,1},{3,0},{4,7},{5,6},{6,5},{7,4},{8,11},{9,10},{10,... | collective-permute-start | bytes 1081352 | tf_op jit(solution)/shard_map/ppermute | solution.py:476
  62.8 7.0 %collective-permute-start.20 = (bf16[400,128]{1,0:T(8,128)(2,1)S(1)}, bf16[400,128]{1,0:T(8,128)(2,1)S(1)}, u32[]{:S(2)}, u32[]{:S(2)}) collective-permute-start(bf16[400,128]{1,0:T(8,128)(2,1)S(1)} %get-tuple-element.61), channel_id=1, source_target_pairs={{0,24},{4,28},{8,16},{12,20},{16,8},{20,12},{24,0},{28,4},{1,25},{... | collective-permute-start | bytes 307208 | tf_op jit(solution)/shard_map/ppermute | solution.py:479
  64.1 12.1 %collective-permute-start.21 = (bf16[400,128]{1,0:T(8,128)(2,1)S(1)}, bf16[400,128]{1,0:T(8,128)(2,1)S(1)}, u32[]{:S(2)}, u32[]{:S(2)}) collective-permute-start(bf16[400,128]{1,0:T(8,128)(2,1)S(1)} %get-tuple-element.62), channel_id=1, source_target_pairs={{0,16},{4,20},{8,24},{12,28},{16,0},{20,4},{24,8},{28,12},{1,17},{... | collective-permute-start | bytes 307208 | tf_op jit(solution)/shard_map/ppermute | solution.py:479
  66.7 9.4 %collective-permute-start.22 = (bf16[400,128]{1,0:T(8,128)(2,1)S(1)}, bf16[400,128]{1,0:T(8,128)(2,1)S(1)}, u32[]{:S(2)}, u32[]{:S(2)}) collective-permute-start(bf16[400,128]{1,0:T(8,128)(2,1)S(1)} %get-tuple-element.63), channel_id=1, source_target_pairs={{0,8},{4,12},{8,0},{12,4},{16,24},{20,28},{24,16},{28,20},{1,9},{5... | collective-permute-start | bytes 307208 | tf_op jit(solution)/shard_map/ppermute | solution.py:479
  76.4 7.1 %collective-permute-start.24 = (bf16[400,128]{1,0:T(8,128)(2,1)S(1)}, bf16[400,128]{1,0:T(8,128)(2,1)S(1)}, u32[]{:S(2)}, u32[]{:S(2)}) collective-permute-start(bf16[400,128]{1,0:T(8,128)(2,1)S(1)} %get-tuple-element.69.refs_0_), channel_id=1, source_target_pairs={{0,16},{4,20},{8,24},{12,28},{16,0},{20,4},{24,8},{28,12},{1,17},{... | collective-permute-start | bytes 307208 | tf_op jit(solution)/shard_map/ppermute | solution.py:479
  78.7 19.5 %collective-permute-start.31 = (bf16[2,128,768]{2,1,0:T(8,128)(2,1)S(1)}, bf16[2,128,768]{2,1,0:T(8,128)(2,1)S(1)}, u32[]{:S(2)}, u32[]{:S(2)}) collective-permute-start(bf16[2,128,768]{2,1,0:T(8,128)(2,1)S(1)} %get-tuple-element.72.refs_4_), channel_id=1, source_target_pairs={{0,8},{4,12},{8,0},{12,4},{16,24},{20,28},{24,16},{28,20},{1,9},{5... | collective-permute-start | bytes 1179656 | tf_op jit(solution)/shard_map/ppermute | solution.py:479
  78.8 15.2 %collective-permute-start.23 = (bf16[400,128]{1,0:T(8,128)(2,1)S(1)}, bf16[400,128]{1,0:T(8,128)(2,1)S(1)}, u32[]{:S(2)}, u32[]{:S(2)}) collective-permute-start(bf16[400,128]{1,0:T(8,128)(2,1)S(1)} %get-tuple-element.69.refs_0_), channel_id=1, source_target_pairs={{0,8},{4,12},{8,0},{12,4},{16,24},{20,28},{24,16},{28,20},{1,9},{5... | collective-permute-start | bytes 307208 | tf_op jit(solution)/shard_map/ppermute | solution.py:479
  83.4 12.7 %collective-permute-start.25 = (bf16[400,128]{1,0:T(8,128)(2,1)S(1)}, bf16[400,128]{1,0:T(8,128)(2,1)S(1)}, u32[]{:S(2)}, u32[]{:S(2)}) collective-permute-start(bf16[400,128]{1,0:T(8,128)(2,1)S(1)} %collective-permute-done.24.refs_2_), channel_id=1, source_target_pairs={{0,8},{4,12},{8,0},{12,4},{16,24},{20,28},{24,16},{28,20},{1,9},{5... | collective-permute-start | bytes 307208 | tf_op jit(solution)/shard_map/ppermute | solution.py:479
  96.2 11.5 %collective-permute-start.28 = (bf16[4,400,128]{2,1,0:T(8,128)(2,1)S(1)}, bf16[4,400,128]{2,1,0:T(8,128)(2,1)S(1)}, u32[]{:S(2)}, u32[]{:S(2)}) collective-permute-start(bf16[4,400,128]{2,1,0:T(8,128)(2,1)S(1)} %shard_map.142.refs_0_), channel_id=1, source_target_pairs={{0,2},{1,3},{2,0},{3,1},{4,6},{5,7},{6,4},{7,5},{8,10},{9,11},{10,... | collective-permute-start | bytes 1228808 | tf_op jit(solution)/shard_map/ppermute | solution.py:476
  97.2 11.1 %collective-permute-start.27 = (bf16[4,400,128]{2,1,0:T(8,128)(2,1)S(1)}, bf16[4,400,128]{2,1,0:T(8,128)(2,1)S(1)}, u32[]{:S(2)}, u32[]{:S(2)}) collective-permute-start(bf16[4,400,128]{2,1,0:T(8,128)(2,1)S(1)} %shard_map.142.refs_0_), channel_id=1, source_target_pairs={{0,1},{1,0},{2,3},{3,2},{4,5},{5,4},{6,7},{7,6},{8,9},{9,8},{10,11... | collective-permute-start | bytes 1228808 | tf_op jit(solution)/shard_map/ppermute | solution.py:476
  98.3 11.5 %collective-permute-start.32 = (bf16[1,128,768]{2,1,0:T(8,128)(2,1)S(1)}, bf16[1,128,768]{2,1,0:T(8,128)(2,1)S(1)}, u32[]{:S(2)}, u32[]{:S(2)}) collective-permute-start(bf16[1,128,768]{2,1,0:T(8,128)(2,1)S(1)} %get-tuple-element.75), channel_id=1, source_target_pairs={{0,16},{4,20},{8,24},{12,28},{16,0},{20,4},{24,8},{28,12},{1,17},{... | collective-permute-start | bytes 589832 | tf_op jit(solution)/shard_map/ppermute | solution.py:479
  98.4 18.5 %collective-permute-start.33 = (bf16[4,400,128]{2,1,0:T(8,128)(2,1)S(1)}, bf16[4,400,128]{2,1,0:T(8,128)(2,1)S(1)}, u32[]{:S(2)}, u32[]{:S(2)}) collective-permute-start(bf16[4,400,128]{2,1,0:T(8,128)(2,1)S(1)} %shard_map.142.refs_0_), channel_id=1, source_target_pairs={{0,4},{4,0},{8,12},{12,8},{16,20},{20,16},{24,28},{28,24},{1,5},{5... | collective-permute-start | bytes 1228808 | tf_op jit(solution)/shard_map/ppermute | solution.py:482
  109.8 7.1 %collective-permute-start.35 = (bf16[4,400,128]{2,1,0:T(8,128)(2,1)S(1)}, bf16[4,400,128]{2,1,0:T(8,128)(2,1)S(1)}, u32[]{:S(2)}, u32[]{:S(2)}) collective-permute-start(bf16[4,400,128]{2,1,0:T(8,128)(2,1)S(1)} %collective-permute-done.28.refs_2_), channel_id=1, source_target_pairs={{0,4},{4,0},{8,12},{12,8},{16,20},{20,16},{24,28},{28,24},{1,5},{5... | collective-permute-start | bytes 1228808 | tf_op jit(solution)/shard_map/ppermute | solution.py:482
  109.8 7.1 %collective-permute-start.34 = (bf16[4,400,128]{2,1,0:T(8,128)(2,1)S(1)}, bf16[4,400,128]{2,1,0:T(8,128)(2,1)S(1)}, u32[]{:S(2)}, u32[]{:S(2)}) collective-permute-start(bf16[4,400,128]{2,1,0:T(8,128)(2,1)S(1)} %collective-permute-done.27.refs_1_), channel_id=1, source_target_pairs={{0,4},{4,0},{8,12},{12,8},{16,20},{20,16},{24,28},{28,24},{1,5},{5... | collective-permute-start | bytes 1228808 | tf_op jit(solution)/shard_map/ppermute | solution.py:482
  (22 other events, 97.4 us)

commit v17 on v15

--- a/solution.py
+++ b/solution.py
@@ -482,12 +482,8 @@
         return lax.ppermute(x, "row", [(s, s ^ 1) for s in range(rs)])
 
     def gather_chips(x):
-        found = {0: x}
-        step = half // 2
-        while step:
-            found.update({d + step: along_chips(found[d], step) for d in list(found)})
-            step //= 2
-        return [found[d] for d in range(half)]
+        far_first = {k: along_chips(x, k) for k in range(half - 1, 0, -1)}
+        return [x] + [far_first[k] for k in range(1, half)]
 
     if rs == 2 * cs:
 

time: 115 us -> 116 us (level)
  transfers between devices with their start and end apart: 38 -> 38, of which waited for: 15 -> 14; matrix products, arithmetic and copies ran while one was open for 1% -> 1% of each run, Pallas kernels for 9% -> 9%
where the time goes in v17:
time: 116 us
  waiting for transfers between devices  57.8 us (50%)
  starting transfers between devices  38.3 us (33%)
  Pallas kernels  15.2 us (13%)
  local copies, waits for them, and re-layouts  2.61 us (2%)
  between operations  1.62 us (1%)
    ppermute x11, waiting for transfers between devices, along_chips(): return lax.ppermute(x, 'row', [(s, s ^ 2 * k) for s in range(rs)])  33.8 us
    ppermute x12, waiting for transfers between devices, along_col(): return lax.ppermute(x, 'col', [(s, s ^ k) for s in range(cs)])  22.3 us
    ppermute x11, starting transfers between devices, along_chips(): return lax.ppermute(x, 'row', [(s, s ^ 2 * k) for s in range(rs)])  15.7 us
    ppermute x12, starting transfers between devices, along_col(): return lax.ppermute(x, 'col', [(s, s ^ k) for s in range(cs)])  12.8 us
    pallas_call x16, Pallas kernels, call(): pl.pallas_call(run, out_shape=outs, in_specs=[SMEM] * smem + [VMEM] * (co...  10.3 us
    ppermute x4, starting transfers between devices, send_own(): return lax.ppermute(block, ('row', 'col'), pairs)  7.37 us
    pallas_call x2, Pallas kernels, assemble(): pl.pallas_call(run, out_shape=[weight, weight, shape((1, hid), F32), *sum...  4.89 us
    unnamed x16, local copies, waits for them, and re-layouts  2.46 us
  transfers between devices with their start and end apart: 38, of which 14 were waited for; matrix products, arithmetic and copies ran while one was open for 1% of the time, Pallas kernels for 9%

profile of v17, /device:TPU:0, one launch (start us, length us, event | category | flops | bytes accessed | tf_op | source)
XLA Modules:
  0.0 115.9 jit_solution(9115536832686665322)
XLA Ops:
  0.6 4.1 %collective-permute-start.1 = (bf16[128,768]{1,0:T(8,128)(2,1)}, bf16[128,768]{1,0:T(8,128)(2,1)S(1)}, u32[]{:S(2)}, u32[]{:S(2)}) collective-permute-start(bf16[128,768]{1,0:T(8,128)(2,1)} %refs_1_.2), channel_id=1, source_target_pairs={{0,16},{4,20},{8,24},{12,28},{16,0},{20,4},{24,8},{28,12},{1,17},{... | collective-permute-start | bytes 589832 | tf_op jit(solution)/shard_map/ppermute | solution.py:479
  4.7 1.6 %collective-permute-start = (bf16[128,768]{1,0:T(8,128)(2,1)}, bf16[128,768]{1,0:T(8,128)(2,1)S(1)}, u32[]{:S(2)}, u32[]{:S(2)}) collective-permute-start(bf16[128,768]{1,0:T(8,128)(2,1)} %refs_1_.2), channel_id=1, source_target_pairs={{0,8},{4,12},{8,0},{12,4},{16,24},{20,28},{24,16},{28,20},{1,9},{5... | collective-permute-start | bytes 589832 | tf_op jit(solution)/shard_map/ppermute | solution.py:479
  9.4 1.5 %shard_map.128 = (bf16[512,1024]{1,0:T(8,128)(2,1)S(1)}, bf16[1024,512]{1,0:T(8,128)(2,1)S(1)}) custom-call(s32[24]{0:T(128)S(1)} %bitcast.12, s32[24]{0:T(128)S(1)} %bitcast.13, s32[1]{0:T(128)} %bitcast.9.refs_2_, bf16[24,128,128]{2,1,0:T(8,128)(2,1)S(1)} %bitcast.10), custom_call_target="tpu_custom_call" | custom-call | flops 524288 | bytes 2883780 | tf_op jit(solution)/shard_map/pallas_call | solution.py:32
  15.6 3.0 %collective-permute-start.6 = (bf16[128,768]{1,0:T(8,128)(2,1)S(1)}, bf16[128,768]{1,0:T(8,128)(2,1)S(1)}, u32[]{:S(2)}, u32[]{:S(2)}) collective-permute-start(bf16[128,768]{1,0:T(8,128)(2,1)S(1)} %collective-permute-done.refs_2_), channel_id=1, source_target_pairs={{0,2},{4,3},{9,8},{13,9},{18,22},{22,23},{27,28},{31,29}} | collective-permute-start | bytes 589832 | tf_op jit(solution)/shard_map/ppermute | solution.py:497
  19.6 2.0 %collective-permute-done.7.refs_2_ = bf16[128,768]{1,0:T(8,128)(2,1)S(1)} collective-permute-done((bf16[128,768]{1,0:T(8,128)(2,1)S(1)}, bf16[128,768]{1,0:T(8,128)(2,1)S(1)}, u32[]{:S(2)}, u32[]{:S(2)}) %collective-permute-start.7) | collective-permute-done | bytes 196640 | tf_op jit(solution)/shard_map/ppermute | solution.py:479
  22.6 2.4 %collective-permute-start.10 = (bf16[128,768]{1,0:T(8,128)(2,1)S(1)}, bf16[128,768]{1,0:T(8,128)(2,1)S(1)}, u32[]{:S(2)}, u32[]{:S(2)}) collective-permute-start(bf16[128,768]{1,0:T(8,128)(2,1)S(1)} %shard_map.131), channel_id=1, source_target_pairs={{0,4},{4,5},{9,14},{13,15},{18,16},{22,17},{27,26},{31,27}} | collective-permute-start | bytes 589832 | tf_op jit(solution)/shard_map/ppermute | solution.py:497
  27.0 1.8 %collective-permute-start.11 = (bf16[128,768]{1,0:T(8,128)(2,1)S(1)}, bf16[128,768]{1,0:T(8,128)(2,1)S(1)}, u32[]{:S(2)}, u32[]{:S(2)}) collective-permute-start(bf16[128,768]{1,0:T(8,128)(2,1)S(1)} %get-tuple-element.46), channel_id=1, source_target_pairs={{0,1},{1,0},{2,3},{3,2},{4,5},{5,4},{6,7},{7,6},{8,9},{9,8},{10,11... | collective-permute-start | bytes 589832 | tf_op jit(solution)/shard_map/ppermute | solution.py:476
  29.0 1.5 %collective-permute-start.13 = (bf16[128,768]{1,0:T(8,128)(2,1)S(1)}, bf16[128,768]{1,0:T(8,128)(2,1)S(1)}, u32[]{:S(2)}, u32[]{:S(2)}) collective-permute-start(bf16[128,768]{1,0:T(8,128)(2,1)S(1)} %get-tuple-element.48), channel_id=1, source_target_pairs={{0,3},{1,2},{2,1},{3,0},{4,7},{5,6},{6,5},{7,4},{8,11},{9,10},{10,... | collective-permute-start | bytes 589832 | tf_op jit(solution)/shard_map/ppermute | solution.py:476
  31.9 1.9 %collective-permute-done.11.refs_1_ = bf16[128,768]{1,0:T(8,128)(2,1)S(1)} collective-permute-done((bf16[128,768]{1,0:T(8,128)(2,1)S(1)}, bf16[128,768]{1,0:T(8,128)(2,1)S(1)}, u32[]{:S(2)}, u32[]{:S(2)}) %collective-permute-start.11) | collective-permute-done | bytes 196640 | tf_op jit(solution)/shard_map/ppermute | solution.py:476
  33.8 6.3 %collective-permute-done.12.refs_2_ = bf16[128,768]{1,0:T(8,128)(2,1)S(1)} collective-permute-done((bf16[128,768]{1,0:T(8,128)(2,1)S(1)}, bf16[128,768]{1,0:T(8,128)(2,1)S(1)}, u32[]{:S(2)}, u32[]{:S(2)}) %collective-permute-start.12) | collective-permute-done | bytes 196640 | tf_op jit(solution)/shard_map/ppermute | solution.py:476
  41.7 1.6 %collective-permute-start.17 = (bf16[128,1408]{1,0:T(8,128)(2,1)S(1)}, bf16[128,1408]{1,0:T(8,128)(2,1)S(1)}, u32[]{:S(2)}, u32[]{:S(2)}) collective-permute-start(bf16[128,1408]{1,0:T(8,128)(2,1)S(1)} %get-tuple-element.53), channel_id=1, source_target_pairs={{0,2},{1,3},{2,0},{3,1},{4,6},{5,7},{6,4},{7,5},{8,10},{9,11},{10,... | collective-permute-start | bytes 1081352 | tf_op jit(solution)/shard_map/ppermute | solution.py:476
  43.4 1.7 %collective-permute-start.18 = (bf16[128,1408]{1,0:T(8,128)(2,1)S(1)}, bf16[128,1408]{1,0:T(8,128)(2,1)S(1)}, u32[]{:S(2)}, u32[]{:S(2)}) collective-permute-start(bf16[128,1408]{1,0:T(8,128)(2,1)S(1)} %get-tuple-element.54), channel_id=1, source_target_pairs={{0,3},{1,2},{2,1},{3,0},{4,7},{5,6},{6,5},{7,4},{8,11},{9,10},{10,... | collective-permute-start | bytes 1081352 | tf_op jit(solution)/shard_map/ppermute | solution.py:476
  45.1 7.7 %collective-permute-done.16.refs_4_.refs_1_ = bf16[128,1408]{1,0:T(8,128)(2,1)S(1)} collective-permute-done((bf16[128,1408]{1,0:T(8,128)(2,1)S(1)}, bf16[128,1408]{1,0:T(8,128)(2,1)S(1)}, u32[]{:S(2)}, u32[]{:S(2)}) %collective-permute-start.16) | collective-permute-done | bytes 360480 | tf_op jit(solution)/shard_map/ppermute | solution.py:476
  54.1 6.0 %collective-permute-done.17.refs_2_.refs_3_ = bf16[128,1408]{1,0:T(8,128)(2,1)S(1)} collective-permute-done((bf16[128,1408]{1,0:T(8,128)(2,1)S(1)}, bf16[128,1408]{1,0:T(8,128)(2,1)S(1)}, u32[]{:S(2)}, u32[]{:S(2)}) %collective-permute-start.17) | collective-permute-done | bytes 360480 | tf_op jit(solution)/shard_map/ppermute | solution.py:476
  61.0 1.7 %collective-permute-done.19.refs_1_ = bf16[4,400,128]{2,1,0:T(8,128)(2,1)S(1)} collective-permute-done((bf16[4,400,128]{2,1,0:T(8,128)(2,1)S(1)}, bf16[4,400,128]{2,1,0:T(8,128)(2,1)S(1)}, u32[]{:S(2)}, u32[]{:S(2)}) %collective-permute-start.19) | collective-permute-done | bytes 409632 | tf_op jit(solution)/shard_map/ppermute | solution.py:482
  64.1 2.7 %collective-permute-start.21 = (bf16[400,128]{1,0:T(8,128)(2,1)S(1)}, bf16[400,128]{1,0:T(8,128)(2,1)S(1)}, u32[]{:S(2)}, u32[]{:S(2)}) collective-permute-start(bf16[400,128]{1,0:T(8,128)(2,1)S(1)} %get-tuple-element.62), channel_id=1, source_target_pairs={{0,16},{4,20},{8,24},{12,28},{16,0},{20,4},{24,8},{28,12},{1,17},{... | collective-permute-start | bytes 307208 | tf_op jit(solution)/shard_map/ppermute | solution.py:479
  70.0 6.3 %collective-permute-done.21.refs_2_ = bf16[400,128]{1,0:T(8,128)(2,1)S(1)} collective-permute-done((bf16[400,128]{1,0:T(8,128)(2,1)S(1)}, bf16[400,128]{1,0:T(8,128)(2,1)S(1)}, u32[]{:S(2)}, u32[]{:S(2)}) %collective-permute-start.21) | collective-permute-done | bytes 102432 | tf_op jit(solution)/shard_map/ppermute | solution.py:479
  77.6 3.2 %collective-permute-start.23 = (bf16[400,128]{1,0:T(8,128)(2,1)S(1)}, bf16[400,128]{1,0:T(8,128)(2,1)S(1)}, u32[]{:S(2)}, u32[]{:S(2)}) collective-permute-start(bf16[400,128]{1,0:T(8,128)(2,1)S(1)} %get-tuple-element.69.refs_0_), channel_id=1, source_target_pairs={{0,8},{4,12},{8,0},{12,4},{16,24},{20,28},{24,16},{28,20},{1,9},{5... | collective-permute-start | bytes 307208 | tf_op jit(solution)/shard_map/ppermute | solution.py:479
  80.9 3.2 %collective-permute-done.25.refs_4_.refs_3_ = bf16[400,128]{1,0:T(8,128)(2,1)S(1)} collective-permute-done((bf16[400,128]{1,0:T(8,128)(2,1)S(1)}, bf16[400,128]{1,0:T(8,128)(2,1)S(1)}, u32[]{:S(2)}, u32[]{:S(2)}) %collective-permute-start.25) | collective-permute-done | bytes 102432 | tf_op jit(solution)/shard_map/ppermute | solution.py:479
  84.1 3.8 %collective-permute-done.24.refs_3_.refs_2_ = bf16[400,128]{1,0:T(8,128)(2,1)S(1)} collective-permute-done((bf16[400,128]{1,0:T(8,128)(2,1)S(1)}, bf16[400,128]{1,0:T(8,128)(2,1)S(1)}, u32[]{:S(2)}, u32[]{:S(2)}) %collective-permute-start.24) | collective-permute-done | bytes 102432 | tf_op jit(solution)/shard_map/ppermute | solution.py:479
  90.3 8.9 %collective-permute-done.31.refs_1_ = bf16[2,128,768]{2,1,0:T(8,128)(2,1)S(1)} collective-permute-done((bf16[2,128,768]{2,1,0:T(8,128)(2,1)S(1)}, bf16[2,128,768]{2,1,0:T(8,128)(2,1)S(1)}, u32[]{:S(2)}, u32[]{:S(2)}) %collective-permute-start.31) | collective-permute-done | bytes 393248 | tf_op jit(solution)/shard_map/ppermute | solution.py:479
  101.8 8.6 %collective-permute-done.32.refs_6_ = bf16[1,128,768]{2,1,0:T(8,128)(2,1)S(1)} collective-permute-done((bf16[1,128,768]{2,1,0:T(8,128)(2,1)S(1)}, bf16[1,128,768]{2,1,0:T(8,128)(2,1)S(1)}, u32[]{:S(2)}, u32[]{:S(2)}) %collective-permute-start.32) | collective-permute-done | bytes 196640 | tf_op jit(solution)/shard_map/ppermute | solution.py:479
  111.0 2.5 %shard_map.144 = (f32[768,1024]{1,0:T(8,128)}, f32[768,1024]{1,0:T(8,128)}, f32[1,1024]{1,0:T(1,128)S(1)}, bf16[128,768]{1,0:T(8,128)(2,1)}) custom-call(bf16[4,400,128]{2,1,0:T(8,128)(2,1)S(1)} %shard_map.142.refs_0_, bf16[4,400,128]{2,1,0:T(8,128)(2,1)S(1)} %collective-permute-done.27.refs_1_, bf16[4,400,128]{2,1,0:T(8,128)(2,1)S(1)} %collective-permute-done.28.refs_2_, ...), custom_call_target="tpu_custom_call" | custom-call | bytes 9437184 | tf_op jit(solution)/shard_map/pallas_call | solution.py:443
  113.5 2.4 %shard_map.145 = (f32[768,1024]{1,0:T(8,128)}, f32[768,1024]{1,0:T(8,128)}, f32[1,1024]{1,0:T(1,128)}) custom-call(bf16[4,400,128]{2,1,0:T(8,128)(2,1)S(1)} %collective-permute-done.33.refs_0_, bf16[4,400,128]{2,1,0:T(8,128)(2,1)S(1)} %collective-permute-done.34.refs_1_, ...), custom_call_target="tpu_custom_call", output_to_operand_aliasing={{0}: (5, {}), {1}: (6, {})} | custom-call | bytes 9437184 | tf_op jit(solution)/shard_map/pallas_call | solution.py:443
  (93 shorter events, 27.8 us)
Async XLA Ops:
  0.6 13.5 %collective-permute-start.1 = (bf16[128,768]{1,0:T(8,128)(2,1)}, bf16[128,768]{1,0:T(8,128)(2,1)S(1)}, u32[]{:S(2)}, u32[]{:S(2)}) collective-permute-start(bf16[128,768]{1,0:T(8,128)(2,1)} %refs_1_.2), channel_id=1, source_target_pairs={{0,16},{4,20},{8,24},{12,28},{16,0},{20,4},{24,8},{28,12},{1,17},{... | collective-permute-start | bytes 589832 | tf_op jit(solution)/shard_map/ppermute | solution.py:479
  4.7 10.9 %collective-permute-start = (bf16[128,768]{1,0:T(8,128)(2,1)}, bf16[128,768]{1,0:T(8,128)(2,1)S(1)}, u32[]{:S(2)}, u32[]{:S(2)}) collective-permute-start(bf16[128,768]{1,0:T(8,128)(2,1)} %refs_1_.2), channel_id=1, source_target_pairs={{0,8},{4,12},{8,0},{12,4},{16,24},{20,28},{24,16},{28,20},{1,9},{5... | collective-permute-start | bytes 589832 | tf_op jit(solution)/shard_map/ppermute | solution.py:479
  6.3 12.3 %collective-permute-start.2 = (bf16[128,768]{1,0:T(8,128)(2,1)}, bf16[128,768]{1,0:T(8,128)(2,1)S(1)}, u32[]{:S(2)}, u32[]{:S(2)}) collective-permute-start(bf16[128,768]{1,0:T(8,128)(2,1)} %refs_1_.2), channel_id=1, source_target_pairs={{0,4},{4,0},{8,12},{12,8},{16,20},{20,16},{24,28},{28,24},{1,5},{5... | collective-permute-start | bytes 589832 | tf_op jit(solution)/shard_map/ppermute | solution.py:482
  12.7 9.1 %collective-permute-start.5 = (bf16[128,768]{1,0:T(8,128)(2,1)S(1)}, bf16[128,768]{1,0:T(8,128)(2,1)S(1)}, u32[]{:S(2)}, u32[]{:S(2)}) collective-permute-start(bf16[128,768]{1,0:T(8,128)(2,1)S(1)} %copy-done.4), channel_id=1, source_target_pairs={{0,0},{4,1},{9,10},{13,11},{18,20},{22,21},{27,30},{31,31}} | collective-permute-start | bytes 589832 | tf_op jit(solution)/shard_map/ppermute | solution.py:497
  14.2 7.5 %collective-permute-start.7 = (bf16[128,768]{1,0:T(8,128)(2,1)S(1)}, bf16[128,768]{1,0:T(8,128)(2,1)S(1)}, u32[]{:S(2)}, u32[]{:S(2)}) collective-permute-start(bf16[128,768]{1,0:T(8,128)(2,1)S(1)} %collective-permute-done.1.refs_3_.refs_0_), channel_id=1, source_target_pairs={{0,8},{4,12},{8,0},{12,4},{16,24},{20,28},{24,16},{28,20},{1,9},{5... | collective-permute-start | bytes 589832 | tf_op jit(solution)/shard_map/ppermute | solution.py:479
  28.8 11.3 %collective-permute-start.12 = (bf16[128,768]{1,0:T(8,128)(2,1)S(1)}, bf16[128,768]{1,0:T(8,128)(2,1)S(1)}, u32[]{:S(2)}, u32[]{:S(2)}) collective-permute-start(bf16[128,768]{1,0:T(8,128)(2,1)S(1)} %get-tuple-element.47), channel_id=1, source_target_pairs={{0,2},{1,3},{2,0},{3,1},{4,6},{5,7},{6,4},{7,5},{8,10},{9,11},{10,... | collective-permute-start | bytes 589832 | tf_op jit(solution)/shard_map/ppermute | solution.py:476
  29.0 11.1 %collective-permute-start.13 = (bf16[128,768]{1,0:T(8,128)(2,1)S(1)}, bf16[128,768]{1,0:T(8,128)(2,1)S(1)}, u32[]{:S(2)}, u32[]{:S(2)}) collective-permute-start(bf16[128,768]{1,0:T(8,128)(2,1)S(1)} %get-tuple-element.48), channel_id=1, source_target_pairs={{0,3},{1,2},{2,1},{3,0},{4,7},{5,6},{6,5},{7,4},{8,11},{9,10},{10,... | collective-permute-start | bytes 589832 | tf_op jit(solution)/shard_map/ppermute | solution.py:476
  41.6 11.2 %collective-permute-start.16 = (bf16[128,1408]{1,0:T(8,128)(2,1)S(1)}, bf16[128,1408]{1,0:T(8,128)(2,1)S(1)}, u32[]{:S(2)}, u32[]{:S(2)}) collective-permute-start(bf16[128,1408]{1,0:T(8,128)(2,1)S(1)} %get-tuple-element.52), channel_id=1, source_target_pairs={{0,1},{1,0},{2,3},{3,2},{4,5},{5,4},{6,7},{7,6},{8,9},{9,8},{10,11... | collective-permute-start | bytes 1081352 | tf_op jit(solution)/shard_map/ppermute | solution.py:476
  41.7 18.4 %collective-permute-start.17 = (bf16[128,1408]{1,0:T(8,128)(2,1)S(1)}, bf16[128,1408]{1,0:T(8,128)(2,1)S(1)}, u32[]{:S(2)}, u32[]{:S(2)}) collective-permute-start(bf16[128,1408]{1,0:T(8,128)(2,1)S(1)} %get-tuple-element.53), channel_id=1, source_target_pairs={{0,2},{1,3},{2,0},{3,1},{4,6},{5,7},{6,4},{7,5},{8,10},{9,11},{10,... | collective-permute-start | bytes 1081352 | tf_op jit(solution)/shard_map/ppermute | solution.py:476
  43.4 16.8 %collective-permute-start.18 = (bf16[128,1408]{1,0:T(8,128)(2,1)S(1)}, bf16[128,1408]{1,0:T(8,128)(2,1)S(1)}, u32[]{:S(2)}, u32[]{:S(2)}) collective-permute-start(bf16[128,1408]{1,0:T(8,128)(2,1)S(1)} %get-tuple-element.54), channel_id=1, source_target_pairs={{0,3},{1,2},{2,1},{3,0},{4,7},{5,6},{6,5},{7,4},{8,11},{9,10},{10,... | collective-permute-start | bytes 1081352 | tf_op jit(solution)/shard_map/ppermute | solution.py:476
  64.1 12.1 %collective-permute-start.21 = (bf16[400,128]{1,0:T(8,128)(2,1)S(1)}, bf16[400,128]{1,0:T(8,128)(2,1)S(1)}, u32[]{:S(2)}, u32[]{:S(2)}) collective-permute-start(bf16[400,128]{1,0:T(8,128)(2,1)S(1)} %get-tuple-element.62), channel_id=1, source_target_pairs={{0,16},{4,20},{8,24},{12,28},{16,0},{20,4},{24,8},{28,12},{1,17},{... | collective-permute-start | bytes 307208 | tf_op jit(solution)/shard_map/ppermute | solution.py:479
  66.7 9.5 %collective-permute-start.22 = (bf16[400,128]{1,0:T(8,128)(2,1)S(1)}, bf16[400,128]{1,0:T(8,128)(2,1)S(1)}, u32[]{:S(2)}, u32[]{:S(2)}) collective-permute-start(bf16[400,128]{1,0:T(8,128)(2,1)S(1)} %get-tuple-element.63), channel_id=1, source_target_pairs={{0,8},{4,12},{8,0},{12,4},{16,24},{20,28},{24,16},{28,20},{1,9},{5... | collective-permute-start | bytes 307208 | tf_op jit(solution)/shard_map/ppermute | solution.py:479
  76.3 11.6 %collective-permute-start.26 = (bf16[4,128,768]{2,1,0:T(8,128)(2,1)S(1)}, bf16[4,128,768]{2,1,0:T(8,128)(2,1)S(1)}, u32[]{:S(2)}, u32[]{:S(2)}) collective-permute-start(bf16[4,128,768]{2,1,0:T(8,128)(2,1)S(1)} %get-tuple-element.71), channel_id=1, source_target_pairs={{0,4},{4,0},{8,12},{12,8},{16,20},{20,16},{24,28},{28,24},{1,5},{5... | collective-permute-start | bytes 2359304 | tf_op jit(solution)/shard_map/ppermute | solution.py:482
  76.4 7.7 %collective-permute-start.25 = (bf16[400,128]{1,0:T(8,128)(2,1)S(1)}, bf16[400,128]{1,0:T(8,128)(2,1)S(1)}, u32[]{:S(2)}, u32[]{:S(2)}) collective-permute-start(bf16[400,128]{1,0:T(8,128)(2,1)S(1)} %get-tuple-element.69.refs_0_), channel_id=1, source_target_pairs={{0,24},{4,28},{8,16},{12,20},{16,8},{20,12},{24,0},{28,4},{1,25},{... | collective-permute-start | bytes 307208 | tf_op jit(solution)/shard_map/ppermute | solution.py:479
  77.6 10.2 %collective-permute-start.24 = (bf16[400,128]{1,0:T(8,128)(2,1)S(1)}, bf16[400,128]{1,0:T(8,128)(2,1)S(1)}, u32[]{:S(2)}, u32[]{:S(2)}) collective-permute-start(bf16[400,128]{1,0:T(8,128)(2,1)S(1)} %get-tuple-element.69.refs_0_), channel_id=1, source_target_pairs={{0,16},{4,20},{8,24},{12,28},{16,0},{20,4},{24,8},{28,12},{1,17},{... | collective-permute-start | bytes 307208 | tf_op jit(solution)/shard_map/ppermute | solution.py:479
  77.6 10.2 %collective-permute-start.23 = (bf16[400,128]{1,0:T(8,128)(2,1)S(1)}, bf16[400,128]{1,0:T(8,128)(2,1)S(1)}, u32[]{:S(2)}, u32[]{:S(2)}) collective-permute-start(bf16[400,128]{1,0:T(8,128)(2,1)S(1)} %get-tuple-element.69.refs_0_), channel_id=1, source_target_pairs={{0,8},{4,12},{8,0},{12,4},{16,24},{20,28},{24,16},{28,20},{1,9},{5... | collective-permute-start | bytes 307208 | tf_op jit(solution)/shard_map/ppermute | solution.py:479
  88.1 11.1 %collective-permute-start.31 = (bf16[2,128,768]{2,1,0:T(8,128)(2,1)S(1)}, bf16[2,128,768]{2,1,0:T(8,128)(2,1)S(1)}, u32[]{:S(2)}, u32[]{:S(2)}) collective-permute-start(bf16[2,128,768]{2,1,0:T(8,128)(2,1)S(1)} %get-tuple-element.72.refs_4_), channel_id=1, source_target_pairs={{0,8},{4,12},{8,0},{12,4},{16,24},{20,28},{24,16},{28,20},{1,9},{5... | collective-permute-start | bytes 1179656 | tf_op jit(solution)/shard_map/ppermute | solution.py:479
  88.2 11.4 %collective-permute-start.28 = (bf16[4,400,128]{2,1,0:T(8,128)(2,1)S(1)}, bf16[4,400,128]{2,1,0:T(8,128)(2,1)S(1)}, u32[]{:S(2)}, u32[]{:S(2)}) collective-permute-start(bf16[4,400,128]{2,1,0:T(8,128)(2,1)S(1)} %shard_map.142.refs_0_), channel_id=1, source_target_pairs={{0,2},{1,3},{2,0},{3,1},{4,6},{5,7},{6,4},{7,5},{8,10},{9,11},{10,... | collective-permute-start | bytes 1228808 | tf_op jit(solution)/shard_map/ppermute | solution.py:476
  89.1 11.8 %collective-permute-start.27 = (bf16[4,400,128]{2,1,0:T(8,128)(2,1)S(1)}, bf16[4,400,128]{2,1,0:T(8,128)(2,1)S(1)}, u32[]{:S(2)}, u32[]{:S(2)}) collective-permute-start(bf16[4,400,128]{2,1,0:T(8,128)(2,1)S(1)} %shard_map.142.refs_0_), channel_id=1, source_target_pairs={{0,1},{1,0},{2,3},{3,2},{4,5},{5,4},{6,7},{7,6},{8,9},{9,8},{10,11... | collective-permute-start | bytes 1228808 | tf_op jit(solution)/shard_map/ppermute | solution.py:476
  99.2 11.1 %collective-permute-start.32 = (bf16[1,128,768]{2,1,0:T(8,128)(2,1)S(1)}, bf16[1,128,768]{2,1,0:T(8,128)(2,1)S(1)}, u32[]{:S(2)}, u32[]{:S(2)}) collective-permute-start(bf16[1,128,768]{2,1,0:T(8,128)(2,1)S(1)} %get-tuple-element.75), channel_id=1, source_target_pairs={{0,16},{4,20},{8,24},{12,28},{16,0},{20,4},{24,8},{28,12},{1,17},{... | collective-permute-start | bytes 589832 | tf_op jit(solution)/shard_map/ppermute | solution.py:479
  99.6 13.9 %collective-permute-start.33 = (bf16[4,400,128]{2,1,0:T(8,128)(2,1)S(1)}, bf16[4,400,128]{2,1,0:T(8,128)(2,1)S(1)}, u32[]{:S(2)}, u32[]{:S(2)}) collective-permute-start(bf16[4,400,128]{2,1,0:T(8,128)(2,1)S(1)} %shard_map.142.refs_0_), channel_id=1, source_target_pairs={{0,4},{4,0},{8,12},{12,8},{16,20},{20,16},{24,28},{28,24},{1,5},{5... | collective-permute-start | bytes 1228808 | tf_op jit(solution)/shard_map/ppermute | solution.py:482
  99.6 10.7 %collective-permute-start.30 = (bf16[2,400,128]{2,1,0:T(8,128)(2,1)S(1)}, bf16[2,400,128]{2,1,0:T(8,128)(2,1)S(1)}, u32[]{:S(2)}, u32[]{:S(2)}) collective-permute-start(bf16[2,400,128]{2,1,0:T(8,128)(2,1)S(1)} %slice.15), channel_id=1, source_target_pairs={{0,1},{1,0},{2,3},{3,2},{4,5},{5,4},{6,7},{7,6},{8,9},{9,8},{10,11... | collective-permute-start | bytes 614408 | tf_op jit(solution)/shard_map/ppermute | solution.py:476
  100.9 10.0 %collective-permute-start.29 = (bf16[2,400,128]{2,1,0:T(8,128)(2,1)S(1)}, bf16[2,400,128]{2,1,0:T(8,128)(2,1)S(1)}, u32[]{:S(2)}, u32[]{:S(2)}) collective-permute-start(bf16[2,400,128]{2,1,0:T(8,128)(2,1)S(1)} %slice.14), channel_id=1, source_target_pairs={{0,2},{1,3},{2,0},{3,1},{4,6},{5,7},{6,4},{7,5},{8,10},{9,11},{10,... | collective-permute-start | bytes 614408 | tf_op jit(solution)/shard_map/ppermute | solution.py:476
  101.8 11.7 %collective-permute-start.35 = (bf16[4,400,128]{2,1,0:T(8,128)(2,1)S(1)}, bf16[4,400,128]{2,1,0:T(8,128)(2,1)S(1)}, u32[]{:S(2)}, u32[]{:S(2)}) collective-permute-start(bf16[4,400,128]{2,1,0:T(8,128)(2,1)S(1)} %collective-permute-done.28.refs_2_), channel_id=1, source_target_pairs={{0,4},{4,0},{8,12},{12,8},{16,20},{20,16},{24,28},{28,24},{1,5},{5... | collective-permute-start | bytes 1228808 | tf_op jit(solution)/shard_map/ppermute | solution.py:482
  (22 other events, 100.2 us)
